TPU v7x, 32 devices: a whole 2x2x4 slice. The times are simulated.
32 devices in a mesh: dp: 4 (over y, x), fsdp: 8 (over z, core).
Axes of the slice: x: 2, y: 2, z: 4, core: 2. Of those that a mesh axis runs over, the one named last changes fastest.
Arguments:
- tokens: bfloat16 [4864, 1024], P(('dp', 'fsdp')), may hold values from -6 to 6
- pos_table: bfloat16 [145, 1024], P(None, 'fsdp'), may hold values from -3 to 3
- index_lo: int32 [50, 4], replicated, may hold values from 0 to 144
- index_hi: int32 [145, 4], replicated, may hold values from 0 to 144
- resolution: int32 [4], replicated, may hold values from 0 to 1, as said below
- gain_attn: bfloat16 [2, 1024], P(None, 'fsdp'), may hold values from 0.099609375 to 1.8984375
- w_qkv: bfloat16 [2, 1024, 3072], P(None, 'fsdp'), may hold values from -0.1875 to 0.1875
- w_out: bfloat16 [2, 1024, 1024], P(None, 'fsdp'), may hold values from -0.75 to 0.75
- gain_mlp: bfloat16 [2, 1024], P(None, 'fsdp'), may hold values from 0.099609375 to 1.8984375
- w_up: bfloat16 [2, 1024, 4096], P(None, 'fsdp'), may hold values from -0.1875 to 0.1875
- w_down: bfloat16 [2, 4096, 1024], P(None, 'fsdp'), may hold values from -0.09375 to 0.09375
- cotangent: bfloat16 [4864, 1024], P(('dp', 'fsdp')), may hold values from -6 to 6
Outputs:
- output: float32 [4864, 1024], P(('dp', 'fsdp'))
- d_tokens: float32 [4864, 1024], P(('dp', 'fsdp'))
- d_pos_table: float32 [145, 1024], P(None, 'fsdp')
- d_gain_attn: float32 [2, 1024], P(None, 'fsdp')
- d_w_qkv: float32 [2, 1024, 3072], P(None, 'fsdp')
- d_w_out: float32 [2, 1024, 1024], P(None, 'fsdp')
- d_gain_mlp: float32 [2, 1024], P(None, 'fsdp')
- d_w_up: float32 [2, 1024, 4096], P(None, 'fsdp')
- d_w_down: float32 [2, 4096, 1024], P(None, 'fsdp')
Inputs may be any that keep to these rules, and one draw needn't show every extreme that they name: 1 marks a group of the higher resolution (145 tokens an image), 0 one of the lower (50); both occur in every draw.
All inputs are finite; a program needn't handle non-finite values.
Results may differ from a plain program's by a relative error of at most 0.025.
Values may be sent and summed in bfloat16 or wider, within the bound.
No kernel may reach another device: no remote copies, remote signals or barrier semaphores. Data moves between devices by JAX's collectives and lax.ppermute only.
A program may use at most 320 MiB of HBM per device.

v0:
```python
import math

import jax
import jax.numpy as jnp
from jax import lax
from jax.sharding import PartitionSpec as P

HEADS = 16


EPS = 1e-06
NEG_FILL = -1e30
MIX_WEIGHTS = (0.5, 0.25, 0.125, 0.125)


def shortened(value):
    return jax.tree.map(lambda a: a.astype(jnp.bfloat16) if a.dtype == jnp.float32 else a, value)


def layer_norm(hidden, gain_row):
    row_mean = jnp.mean(hidden, axis=-1, keepdims=True)
    center = hidden - row_mean
    spread = jnp.mean(center * center, axis=-1, keepdims=True)
    return center * lax.rsqrt(spread + EPS) * gain_row


def gelu_exact(pre_act):
    return jax.nn.gelu(pre_act, approximate=False)


def fetch_attention(w_qkv, w_out, depth):
    return (
        lax.all_gather(w_qkv[depth], "fsdp", axis=0, tiled=True),
        lax.all_gather(w_out[depth], "fsdp", axis=0, tiled=True),
    )


def fetch_mlp(w_up, w_down, depth):
    return (
        lax.all_gather(w_up[depth], "fsdp", axis=0, tiled=True),
        lax.all_gather(w_down[depth], "fsdp", axis=0, tiled=True),
    )


def masked_scores(queries, key_rows, same_image, score_scale):
    scores = (
        jnp.einsum("qhd,khd->hqk", queries, key_rows, preferred_element_type=jnp.float32)
        * score_scale
    )
    return jnp.where(same_image[None], scores, NEG_FILL)


def group_total(shares):
    return jax.tree.map(lambda part: part.astype(jnp.float32), lax.psum(shortened(shares), "dp"))


def local(
    tokens,
    pos_table,
    index_lo,
    index_hi,
    resolution,
    gain_attn,
    w_qkv,
    w_out,
    gain_mlp,
    w_up,
    w_down,
    cotangent,
):
    row_count, model_width = tokens.shape
    layers = w_qkv.shape[0]
    head_size = model_width // HEADS
    score_scale = 1.0 / math.sqrt(head_size)
    len_low = index_lo.shape[0]
    len_high = index_hi.shape[0]
    group_flag = resolution[lax.axis_index("dp")]
    length = jnp.where(group_flag == 1, len_high, len_low).astype(jnp.int32)
    image_count = jnp.where(group_flag == 1, row_count // len_high, row_count // len_low).astype(
        jnp.int32
    )
    row_ids = jnp.arange(row_count, dtype=jnp.int32)
    live_rows = row_ids < image_count * length
    image_ids = jnp.where(live_rows, row_ids // length, image_count)
    same_image = image_ids[:, None] == image_ids[None, :]
    picked = jnp.where(group_flag == 1, index_hi[row_ids % len_high], index_lo[row_ids % len_low])
    table_ids = jnp.arange(len_high, dtype=jnp.int32)
    mixing = jnp.zeros((row_count, len_high), jnp.float32)
    for slot in range(4):
        mixing = mixing + MIX_WEIGHTS[slot] * (
            picked[:, slot : slot + 1] == table_ids[None, :]
        ).astype(jnp.float32)
    mixing = mixing * live_rows[:, None].astype(jnp.float32)
    group_count = resolution.shape[0]
    shard_count = lax.axis_size("fsdp")
    high_groups = jnp.sum(resolution)
    tokens_low = (
        (group_count - high_groups) * shard_count * (row_count // len_low) * len_low
    ).astype(jnp.float32)
    tokens_high = (high_groups * shard_count * (row_count // len_high) * len_high).astype(
        jnp.float32
    )
    token_share = (
        2.0 * jnp.where(group_flag == 1, tokens_high, tokens_low) / (tokens_low + tokens_high)
    )
    weight = jnp.where(live_rows, token_share, 0.0)
    small_local = jnp.concatenate([gain_attn, gain_mlp, pos_table], axis=0)
    small_full, first_qkv, first_out = (
        lax.all_gather(small_local, "fsdp", axis=1, tiled=True),
        lax.all_gather(w_qkv[0], "fsdp", axis=0, tiled=True),
        lax.all_gather(w_out[0], "fsdp", axis=0, tiled=True),
    )
    gains_a = small_full[:layers].astype(jnp.float32)
    gains_m = small_full[layers : 2 * layers].astype(jnp.float32)
    table = small_full[2 * layers :]
    hidden = tokens.astype(jnp.float32) + jnp.dot(
        mixing.astype(jnp.bfloat16), table, preferred_element_type=jnp.float32
    )
    saved = []
    for depth in range(layers):
        if depth == 0:
            attn_w = (first_qkv, first_out)
        else:
            attn_w = fetch_attention(w_qkv, w_out, depth)
        mlp_w = fetch_mlp(w_up, w_down, depth)
        normed_attn = layer_norm(hidden, gains_a[depth]).astype(jnp.bfloat16)
        projected = jnp.dot(normed_attn, attn_w[0], preferred_element_type=jnp.float32).astype(
            jnp.bfloat16
        )
        queries = projected[:, :model_width].reshape(row_count, HEADS, head_size)
        key_rows = projected[:, model_width : 2 * model_width].reshape(row_count, HEADS, head_size)
        values = projected[:, 2 * model_width :].reshape(row_count, HEADS, head_size)
        scores = masked_scores(queries, key_rows, same_image, score_scale)
        row_max = jnp.max(scores, axis=-1, keepdims=True)
        powers = jnp.exp(scores - row_max)
        row_total = jnp.sum(powers, axis=-1, keepdims=True)
        log_total = row_max + jnp.log(row_total)
        probs = (powers / row_total).astype(jnp.bfloat16)
        attended = jnp.einsum("hqk,khd->qhd", probs, values, preferred_element_type=jnp.float32)
        attended = attended.reshape(row_count, model_width).astype(jnp.bfloat16)
        middle = hidden + jnp.dot(attended, attn_w[1], preferred_element_type=jnp.float32)
        normed_mlp = layer_norm(middle, gains_m[depth]).astype(jnp.bfloat16)
        pre_act = jnp.dot(normed_mlp, mlp_w[0], preferred_element_type=jnp.float32)
        activated = gelu_exact(pre_act).astype(jnp.bfloat16)
        result = middle + jnp.dot(activated, mlp_w[1], preferred_element_type=jnp.float32)
        saved.append(
            (
                hidden,
                normed_attn,
                queries,
                key_rows,
                values,
                log_total,
                attended,
                middle,
                normed_mlp,
                pre_act,
                activated,
                attn_w,
                mlp_w,
            )
        )
        hidden = result
    gradient = cotangent.astype(jnp.float32) * weight[:, None]
    gain_a_terms = [None] * layers
    gain_m_terms = [None] * layers
    mlp_shares = [None] * layers
    attn_shares = [None] * layers
    first_terms = None
    for depth in reversed(range(layers)):
        (
            hidden_in,
            normed_attn,
            queries,
            key_rows,
            values,
            log_total,
            attended,
            middle,
            normed_mlp,
            pre_act,
            activated,
            attn_kept,
            mlp_kept,
        ) = saved[depth]
        mlp_w = mlp_kept
        attn_w = attn_kept
        d_result = gradient.astype(jnp.bfloat16)
        grad_down = jnp.dot(activated.T, d_result, preferred_element_type=jnp.float32)
        d_activated = jnp.dot(d_result, mlp_w[1].T, preferred_element_type=jnp.float32)
        _, pullback = jax.vjp(gelu_exact, pre_act)
        d_pre = pullback(d_activated)[0].astype(jnp.bfloat16)
        grad_up = jnp.dot(normed_mlp.T, d_pre, preferred_element_type=jnp.float32)
        d_normed_mlp = jnp.dot(d_pre, mlp_w[0].T, preferred_element_type=jnp.float32)
        _, pullback = jax.vjp(layer_norm, middle, gains_m[depth])
        d_middle_part, gain_m_terms[depth] = pullback(d_normed_mlp)
        d_middle = gradient + d_middle_part
        up_share, down_share = (
            lax.psum_scatter(
                grad_up.astype(jnp.bfloat16), "fsdp", scatter_dimension=0, tiled=True
            ).astype(jnp.float32),
            lax.psum_scatter(
                grad_down.astype(jnp.bfloat16), "fsdp", scatter_dimension=0, tiled=True
            ).astype(jnp.float32),
        )
        mlp_shares[depth] = group_total((up_share, down_share))
        d_attn = d_middle.astype(jnp.bfloat16)
        grad_out = jnp.dot(attended.T, d_attn, preferred_element_type=jnp.float32)
        d_attended = jnp.dot(d_attn, attn_w[1].T, preferred_element_type=jnp.float32)
        d_attended = d_attended.astype(jnp.bfloat16).reshape(row_count, HEADS, head_size)
        scores = masked_scores(queries, key_rows, same_image, score_scale)
        probs = jnp.exp(scores - log_total)
        d_values = jnp.einsum(
            "hqk,qhd->khd",
            probs.astype(jnp.bfloat16),
            d_attended,
            preferred_element_type=jnp.float32,
        )
        d_probs = jnp.einsum("qhd,khd->hqk", d_attended, values, preferred_element_type=jnp.float32)
        centre = jnp.sum(probs * d_probs, axis=-1, keepdims=True)
        d_scores = (probs * (d_probs - centre)).astype(jnp.bfloat16)
        d_queries = (
            jnp.einsum("hqk,khd->qhd", d_scores, key_rows, preferred_element_type=jnp.float32)
            * score_scale
        )
        d_keys = (
            jnp.einsum("hqk,qhd->khd", d_scores, queries, preferred_element_type=jnp.float32)
            * score_scale
        )
        d_projected = jnp.concatenate(
            [
                d_queries.reshape(row_count, model_width),
                d_keys.reshape(row_count, model_width),
                d_values.reshape(row_count, model_width),
            ],
            axis=1,
        ).astype(jnp.bfloat16)
        grad_qkv = jnp.dot(normed_attn.T, d_projected, preferred_element_type=jnp.float32)
        d_normed_attn = jnp.dot(d_projected, attn_w[0].T, preferred_element_type=jnp.float32)
        _, pullback = jax.vjp(layer_norm, hidden_in, gains_a[depth])
        d_input_part, gain_a_terms[depth] = pullback(d_normed_attn)
        gradient = d_middle + d_input_part
        if depth > 0:
            qkv_share, out_share = (
                lax.psum_scatter(
                    grad_qkv.astype(jnp.bfloat16), "fsdp", scatter_dimension=0, tiled=True
                ).astype(jnp.float32),
                lax.psum_scatter(
                    grad_out.astype(jnp.bfloat16), "fsdp", scatter_dimension=0, tiled=True
                ).astype(jnp.float32),
            )
            attn_shares[depth] = group_total((qkv_share, out_share))
        else:
            first_terms = (grad_qkv, grad_out)
    table_term = jnp.dot(mixing.T, gradient, precision=lax.Precision.HIGHEST)
    small_terms = jnp.concatenate(
        [jnp.stack(gain_a_terms), jnp.stack(gain_m_terms), table_term], axis=0
    )
    small_share, qkv_first, out_first = (
        lax.psum_scatter(
            small_terms.astype(jnp.bfloat16), "fsdp", scatter_dimension=1, tiled=True
        ).astype(jnp.float32),
        lax.psum_scatter(
            first_terms[0].astype(jnp.bfloat16), "fsdp", scatter_dimension=0, tiled=True
        ).astype(jnp.float32),
        lax.psum_scatter(
            first_terms[1].astype(jnp.bfloat16), "fsdp", scatter_dimension=0, tiled=True
        ).astype(jnp.float32),
    )
    small_share, qkv_first, out_first = group_total((small_share, qkv_first, out_first))
    attn_shares[0] = (qkv_first, out_first)
    d_w_qkv = jnp.stack([attn_shares[depth][0] for depth in range(layers)])
    d_w_out = jnp.stack([attn_shares[depth][1] for depth in range(layers)])
    d_w_up = jnp.stack([mlp_shares[depth][0] for depth in range(layers)])
    d_w_down = jnp.stack([mlp_shares[depth][1] for depth in range(layers)])
    d_gain_attn = small_share[:layers]
    d_gain_mlp = small_share[layers : 2 * layers]
    d_pos_table = small_share[2 * layers :]
    return (
        hidden,
        gradient,
        d_pos_table,
        d_gain_attn,
        d_w_qkv,
        d_w_out,
        d_gain_mlp,
        d_w_up,
        d_w_down,
    )


def solution(mesh):
    in_specs = (
        P(("dp", "fsdp"), None),
        P(None, "fsdp"),
        P(),
        P(),
        P(),
        P(None, "fsdp"),
        P(None, "fsdp", None),
        P(None, "fsdp", None),
        P(None, "fsdp"),
        P(None, "fsdp", None),
        P(None, "fsdp", None),
        P(("dp", "fsdp"), None),
    )
    out_specs = (
        P(("dp", "fsdp"), None),
        P(("dp", "fsdp"), None),
        P(None, "fsdp"),
        P(None, "fsdp"),
        P(None, "fsdp", None),
        P(None, "fsdp", None),
        P(None, "fsdp"),
        P(None, "fsdp", None),
        P(None, "fsdp", None),
    )
    return jax.shard_map(local, mesh=mesh, in_specs=in_specs, out_specs=out_specs, check_vma=False)
```

profile of v0, /device:TPU:0, one launch (start us, length us, event | category | flops | bytes accessed | tf_op | source)
XLA Modules:
  0.0 1335.1 jit_solution(12301756220912282719)
XLA Ops:
  7.2 2.8 fusion.138
  12.6 3.0 fusion.136
  23.9 17.2 %all_gather.27 = bf16[149,1024]{1,0:T(8,128)(2,1)S(1)} all-gather(bf16[149,128]{1,0:T(8,128)(2,1)S(1)} %pad_maximum_fusion.6), channel_id=1, replica_groups=mesh['dp'=4,'fsdp'=8] {'fsdp'}, dimensions={1}, use_global_device_ids=true | all-gather | bytes 343296 | tf_op jit(solution)/shard_map/all_gather | solution.py:109
  42.4 37.6 %all-gather.17.cloned.1.call-done = bf16[1,1024,3072]{2,1,0:T(8,128)(2,1)} async-done(((bf16[1,128,3072]{2,1,0:T(8,128)(2,1)}), bf16[1,1024,3072]{2,1,0:T(8,128)(2,1)}) %all-gather.17.cloned.1.call-update) | async-done | bytes 6291472 | tf_op jit(solution)/shard_map/all_gather | solution.py:110
  80.1 4.0 fusion.24
  90.1 19.9 %all-gather.19.cloned.1.call-done = bf16[1,1024,1024]{2,1,0:T(8,128)(2,1)} async-done(((bf16[1,128,1024]{2,1,0:T(8,128)(2,1)}), bf16[1,1024,1024]{2,1,0:T(8,128)(2,1)}) %all-gather.19.cloned.1.call-update) | async-done | bytes 2097168 | tf_op jit(solution)/shard_map/all_gather | solution.py:111
  110.1 2.5 fusion.147
  112.8 81.0 %all-gather.21.cloned.1.call-done = bf16[1,1024,4096]{2,1,0:T(8,128)(2,1)} async-done(((bf16[1,128,4096]{2,1,0:T(8,128)(2,1)}), bf16[1,1024,4096]{2,1,0:T(8,128)(2,1)}) %all-gather.21.cloned.1.call-update) | async-done | bytes 8388624 | tf_op jit(solution)/shard_map/all_gather | solution.py:40
  193.8 10.8 multiply_convert_fusion.3
  204.7 71.8 %all-gather.23.cloned.1.call-done = bf16[1,4096,1024]{2,1,0:T(8,128)(2,1)} async-done(((bf16[1,512,1024]{2,1,0:T(8,128)(2,1)}), bf16[1,4096,1024]{2,1,0:T(8,128)(2,1)}) %all-gather.23.cloned.1.call-update) | async-done | bytes 8388624 | tf_op jit(solution)/shard_map/all_gather | solution.py:41
  276.5 5.3 fusion.148
  282.9 59.0 %all-gather.25.cloned.1.call-done = bf16[1,1024,3072]{2,1,0:T(8,128)(2,1)} async-done(((bf16[1,128,3072]{2,1,0:T(8,128)(2,1)}), bf16[1,1024,3072]{2,1,0:T(8,128)(2,1)}) %all-gather.25.cloned.1.call-update) | async-done | bytes 6291472 | tf_op jit(solution)/shard_map/all_gather | solution.py:33
  341.9 4.2 fusion.27
  348.1 2.2 copy.113
  356.0 15.1 %all-gather.27.cloned.1.call-done = bf16[1,1024,1024]{2,1,0:T(8,128)(2,1)} async-done(((bf16[1,128,1024]{2,1,0:T(8,128)(2,1)}), bf16[1,1024,1024]{2,1,0:T(8,128)(2,1)}) %all-gather.27.cloned.1.call-update) | async-done | bytes 2097168 | tf_op jit(solution)/shard_map/all_gather | solution.py:34
  371.1 2.5 fusion.150
  373.8 81.0 %all-gather.29.cloned.1.call-done = bf16[1,1024,4096]{2,1,0:T(8,128)(2,1)} async-done(((bf16[1,128,4096]{2,1,0:T(8,128)(2,1)}), bf16[1,1024,4096]{2,1,0:T(8,128)(2,1)}) %all-gather.29.cloned.1.call-update) | async-done | bytes 8388624 | tf_op jit(solution)/shard_map/all_gather | solution.py:40
  454.8 10.4 multiply_convert_fusion.2
  465.3 71.8 %all-gather.31.cloned.1.call-done = bf16[1,4096,1024]{2,1,0:T(8,128)(2,1)} async-done(((bf16[1,512,1024]{2,1,0:T(8,128)(2,1)}), bf16[1,4096,1024]{2,1,0:T(8,128)(2,1)}) %all-gather.31.cloned.1.call-update) | async-done | bytes 8388624 | tf_op jit(solution)/shard_map/all_gather | solution.py:41
  537.1 11.0 add_convert_fusion.1
  548.1 3.6 multiply_reduce_fusion.2
  555.7 3.3 fusion.81
  561.0 3.3 convolution_convert_fusion.9
  568.7 6.5 multiply_reduce_fusion.4
  577.1 8.7 add_convert_fusion
  585.9 3.6 multiply_reduce_fusion.3
  592.9 3.4 fusion.78
  604.0 4.7 convolution_convert_fusion.5
  610.3 4.6 convolution_convert_fusion.4
  616.4 5.8 convolution_convert_fusion.3
  623.5 5.8 convolution_convert_fusion.2
  630.7 5.7 convolution_convert_fusion.1
  637.7 5.7 convolution_convert_fusion
  646.1 5.7 multiply_reduce_fusion.5
  655.0 55.7 %reduce-scatter.12.cloned.1.call-done = bf16[128,3072]{1,0:T(8,128)(2,1)} async-done(((bf16[1024,3072]{1,0:T(8,128)(2,1)}), bf16[128,3072]{1,0:T(8,128)(2,1)}) %reduce-scatter.12.cloned.1.call-update) | async-done | bytes 786448 | tf_op jit(solution)/shard_map/reduce_scatter | solution.py:263
  710.7 70.3 %reduce-scatter.14.cloned.1.call-done = bf16[128,3072]{1,0:T(8,128)(2,1)} async-done(((bf16[1024,3072]{1,0:T(8,128)(2,1)}), bf16[128,3072]{1,0:T(8,128)(2,1)}) %reduce-scatter.14.cloned.1.call-update) | async-done | bytes 786448 | tf_op jit(solution)/shard_map/reduce_scatter | solution.py:245
  781.1 90.3 %reduce-scatter.20.cloned.1.call-done = bf16[128,4096]{1,0:T(8,128)(2,1)} async-done(((bf16[1024,4096]{1,0:T(8,128)(2,1)}), bf16[128,4096]{1,0:T(8,128)(2,1)}) %reduce-scatter.20.cloned.1.call-update) | async-done | bytes 1048592 | tf_op jit(solution)/shard_map/reduce_scatter | solution.py:199
  871.4 90.1 %reduce-scatter.22.cloned.1.call-done = bf16[128,4096]{1,0:T(8,128)(2,1)} async-done(((bf16[1024,4096]{1,0:T(8,128)(2,1)}), bf16[128,4096]{1,0:T(8,128)(2,1)}) %reduce-scatter.22.cloned.1.call-update) | async-done | bytes 1048592 | tf_op jit(solution)/shard_map/reduce_scatter | solution.py:199
  961.5 90.1 %reduce-scatter.24.cloned.1.call-done = bf16[512,1024]{1,0:T(8,128)(2,1)} async-done(((bf16[4096,1024]{1,0:T(8,128)(2,1)}), bf16[512,1024]{1,0:T(8,128)(2,1)}) %reduce-scatter.24.cloned.1.call-update) | async-done | bytes 1048592 | tf_op jit(solution)/shard_map/reduce_scatter | solution.py:202
  1051.6 90.1 %reduce-scatter.26.cloned.1.call-done = bf16[512,1024]{1,0:T(8,128)(2,1)} async-done(((bf16[4096,1024]{1,0:T(8,128)(2,1)}), bf16[512,1024]{1,0:T(8,128)(2,1)}) %reduce-scatter.26.cloned.1.call-update) | async-done | bytes 1048592 | tf_op jit(solution)/shard_map/reduce_scatter | solution.py:202
  1141.8 5.7 fusion.75
  1147.5 26.3 %reduce-scatter.28.cloned.1.call-done = bf16[128,149]{1,0:T(8,128)(2,1)} async-done(((bf16[1024,149]{1,0:T(8,128)(2,1)}), bf16[128,149]{1,0:T(8,128)(2,1)}) %reduce-scatter.28.cloned.1.call-update) | async-done | bytes 38160
  1174.7 17.4 %psum.63 = bf16[149,128]{1,0:T(8,128)(2,1)S(1)} all-reduce(bf16[149,128]{1,0:T(8,128)(2,1)S(1)} %copy.108), channel_id=1, replica_groups=mesh['dp'=4,'fsdp'=8] {'dp'}, use_global_device_ids=true, to_apply=%region_28.29 | all-reduce | flops 19072 | bytes 76288 | tf_op jit(solution)/shard_map/psum | solution.py:54
  1193.3 124.7 %all-reduce.3.cloned.1.call-done = (bf16[1,128,3072]{2,1,0:T(8,128)(2,1)}, bf16[1,128,3072]{2,1,0:T(8,128)(2,1)}, bf16[1,128,1024]{2,1,0:T(8,128)(2,1)}, bf16[1,...) async-done(((bf16[1,128,3072]{2,1,0:T(8,128)(2,1)}, ...) | async-done | bytes 6291472 | tf_op jit(solution)/shard_map/psum | solution.py:54
  1318.0 2.1 maximum_convert_fusion.3
  1320.0 3.4 maximum_convert_fusion.2
  1323.4 2.3 maximum_convert_fusion
  1325.8 2.3 maximum_convert_fusion.1
  (292 shorter events, 63.1 us)
Async XLA Ops:
  7.2 3.8 copy-start.39
  7.2 72.9 %all-gather.17.cloned.1.call-start = ((), (), s32[]{:S(2)}) async-start(), calls=%async_computation.17 | async-start | bytes 7077888 | tf_op jit(solution)/shard_map/all_gather | solution.py:110
  10.1 100.0 %all-gather.19.cloned.1.call-start = ((), (), s32[]{:S(2)}) async-start(), calls=%async_computation.18 | async-start | bytes 2359296 | tf_op jit(solution)/shard_map/all_gather | solution.py:111
  11.0 182.9 %all-gather.21.cloned.1.call-start = ((), (), s32[]{:S(2)}) async-start(), calls=%async_computation.19 | async-start | bytes 9437184 | tf_op jit(solution)/shard_map/all_gather | solution.py:40
  12.5 264.0 %all-gather.23.cloned.1.call-start = ((), (), s32[]{:S(2)}) async-start(), calls=%async_computation.20 | async-start | bytes 9437184 | tf_op jit(solution)/shard_map/all_gather | solution.py:41
  15.6 6.0 copy-start.70
  15.6 6.1 copy-start.61
  15.6 7.8 copy-start.54
  15.6 7.8 copy-start.73
  15.6 7.8 copy-start.74
  15.6 326.2 %all-gather.25.cloned.1.call-start = ((), (), s32[]{:S(2)}) async-start(), calls=%async_computation.21 | async-start | bytes 7077888 | tf_op jit(solution)/shard_map/all_gather | solution.py:33
  16.2 24.8 %copy-start.75 = (bf16[152,1024]{1,0:T(8,128)(2,1)S(1)}, bf16[152,1024]{1,0:T(8,128)(2,1)}, u32[]{:S(2)}) copy-start(bf16[152,1024]{1,0:T(8,128)(2,1)} %param.12) | copy-start | bytes 933892
  16.2 354.8 %all-gather.27.cloned.1.call-start = ((), (), s32[]{:S(2)}) async-start(), calls=%async_computation.22 | async-start | bytes 2359296 | tf_op jit(solution)/shard_map/all_gather | solution.py:34
  16.8 438.0 %all-gather.29.cloned.1.call-start = ((), (), s32[]{:S(2)}) async-start(), calls=%async_computation.23 | async-start | bytes 9437184 | tf_op jit(solution)/shard_map/all_gather | solution.py:40
  17.6 519.5 %all-gather.31.cloned.1.call-start = ((), (), s32[]{:S(2)}) async-start(), calls=%async_computation.24 | async-start | bytes 9437184 | tf_op jit(solution)/shard_map/all_gather | solution.py:41
  18.3 636.6 %reduce-scatter.18.cloned.1.call-start = ((), (), s32[]{:S(2)}) async-start(), calls=%async_computation.12 | async-start | bytes 2359296 | tf_op jit(solution)/shard_map/reduce_scatter | solution.py:248
  23.3 60.8 %copy-start.71 = (f32[152]{0:T(256)}, f32[152]{0:T(256)S(1)}, u32[]{:S(2)}) copy-start(f32[152]{0:T(256)S(1)} %fusion.115) | copy-start | bytes 1828
  23.8 60.3 %copy-start.62 = (s32[152]{0:T(256)}, s32[152]{0:T(256)S(1)}, u32[]{:S(2)}) copy-start(s32[152]{0:T(256)S(1)} %get-tuple-element.17) | copy-start | bytes 1828
  23.8 60.3 %copy-start.64 = (s32[152]{0:T(256)}, s32[152]{0:T(256)S(1)}, u32[]{:S(2)}) copy-start(s32[152]{0:T(256)S(1)} %get-tuple-element.18) | copy-start | bytes 1828
  23.8 60.3 %copy-start.66 = (s32[152]{0:T(256)}, s32[152]{0:T(256)S(1)}, u32[]{:S(2)}) copy-start(s32[152]{0:T(256)S(1)} %get-tuple-element.19) | copy-start | bytes 1828
  23.8 60.3 %copy-start.68 = (s32[152]{0:T(256)}, s32[152]{0:T(256)S(1)}, u32[]{:S(2)}) copy-start(s32[152]{0:T(256)S(1)} %get-tuple-element.20) | copy-start | bytes 1828
  41.5 42.6 %copy-start.8 = (f32[152,1024]{1,0:T(8,128)}, f32[152,1024]{1,0:T(8,128)S(1)}, u32[]{:S(2)}) copy-start(f32[152,1024]{1,0:T(8,128)S(1)} %get-tuple-element.60) | copy-start | bytes 1867780
  41.8 561.5 %copy-start.56 = (f32[152]{0:T(256)}, f32[152]{0:T(256)S(1)}, u32[]{:S(2)}) copy-start(f32[152]{0:T(256)S(1)} %fusion.116) | copy-start | bytes 1828
  112.5 163.9 %copy-start.2 = (f32[152,1024]{1,0:T(8,128)}, f32[152,1024]{1,0:T(8,128)S(1)}, u32[]{:S(2)}) copy-start(f32[152,1024]{1,0:T(8,128)S(1)} %get-tuple-element.64) | copy-start | bytes 1867780
  348.1 4.9 copy-start.29
  454.8 82.2 %copy-start.32 = (bf16[152,1024]{1,0:T(8,128)(2,1)S(1)}, bf16[152,1024]{1,0:T(8,128)(2,1)}, u32[]{:S(2)}) copy-start(bf16[152,1024]{1,0:T(8,128)(2,1)} %param.23) | copy-start | bytes 933892
  537.1 11.0 copy-start.15
  568.6 86.4 %reduce-scatter.16.cloned.1.call-start = ((), (), s32[]{:S(2)}) async-start(), calls=%async_computation.11 | async-start | bytes 2359296 | tf_op jit(solution)/shard_map/reduce_scatter | solution.py:266
  568.7 7.1 slice-start
  568.7 6.5 copy-start.6
  568.7 6.8 copy-start.19
  568.7 7.1 slice-start.1
  575.2 10.6 slice-start.2
  575.8 14.0 %copy-start.16 = (f32[152,1024]{1,0:T(8,128)}, f32[152,1024]{1,0:T(8,128)S(1)}, u32[]{:S(2)}) copy-start(f32[152,1024]{1,0:T(8,128)S(1)} %add_add_fusion.6) | copy-start | bytes 1867780
  577.1 8.7 copy-start.3
  577.1 8.7 slice-start.3
  592.8 117.9 %reduce-scatter.12.cloned.1.call-start = ((), (), s32[]{:S(2)}) async-start(), calls=%async_computation.9 | async-start | bytes 7077888 | tf_op jit(solution)/shard_map/reduce_scatter | solution.py:263
  608.7 172.3 %reduce-scatter.14.cloned.1.call-start = ((), (), s32[]{:S(2)}) async-start(), calls=%async_computation.10 | async-start | bytes 7077888 | tf_op jit(solution)/shard_map/reduce_scatter | solution.py:245
  614.9 256.5 %reduce-scatter.20.cloned.1.call-start = ((), (), s32[]{:S(2)}) async-start(), calls=%async_computation.13 | async-start | bytes 9437184 | tf_op jit(solution)/shard_map/reduce_scatter | solution.py:199
  622.2 339.3 %reduce-scatter.22.cloned.1.call-start = ((), (), s32[]{:S(2)}) async-start(), calls=%async_computation.14 | async-start | bytes 9437184 | tf_op jit(solution)/shard_map/reduce_scatter | solution.py:199
  629.3 422.4 %reduce-scatter.24.cloned.1.call-start = ((), (), s32[]{:S(2)}) async-start(), calls=%async_computation.15 | async-start | bytes 9437184 | tf_op jit(solution)/shard_map/reduce_scatter | solution.py:202
  636.4 505.3 %reduce-scatter.26.cloned.1.call-start = ((), (), s32[]{:S(2)}) async-start(), calls=%async_computation.16 | async-start | bytes 9437184 | tf_op jit(solution)/shard_map/reduce_scatter | solution.py:202
  643.5 530.3 %reduce-scatter.28.cloned.1.call-start = ((), (), s32[]{:S(2)}) async-start(), calls=%async_computation.25 | async-start | bytes 589824
  646.1 5.8 copy-start.59
  646.1 5.9 copy-start.57
  646.1 6.2 copy-start.14
  652.5 489.3 %copy-start.34 = (f32[152,1024]{1,0:T(8,128)}, f32[152,1024]{1,0:T(8,128)S(1)}, u32[]{:S(2)}) copy-start(f32[152,1024]{1,0:T(8,128)S(1)} %add_add_fusion.4) | copy-start | bytes 1867780
  654.9 663.1 %all-reduce.3.cloned.1.call-start = ((), (), s32[]{:S(2)}) async-start(), calls=%async_computation.26 | async-start | bytes 12582912 | tf_op jit(solution)/shard_map/psum | solution.py:54
  (52 other events, 90.8 us)
Sparse Core Ops, SparseCore 0:
  10.2 69.8 all-gather.16
  82.3 27.7 all-gather.18
  112.2 81.5 all-gather.20
  195.8 80.5 all-gather.22
  278.5 63.2 all-gather.24
  343.3 27.7 all-gather.26
  373.3 81.5 all-gather.28
  456.4 80.5 all-gather.30
  568.8 34.3 reduce-scatter.17
  605.9 34.1 reduce-scatter.15
  642.4 68.2 reduce-scatter.11
  712.9 68.1 reduce-scatter.13
  783.4 87.9 reduce-scatter.19
  873.5 87.9 reduce-scatter.21
  963.7 87.9 reduce-scatter.23
  1053.8 87.9 reduce-scatter.25
  1144.5 29.2 reduce-scatter.27
  1178.7 139.2 all-reduce.2
where the time goes:
time: 1340 us
  waiting for transfers between devices  1080 us (81%)
  matrix products  145 us (11%)
  local copies, waits for them, and re-layouts  43.3 us (3%)
  blocking collectives  34.6 us (3%)
  between operations  17.6 us (1%)
  other arithmetic  15.7 us (1%)
    reduce_scatter x2, waiting for transfers between devices, local(): lax.psum_scatter(grad_up.astype(jnp.bfloat16), 'fsdp', scatter_dimension=...  180 us
    reduce_scatter x2, waiting for transfers between devices, local(): lax.psum_scatter(grad_down.astype(jnp.bfloat16), 'fsdp', scatter_dimensio...  180 us
    all_gather x2, waiting for transfers between devices, fetch_mlp(): lax.all_gather(w_up[depth], 'fsdp', axis=0, tiled=True)  162 us
    all_gather x2, waiting for transfers between devices, fetch_mlp(): lax.all_gather(w_down[depth], 'fsdp', axis=0, tiled=True)  144 us
    psum x1, waiting for transfers between devices, group_total(): lax.psum(shortened(shares), 'dp')  125 us
    reduce_scatter x1, waiting for transfers between devices, local(): lax.psum_scatter(grad_qkv.astype(jnp.bfloat16), 'fsdp', scatter_dimension...  70.3 us
    all_gather x1, waiting for transfers between devices, fetch_attention(): lax.all_gather(w_qkv[depth], 'fsdp', axis=0, tiled=True)  59 us
    reduce_scatter x1, waiting for transfers between devices, local(): lax.psum_scatter(first_terms[0].astype(jnp.bfloat16), 'fsdp', scatter_dim...  55.7 us
  transfers between devices with their start and end apart: 18, of which 16 were waited for; matrix products, arithmetic and copies ran while one was open for 11% of the time, Pallas kernels for 0%

commit v1 on v0

v1 whole, which is shorter than its diff:
```python
import math

import jax
import jax.numpy as jnp
from jax import lax
from jax.sharding import PartitionSpec as P

HEADS = 16
EPS = 1e-06
NEG_FILL = -1e30
MIX_WEIGHTS = (0.5, 0.25, 0.125, 0.125)
BF16 = jnp.bfloat16
F32 = jnp.float32


def dot(a, b):
    return jnp.dot(a, b, preferred_element_type=F32)


def dot_t(a, b):
    return lax.dot_general(a, b, (((0,), (0,)), ((), ())), preferred_element_type=F32)


def dot_nt(a, b):
    return lax.dot_general(a, b, (((1,), (1,)), ((), ())), preferred_element_type=F32)


def normalize(hidden):
    center = hidden - jnp.mean(hidden, axis=-1, keepdims=True)
    rstd = lax.rsqrt(jnp.mean(center * center, axis=-1, keepdims=True) + EPS)
    return center * rstd, rstd


def norm_backward(e, xhat, rstd):
    return rstd * (
        e
        - jnp.mean(e, axis=-1, keepdims=True)
        - xhat * jnp.mean(e * xhat, axis=-1, keepdims=True)
    )


def gelu_exact(pre_act):
    return jax.nn.gelu(pre_act, approximate=False)


class Square:
    def __init__(self):
        self.count = lax.axis_size("dp")
        self.me = lax.axis_index("dp")
        self.pairs = self.count == 4

    def owners(self):
        if self.pairs:
            return [self.me ^ k for k in range(self.count)]
        return [jnp.int32(k) for k in range(self.count)]

    def swap(self, block, k):
        return lax.ppermute(block, "dp", [(i, i ^ k) for i in range(self.count)])

    def spread(self, block):
        if self.pairs:
            return [block] + [self.swap(block, k) for k in range(1, self.count)]
        full = lax.all_gather(block, "dp")
        return [full[k] for k in range(self.count)]

    def collect(self, parts):
        if self.pairs:
            total = parts[0].astype(F32)
            for k in range(1, self.count):
                total = total + self.swap(parts[k].astype(BF16), k).astype(F32)
            return total
        stacked = jnp.stack([part.astype(BF16) for part in parts])
        return lax.psum_scatter(stacked, "dp", scatter_dimension=0, tiled=False).astype(F32)

    def gather(self, piece):
        if not self.pairs:
            return lax.all_gather(piece, "dp")
        got = [piece] + [self.swap(piece, k) for k in range(1, self.count)]
        odd = (self.me & 1) == 1
        high = (self.me & 2) == 2
        low_pair = (jnp.where(odd, got[1], got[0]), jnp.where(odd, got[0], got[1]))
        far_pair = (jnp.where(odd, got[3], got[2]), jnp.where(odd, got[2], got[3]))
        return jnp.stack(
            [
                jnp.where(high, far_pair[0], low_pair[0]),
                jnp.where(high, far_pair[1], low_pair[1]),
                jnp.where(high, low_pair[0], far_pair[0]),
                jnp.where(high, low_pair[1], far_pair[1]),
            ]
        )

    def total(self, piece):
        if not self.pairs:
            return lax.psum(piece.astype(BF16), "dp").astype(F32)
        own = piece.astype(BF16)
        got = [own.astype(F32)] + [self.swap(own, k).astype(F32) for k in range(1, self.count)]
        return (got[0] + got[1]) + (got[2] + got[3])


def select(index, choices):
    out = choices[0]
    for k in range(1, len(choices)):
        out = jnp.where(index == k, choices[k], out)
    return out


def local(
    tokens,
    pos_table,
    index_lo,
    index_hi,
    resolution,
    gain_attn,
    w_qkv,
    w_out,
    gain_mlp,
    w_up,
    w_down,
    cotangent,
):
    row_count, width = tokens.shape
    layers, shard_rows, _ = w_qkv.shape
    hidden_units = w_up.shape[2]
    shard_count = lax.axis_size("fsdp")
    shard = lax.axis_index("fsdp")
    square = Square()
    group_count = square.count
    me = square.me
    head_size = width // HEADS
    my_heads = HEADS // group_count
    part = my_heads * head_size
    unit_part = hidden_units // group_count
    fine = square.pairs and shard_count * 2 == HEADS
    score_scale = 1.0 / math.sqrt(head_size)
    len_low = index_lo.shape[0]
    len_high = index_hi.shape[0]

    row_ids = jnp.arange(row_count, dtype=jnp.int32)

    def layout(flag):
        length = jnp.where(flag == 1, len_high, len_low).astype(jnp.int32)
        images = jnp.where(flag == 1, row_count // len_high, row_count // len_low).astype(jnp.int32)
        live = row_ids < images * length
        return live, jnp.where(live, row_ids // length, images)

    flag = resolution[me]
    live_rows, _ = layout(flag)
    block_ids = jnp.stack([layout(resolution[owner])[1] for owner in square.owners()])
    same_image = block_ids[:, :, None] == block_ids[:, None, :]
    picked = jnp.where(flag == 1, index_hi[row_ids % len_high], index_lo[row_ids % len_low])
    table_ids = jnp.arange(len_high, dtype=jnp.int32)
    mixing = jnp.zeros((row_count, len_high), F32)
    for slot in range(4):
        mixing = mixing + MIX_WEIGHTS[slot] * (
            picked[:, slot : slot + 1] == table_ids[None, :]
        ).astype(F32)
    mixing = (mixing * live_rows[:, None].astype(F32)).astype(BF16)
    high_groups = jnp.sum(resolution)
    tokens_low = (
        (group_count - high_groups) * shard_count * (row_count // len_low) * len_low
    ).astype(F32)
    tokens_high = (high_groups * shard_count * (row_count // len_high) * len_high).astype(F32)
    token_share = 2.0 * jnp.where(flag == 1, tokens_high, tokens_low) / (tokens_low + tokens_high)
    weight = jnp.where(live_rows, token_share, 0.0)

    half = shard_rows // 4
    core = shard % 2
    swap_core = [(j, j ^ 1) for j in range(shard_count)]
    pair_side, head_side = me & 1, (me >> 1) & 1

    def qkv_part(w):
        if fine:
            view = w.reshape(shard_rows, 3 * HEADS // 4, 2, 2, head_size)
            view = select(pair_side, [view[:, :, 0], view[:, :, 1]])
            view = select(head_side, [view[:, :, 0], view[:, :, 1]])
            return view.reshape(shard_rows, 3 * part)
        view = w.reshape(shard_rows, 3, group_count, part)
        return lax.dynamic_index_in_dim(view, me, 2, keepdims=False).reshape(shard_rows, 3 * part)

    def up_part(w):
        view = w.reshape(shard_rows, shard_count, group_count, unit_part // shard_count)
        return lax.dynamic_index_in_dim(view, me, 2, keepdims=False).reshape(shard_rows, unit_part)

    def down_part(w):
        rows = unit_part // shard_count
        return lax.dynamic_slice_in_dim(w, me * rows, rows, 0)

    def out_part(w):
        if fine:
            view = w.reshape(2, 2, half, width)
            mine = select(head_side, [view[0], view[1]])
            keep = select(core, [mine[0], mine[1]])
            give = select(core, [mine[1], mine[0]])
            got = lax.ppermute(give, "fsdp", swap_core)
            return jnp.where(core == pair_side, keep, got)
        return w

    def fetch(piece):
        return lax.all_gather(piece, "fsdp", axis=0, tiled=False)

    weights = []
    table = lax.all_gather(pos_table, "fsdp", axis=1, tiled=True)
    for depth in range(layers):
        gain_a = gain_attn[depth].astype(F32)[:, None]
        gain_m = gain_mlp[depth].astype(F32)[:, None]
        qkv = (qkv_part(w_qkv[depth]).astype(F32) * gain_a).astype(BF16)
        up = (up_part(w_up[depth]).astype(F32) * gain_m).astype(BF16)
        down = down_part(w_down[depth])
        out = out_part(w_out[depth])
        qkv_all = fetch(qkv).reshape(width, 3 * part)
        a = up.size // width
        b = a + down.shape[0]
        rest = fetch(jnp.concatenate([up.reshape(a, width), down, out], axis=0))
        up_all = rest[:, :a].reshape(width, unit_part)
        down_all = rest[:, a:b].reshape(unit_part, width)
        out_all = rest[:, b:].reshape(-1, width)
        if not fine:
            out_all = lax.dynamic_slice_in_dim(out_all, me * part, part, 0)
        weights.append((qkv_all, out_all, up_all, down_all))

    def split_heads(block):
        return block.reshape(group_count, row_count, my_heads, head_size)

    def scores_of(queries, key_rows):
        scores = (
            jnp.einsum("bqhd,bkhd->bhqk", queries, key_rows, preferred_element_type=F32)
            * score_scale
        )
        return jnp.where(same_image[:, None], scores, NEG_FILL)

    def spread(block):
        return jnp.concatenate(square.spread(block), axis=0)

    def collect(partial):
        return square.collect([partial[k * row_count : (k + 1) * row_count] for k in range(group_count)])

    hidden = tokens.astype(F32) + dot(mixing, table)
    saved = []
    for depth in range(layers):
        qkv_w, out_w, up_w, down_w = weights[depth]
        xhat_a, rstd_a = normalize(hidden)
        rows_a = spread(xhat_a.astype(BF16))
        projected = dot(rows_a, qkv_w).astype(BF16)
        queries = split_heads(projected[:, :part])
        key_rows = split_heads(projected[:, part : 2 * part])
        values = split_heads(projected[:, 2 * part :])
        scores = scores_of(queries, key_rows)
        row_max = jnp.max(scores, axis=-1, keepdims=True)
        powers = jnp.exp(scores - row_max)
        row_total = jnp.sum(powers, axis=-1, keepdims=True)
        log_total = row_max + jnp.log(row_total)
        probs = (powers / row_total).astype(BF16)
        attended = jnp.einsum("bhqk,bkhd->bqhd", probs, values, preferred_element_type=F32)
        attended = attended.reshape(group_count * row_count, part).astype(BF16)
        middle = hidden + collect(dot(attended, out_w).astype(BF16))
        xhat_m, rstd_m = normalize(middle)
        rows_m = spread(xhat_m.astype(BF16))
        pre_act = dot(rows_m, up_w)
        activated = gelu_exact(pre_act).astype(BF16)
        result = middle + collect(dot(activated, down_w).astype(BF16))
        saved.append(
            (xhat_a, rstd_a, rows_a, queries, key_rows, values, log_total, attended,
             xhat_m, rstd_m, rows_m, pre_act, activated)
        )
        hidden = result

    gradient = cotangent.astype(F32) * weight[:, None]
    shares = [None] * layers
    for depth in reversed(range(layers)):
        qkv_w, out_w, up_w, down_w = weights[depth]
        (xhat_a, rstd_a, rows_a, queries, key_rows, values, log_total, attended,
         xhat_m, rstd_m, rows_m, pre_act, activated) = saved[depth]
        d_result = spread(gradient.astype(BF16))
        grad_down = dot_t(activated, d_result).astype(BF16)
        d_activated = dot_nt(d_result, down_w)
        _, pullback = jax.vjp(gelu_exact, pre_act)
        d_pre = pullback(d_activated)[0].astype(BF16)
        grad_up = dot_t(rows_m, d_pre).astype(BF16)
        e = collect(dot_nt(d_pre, up_w).astype(BF16))
        d_middle = gradient + norm_backward(e, xhat_m, rstd_m)
        d_attn = spread(d_middle.astype(BF16))
        grad_out = dot_t(attended, d_attn).astype(BF16)
        d_attended = split_heads(dot_nt(d_attn, out_w).astype(BF16))
        probs = jnp.exp(scores_of(queries, key_rows) - log_total)
        d_values = jnp.einsum(
            "bhqk,bqhd->bkhd", probs.astype(BF16), d_attended, preferred_element_type=F32
        )
        d_probs = jnp.einsum("bqhd,bkhd->bhqk", d_attended, values, preferred_element_type=F32)
        centre = jnp.sum(probs * d_probs, axis=-1, keepdims=True)
        d_scores = (probs * (d_probs - centre)).astype(BF16)
        d_queries = (
            jnp.einsum("bhqk,bkhd->bqhd", d_scores, key_rows, preferred_element_type=F32)
            * score_scale
        )
        d_keys = (
            jnp.einsum("bhqk,bqhd->bkhd", d_scores, queries, preferred_element_type=F32)
            * score_scale
        )
        d_projected = jnp.concatenate(
            [x.astype(BF16).reshape(group_count * row_count, part) for x in (d_queries, d_keys, d_values)],
            axis=1,
        )
        grad_qkv = dot_t(rows_a, d_projected).astype(BF16)
        e = collect(dot_nt(d_projected, qkv_w).astype(BF16))
        gradient = d_middle + norm_backward(e, xhat_a, rstd_a)
        shares[depth] = (grad_qkv, grad_out, grad_up, grad_down)

    def home(term):
        return lax.psum_scatter(term, "fsdp", scatter_dimension=0, tiled=True)

    grads_qkv, grads_out, grads_up, grads_down, gains_a, gains_m = [], [], [], [], [], []
    for depth in reversed(range(layers)):
        grad_qkv, grad_out, grad_up, grad_down = shares[depth]
        rest = [
            grad_up.reshape(shard_count, -1, width),
            grad_down.reshape(shard_count, -1, width),
        ]
        if fine:
            rest.append(grad_out.reshape(shard_count, -1, width))
        else:
            full = jnp.zeros((width, width), BF16)
            full = lax.dynamic_update_slice_in_dim(full, grad_out, me * part, 0)
            rest.append(full.reshape(shard_count, -1, width))
        sizes = [x.shape[1] for x in rest]
        rest = home(jnp.concatenate(rest, axis=1))[0]
        qkv = square.gather(home(grad_qkv))
        if not fine:
            out = square.total(rest[sizes[0] + sizes[1] :])
            rest = rest[: sizes[0] + sizes[1]]
        rest = square.gather(rest)
        up = rest[:, : sizes[0]].reshape(group_count, shard_rows, shard_count, -1)
        up = up.transpose(1, 2, 0, 3).reshape(shard_rows, hidden_units).astype(F32)
        down = rest[:, sizes[0] : sizes[0] + sizes[1]].reshape(-1, width).astype(F32)
        if fine:
            pieces = rest[:, sizes[0] + sizes[1] :].reshape(2, 2, half, width)
            keep = select(core, [pieces[:, 0], pieces[:, 1]])
            give = select(core, [pieces[:, 1], pieces[:, 0]])
            got = lax.ppermute(give, "fsdp", swap_core)
            first = select(core, [keep, got])
            second = select(core, [got, keep])
            out = jnp.stack([first, second], axis=1).reshape(shard_rows, width).astype(F32)
            qkv = qkv.reshape(2, 2, shard_rows, 3 * my_heads, head_size).transpose(2, 3, 1, 0, 4)
        else:
            qkv = qkv.reshape(group_count, shard_rows, 3, part).transpose(1, 2, 0, 3)
        qkv = qkv.reshape(shard_rows, 3 * width).astype(F32)
        gains_a.append(jnp.sum(qkv * w_qkv[depth].astype(F32), axis=1))
        gains_m.append(jnp.sum(up * w_up[depth].astype(F32), axis=1))
        grads_qkv.append(qkv * gain_attn[depth].astype(F32)[:, None])
        grads_up.append(up * gain_mlp[depth].astype(F32)[:, None])
        grads_out.append(out)
        grads_down.append(down)

    high_part = gradient.astype(BF16)
    low_part = (gradient - high_part.astype(F32)).astype(BF16)
    table_term = dot_t(mixing, high_part) + dot_t(mixing, low_part)
    table_share = lax.psum_scatter(table_term.astype(BF16), "fsdp", scatter_dimension=1, tiled=True)
    d_table = square.total(table_share)
    return (
        hidden,
        gradient,
        d_table,
        jnp.stack(gains_a[::-1]),
        jnp.stack(grads_qkv[::-1]),
        jnp.stack(grads_out[::-1]),
        jnp.stack(gains_m[::-1]),
        jnp.stack(grads_up[::-1]),
        jnp.stack(grads_down[::-1]),
    )


def solution(mesh):
    in_specs = (
        P(("dp", "fsdp"), None),
        P(None, "fsdp"),
        P(),
        P(),
        P(),
        P(None, "fsdp"),
        P(None, "fsdp", None),
        P(None, "fsdp", None),
        P(None, "fsdp"),
        P(None, "fsdp", None),
        P(None, "fsdp", None),
        P(("dp", "fsdp"), None),
    )
    out_specs = (
        P(("dp", "fsdp"), None),
        P(("dp", "fsdp"), None),
        P(None, "fsdp"),
        P(None, "fsdp"),
        P(None, "fsdp", None),
        P(None, "fsdp", None),
        P(None, "fsdp"),
        P(None, "fsdp", None),
        P(None, "fsdp", None),
    )
    return jax.shard_map(local, mesh=mesh, in_specs=in_specs, out_specs=out_specs, check_vma=False)
```

time: 1340 us -> 700 us (0.52)
  waiting for transfers between devices: 1080 us -> 359 us
  starting transfers between devices: 1.12 us -> 75.4 us
  matrix products: 145 us -> 77.2 us
  local copies, waits for them, and re-layouts: 43.3 us -> 89.2 us
  other arithmetic: 15.7 us -> 54 us
  blocking collectives: 34.6 us -> 17.2 us
    all_gather x8 -> x4, waiting for transfers between devices: 437 us -> 22.4 us  [fetch(): return lax.all_gather(piece, 'fsdp', axis=0, tiled=False)]
    reduce_scatter x8 -> x4, waiting for transfers between devices: 487 us -> 113 us  [home(): return lax.psum_scatter(term, 'fsdp', scatter_dimension=0, tiled=True)]
    ppermute x0 -> x67, waiting for transfers between devices: none -> 219 us  [the longest x63 219 us: swap(): return lax.ppermute(block, 'dp', [(i, i ^ k) for i in range(self.count)])]
    psum x1 -> x0, waiting for transfers between devices: 125 us -> none  [group_total(): lax.psum(shortened(shares), 'dp')]
    ppermute x0 -> x67, starting transfers between devices: none -> 73.9 us  [the longest x63 73.2 us: swap(): return lax.ppermute(block, 'dp', [(i, i ^ k) for i in range(self.count)])]
    dot_general x38 -> x39, matrix products: 145 us -> 77.2 us  [the longest x9 27.2 us: dot(): return jnp.dot(a, b, preferred_element_type=F32)]
    unnamed x19 -> x10, waiting for transfers between devices: 28.9 us -> 5.04 us
    convert_element_type x0 -> x20, local copies, waits for them, and re-layouts: none -> 22.2 us  [the longest x4 9.06 us: local(): up = up.transpose(1, 2, 0, 3).reshape(shard_rows, hidden_units).astype(F32)]
  transfers between devices with their start and end apart: 18 -> 76, of which waited for: 16 -> 57; matrix products, arithmetic and copies ran while one was open for 11% -> 18% of each run, Pallas kernels for 0% -> 0%
where the time goes in v1:
time: 700 us; the launch traced here: 693 us
  waiting for transfers between devices  359 us (51%)
  local copies, waits for them, and re-layouts  89.2 us (13%)
  matrix products  77.2 us (11%)
  starting transfers between devices  75.4 us (11%)
  other arithmetic  54 us (8%)
  between operations  20.7 us (3%)
  blocking collectives  17.2 us (2%)
    ppermute x63, waiting for transfers between devices, swap(): return lax.ppermute(block, 'dp', [(i, i ^ k) for i in range(self.count)])  219 us
    reduce_scatter x4, waiting for transfers between devices, home(): return lax.psum_scatter(term, 'fsdp', scatter_dimension=0, tiled=True)  113 us
    ppermute x63, starting transfers between devices, swap(): return lax.ppermute(block, 'dp', [(i, i ^ k) for i in range(self.count)])  73.2 us
    dot_general x9, matrix products, dot(): return jnp.dot(a, b, preferred_element_type=F32)  27.2 us
    all_gather x4, waiting for transfers between devices, fetch(): return lax.all_gather(piece, 'fsdp', axis=0, tiled=False)  22.4 us
    reshape x16, local copies, waits for them, and re-layouts, split_heads(): return block.reshape(group_count, row_count, my_heads, head_size)  20.9 us
    dot_general x10, matrix products, dot_t(): lax.dot_general(a, b, (((0,), (0,)), ((), ())), preferred_element_type=F32)  19.6 us
    unnamed x313, local copies, waits for them, and re-layouts  19.2 us
  transfers between devices with their start and end apart: 76, of which 57 were waited for; matrix products, arithmetic and copies ran while one was open for 18% of the time, Pallas kernels for 0%

profile of v1, /device:TPU:0, one launch (start us, length us, event | category | flops | bytes accessed | tf_op | source)
XLA Modules:
  0.0 692.6 jit_solution(18404452656196385090)
XLA Ops:
  27.6 17.2 %all_gather.23 = bf16[145,1024]{1,0:T(8,128)(2,1)S(1)} all-gather(bf16[145,128]{1,0:T(8,128)(2,1)S(1)} %copy-done.73), channel_id=1, replica_groups=mesh['dp'=4,'fsdp'=8] {'fsdp'}, dimensions={1}, use_global_device_ids=true | all-gather | bytes 334080 | tf_op jit(solution)/shard_map/all_gather | solution.py:202
  53.2 4.2 collective-permute-done.2
  57.4 6.1 collective-permute-done.1
  73.5 22.1 %all-gather.11.cloned.1.call-done = bf16[2304,1024]{1,0:T(8,128)(2,1)} async-done(((bf16[288,1024]{1,0:T(8,128)(2,1)}), bf16[2304,1024]{1,0:T(8,128)(2,1)}) %all-gather.11.cloned.1.call-update) | async-done | bytes 4718608 | tf_op jit(solution)/shard_map/all_gather | solution.py:199
  104.2 5.4 collective-permute-done.4
  109.6 7.1 %collective-permute-done.6 = bf16[152,1024]{1,0:T(8,128)(2,1)} collective-permute-done((bf16[152,1024]{1,0:T(8,128)(2,1)}, bf16[152,1024]{1,0:T(8,128)(2,1)}, u32[]{:S(2)}, u32[]{:S(2)}) %collective-permute-start.6) | collective-permute-done | bytes 311328 | tf_op jit(solution)/shard_map/ppermute | solution.py:58
  126.4 5.0 collective-permute-done.9
  131.3 4.4 collective-permute-done.8
  135.8 9.7 %multiply_convert_fusion.3 = (bf16[608,1024]{1,0:T(8,128)(2,1)S(1)}, f32[608,1024]{1,0:T(8,128)}, f32[608,1024]{1,0:T(8,128)}) fusion(bf16[1024,1024]{1,0:T(8,128)(2,1)S(1)} %bitcast.363, bf16[152,1024]{1,0:T(8,128)(2,1)S(1)} %collective-permute-done.9, bf16[152,1024]{1,0:T(8,128)(2,1)S(1)} %collective-permute-done.8, ...), kind=kOutput, calls=%fused_computation.34 | convolution fusion | flops 1320517632 | bytes 9568256 | tf_op jit(solution)/shard_map/dot_general | solution.py:17
  150.7 6.7 collective-permute-done.10
  157.4 5.9 collective-permute-done.12
  173.7 3.6 collective-permute-done.15
  177.3 3.6 collective-permute-done.14
  211.0 3.7 collective-permute-done.17
  214.7 7.6 %collective-permute-done.19 = bf16[152,1024]{1,0:T(8,128)(2,1)S(1)} collective-permute-done((bf16[152,1024]{1,0:T(8,128)(2,1)S(1)}, bf16[152,1024]{1,0:T(8,128)(2,1)S(1)}, u32[]{:S(2)}, u32[]{:S(2)}) %collective-permute-start.19) | collective-permute-done | bytes 311328 | tf_op jit(solution)/shard_map/ppermute | solution.py:58
  222.3 12.0 %collective-permute-done.18 = bf16[152,1024]{1,0:T(8,128)(2,1)S(1)} collective-permute-done((bf16[152,1024]{1,0:T(8,128)(2,1)S(1)}, bf16[152,1024]{1,0:T(8,128)(2,1)S(1)}, u32[]{:S(2)}, u32[]{:S(2)}) %collective-permute-start.18) | collective-permute-done | bytes 311328 | tf_op jit(solution)/shard_map/ppermute | solution.py:58
  243.6 5.9 collective-permute-done.21
  249.5 6.5 multiply_convert_fusion.2
  256.1 3.9 add_convert_fusion.1
  272.5 6.2 collective-permute-done.31
  280.4 5.0 collective-permute-done.23
  285.3 4.1 collective-permute-done.25
  295.7 6.3 collective-permute-done.34
  338.3 6.8 collective-permute-done.35
  345.1 5.2 collective-permute-done.37
  356.0 6.2 collective-permute-done.40
  365.4 3.9 add_convert_fusion
  374.5 6.8 collective-permute-done.41
  384.6 5.3 collective-permute-done.42
  391.4 3.5 collective-permute-start.44
  394.9 4.4 collective-permute-done.46
  418.2 3.3 collective-permute-done.47
  421.6 4.3 collective-permute-done.49
  431.3 3.7 convolution_convert_fusion.4
  435.2 3.6 convolution_convert_fusion.5
  439.0 3.3 convolution_convert_fusion
  456.8 4.9 reduce-scatter.16.cloned.1.call-done
  466.2 30.8 %reduce-scatter.10.cloned.1.call-done = bf16[128,768]{1,0:T(8,128)(2,1)} async-done(((bf16[1024,768]{1,0:T(8,128)(2,1)}), bf16[128,768]{1,0:T(8,128)(2,1)}) %reduce-scatter.10.cloned.1.call-update) | async-done | bytes 196624 | tf_op jit(solution)/shard_map/reduce_scatter | solution.py:309
  509.6 22.7 %reduce-scatter.8.cloned.1.call-done = bf16[128,768]{1,0:T(8,128)(2,1)} async-done(((bf16[1024,768]{1,0:T(8,128)(2,1)}), bf16[128,768]{1,0:T(8,128)(2,1)}) %reduce-scatter.8.cloned.1.call-update) | async-done | bytes 196624 | tf_op jit(solution)/shard_map/reduce_scatter | solution.py:309
  543.7 43.7 %reduce-scatter.14.cloned.1.call-done = bf16[1,288,1024]{2,1,0:T(8,128)(2,1)} async-done(((bf16[8,288,1024]{2,1,0:T(8,128)(2,1)}), bf16[1,288,1024]{2,1,0:T(8,128)(2,1)}) %reduce-scatter.14.cloned.1.call-update) | async-done | bytes 589840 | tf_op jit(solution)/shard_map/reduce_scatter | solution.py:309
  590.9 3.3 pad_maximum_fusion.3
  594.2 3.6 copy.245
  598.9 5.1 collective-permute-done.65
  604.0 10.5 %collective-permute-done.64 = bf16[288,1024]{1,0:T(8,128)(2,1)} collective-permute-done((bf16[288,1024]{1,0:T(8,128)(2,1)}, bf16[288,1024]{1,0:T(8,128)(2,1)}, u32[]{:S(2)}, u32[]{:S(2)}) %collective-permute-start.64) | collective-permute-done | bytes 589856 | tf_op jit(solution)/shard_map/ppermute | solution.py:58
  624.5 3.3 broadcast_multiply_fusion
  627.8 15.4 %reduce-scatter.12.cloned.1.call-done = bf16[1,288,1024]{2,1,0:T(8,128)(2,1)} async-done(((bf16[8,288,1024]{2,1,0:T(8,128)(2,1)}), bf16[1,288,1024]{2,1,0:T(8,128)(2,1)}) %reduce-scatter.12.cloned.1.call-update) | async-done | bytes 589840 | tf_op jit(solution)/shard_map/reduce_scatter | solution.py:309
  649.0 10.7 %collective-permute-done.61 = bf16[288,1024]{1,0:T(8,128)(2,1)S(1)} collective-permute-done((bf16[288,1024]{1,0:T(8,128)(2,1)}, bf16[288,1024]{1,0:T(8,128)(2,1)S(1)}, u32[]{:S(2)}, u32[]{:S(2)}) %collective-permute-start.61) | collective-permute-done | bytes 589856 | tf_op jit(solution)/shard_map/ppermute | solution.py:58
  659.7 10.5 %collective-permute-done.60 = bf16[288,1024]{1,0:T(8,128)(2,1)S(1)} collective-permute-done((bf16[288,1024]{1,0:T(8,128)(2,1)}, bf16[288,1024]{1,0:T(8,128)(2,1)S(1)}, u32[]{:S(2)}, u32[]{:S(2)}) %collective-permute-start.60) | collective-permute-done | bytes 589856 | tf_op jit(solution)/shard_map/ppermute | solution.py:58
  (640 shorter events, 284.8 us)
Async XLA Ops:
  7.2 56.4 %all-gather.7.cloned.1.call-start = ((), (), s32[]{:S(2)}) async-start(), calls=%async_computation.5 | async-start | bytes 1769472 | tf_op jit(solution)/shard_map/all_gather | solution.py:199
  12.6 83.0 %all-gather.11.cloned.1.call-start = ((), (), s32[]{:S(2)}) async-start(), calls=%async_computation.11 | async-start | bytes 5308416 | tf_op jit(solution)/shard_map/all_gather | solution.py:199
  21.9 149.7 %all-gather.13.cloned.1.call-start = ((), (), s32[]{:S(2)}) async-start(), calls=%async_computation.12 | async-start | bytes 5308416 | tf_op jit(solution)/shard_map/all_gather | solution.py:199
  24.2 149.5 %all-gather.9.cloned.1.call-start = ((), (), s32[]{:S(2)}) async-start(), calls=%async_computation.6 | async-start | bytes 1769472 | tf_op jit(solution)/shard_map/all_gather | solution.py:199
  48.7 14.8 %collective-permute-start.1 = (bf16[152,1024]{1,0:T(8,128)(2,1)S(1)}, bf16[152,1024]{1,0:T(8,128)(2,1)S(1)}, u32[]{:S(2)}, u32[]{:S(2)}) collective-permute-start(bf16[152,1024]{1,0:T(8,128)(2,1)S(1)} %fusion.42), channel_id=1, source_target_pairs={{0,16},{8,24},{16,0},{24,8},{1,17},{9,25},{17,1},{25,9},{2,18},{10... | collective-permute-start | bytes 933896 | tf_op jit(solution)/shard_map/ppermute | solution.py:58
  49.2 14.3 %collective-permute-start = (bf16[152,1024]{1,0:T(8,128)(2,1)S(1)}, bf16[152,1024]{1,0:T(8,128)(2,1)S(1)}, u32[]{:S(2)}, u32[]{:S(2)}) collective-permute-start(bf16[152,1024]{1,0:T(8,128)(2,1)S(1)} %fusion.42), channel_id=1, source_target_pairs={{0,8},{8,0},{16,24},{24,16},{1,9},{9,1},{17,25},{25,17},{2,10},{10... | collective-permute-start | bytes 933896 | tf_op jit(solution)/shard_map/ppermute | solution.py:58
  100.7 16.0 %collective-permute-start.6 = (bf16[152,1024]{1,0:T(8,128)(2,1)}, bf16[152,1024]{1,0:T(8,128)(2,1)}, u32[]{:S(2)}, u32[]{:S(2)}) collective-permute-start(bf16[152,1024]{1,0:T(8,128)(2,1)} %get-tuple-element.108), channel_id=1, source_target_pairs={{0,24},{8,16},{16,8},{24,0},{1,25},{9,17},{17,9},{25,1},{2,26},{10... | collective-permute-start | bytes 933896 | tf_op jit(solution)/shard_map/ppermute | solution.py:58
  102.1 15.9 %collective-permute-start.5 = (bf16[152,1024]{1,0:T(8,128)(2,1)}, bf16[152,1024]{1,0:T(8,128)(2,1)}, u32[]{:S(2)}, u32[]{:S(2)}) collective-permute-start(bf16[152,1024]{1,0:T(8,128)(2,1)} %get-tuple-element.109), channel_id=1, source_target_pairs={{0,16},{8,24},{16,0},{24,8},{1,17},{9,25},{17,1},{25,9},{2,18},{10... | collective-permute-start | bytes 933896 | tf_op jit(solution)/shard_map/ppermute | solution.py:58
  103.6 358.1 %reduce-scatter.16.cloned.1.call-start = ((), (), s32[]{:S(2)}) async-start(), calls=%async_computation.13 | async-start | bytes 589824
  121.6 14.2 %collective-permute-start.8 = (bf16[152,1024]{1,0:T(8,128)(2,1)S(1)}, bf16[152,1024]{1,0:T(8,128)(2,1)S(1)}, u32[]{:S(2)}, u32[]{:S(2)}) collective-permute-start(bf16[152,1024]{1,0:T(8,128)(2,1)S(1)} %fusion.43), channel_id=1, source_target_pairs={{0,16},{8,24},{16,0},{24,8},{1,17},{9,25},{17,1},{25,9},{2,18},{10... | collective-permute-start | bytes 933896 | tf_op jit(solution)/shard_map/ppermute | solution.py:58
  123.1 12.7 %collective-permute-start.7 = (bf16[152,1024]{1,0:T(8,128)(2,1)S(1)}, bf16[152,1024]{1,0:T(8,128)(2,1)S(1)}, u32[]{:S(2)}, u32[]{:S(2)}) collective-permute-start(bf16[152,1024]{1,0:T(8,128)(2,1)S(1)} %fusion.43), channel_id=1, source_target_pairs={{0,8},{8,0},{16,24},{24,16},{1,9},{9,1},{17,25},{25,17},{2,10},{10... | collective-permute-start | bytes 933896 | tf_op jit(solution)/shard_map/ppermute | solution.py:58
  148.0 15.3 %collective-permute-start.12 = (bf16[152,1024]{1,0:T(8,128)(2,1)S(1)}, bf16[152,1024]{1,0:T(8,128)(2,1)S(1)}, u32[]{:S(2)}, u32[]{:S(2)}) collective-permute-start(bf16[152,1024]{1,0:T(8,128)(2,1)S(1)} %get-tuple-element.105), channel_id=1, source_target_pairs={{0,24},{8,16},{16,8},{24,0},{1,25},{9,17},{17,9},{25,1},{2,26},{10... | collective-permute-start | bytes 933896 | tf_op jit(solution)/shard_map/ppermute | solution.py:58
  149.2 15.5 %collective-permute-start.11 = (bf16[152,1024]{1,0:T(8,128)(2,1)S(1)}, bf16[152,1024]{1,0:T(8,128)(2,1)S(1)}, u32[]{:S(2)}, u32[]{:S(2)}) collective-permute-start(bf16[152,1024]{1,0:T(8,128)(2,1)S(1)} %get-tuple-element.106), channel_id=1, source_target_pairs={{0,16},{8,24},{16,0},{24,8},{1,17},{9,25},{17,1},{25,9},{2,18},{10... | collective-permute-start | bytes 933896 | tf_op jit(solution)/shard_map/ppermute | solution.py:58
  166.0 11.4 %collective-permute-start.15 = (bf16[152,1024]{1,0:T(8,128)(2,1)S(1)}, bf16[152,1024]{1,0:T(8,128)(2,1)}, u32[]{:S(2)}, u32[]{:S(2)}) collective-permute-start(bf16[152,1024]{1,0:T(8,128)(2,1)S(1)} %fusion.44), channel_id=1, source_target_pairs={{0,24},{8,16},{16,8},{24,0},{1,25},{9,17},{17,9},{25,1},{2,26},{10... | collective-permute-start | bytes 933896 | tf_op jit(solution)/shard_map/ppermute | solution.py:58
  167.3 13.6 %collective-permute-start.14 = (bf16[152,1024]{1,0:T(8,128)(2,1)S(1)}, bf16[152,1024]{1,0:T(8,128)(2,1)}, u32[]{:S(2)}, u32[]{:S(2)}) collective-permute-start(bf16[152,1024]{1,0:T(8,128)(2,1)S(1)} %fusion.44), channel_id=1, source_target_pairs={{0,16},{8,24},{16,0},{24,8},{1,17},{9,25},{17,1},{25,9},{2,18},{10... | collective-permute-start | bytes 933896 | tf_op jit(solution)/shard_map/ppermute | solution.py:58
  169.0 12.0 %collective-permute-start.13 = (bf16[152,1024]{1,0:T(8,128)(2,1)S(1)}, bf16[152,1024]{1,0:T(8,128)(2,1)}, u32[]{:S(2)}, u32[]{:S(2)}) collective-permute-start(bf16[152,1024]{1,0:T(8,128)(2,1)S(1)} %fusion.44), channel_id=1, source_target_pairs={{0,8},{8,0},{16,24},{24,16},{1,9},{9,1},{17,25},{25,17},{2,10},{10... | collective-permute-start | bytes 933896 | tf_op jit(solution)/shard_map/ppermute | solution.py:58
  205.9 16.5 %collective-permute-start.19 = (bf16[152,1024]{1,0:T(8,128)(2,1)S(1)}, bf16[152,1024]{1,0:T(8,128)(2,1)S(1)}, u32[]{:S(2)}, u32[]{:S(2)}) collective-permute-start(bf16[152,1024]{1,0:T(8,128)(2,1)S(1)} %get-tuple-element.102), channel_id=1, source_target_pairs={{0,24},{8,16},{16,8},{24,0},{1,25},{9,17},{17,9},{25,1},{2,26},{10... | collective-permute-start | bytes 933896 | tf_op jit(solution)/shard_map/ppermute | solution.py:58
  207.4 27.0 %collective-permute-start.18 = (bf16[152,1024]{1,0:T(8,128)(2,1)S(1)}, bf16[152,1024]{1,0:T(8,128)(2,1)S(1)}, u32[]{:S(2)}, u32[]{:S(2)}) collective-permute-start(bf16[152,1024]{1,0:T(8,128)(2,1)S(1)} %get-tuple-element.103), channel_id=1, source_target_pairs={{0,16},{8,24},{16,0},{24,8},{1,17},{9,25},{17,1},{25,9},{2,18},{10... | collective-permute-start | bytes 933896 | tf_op jit(solution)/shard_map/ppermute | solution.py:58
  208.1 47.9 %collective-permute-start.28 = (bf16[152,1024]{1,0:T(8,128)(2,1)S(1)}, bf16[152,1024]{1,0:T(8,128)(2,1)S(1)}, u32[]{:S(2)}, u32[]{:S(2)}) collective-permute-start(bf16[152,1024]{1,0:T(8,128)(2,1)S(1)} %fusion.39), channel_id=1, source_target_pairs={{0,24},{8,16},{16,8},{24,0},{1,25},{9,17},{17,9},{25,1},{2,26},{10... | collective-permute-start | bytes 933896 | tf_op jit(solution)/shard_map/ppermute | solution.py:58
  209.6 46.4 %collective-permute-start.27 = (bf16[152,1024]{1,0:T(8,128)(2,1)S(1)}, bf16[152,1024]{1,0:T(8,128)(2,1)S(1)}, u32[]{:S(2)}, u32[]{:S(2)}) collective-permute-start(bf16[152,1024]{1,0:T(8,128)(2,1)S(1)} %fusion.39), channel_id=1, source_target_pairs={{0,16},{8,24},{16,0},{24,8},{1,17},{9,25},{17,1},{25,9},{2,18},{10... | collective-permute-start | bytes 933896 | tf_op jit(solution)/shard_map/ppermute | solution.py:58
  236.5 12.9 %collective-permute-start.21 = (bf16[152,1024]{1,0:T(8,128)(2,1)S(1)}, bf16[152,1024]{1,0:T(8,128)(2,1)S(1)}, u32[]{:S(2)}, u32[]{:S(2)}) collective-permute-start(bf16[152,1024]{1,0:T(8,128)(2,1)S(1)} %fusion.45), channel_id=1, source_target_pairs={{0,16},{8,24},{16,0},{24,8},{1,17},{9,25},{17,1},{25,9},{2,18},{10... | collective-permute-start | bytes 933896 | tf_op jit(solution)/shard_map/ppermute | solution.py:58
  237.1 12.3 %collective-permute-start.20 = (bf16[152,1024]{1,0:T(8,128)(2,1)S(1)}, bf16[152,1024]{1,0:T(8,128)(2,1)S(1)}, u32[]{:S(2)}, u32[]{:S(2)}) collective-permute-start(bf16[152,1024]{1,0:T(8,128)(2,1)S(1)} %fusion.45), channel_id=1, source_target_pairs={{0,8},{8,0},{16,24},{24,16},{1,9},{9,1},{17,25},{25,17},{2,10},{10... | collective-permute-start | bytes 933896 | tf_op jit(solution)/shard_map/ppermute | solution.py:58
  243.0 13.0 %collective-permute-start.26 = (bf16[152,1024]{1,0:T(8,128)(2,1)S(1)}, bf16[152,1024]{1,0:T(8,128)(2,1)S(1)}, u32[]{:S(2)}, u32[]{:S(2)}) collective-permute-start(bf16[152,1024]{1,0:T(8,128)(2,1)S(1)} %fusion.39), channel_id=1, source_target_pairs={{0,8},{8,0},{16,24},{24,16},{1,9},{9,1},{17,25},{25,17},{2,10},{10... | collective-permute-start | bytes 933896 | tf_op jit(solution)/shard_map/ppermute | solution.py:58
  262.0 16.6 %collective-permute-start.31 = (bf16[152,1024]{1,0:T(8,128)(2,1)S(1)}, bf16[152,1024]{1,0:T(8,128)(2,1)S(1)}, u32[]{:S(2)}, u32[]{:S(2)}) collective-permute-start(bf16[152,1024]{1,0:T(8,128)(2,1)S(1)} %get-tuple-element.96), channel_id=1, source_target_pairs={{0,24},{8,16},{16,8},{24,0},{1,25},{9,17},{17,9},{25,1},{2,26},{10... | collective-permute-start | bytes 933896 | tf_op jit(solution)/shard_map/ppermute | solution.py:58
  263.6 16.3 %collective-permute-start.30 = (bf16[152,1024]{1,0:T(8,128)(2,1)S(1)}, bf16[152,1024]{1,0:T(8,128)(2,1)S(1)}, u32[]{:S(2)}, u32[]{:S(2)}) collective-permute-start(bf16[152,1024]{1,0:T(8,128)(2,1)S(1)} %get-tuple-element.97), channel_id=1, source_target_pairs={{0,16},{8,24},{16,0},{24,8},{1,17},{9,25},{17,1},{25,9},{2,18},{10... | collective-permute-start | bytes 933896 | tf_op jit(solution)/shard_map/ppermute | solution.py:58
  266.7 18.6 %collective-permute-start.23 = (bf16[152,1024]{1,0:T(8,128)(2,1)S(1)}, bf16[152,1024]{1,0:T(8,128)(2,1)S(1)}, u32[]{:S(2)}, u32[]{:S(2)}) collective-permute-start(bf16[152,1024]{1,0:T(8,128)(2,1)S(1)} %get-tuple-element.98), channel_id=1, source_target_pairs={{0,8},{8,0},{16,24},{24,16},{1,9},{9,1},{17,25},{25,17},{2,10},{10... | collective-permute-start | bytes 933896 | tf_op jit(solution)/shard_map/ppermute | solution.py:58
  267.1 22.4 %collective-permute-start.25 = (bf16[152,1024]{1,0:T(8,128)(2,1)S(1)}, bf16[152,1024]{1,0:T(8,128)(2,1)S(1)}, u32[]{:S(2)}, u32[]{:S(2)}) collective-permute-start(bf16[152,1024]{1,0:T(8,128)(2,1)S(1)} %get-tuple-element.99), channel_id=1, source_target_pairs={{0,24},{8,16},{16,8},{24,0},{1,25},{9,17},{17,9},{25,1},{2,26},{10... | collective-permute-start | bytes 933896 | tf_op jit(solution)/shard_map/ppermute | solution.py:58
  271.9 18.8 %collective-permute-start.24 = (bf16[152,1024]{1,0:T(8,128)(2,1)S(1)}, bf16[152,1024]{1,0:T(8,128)(2,1)S(1)}, u32[]{:S(2)}, u32[]{:S(2)}) collective-permute-start(bf16[152,1024]{1,0:T(8,128)(2,1)S(1)} %get-tuple-element.100), channel_id=1, source_target_pairs={{0,16},{8,24},{16,0},{24,8},{1,17},{9,25},{17,1},{25,9},{2,18},{10... | collective-permute-start | bytes 933896 | tf_op jit(solution)/shard_map/ppermute | solution.py:58
  293.6 11.6 %collective-permute-start.33 = (bf16[152,1024]{1,0:T(8,128)(2,1)S(1)}, bf16[152,1024]{1,0:T(8,128)(2,1)S(1)}, u32[]{:S(2)}, u32[]{:S(2)}) collective-permute-start(bf16[152,1024]{1,0:T(8,128)(2,1)S(1)} %get-tuple-element.52), channel_id=1, source_target_pairs={{0,16},{8,24},{16,0},{24,8},{1,17},{9,25},{17,1},{25,9},{2,18},{10... | collective-permute-start | bytes 933896 | tf_op jit(solution)/shard_map/ppermute | solution.py:58
  336.4 13.9 %collective-permute-start.37 = (bf16[152,1024]{1,0:T(8,128)(2,1)S(1)}, bf16[152,1024]{1,0:T(8,128)(2,1)S(1)}, u32[]{:S(2)}, u32[]{:S(2)}) collective-permute-start(bf16[152,1024]{1,0:T(8,128)(2,1)S(1)} %get-tuple-element.93), channel_id=1, source_target_pairs={{0,24},{8,16},{16,8},{24,0},{1,25},{9,17},{17,9},{25,1},{2,26},{10... | collective-permute-start | bytes 933896 | tf_op jit(solution)/shard_map/ppermute | solution.py:58
  338.0 13.7 %collective-permute-start.36 = (bf16[152,1024]{1,0:T(8,128)(2,1)S(1)}, bf16[152,1024]{1,0:T(8,128)(2,1)S(1)}, u32[]{:S(2)}, u32[]{:S(2)}) collective-permute-start(bf16[152,1024]{1,0:T(8,128)(2,1)S(1)} %get-tuple-element.94), channel_id=1, source_target_pairs={{0,16},{8,24},{16,0},{24,8},{1,17},{9,25},{17,1},{25,9},{2,18},{10... | collective-permute-start | bytes 933896 | tf_op jit(solution)/shard_map/ppermute | solution.py:58
  353.9 11.5 %collective-permute-start.39 = (bf16[152,1024]{1,0:T(8,128)(2,1)S(1)}, bf16[152,1024]{1,0:T(8,128)(2,1)S(1)}, u32[]{:S(2)}, u32[]{:S(2)}) collective-permute-start(bf16[152,1024]{1,0:T(8,128)(2,1)S(1)} %get-tuple-element.50), channel_id=1, source_target_pairs={{0,16},{8,24},{16,0},{24,8},{1,17},{9,25},{17,1},{25,9},{2,18},{10... | collective-permute-start | bytes 933896 | tf_op jit(solution)/shard_map/ppermute | solution.py:58
  371.4 13.1 %collective-permute-start.43 = (bf16[152,1024]{1,0:T(8,128)(2,1)S(1)}, bf16[152,1024]{1,0:T(8,128)(2,1)S(1)}, u32[]{:S(2)}, u32[]{:S(2)}) collective-permute-start(bf16[152,1024]{1,0:T(8,128)(2,1)S(1)} %get-tuple-element.90), channel_id=1, source_target_pairs={{0,24},{8,16},{16,8},{24,0},{1,25},{9,17},{17,9},{25,1},{2,26},{10... | collective-permute-start | bytes 933896 | tf_op jit(solution)/shard_map/ppermute | solution.py:58
  373.1 16.8 %collective-permute-start.42 = (bf16[152,1024]{1,0:T(8,128)(2,1)S(1)}, bf16[152,1024]{1,0:T(8,128)(2,1)S(1)}, u32[]{:S(2)}, u32[]{:S(2)}) collective-permute-start(bf16[152,1024]{1,0:T(8,128)(2,1)S(1)} %get-tuple-element.91), channel_id=1, source_target_pairs={{0,16},{8,24},{16,0},{24,8},{1,17},{9,25},{17,1},{25,9},{2,18},{10... | collective-permute-start | bytes 933896 | tf_op jit(solution)/shard_map/ppermute | solution.py:58
  431.1 66.0 %reduce-scatter.10.cloned.1.call-start = ((), (), s32[]{:S(2)}) async-start(), calls=%async_computation.8 | async-start | bytes 1769472 | tf_op jit(solution)/shard_map/reduce_scatter | solution.py:309
  435.1 97.1 %reduce-scatter.8.cloned.1.call-start = ((), (), s32[]{:S(2)}) async-start(), calls=%async_computation.7 | async-start | bytes 1769472 | tf_op jit(solution)/shard_map/reduce_scatter | solution.py:309
  438.9 148.5 %reduce-scatter.14.cloned.1.call-start = ((), (), s32[]{:S(2)}) async-start(), calls=%async_computation.10 | async-start | bytes 5308416 | tf_op jit(solution)/shard_map/reduce_scatter | solution.py:309
  447.4 195.8 %reduce-scatter.12.cloned.1.call-start = ((), (), s32[]{:S(2)}) async-start(), calls=%async_computation.9 | async-start | bytes 5308416 | tf_op jit(solution)/shard_map/reduce_scatter | solution.py:309
  462.7 37.1 %collective-permute-start.52 = (bf16[145,128]{1,0:T(8,128)(2,1)S(1)}, bf16[145,128]{1,0:T(8,128)(2,1)S(1)}, u32[]{:S(2)}, u32[]{:S(2)}) collective-permute-start(bf16[145,128]{1,0:T(8,128)(2,1)S(1)} %copy.255), channel_id=1, source_target_pairs={{0,24},{8,16},{16,8},{24,0},{1,25},{9,17},{17,9},{25,1},{2,26},{10... | collective-permute-start | bytes 111368 | tf_op jit(solution)/shard_map/ppermute | solution.py:58
  465.1 35.4 %collective-permute-start.51 = (bf16[145,128]{1,0:T(8,128)(2,1)S(1)}, bf16[145,128]{1,0:T(8,128)(2,1)S(1)}, u32[]{:S(2)}, u32[]{:S(2)}) collective-permute-start(bf16[145,128]{1,0:T(8,128)(2,1)S(1)} %copy.255), channel_id=1, source_target_pairs={{0,16},{8,24},{16,0},{24,8},{1,17},{9,25},{17,1},{25,9},{2,18},{10... | collective-permute-start | bytes 111368 | tf_op jit(solution)/shard_map/ppermute | solution.py:58
  465.6 34.9 %collective-permute-start.50 = (bf16[145,128]{1,0:T(8,128)(2,1)S(1)}, bf16[145,128]{1,0:T(8,128)(2,1)S(1)}, u32[]{:S(2)}, u32[]{:S(2)}) collective-permute-start(bf16[145,128]{1,0:T(8,128)(2,1)S(1)} %copy.255), channel_id=1, source_target_pairs={{0,8},{8,0},{16,24},{24,16},{1,9},{9,1},{17,25},{25,17},{2,10},{10... | collective-permute-start | bytes 111368 | tf_op jit(solution)/shard_map/ppermute | solution.py:58
  587.4 16.6 %collective-permute-start.65 = (bf16[288,1024]{1,0:T(8,128)(2,1)}, bf16[288,1024]{1,0:T(8,128)(2,1)}, u32[]{:S(2)}, u32[]{:S(2)}) collective-permute-start(bf16[288,1024]{1,0:T(8,128)(2,1)} %bitcast.382), channel_id=1, source_target_pairs={{0,8},{8,0},{16,24},{24,16},{1,9},{9,1},{17,25},{25,17},{2,10},{10... | collective-permute-start | bytes 1769480 | tf_op jit(solution)/shard_map/ppermute | solution.py:58
  588.9 25.6 %collective-permute-start.64 = (bf16[288,1024]{1,0:T(8,128)(2,1)}, bf16[288,1024]{1,0:T(8,128)(2,1)}, u32[]{:S(2)}, u32[]{:S(2)}) collective-permute-start(bf16[288,1024]{1,0:T(8,128)(2,1)} %bitcast.383), channel_id=1, source_target_pairs={{0,16},{8,24},{16,0},{24,8},{1,17},{9,25},{17,1},{25,9},{2,18},{10... | collective-permute-start | bytes 1769480 | tf_op jit(solution)/shard_map/ppermute | solution.py:58
  590.4 24.1 %collective-permute-start.63 = (bf16[288,1024]{1,0:T(8,128)(2,1)}, bf16[288,1024]{1,0:T(8,128)(2,1)}, u32[]{:S(2)}, u32[]{:S(2)}) collective-permute-start(bf16[288,1024]{1,0:T(8,128)(2,1)} %bitcast.384), channel_id=1, source_target_pairs={{0,24},{8,16},{16,8},{24,0},{1,25},{9,17},{17,9},{25,1},{2,26},{10... | collective-permute-start | bytes 1769480 | tf_op jit(solution)/shard_map/ppermute | solution.py:58
  616.8 31.4 %collective-permute-start.66 = (bf16[2,32,1024]{2,1,0:T(8,128)(2,1)}, bf16[2,32,1024]{2,1,0:T(8,128)(2,1)S(1)}, u32[]{:S(2)}, u32[]{:S(2)}) collective-permute-start(bf16[2,32,1024]{2,1,0:T(8,128)(2,1)} %select_bitcast_fusion.16), channel_id=1, source_target_pairs={{0,1},{1,0},{2,3},{3,2},{4,5},{5,4},{6,7},{7,6},{8,9},{9,8},{10,11... | collective-permute-start | bytes 393224 | tf_op jit(solution)/shard_map/ppermute | solution.py:338
  643.2 16.5 %collective-permute-start.61 = (bf16[288,1024]{1,0:T(8,128)(2,1)}, bf16[288,1024]{1,0:T(8,128)(2,1)S(1)}, u32[]{:S(2)}, u32[]{:S(2)}) collective-permute-start(bf16[288,1024]{1,0:T(8,128)(2,1)} %bitcast.379), channel_id=1, source_target_pairs={{0,8},{8,0},{16,24},{24,16},{1,9},{9,1},{17,25},{25,17},{2,10},{10... | collective-permute-start | bytes 1769480 | tf_op jit(solution)/shard_map/ppermute | solution.py:58
  644.7 25.5 %collective-permute-start.60 = (bf16[288,1024]{1,0:T(8,128)(2,1)}, bf16[288,1024]{1,0:T(8,128)(2,1)S(1)}, u32[]{:S(2)}, u32[]{:S(2)}) collective-permute-start(bf16[288,1024]{1,0:T(8,128)(2,1)} %bitcast.380), channel_id=1, source_target_pairs={{0,16},{8,24},{16,0},{24,8},{1,17},{9,25},{17,1},{25,9},{2,18},{10... | collective-permute-start | bytes 1769480 | tf_op jit(solution)/shard_map/ppermute | solution.py:58
  646.1 24.0 %collective-permute-start.59 = (bf16[288,1024]{1,0:T(8,128)(2,1)}, bf16[288,1024]{1,0:T(8,128)(2,1)S(1)}, u32[]{:S(2)}, u32[]{:S(2)}) collective-permute-start(bf16[288,1024]{1,0:T(8,128)(2,1)} %bitcast.381), channel_id=1, source_target_pairs={{0,24},{8,16},{16,8},{24,0},{1,25},{9,17},{17,9},{25,1},{2,26},{10... | collective-permute-start | bytes 1769480 | tf_op jit(solution)/shard_map/ppermute | solution.py:58
  (178 other events, 1510.0 us)
Sparse Core Ops, SparseCore 0:
  12.7 29.1 all-gather.6
  44.1 51.4 all-gather.10
  97.8 50.5 all-gather.12
  149.8 23.8 all-gather.8
  431.1 30.5 reduce-scatter.15
  464.6 32.4 reduce-scatter.9
  500.0 32.2 reduce-scatter.7
  534.6 52.7 reduce-scatter.13
  589.9 53.3 reduce-scatter.11

commit v2 on v1

--- a/solution.py
+++ b/solution.py
@@ -3,6 +3,8 @@
 import jax
 import jax.numpy as jnp
 from jax import lax
+from jax.experimental import pallas as pl
+from jax.experimental.pallas import tpu as pltpu
 from jax.sharding import PartitionSpec as P
 
 HEADS = 16
@@ -104,7 +106,7 @@
     return out
 
 
-def local(
+def local_general(
     tokens,
     pos_table,
     index_lo,
@@ -368,6 +370,638 @@
     )
 
 
+VMEM = pltpu.VMEM
+LANES = 128
+
+
+def whole(shape):
+    return pl.BlockSpec(tuple(shape), lambda *_: (0,) * len(shape))
+
+
+def scalars():
+    return pl.BlockSpec(memory_space=pltpu.SMEM)
+
+
+def call(body, outs, args, specs=None, scratch=(), flops=0, reads=0, aliases=None, out_specs=None, limit=40):
+    specs = [whole(a.shape) if s is None else s for a, s in zip(args, specs or [None] * len(args))]
+    out_shape = [jax.ShapeDtypeStruct(shape, dtype) for shape, dtype in outs]
+    moved = sum(math.prod(s) * jnp.dtype(d).itemsize for s, d in outs) + reads
+    return pl.pallas_call(
+        body,
+        grid=(1,),
+        in_specs=specs,
+        out_specs=out_specs or [whole(shape) for shape, _ in outs],
+        out_shape=out_shape,
+        scratch_shapes=list(scratch),
+        input_output_aliases=aliases or {},
+        cost_estimate=pl.CostEstimate(flops=int(flops), bytes_accessed=int(moved), transcendentals=0),
+        compiler_params=pltpu.CompilerParams(vmem_limit_bytes=limit << 20),
+    )(*args)
+
+
+def diagonal(gain_row):
+    r = lax.broadcasted_iota(jnp.int32, (LANES, LANES), 0)
+    c = lax.broadcasted_iota(jnp.int32, (LANES, LANES), 1)
+    return jnp.where(r == c, jnp.broadcast_to(gain_row.astype(F32), (LANES, LANES)), 0.0)
+
+
+def lane_low(rows):
+    return lax.broadcasted_iota(jnp.int32, (rows, LANES), 1) < LANES // 2
+
+
+def lane_swap(block):
+    return jnp.concatenate([block[:, LANES // 2 :], block[:, : LANES // 2]], axis=1)
+
+
+def prepare_attention(me_ref, w_ref, gain_ref, out_ref, packed_ref):
+    side, second = me_ref[0] & 1, me_ref[0] >> 1
+    diag = diagonal(gain_ref[0]).astype(BF16)
+    rows = w_ref.shape[1]
+    low = lane_low(rows)
+
+    def head(t):
+        chunk = pl.multiple_of(((t // 4) * 8 + 2 * (t % 4) + side) * LANES, LANES)
+        got = dot(diag, w_ref[0, :, pl.ds(chunk, LANES)])
+        turned = lane_swap(got)
+        if t % 2 == 0:
+            return jnp.where(second == 0, got, turned)
+        return jnp.where(second == 0, turned, got)
+
+    for u in range(6):
+        pair = jnp.where(low, head(2 * u), head(2 * u + 1))
+        packed_ref[:, u * LANES : (u + 1) * LANES] = pair.astype(BF16)
+    for c in range(4):
+        packed_ref[c * 32 : (c + 1) * 32, 768:1024] = out_ref[:, c * 256 : (c + 1) * 256]
+
+
+def prepare_mlp(me_ref, up_ref, gain_ref, down_ref, packed_ref):
+    me = me_ref[0]
+    diag = diagonal(gain_ref[0]).astype(BF16)
+    for j in range(8):
+        chunk = pl.multiple_of((j * 4 + me) * LANES, LANES)
+        packed_ref[:LANES, j * LANES : (j + 1) * LANES] = dot(
+            diag, up_ref[0, :, pl.ds(chunk, LANES)]
+        ).astype(BF16)
+    packed_ref[LANES:, :] = down_ref[0, pl.ds(pl.multiple_of(me * LANES, LANES), LANES), :]
+
+
+def image_numbers(rows, flag, lens):
+    counts = [sum((rows >= t * n).astype(jnp.int32) for t in range(1, most + 1)) for n, most in lens]
+    return jnp.where(flag == 1, counts[1], counts[0])
+
+
+def make_mixing(flag_ref, low_ref, high_ref, mixing_ref, *, lens):
+    rows = mixing_ref.shape[0]
+    flag = flag_ref[0]
+
+    def spread_rows(index_ref, length, most):
+        count = index_ref.shape[0]
+        columns = lax.broadcasted_iota(jnp.int32, (count, mixing_ref.shape[1]), 1)
+        mix = jnp.zeros((count, mixing_ref.shape[1]), F32)
+        for slot in range(4):
+            mix = mix + MIX_WEIGHTS[slot] * (index_ref[:, slot : slot + 1] == columns).astype(F32)
+        r = lax.broadcasted_iota(jnp.int32, (rows, count), 0)
+        c = lax.broadcasted_iota(jnp.int32, (rows, count), 1)
+        image = sum((r >= t * length).astype(jnp.int32) for t in range(1, most + 1))
+        pick = ((r - image * length == c) & (r < most * length)).astype(BF16)
+        return dot(pick, mix.astype(BF16))
+
+    low = spread_rows(low_ref, *lens[0])
+    high = spread_rows(high_ref, *lens[1])
+    mixing_ref[...] = jnp.where(flag == 1, high, low).astype(BF16)
+
+
+def write_norm(hidden, xhat_ref, rstd_ref):
+    xhat, rstd = normalize(hidden)
+    xhat_ref[...] = xhat.astype(BF16)
+    rstd_ref[...] = jnp.broadcast_to(rstd, rstd_ref.shape)
+
+
+def embed(z_ref, tokens_ref, mixing_ref, t0, t1, t2, t3, hidden_ref, xhat_ref, rstd_ref, table):
+    z = z_ref[0]
+    for k, piece in enumerate((t0, t1, t2, t3)):
+        table[:, pl.ds(pl.multiple_of((z ^ k) * 256, 256), 256)] = piece[...].astype(F32)
+    hidden = tokens_ref[...].astype(F32) + dot(mixing_ref[...], table[...].astype(BF16))
+    hidden_ref[...] = hidden
+    write_norm(hidden, xhat_ref, rstd_ref)
+
+
+def added(p0, r1, r2, r3):
+    return (p0[...].astype(F32) + r1[...].astype(F32)) + (r2[...].astype(F32) + r3[...].astype(F32))
+
+
+def add_norm(h_ref, p0, r1, r2, r3, middle_ref, xhat_ref, rstd_ref):
+    middle = h_ref[...] + added(p0, r1, r2, r3)
+    middle_ref[...] = middle
+    write_norm(middle, xhat_ref, rstd_ref)
+
+
+def add_norm_backward(g_ref, p0, r1, r2, r3, xhat_ref, rstd_ref, d_ref, low_ref):
+    e = added(p0, r1, r2, r3)
+    d = g_ref[...] + norm_backward(e, xhat_ref[...].astype(F32), rstd_ref[:, :1])
+    d_ref[...] = d
+    low_ref[...] = d.astype(BF16)
+
+
+def out_chunk(packed_ref, c):
+    return packed_ref[:, c * 32 : (c + 1) * 32, 768:1024].reshape(256, 256)
+
+
+def attention_forward(flag_ref, x_ref, w_ref, proj_ref, att_ref, p_ref, *, lens):
+    rows = x_ref.shape[0]
+    flag = flag_ref[0]
+    width = x_ref.shape[1]
+    mask = image_numbers(lax.broadcasted_iota(jnp.int32, (rows, 1), 0), flag, lens) == image_numbers(
+        lax.broadcasted_iota(jnp.int32, (1, rows), 1), flag, lens
+    )
+    for c in range(3):
+        w = w_ref[:, :, c * 256 : (c + 1) * 256].reshape(width, 256)
+        proj_ref[:, c * 256 : (c + 1) * 256] = dot(x_ref[...], w).astype(BF16)
+    low = lane_low(rows)
+    zero = jnp.zeros((), BF16)
+    for u in range(2):
+        q = proj_ref[:, u * LANES : (u + 1) * LANES] * jnp.asarray(0.125, BF16)
+        k = proj_ref[:, 256 + u * LANES : 256 + (u + 1) * LANES]
+        v = proj_ref[:, 512 + u * LANES : 512 + (u + 1) * LANES]
+        total = None
+        for keep in (low, ~low):
+            s = dot_nt(jnp.where(keep, q, zero), k)
+            s = jnp.where(mask, s, NEG_FILL)
+            powers = jnp.exp(s - jnp.max(s, axis=-1, keepdims=True))
+            probs = powers * (1.0 / jnp.sum(powers, axis=-1, keepdims=True))
+            o = dot(probs.astype(BF16), jnp.where(keep, v, zero))
+            total = o if total is None else total + o
+        att_ref[:, u * LANES : (u + 1) * LANES] = total.astype(BF16)
+    for c in range(4):
+        p_ref[:, c * 256 : (c + 1) * 256] = dot(att_ref[...], out_chunk(w_ref, c)).astype(BF16)
+
+
+def attention_backward(flag_ref, d_ref, proj_ref, w_ref, dproj_ref, p_ref, *, lens):
+    rows, width = d_ref.shape
+    flag = flag_ref[0]
+    mask = image_numbers(lax.broadcasted_iota(jnp.int32, (rows, 1), 0), flag, lens) == image_numbers(
+        lax.broadcasted_iota(jnp.int32, (1, rows), 1), flag, lens
+    )
+    d_o = sum(dot_nt(d_ref[:, c * 256 : (c + 1) * 256], out_chunk(w_ref, c)) for c in range(4))
+    d_o = d_o.astype(BF16)
+    low = lane_low(rows)
+    zero = jnp.zeros((), BF16)
+    scale = jnp.asarray(0.125, BF16)
+    for u in range(2):
+        q = proj_ref[:, u * LANES : (u + 1) * LANES] * scale
+        k = proj_ref[:, 256 + u * LANES : 256 + (u + 1) * LANES]
+        v = proj_ref[:, 512 + u * LANES : 512 + (u + 1) * LANES]
+        g = d_o[:, u * LANES : (u + 1) * LANES]
+        dq = dk = dv = None
+        for keep in (low, ~low):
+            k_own = jnp.where(keep, k, zero)
+            s = jnp.where(mask, dot_nt(k_own, q), NEG_FILL)
+            powers = jnp.exp(s - jnp.max(s, axis=0, keepdims=True))
+            probs = powers * (1.0 / jnp.sum(powers, axis=0, keepdims=True))
+            d_probs = dot_nt(jnp.where(keep, v, zero), g)
+            centre = jnp.sum(probs * d_probs, axis=0, keepdims=True)
+            d_scores = (probs * (d_probs - centre)).astype(BF16)
+            terms = (
+                dot_t(d_scores, k_own),
+                dot(d_scores, jnp.where(keep, q, zero)),
+                dot(probs.astype(BF16), jnp.where(keep, g, zero)),
+            )
+            dq, dk, dv = terms if dq is None else (dq + terms[0], dk + terms[1], dv + terms[2])
+        dproj_ref[:, u * LANES : (u + 1) * LANES] = (dq * 0.125).astype(BF16)
+        dproj_ref[:, 256 + u * LANES : 256 + (u + 1) * LANES] = dk.astype(BF16)
+        dproj_ref[:, 512 + u * LANES : 512 + (u + 1) * LANES] = dv.astype(BF16)
+    total = None
+    for c in range(3):
+        w = w_ref[:, :, c * 256 : (c + 1) * 256].reshape(width, 256)
+        term = dot_nt(dproj_ref[:, c * 256 : (c + 1) * 256], w)
+        total = term if total is None else total + term
+    p_ref[...] = total.astype(BF16)
+
+
+def gelu_parts(pre):
+    upto = 0.5 * (1.0 + lax.erf(pre * math.sqrt(0.5)))
+    density = jnp.exp(-0.5 * pre * pre) * (1.0 / math.sqrt(2.0 * math.pi))
+    return pre * upto, upto + pre * density
+
+
+def mlp_forward(x_ref, up_ref, down_ref, act_ref, slope_ref, p_ref):
+    width = x_ref.shape[1]
+    for c in range(4):
+        cols = slice(c * 256, (c + 1) * 256)
+        act, slope = gelu_parts(dot(x_ref[...], up_ref[:, :, cols].reshape(width, 256)))
+        act_ref[:, cols] = act.astype(BF16)
+        slope_ref[:, cols] = slope.astype(BF16)
+    p_ref[...] = dot(act_ref[...], down_ref[...].reshape(width, width)).astype(BF16)
+
+
+def mlp_backward(d_ref, slope_ref, up_ref, down_ref, dpre_ref, p_ref):
+    width = d_ref.shape[1]
+    for c in range(4):
+        cols = slice(c * 256, (c + 1) * 256)
+        d_act = dot_nt(d_ref[...], down_ref[2 * c : 2 * c + 2].reshape(256, width))
+        dpre_ref[:, cols] = (d_act * slope_ref[:, cols].astype(F32)).astype(BF16)
+    p_ref[...] = dot_nt(dpre_ref[...], up_ref[...].reshape(width, width)).astype(BF16)
+
+
+def mlp_both(x_ref, d_ref, up_ref, down_ref, act_ref, dpre_ref, p_ref, back_ref):
+    width = x_ref.shape[1]
+    for c in range(4):
+        cols = slice(c * 256, (c + 1) * 256)
+        act, slope = gelu_parts(dot(x_ref[...], up_ref[:, :, cols].reshape(width, 256)))
+        act_ref[:, cols] = act.astype(BF16)
+        d_act = dot_nt(d_ref[...], down_ref[2 * c : 2 * c + 2].reshape(256, width))
+        dpre_ref[:, cols] = (d_act * slope).astype(BF16)
+    back_ref[...] = dot_nt(dpre_ref[...], up_ref[...].reshape(width, width)).astype(BF16)
+    p_ref[...] = dot(act_ref[...], down_ref[...].reshape(width, width)).astype(BF16)
+
+
+def grads_mlp(*refs):
+    x, dpre, act, d, out_ref = refs[:4], refs[4:8], refs[8:12], refs[12:16], refs[16]
+    for half, (left, right) in enumerate(((x, dpre), (act, d))):
+        for j in range(8):
+            rows = slice(j * LANES, (j + 1) * LANES)
+            total = None
+            for a, b in zip(left, right):
+                term = dot_t(a[:, rows], b[...])
+                total = term if total is None else total + term
+            out_ref[j, half * LANES : (half + 1) * LANES, :] = total.astype(BF16)
+
+
+def grads_attention(*refs):
+    x, dproj, att, d, out_ref = refs[:4], refs[4:8], refs[8:12], refs[12:16], refs[16]
+    for j in range(8):
+        rows = slice(j * LANES, (j + 1) * LANES)
+        total = None
+        for a, b in zip(x, dproj):
+            term = dot_t(a[:, rows], b[...])
+            total = term if total is None else total + term
+        out_ref[j, :, :768] = total.astype(BF16)
+    for c in range(4):
+        cols = slice(c * 256, (c + 1) * 256)
+        total = None
+        for a, b in zip(att, d):
+            term = dot_t(a[...], b[:, cols])
+            total = term if total is None else total + term
+        out_ref[:, c * 32 : (c + 1) * 32, 768:1024] = total.astype(BF16).reshape(8, 32, 256)
+
+
+def finish_mlp(me_ref, g0, g1, g2, g3, up_ref, gain_ref, *rest):
+    dup_ref, ddown_ref, dgain_ref = rest[-3:]
+    me = me_ref[0]
+    diag = diagonal(gain_ref[0])
+    total = jnp.zeros((LANES, LANES), F32)
+    column = jnp.sum(diag, axis=1, keepdims=True)
+    for k, piece in enumerate((g0, g1, g2, g3)):
+        owner = me ^ k
+        ddown_ref[0, pl.ds(pl.multiple_of(owner * LANES, LANES), LANES), :] = piece[LANES:, :].astype(F32)
+    for i in range(4):
+        got = jnp.where(
+            me == i, g0[:LANES, :], jnp.where(me == i ^ 1, g1[:LANES, :], jnp.where(me == i ^ 2, g2[:LANES, :], g3[:LANES, :]))
+        ).astype(F32)
+        for j in range(8):
+            cols = slice((j * 4 + i) * LANES, (j * 4 + i + 1) * LANES)
+            part = got[:, j * LANES : (j + 1) * LANES]
+            dup_ref[0, :, cols] = part * column
+            total = total + part * up_ref[0, :, cols].astype(F32)
+    dgain_ref[0] = jnp.sum(total.T, axis=0, keepdims=True)
+
+
+def finish_attention(me_ref, g0, g1, g2, g3, w_ref, gain_ref, out_ref, *rest):
+    dqkv_ref, dout_ref, dgain_ref = rest[-3:]
+    me = me_ref[0]
+    column = jnp.sum(diagonal(gain_ref[0]), axis=1, keepdims=True)
+    total = jnp.zeros((LANES, LANES), F32)
+    low = lane_low(LANES)
+    owned = []
+    for i in range(4):
+        owned.append(
+            jnp.where(
+                me == i, g0[:, :768], jnp.where(me == i ^ 1, g1[:, :768], jnp.where(me == i ^ 2, g2[:, :768], g3[:, :768]))
+            ).astype(F32)
+        )
+    for t in range(12):
+        u = t // 2
+        for side in range(2):
+            first = owned[side][:, u * LANES : (u + 1) * LANES]
+            second = owned[side + 2][:, u * LANES : (u + 1) * LANES]
+            if t % 2 == 0:
+                part = jnp.where(low, first, lane_swap(second))
+            else:
+                part = jnp.where(low, lane_swap(first), second)
+            chunk = (t // 4) * 8 + 2 * (t % 4) + side
+            cols = slice(chunk * LANES, (chunk + 1) * LANES)
+            dqkv_ref[0, :, cols] = part * column
+            total = total + part * w_ref[0, :, cols].astype(F32)
+    dgain_ref[0] = jnp.sum(total.T, axis=0, keepdims=True)
+    for h in range(4):
+        for c in range(4):
+            dout_ref[0, h * 32 : (h + 1) * 32, c * 256 : (c + 1) * 256] = out_ref[
+                h, c * 32 : (c + 1) * 32, :
+            ].astype(F32)
+
+
+def local_fast(
+    tokens,
+    pos_table,
+    index_lo,
+    index_hi,
+    resolution,
+    gain_attn,
+    w_qkv,
+    w_out,
+    gain_mlp,
+    w_up,
+    w_down,
+    cotangent,
+):
+    rows, width = tokens.shape
+    layers = w_qkv.shape[0]
+    square = Square()
+    me = square.me
+    me1 = me.reshape(1).astype(jnp.int32)
+    shard = lax.axis_index("fsdp")
+    core, deep = shard % 2, shard // 2
+    deep1 = deep.reshape(1).astype(jnp.int32)
+    len_low, len_high = index_lo.shape[0], index_hi.shape[0]
+    lens = ((len_low, rows // len_low), (len_high, rows // len_high))
+    block = (rows, width)
+    blocks = range(4)
+
+    def over_fsdp(x, k):
+        return lax.ppermute(x, "fsdp", [(j, j ^ k) for j in range(8)])
+
+    def layer_of(array, depth):
+        return pl.BlockSpec((1,) + array.shape[1:], lambda *_: (depth,) + (0,) * (array.ndim - 1))
+
+    pair_side, head_side = me & 1, me >> 1
+    view = w_out.reshape(layers, 2, 2, 32, width)
+    mine = jnp.where(head_side == 1, view[:, 1], view[:, 0])
+    keep = jnp.where(core == 1, mine[:, 1], mine[:, 0])
+    give = jnp.where(core == 1, mine[:, 0], mine[:, 1])
+    out_pieces = jnp.where(core == pair_side, keep, over_fsdp(give, 1))
+    gains_a = gain_attn.reshape(layers, 1, LANES)
+    gains_m = gain_mlp.reshape(layers, 1, LANES)
+    attn_w, mlp_w = [], []
+    for depth in range(layers):
+        (packed,) = call(
+            prepare_attention,
+            [((LANES, width), BF16)],
+            [me1, w_qkv, gains_a, out_pieces[depth]],
+            [scalars(), layer_of(w_qkv, depth), layer_of(gains_a, depth), None],
+        )
+        attn_w.append(lax.all_gather(packed, "fsdp", axis=0, tiled=False))
+        (packed,) = call(
+            prepare_mlp,
+            [((2 * LANES, width), BF16)],
+            [me1, w_up, gains_m, w_down],
+            [scalars(), layer_of(w_up, depth), layer_of(gains_m, depth), layer_of(w_down, depth)],
+        )
+        mlp_w.append(lax.all_gather(packed, "fsdp", axis=0, tiled=False))
+    up_spec = pl.BlockSpec((8, LANES, width), lambda *_: (0, 0, 0))
+    down_spec = pl.BlockSpec((8, LANES, width), lambda *_: (0, 1, 0))
+
+    flag = resolution[me]
+    flag1 = flag.reshape(1)
+    flags = [resolution[owner].reshape(1) for owner in square.owners()]
+    shard_count, group_count = 8, resolution.shape[0]
+    high_groups = jnp.sum(resolution)
+    tokens_low = ((group_count - high_groups) * shard_count * lens[0][1] * len_low).astype(F32)
+    tokens_high = (high_groups * shard_count * lens[1][1] * len_high).astype(F32)
+    token_share = 2.0 * jnp.where(flag == 1, tokens_high, tokens_low) / (tokens_low + tokens_high)
+    live = jnp.where(flag == 1, lens[1][1] * len_high, lens[0][1] * len_low)
+    weight = jnp.where(jnp.arange(rows, dtype=jnp.int32) < live, token_share, 0.0)
+    gradient = cotangent.astype(F32) * weight[:, None]
+
+    other = over_fsdp(pos_table, 1)
+    pair = jnp.concatenate(
+        [jnp.where(core == 0, pos_table, other), jnp.where(core == 0, other, pos_table)], axis=1
+    )
+    pieces = [pair] + [over_fsdp(pair, 2 * k) for k in range(1, 4)]
+    (mixing,) = call(
+        lambda *refs: make_mixing(*refs, lens=lens),
+        [((rows, len_high), BF16)],
+        [flag1, index_lo, index_hi],
+        [scalars(), None, None],
+    )
+    hidden, xhat, rstd = call(
+        embed,
+        [(block, F32), (block, BF16), ((rows, LANES), F32)],
+        [deep1, tokens, mixing] + pieces,
+        [scalars()] + [None] * 6,
+        scratch=[VMEM((len_high, width), F32)],
+        flops=2 * rows * len_high * width,
+    )
+
+    def collect(parts):
+        return [parts[0]] + [square.swap(parts[k], k) for k in range(1, 4)]
+
+    d_top = square.spread(gradient.astype(BF16))
+    saved = []
+    for depth in range(layers):
+        a_w, m_w = attn_w[depth], mlp_w[depth]
+        xs = square.spread(xhat)
+        got = [
+            call(
+                lambda *refs: attention_forward(*refs, lens=lens),
+                [((rows, 768), BF16), ((rows, 256), BF16), (block, BF16)],
+                [flags[k], xs[k], a_w],
+                [scalars(), None, None],
+                flops=2 * rows * width * 1024,
+                reads=2 * a_w.size,
+            )
+            for k in blocks
+        ]
+        projs, atts = [g[0] for g in got], [g[1] for g in got]
+        middle, xhat_m, rstd_m = call(
+            add_norm,
+            [(block, F32), (block, BF16), ((rows, LANES), F32)],
+            [hidden] + collect([g[2] for g in got]),
+            reads=4 * rows * width,
+        )
+        ms = square.spread(xhat_m)
+        last = depth == layers - 1
+        if last:
+            got = [
+                call(
+                    mlp_both,
+                    [(block, BF16)] * 4,
+                    [ms[k], d_top[k], m_w, m_w],
+                    [None, None, up_spec, down_spec],
+                    flops=8 * rows * width * width,
+                    reads=2 * m_w.size,
+                )
+                for k in blocks
+            ]
+            acts, dpres, ps, backs = ([g[t] for g in got] for t in range(4))
+            slopes = None
+        else:
+            got = [
+                call(
+                    mlp_forward,
+                    [(block, BF16)] * 3,
+                    [ms[k], m_w, m_w],
+                    [None, up_spec, down_spec],
+                    flops=4 * rows * width * width,
+                    reads=2 * m_w.size,
+                )
+                for k in blocks
+            ]
+            acts, slopes, ps = ([g[t] for g in got] for t in range(3))
+            dpres = backs = None
+        saved.append((xhat, rstd, xs, projs, atts, xhat_m, rstd_m, ms, acts, slopes))
+        if last:
+            output_parts = ps
+        else:
+            hidden, xhat, rstd = call(
+                add_norm,
+                [(block, F32), (block, BF16), ((rows, LANES), F32)],
+                [middle] + collect(ps),
+                reads=4 * rows * width,
+            )
+
+    homes_m, homes_a = [None] * layers, [None] * layers
+    held = None
+    output = None
+    for depth in reversed(range(layers)):
+        a_w, m_w = attn_w[depth], mlp_w[depth]
+        xhat, rstd, xs, projs, atts, xhat_m, rstd_m, ms, acts, slopes = saved[depth]
+        if depth == layers - 1:
+            ds = d_top
+        else:
+            ds = square.spread(low)
+            got = [
+                call(
+                    mlp_backward,
+                    [(block, BF16)] * 2,
+                    [ds[k], slopes[k], m_w, m_w],
+                    [None, None, up_spec, down_spec],
+                    flops=4 * rows * width * width,
+                    reads=2 * m_w.size,
+                )
+                for k in blocks
+            ]
+            dpres, backs = ([g[t] for g in got] for t in range(2))
+        es = collect(backs)
+        (term,) = call(
+            grads_mlp,
+            [((8, 2 * LANES, width), BF16)],
+            list(ms) + list(dpres) + list(acts) + list(ds),
+            flops=16 * rows * width * width,
+        )
+        es, term = lax.optimization_barrier((es, term))
+        homes_m[depth] = lax.psum_scatter(term, "fsdp", scatter_dimension=0, tiled=False)
+        if depth == layers - 1:
+            outs = collect(output_parts)
+            output = middle + ((outs[0].astype(F32) + outs[1].astype(F32)) + (outs[2].astype(F32) + outs[3].astype(F32)))
+        else:
+            es, homes_m[depth + 1] = lax.optimization_barrier((es, homes_m[depth + 1]))
+        d_middle, low = call(
+            add_norm_backward,
+            [(block, F32), (block, BF16)],
+            [gradient] + es + [xhat_m, rstd_m],
+            reads=8 * rows * width,
+        )
+        ds = square.spread(low)
+        got = [
+            call(
+                lambda *refs: attention_backward(*refs, lens=lens),
+                [((rows, 768), BF16), (block, BF16)],
+                [flags[k], ds[k], projs[k], a_w],
+                [scalars(), None, None, None],
+                flops=2 * rows * width * 1536,
+                reads=2 * a_w.size,
+            )
+            for k in blocks
+        ]
+        dprojs = [g[0] for g in got]
+        es = collect([g[1] for g in got])
+        (term,) = call(
+            grads_attention,
+            [((8, LANES, width), BF16)],
+            list(xs) + dprojs + atts + list(ds),
+            flops=8 * rows * width * width,
+        )
+        es, term = lax.optimization_barrier((es, term))
+        homes_a[depth] = lax.psum_scatter(term, "fsdp", scatter_dimension=0, tiled=False)
+        if depth < layers - 1:
+            es, homes_a[depth + 1] = lax.optimization_barrier((es, homes_a[depth + 1]))
+        gradient, low = call(
+            add_norm_backward,
+            [(block, F32), (block, BF16)],
+            [d_middle] + es + [xhat, rstd],
+            reads=8 * rows * width,
+        )
+
+    rest = (gradient - low.astype(F32)).astype(BF16)
+    table_term = (dot_t(mixing, low) + dot_t(mixing, rest)).astype(BF16).reshape(len_high, 4, 256)
+    table_term = table_term.transpose(1, 0, 2)
+    mine = lax.dynamic_index_in_dim(table_term, deep, 0, keepdims=False).astype(F32)
+    for k in range(1, 4):
+        sent = lax.dynamic_index_in_dim(table_term, deep ^ k, 0, keepdims=False)
+        mine = mine + over_fsdp(sent, 2 * k).astype(F32)
+    mine = mine.astype(BF16)
+    keep = jnp.where(core == 0, mine[:, :LANES], mine[:, LANES:])
+    give = jnp.where(core == 0, mine[:, LANES:], mine[:, :LANES])
+    d_table = square.total(keep.astype(F32) + over_fsdp(give, 1).astype(F32))
+
+    big = [None] * 6
+    for depth in reversed(range(layers)):
+        pieces = square.spread(homes_m[depth])
+        prior = big[3:]
+        names = [(w_up.shape, F32), (w_down.shape, F32), (gains_m.shape, F32)]
+        args = [me1] + pieces + [w_up, gains_m]
+        specs = [scalars()] + [None] * 4 + [layer_of(w_up, depth), layer_of(gains_m, depth)]
+        extra = [] if prior[0] is None else prior
+        big[3:] = call(
+            finish_mlp,
+            names,
+            args + extra,
+            specs + [pl.BlockSpec(memory_space=pl.ANY)] * len(extra),
+            aliases={len(args) + t: t for t in range(len(extra))},
+            out_specs=[layer_of(jax.ShapeDtypeStruct(s, d), depth) for s, d in names],
+        )
+        pieces = square.spread(homes_a[depth])
+        packed = [piece[:, 768:1024] for piece in pieces]
+        odd_me = (me & 1) == 1
+        even = [jnp.where(odd_me, packed[1], packed[0]), jnp.where(odd_me, packed[3], packed[2])]
+        odd = [jnp.where(odd_me, packed[0], packed[1]), jnp.where(odd_me, packed[2], packed[3])]
+        keep = [jnp.where(core == 0, a, b) for a, b in zip(even, odd)]
+        give = jnp.stack([jnp.where(core == 0, b, a) for a, b in zip(even, odd)])
+        got = over_fsdp(give, 1)
+        high_me = head_side == 1
+        keep = [jnp.where(high_me, keep[1], keep[0]), jnp.where(high_me, keep[0], keep[1])]
+        got = [jnp.where(high_me, got[1], got[0]), jnp.where(high_me, got[0], got[1])]
+        halves = []
+        for h in range(2):
+            halves.append(jnp.where(core == 0, keep[h], got[h]))
+            halves.append(jnp.where(core == 0, got[h], keep[h]))
+        outs = jnp.stack(halves)
+        prior = big[:3]
+        names = [(w_qkv.shape, F32), (w_out.shape, F32), (gains_a.shape, F32)]
+        args = [me1] + pieces + [w_qkv, gains_a, outs]
+        specs = [scalars()] + [None] * 4 + [layer_of(w_qkv, depth), layer_of(gains_a, depth), None]
+        extra = [] if prior[0] is None else prior
+        big[:3] = call(
+            finish_attention,
+            names,
+            args + extra,
+            specs + [pl.BlockSpec(memory_space=pl.ANY)] * len(extra),
+            aliases={len(args) + t: t for t in range(len(extra))},
+            out_specs=[layer_of(jax.ShapeDtypeStruct(s, d), depth) for s, d in names],
+        )
+    return (
+        output,
+        gradient,
+        d_table,
+        big[2].reshape(layers, LANES),
+        big[0],
+        big[1],
+        big[5].reshape(layers, LANES),
+        big[3],
+        big[4],
+    )
+
+
 def solution(mesh):
     in_specs = (
         P(("dp", "fsdp"), None),
@@ -394,4 +1028,6 @@
         P(None, "fsdp", None),
         P(None, "fsdp", None),
     )
+    fast = mesh.shape["dp"] == 4 and mesh.shape["fsdp"] == 8
+    local = local_fast if fast else local_general
     return jax.shard_map(local, mesh=mesh, in_specs=in_specs, out_specs=out_specs, check_vma=False)

time: 700 us -> 476 us (0.68)
  waiting for transfers between devices: 359 us -> 151 us
  Pallas kernels: 0 us -> 126 us
  matrix products: 77.2 us -> 2.47 us
  other arithmetic: 54 us -> 10.9 us
  local copies, waits for them, and re-layouts: 89.2 us -> 69.5 us
  blocking collectives: 17.2 us -> 0 us
  starting transfers between devices: 75.4 us -> 91.4 us
    pallas_call x0 -> x49, Pallas kernels: none -> 126 us  [call(): pl.pallas_call(body, grid=(1,), in_specs=specs, out_specs=out_specs or [w...]
    ppermute x63, waiting for transfers between devices: 219 us -> 93.6 us  [swap(): return lax.ppermute(block, 'dp', [(i, i ^ k) for i in range(self.count)])]
    reduce_scatter x4, waiting for transfers between devices: 113 us -> 24.4 us  [local_fast(): lax.psum_scatter(term, 'fsdp', scatter_dimension=0, tiled=False)]
    dot_general x29 -> x0, matrix products: 57.6 us -> none  [the longest x9 27.2 us: dot(): return jnp.dot(a, b, preferred_element_type=F32)]
    unnamed x313 -> x271, local copies, waits for them, and re-layouts: 19.2 us -> 62.3 us
    reshape x22 -> x3, local copies, waits for them, and re-layouts: 27.7 us -> 2.48 us  [the longest x1 1.82 us: local_fast(): (dot_t(mixing, low) + dot_t(mixing, rest)).astype(BF16)]
    convert_element_type x20 -> x0, local copies, waits for them, and re-layouts: 22.2 us -> none  [the longest x4 9.06 us: local(): up = up.transpose(1, 2, 0, 3).reshape(shard_rows, hidden_units).astype(F32)]
    all_gather x1 -> x0, blocking collectives: 17.2 us -> none  [local(): table = lax.all_gather(pos_table, 'fsdp', axis=1, tiled=True)]
  transfers between devices with their start and end apart: 76 -> 82, of which waited for: 57 -> 28; matrix products, arithmetic and copies ran while one was open for 18% -> 5% of each run, Pallas kernels for 0% -> 26%
where the time goes in v2:
time: 476 us; the launch traced here: 469 us
  waiting for transfers between devices  151 us (32%)
  Pallas kernels  126 us (26%)
  starting transfers between devices  91.4 us (19%)
  local copies, waits for them, and re-layouts  69.5 us (15%)
  between operations  17.5 us (4%)
  other arithmetic  10.9 us (2%)
    pallas_call x49, Pallas kernels, call(): pl.pallas_call(body, grid=(1,), in_specs=specs, out_specs=out_specs or [w...  126 us
    ppermute x63, waiting for transfers between devices, swap(): return lax.ppermute(block, 'dp', [(i, i ^ k) for i in range(self.count)])  93.6 us
    ppermute x63, starting transfers between devices, swap(): return lax.ppermute(block, 'dp', [(i, i ^ k) for i in range(self.count)])  79.6 us
    unnamed x271, local copies, waits for them, and re-layouts  62.3 us
    reduce_scatter x4, waiting for transfers between devices, local_fast(): lax.psum_scatter(term, 'fsdp', scatter_dimension=0, tiled=False)  24.4 us
    all_gather x2, waiting for transfers between devices, local_fast(): mlp_w.append(lax.all_gather(packed, 'fsdp', axis=0, tiled=False))  19.1 us
    ppermute x11, waiting for transfers between devices, over_fsdp(): return lax.ppermute(x, 'fsdp', [(j, j ^ k) for j in range(8)])  12.8 us
    ppermute x11, starting transfers between devices, over_fsdp(): return lax.ppermute(x, 'fsdp', [(j, j ^ k) for j in range(8)])  11 us
  transfers between devices with their start and end apart: 82, of which 28 were waited for; matrix products, arithmetic and copies ran while one was open for 5% of the time, Pallas kernels for 26%

profile of v2, /device:TPU:0, one launch (start us, length us, event | category | flops | bytes accessed | tf_op | source)
XLA Modules:
  0.0 469.3 jit_solution(8744675220880474387)
XLA Ops:
  21.9 3.0 collective-permute-start.1
  24.9 2.6 collective-permute-start.2
  29.4 3.7 collective-permute-done.1.t1
  33.1 5.5 %collective-permute-done.2.t2 = bf16[145,256]{1,0:T(8,128)(2,1)S(1)} collective-permute-done((bf16[145,256]{1,0:T(8,128)(2,1)S(1)}, bf16[145,256]{1,0:T(8,128)(2,1)S(1)}, u32[]{:S(2)}, u32[]{:S(2)}) %collective-permute-start.2) | collective-permute-done | bytes 74272 | tf_op jit(solution)/shard_map/ppermute | solution.py:731
  39.9 2.4 collective-permute-start.9
  43.4 7.8 %collective-permute-done.9.refs_1_.refs_3_ = bf16[152,1024]{1,0:T(8,128)(2,1)S(1)} collective-permute-done((bf16[152,1024]{1,0:T(8,128)(2,1)S(1)}, bf16[152,1024]{1,0:T(8,128)(2,1)S(1)}, u32[]{:S(2)}, u32[]{:S(2)}) %collective-permute-start.9) | collective-permute-done | bytes 311328 | tf_op jit(solution)/shard_map/ppermute | solution.py:60
  53.3 2.4 shard_map.193
  57.0 2.4 collective-permute-start.10
  69.3 4.7 %collective-permute-done.8.r2 = bf16[152,1024]{1,0:T(8,128)(2,1)S(1)} collective-permute-done((bf16[152,1024]{1,0:T(8,128)(2,1)S(1)}, bf16[152,1024]{1,0:T(8,128)(2,1)S(1)}, u32[]{:S(2)}, u32[]{:S(2)}) %collective-permute-start.8) | collective-permute-done | bytes 311328 | tf_op jit(solution)/shard_map/ppermute | solution.py:60
  80.2 6.8 %collective-permute-done.11.x_ref.refs_1_ = bf16[152,1024]{1,0:T(8,128)(2,1)S(1)} collective-permute-done((bf16[152,1024]{1,0:T(8,128)(2,1)S(1)}, bf16[152,1024]{1,0:T(8,128)(2,1)S(1)}, u32[]{:S(2)}, u32[]{:S(2)}) %collective-permute-start.11) | collective-permute-done | bytes 311328 | tf_op jit(solution)/shard_map/ppermute | solution.py:60
  87.0 12.8 %all-gather.11.cloned.1.call-done = bf16[2048,1024]{1,0:T(8,128)(2,1)} async-done(((bf16[256,1024]{1,0:T(8,128)(2,1)}), bf16[2048,1024]{1,0:T(8,128)(2,1)}) %all-gather.11.cloned.1.call-update) | async-done | bytes 4194320 | tf_op jit(solution)/shard_map/all_gather | solution.py:759
  116.6 7.7 %collective-permute-done.14.r2 = bf16[152,1024]{1,0:T(8,128)(2,1)S(1)} collective-permute-done((bf16[152,1024]{1,0:T(8,128)(2,1)S(1)}, bf16[152,1024]{1,0:T(8,128)(2,1)S(1)}, u32[]{:S(2)}, u32[]{:S(2)}) %collective-permute-start.14) | collective-permute-done | bytes 311328 | tf_op jit(solution)/shard_map/ppermute | solution.py:60
  132.1 5.2 %collective-permute-done.21.refs_1_.refs_3_ = bf16[152,1024]{1,0:T(8,128)(2,1)S(1)} collective-permute-done((bf16[152,1024]{1,0:T(8,128)(2,1)S(1)}, bf16[152,1024]{1,0:T(8,128)(2,1)S(1)}, u32[]{:S(2)}, u32[]{:S(2)}) %collective-permute-start.21) | collective-permute-done | bytes 311328 | tf_op jit(solution)/shard_map/ppermute | solution.py:60
  139.2 2.5 shard_map.205
  148.9 3.1 shard_map.203
  157.9 4.2 collective-permute-done.18.r1
  172.0 6.3 %all-gather.15.cloned.1.call-done = bf16[2048,1024]{1,0:T(8,128)(2,1)} async-done(((bf16[256,1024]{1,0:T(8,128)(2,1)}), bf16[2048,1024]{1,0:T(8,128)(2,1)}) %all-gather.15.cloned.1.call-update) | async-done | bytes 4194320 | tf_op jit(solution)/shard_map/all_gather | solution.py:759
  181.4 4.0 shard_map.209
  186.9 3.2 collective-permute-done.26.x_ref.refs_2_
  190.1 3.7 shard_map.210
  194.9 3.7 shard_map.211
  200.8 13.8 %shard_map.208 = (bf16[152,1024]{1,0:T(8,128)(2,1)S(1)}, bf16[152,1024]{1,0:T(8,128)(2,1)S(1)}, bf16[152,1024]{1,0:T(8,128)(2,1)S(1)}, bf16[152,1024]{1,0:T(8,128)(2,1)S(1)}) custom-call(bf16[152,1024]{1,0:T(8,128)(2,1)} %get-tuple-element.166.x_ref.refs_0_.xhat_ref, bf16[152,1024]{1,0:T(8,128)(2,1)} %get-tuple-element.312.d_ref.refs_12_, ...), custom_call_target="tpu_custom_call" | custom-call | flops 1275068416 | bytes 5439488 | tf_op jit(solution)/shard_map/pallas_call | solution.py:389
  216.1 6.1 %shard_map.212 = bf16[8,256,1024]{2,1,0:T(8,128)(2,1)S(1)} custom-call(bf16[152,1024]{1,0:T(8,128)(2,1)} %get-tuple-element.166.x_ref.refs_0_.xhat_ref, bf16[152,1024]{1,0:T(8,128)(2,1)} %collective-permute-done.23.x_ref.refs_1_, bf16[152,1024]{1,0:T(8,128)(2,1)} %collective-permute-done.26.x_ref.refs_2_, ...), custom_call_target="tpu_custom_call" | custom-call | flops 2550136832 | bytes 4194304 | tf_op jit(solution)/shard_map/pallas_call | solution.py:389
  232.2 6.0 %collective-permute-done.39.refs_1_.refs_15_ = bf16[152,1024]{1,0:T(8,128)(2,1)S(1)} collective-permute-done((bf16[152,1024]{1,0:T(8,128)(2,1)S(1)}, bf16[152,1024]{1,0:T(8,128)(2,1)S(1)}, u32[]{:S(2)}, u32[]{:S(2)}) %collective-permute-start.39) | collective-permute-done | bytes 311328 | tf_op jit(solution)/shard_map/ppermute | solution.py:60
  240.8 3.4 shard_map.217
  246.5 3.5 shard_map.216
  250.7 3.4 shard_map.215
  254.7 2.6 shard_map.214
  258.0 3.4 shard_map.218
  271.3 4.4 collective-permute-done.45.d_ref.refs_15_
  293.3 5.5 %shard_map.224 = bf16[8,256,1024]{2,1,0:T(8,128)(2,1)S(1)} custom-call(bf16[152,1024]{1,0:T(8,128)(2,1)S(1)} %copy-done.21, bf16[152,1024]{1,0:T(8,128)(2,1)S(1)} %copy-done.52, bf16[152,1024]{1,0:T(8,128)(2,1)S(1)} %copy-done.54, bf16[152,1024]{1,0:T(8,128)(2,1)} %collective-permute-done.15.x_ref.refs_3_, bf16[152,1024]{1,0:T(8,128)(2,1)S(1)} %get-tuple-element.221.refs_4_, ...), custom_call_target="tpu_custom_call" | custom-call | flops 2550136832 | bytes 4194304 | tf_op jit(solution)/shard_map/pallas_call | solution.py:389
  309.5 7.5 %collective-permute-done.51.refs_1_.refs_15_ = bf16[152,1024]{1,0:T(8,128)(2,1)S(1)} collective-permute-done((bf16[152,1024]{1,0:T(8,128)(2,1)S(1)}, bf16[152,1024]{1,0:T(8,128)(2,1)S(1)}, u32[]{:S(2)}, u32[]{:S(2)}) %collective-permute-start.51) | collective-permute-done | bytes 311328 | tf_op jit(solution)/shard_map/ppermute | solution.py:60
  318.0 3.5 shard_map.229
  322.6 3.7 shard_map.228
  328.1 3.4 shard_map.227
  332.1 2.6 shard_map.226
  335.5 3.8 shard_map.230
  347.2 2.8 constant_dynamic-slice_fusion.3
  353.5 2.8 collective-permute-start.55
  364.3 3.7 collective-permute-done.28
  372.9 7.0 %collective-permute-done.72.g2 = bf16[256,1024]{1,0:T(8,128)(2,1)S(1)} collective-permute-done((bf16[256,1024]{1,0:T(8,128)(2,1)S(1)}, bf16[256,1024]{1,0:T(8,128)(2,1)S(1)}, u32[]{:S(2)}, u32[]{:S(2)}) %collective-permute-start.72) | collective-permute-done | bytes 524320 | tf_op jit(solution)/shard_map/ppermute | solution.py:60
  379.9 2.6 shard_map.234
  391.8 3.6 collective-permute-done.65.g2
  401.7 24.4 %reduce-scatter.11.cloned.1.call-done = bf16[1,256,1024]{2,1,0:T(8,128)(2,1)} async-done(((bf16[8,256,1024]{2,1,0:T(8,128)(2,1)}), bf16[1,256,1024]{2,1,0:T(8,128)(2,1)}) %reduce-scatter.11.cloned.1.call-update) | async-done | bytes 524304 | tf_op jit(solution)/shard_map/reduce_scatter | solution.py:892
  430.5 2.4 collective-permute-start.59
  433.1 17.8 %collective-permute-done.59 = bf16[145,128]{1,0:T(8,128)(2,1)S(1)} collective-permute-done((bf16[145,128]{1,0:T(8,128)(2,1)S(1)}, bf16[145,128]{1,0:T(8,128)(2,1)S(1)}, u32[]{:S(2)}, u32[]{:S(2)}) %collective-permute-start.59) | collective-permute-done | bytes 37152 | tf_op jit(solution)/shard_map/ppermute | solution.py:60
  453.4 2.6 shard_map.235
  457.4 2.9 shard_map.232
  (477 shorter events, 205.1 us)
Async XLA Ops:
  7.2 44.5 %all-gather.9.cloned.1.call-start = ((), (), s32[]{:S(2)}) async-start(), calls=%async_computation.8 | async-start | bytes 2359296 | tf_op jit(solution)/shard_map/all_gather | solution.py:752
  12.6 87.2 %all-gather.11.cloned.1.call-start = ((), (), s32[]{:S(2)}) async-start(), calls=%async_computation.9 | async-start | bytes 4718592 | tf_op jit(solution)/shard_map/all_gather | solution.py:759
  15.3 116.8 %all-gather.13.cloned.1.call-start = ((), (), s32[]{:S(2)}) async-start(), calls=%async_computation.10 | async-start | bytes 2359296 | tf_op jit(solution)/shard_map/all_gather | solution.py:752
  17.8 160.5 %all-gather.15.cloned.1.call-start = ((), (), s32[]{:S(2)}) async-start(), calls=%async_computation.11 | async-start | bytes 4718592 | tf_op jit(solution)/shard_map/all_gather | solution.py:759
  20.5 280.3 %reduce-scatter.5.cloned.1.call-start = ((), (), s32[]{:S(2)}) async-start(), calls=%async_computation.4 | async-start | bytes 4718592 | tf_op jit(solution)/shard_map/reduce_scatter | solution.py:892
  42.3 17.0 %collective-permute-start.7 = (bf16[152,1024]{1,0:T(8,128)(2,1)S(1)}, bf16[152,1024]{1,0:T(8,128)(2,1)S(1)}, u32[]{:S(2)}, u32[]{:S(2)}) collective-permute-start(bf16[152,1024]{1,0:T(8,128)(2,1)S(1)} %get-tuple-element.148.refs_1_.refs_0_.xhat_ref), channel_id=1, source_target_pairs={{0,16},{8,24},{16,0},{24,8},{1,17},{9,25},{17,1},{25,9},{2,18},{10... | collective-permute-start | bytes 933896 | tf_op jit(solution)/shard_map/ppermute | solution.py:60
  42.8 20.8 %collective-permute-start.5 = (bf16[152,1024]{1,0:T(8,128)(2,1)S(1)}, bf16[152,1024]{1,0:T(8,128)(2,1)S(1)}, u32[]{:S(2)}, u32[]{:S(2)}) collective-permute-start(bf16[152,1024]{1,0:T(8,128)(2,1)S(1)} %get-tuple-element.148.refs_1_.refs_0_.xhat_ref), channel_id=1, source_target_pairs={{0,8},{8,0},{16,24},{24,16},{1,9},{9,1},{17,25},{25,17},{2,10},{10... | collective-permute-start | bytes 933896 | tf_op jit(solution)/shard_map/ppermute | solution.py:60
  77.4 28.4 %collective-permute-start.13 = (bf16[152,1024]{1,0:T(8,128)(2,1)S(1)}, bf16[152,1024]{1,0:T(8,128)(2,1)S(1)}, u32[]{:S(2)}, u32[]{:S(2)}) collective-permute-start(bf16[152,1024]{1,0:T(8,128)(2,1)S(1)} %get-tuple-element.154.x_ref.refs_0_.xhat_ref), channel_id=1, source_target_pairs={{0,16},{8,24},{16,0},{24,8},{1,17},{9,25},{17,1},{25,9},{2,18},{10... | collective-permute-start | bytes 933896 | tf_op jit(solution)/shard_map/ppermute | solution.py:60
  78.9 31.0 %collective-permute-start.15 = (bf16[152,1024]{1,0:T(8,128)(2,1)S(1)}, bf16[152,1024]{1,0:T(8,128)(2,1)}, u32[]{:S(2)}, u32[]{:S(2)}) collective-permute-start(bf16[152,1024]{1,0:T(8,128)(2,1)S(1)} %get-tuple-element.154.x_ref.refs_0_.xhat_ref), channel_id=1, source_target_pairs={{0,24},{8,16},{16,8},{24,0},{1,25},{9,17},{17,9},{25,1},{2,26},{10... | collective-permute-start | bytes 933896 | tf_op jit(solution)/shard_map/ppermute | solution.py:60
  108.4 15.9 %collective-permute-start.14 = (bf16[152,1024]{1,0:T(8,128)(2,1)S(1)}, bf16[152,1024]{1,0:T(8,128)(2,1)S(1)}, u32[]{:S(2)}, u32[]{:S(2)}) collective-permute-start(bf16[152,1024]{1,0:T(8,128)(2,1)S(1)} %get-tuple-element.157), channel_id=1, source_target_pairs={{0,16},{8,24},{16,0},{24,8},{1,17},{9,25},{17,1},{25,9},{2,18},{10... | collective-permute-start | bytes 933896 | tf_op jit(solution)/shard_map/ppermute | solution.py:60
  127.6 16.9 %collective-permute-start.19 = (bf16[152,1024]{1,0:T(8,128)(2,1)S(1)}, bf16[152,1024]{1,0:T(8,128)(2,1)S(1)}, u32[]{:S(2)}, u32[]{:S(2)}) collective-permute-start(bf16[152,1024]{1,0:T(8,128)(2,1)S(1)} %get-tuple-element.160.refs_1_.refs_0_.xhat_ref), channel_id=1, source_target_pairs={{0,16},{8,24},{16,0},{24,8},{1,17},{9,25},{17,1},{25,9},{2,18},{10... | collective-permute-start | bytes 933896 | tf_op jit(solution)/shard_map/ppermute | solution.py:60
  128.3 20.6 %collective-permute-start.17 = (bf16[152,1024]{1,0:T(8,128)(2,1)S(1)}, bf16[152,1024]{1,0:T(8,128)(2,1)}, u32[]{:S(2)}, u32[]{:S(2)}) collective-permute-start(bf16[152,1024]{1,0:T(8,128)(2,1)S(1)} %get-tuple-element.160.refs_1_.refs_0_.xhat_ref), channel_id=1, source_target_pairs={{0,8},{8,0},{16,24},{24,16},{1,9},{9,1},{17,25},{25,17},{2,10},{10... | collective-permute-start | bytes 933896 | tf_op jit(solution)/shard_map/ppermute | solution.py:60
  143.1 14.8 %collective-permute-start.22 = (bf16[152,1024]{1,0:T(8,128)(2,1)S(1)}, bf16[152,1024]{1,0:T(8,128)(2,1)S(1)}, u32[]{:S(2)}, u32[]{:S(2)}) collective-permute-start(bf16[152,1024]{1,0:T(8,128)(2,1)S(1)} %get-tuple-element.164), channel_id=1, source_target_pairs={{0,24},{8,16},{16,8},{24,0},{1,25},{9,17},{17,9},{25,1},{2,26},{10... | collective-permute-start | bytes 933896 | tf_op jit(solution)/shard_map/ppermute | solution.py:60
  154.3 15.2 %collective-permute-start.24 = (bf16[152,1024]{1,0:T(8,128)(2,1)}, bf16[152,1024]{1,0:T(8,128)(2,1)S(1)}, u32[]{:S(2)}, u32[]{:S(2)}) collective-permute-start(bf16[152,1024]{1,0:T(8,128)(2,1)} %get-tuple-element.312.d_ref.refs_12_), channel_id=1, source_target_pairs={{0,8},{8,0},{16,24},{24,16},{1,9},{9,1},{17,25},{25,17},{2,10},{10... | collective-permute-start | bytes 933896 | tf_op jit(solution)/shard_map/ppermute | solution.py:60
  166.3 20.6 %collective-permute-start.27 = (bf16[152,1024]{1,0:T(8,128)(2,1)}, bf16[152,1024]{1,0:T(8,128)(2,1)}, u32[]{:S(2)}, u32[]{:S(2)}) collective-permute-start(bf16[152,1024]{1,0:T(8,128)(2,1)} %get-tuple-element.312.d_ref.refs_12_), channel_id=1, source_target_pairs={{0,16},{8,24},{16,0},{24,8},{1,17},{9,25},{17,1},{25,9},{2,18},{10... | collective-permute-start | bytes 933896 | tf_op jit(solution)/shard_map/ppermute | solution.py:60
  166.8 23.3 %collective-permute-start.26 = (bf16[152,1024]{1,0:T(8,128)(2,1)}, bf16[152,1024]{1,0:T(8,128)(2,1)}, u32[]{:S(2)}, u32[]{:S(2)}) collective-permute-start(bf16[152,1024]{1,0:T(8,128)(2,1)} %get-tuple-element.166.x_ref.refs_0_.xhat_ref), channel_id=1, source_target_pairs={{0,16},{8,24},{16,0},{24,8},{1,17},{9,25},{17,1},{25,9},{2,18},{10... | collective-permute-start | bytes 933896 | tf_op jit(solution)/shard_map/ppermute | solution.py:60
  168.3 26.6 %collective-permute-start.30 = (bf16[152,1024]{1,0:T(8,128)(2,1)}, bf16[152,1024]{1,0:T(8,128)(2,1)}, u32[]{:S(2)}, u32[]{:S(2)}) collective-permute-start(bf16[152,1024]{1,0:T(8,128)(2,1)} %get-tuple-element.312.d_ref.refs_12_), channel_id=1, source_target_pairs={{0,24},{8,16},{16,8},{24,0},{1,25},{9,17},{17,9},{25,1},{2,26},{10... | collective-permute-start | bytes 933896 | tf_op jit(solution)/shard_map/ppermute | solution.py:60
  170.2 24.7 %collective-permute-start.29 = (bf16[152,1024]{1,0:T(8,128)(2,1)}, bf16[152,1024]{1,0:T(8,128)(2,1)}, u32[]{:S(2)}, u32[]{:S(2)}) collective-permute-start(bf16[152,1024]{1,0:T(8,128)(2,1)} %get-tuple-element.166.x_ref.refs_0_.xhat_ref), channel_id=1, source_target_pairs={{0,24},{8,16},{16,8},{24,0},{1,25},{9,17},{17,9},{25,1},{2,26},{10... | collective-permute-start | bytes 933896 | tf_op jit(solution)/shard_map/ppermute | solution.py:60
  185.4 38.8 %collective-permute-start.32 = (bf16[152,1024]{1,0:T(8,128)(2,1)}, bf16[152,1024]{1,0:T(8,128)(2,1)}, u32[]{:S(2)}, u32[]{:S(2)}) collective-permute-start(bf16[152,1024]{1,0:T(8,128)(2,1)} %get-tuple-element.172), channel_id=1, source_target_pairs={{0,8},{8,0},{16,24},{24,16},{1,9},{9,1},{17,25},{25,17},{2,10},{10... | collective-permute-start | bytes 933896 | tf_op jit(solution)/shard_map/ppermute | solution.py:60
  193.8 30.4 %collective-permute-start.33 = (bf16[152,1024]{1,0:T(8,128)(2,1)}, bf16[152,1024]{1,0:T(8,128)(2,1)}, u32[]{:S(2)}, u32[]{:S(2)}) collective-permute-start(bf16[152,1024]{1,0:T(8,128)(2,1)} %get-tuple-element.173), channel_id=1, source_target_pairs={{0,16},{8,24},{16,0},{24,8},{1,17},{9,25},{17,1},{25,9},{2,18},{10... | collective-permute-start | bytes 933896 | tf_op jit(solution)/shard_map/ppermute | solution.py:60
  199.3 24.9 %collective-permute-start.34 = (bf16[152,1024]{1,0:T(8,128)(2,1)}, bf16[152,1024]{1,0:T(8,128)(2,1)}, u32[]{:S(2)}, u32[]{:S(2)}) collective-permute-start(bf16[152,1024]{1,0:T(8,128)(2,1)} %get-tuple-element.174), channel_id=1, source_target_pairs={{0,24},{8,16},{16,8},{24,0},{1,25},{9,17},{17,9},{25,1},{2,26},{10... | collective-permute-start | bytes 933896 | tf_op jit(solution)/shard_map/ppermute | solution.py:60
  224.2 117.4 %reduce-scatter.7.cloned.1.call-start = ((), (), s32[]{:S(2)}) async-start(), calls=%async_computation.5 | async-start | bytes 2359296 | tf_op jit(solution)/shard_map/reduce_scatter | solution.py:925
  230.2 16.3 %collective-permute-start.37 = (bf16[152,1024]{1,0:T(8,128)(2,1)S(1)}, bf16[152,1024]{1,0:T(8,128)(2,1)S(1)}, u32[]{:S(2)}, u32[]{:S(2)}) collective-permute-start(bf16[152,1024]{1,0:T(8,128)(2,1)S(1)} %get-tuple-element.189.refs_1_.refs_12_), channel_id=1, source_target_pairs={{0,16},{8,24},{16,0},{24,8},{1,17},{9,25},{17,1},{25,9},{2,18},{10... | collective-permute-start | bytes 933896 | tf_op jit(solution)/shard_map/ppermute | solution.py:60
  231.1 19.6 %collective-permute-start.35 = (bf16[152,1024]{1,0:T(8,128)(2,1)S(1)}, bf16[152,1024]{1,0:T(8,128)(2,1)S(1)}, u32[]{:S(2)}, u32[]{:S(2)}) collective-permute-start(bf16[152,1024]{1,0:T(8,128)(2,1)S(1)} %get-tuple-element.189.refs_1_.refs_12_), channel_id=1, source_target_pairs={{0,8},{8,0},{16,24},{24,16},{1,9},{9,1},{17,25},{25,17},{2,10},{10... | collective-permute-start | bytes 933896 | tf_op jit(solution)/shard_map/ppermute | solution.py:60
  244.2 18.6 %collective-permute-start.40 = (bf16[152,1024]{1,0:T(8,128)(2,1)}, bf16[152,1024]{1,0:T(8,128)(2,1)S(1)}, u32[]{:S(2)}, u32[]{:S(2)}) collective-permute-start(bf16[152,1024]{1,0:T(8,128)(2,1)} %get-tuple-element.197), channel_id=1, source_target_pairs={{0,24},{8,16},{16,8},{24,0},{1,25},{9,17},{17,9},{25,1},{2,26},{10... | collective-permute-start | bytes 933896 | tf_op jit(solution)/shard_map/ppermute | solution.py:60
  262.9 127.0 %reduce-scatter.9.cloned.1.call-start = ((), (), s32[]{:S(2)}) async-start(), calls=%async_computation.6 | async-start | bytes 2359296 | tf_op jit(solution)/shard_map/reduce_scatter | solution.py:925
  270.7 16.2 %collective-permute-start.41 = (bf16[152,1024]{1,0:T(8,128)(2,1)S(1)}, bf16[152,1024]{1,0:T(8,128)(2,1)S(1)}, u32[]{:S(2)}, u32[]{:S(2)}) collective-permute-start(bf16[152,1024]{1,0:T(8,128)(2,1)S(1)} %get-tuple-element.212.d_ref.refs_12_), channel_id=1, source_target_pairs={{0,8},{8,0},{16,24},{24,16},{1,9},{9,1},{17,25},{25,17},{2,10},{10... | collective-permute-start | bytes 933896 | tf_op jit(solution)/shard_map/ppermute | solution.py:60
  280.2 20.5 %collective-permute-start.46 = (bf16[152,1024]{1,0:T(8,128)(2,1)}, bf16[152,1024]{1,0:T(8,128)(2,1)S(1)}, u32[]{:S(2)}, u32[]{:S(2)}) collective-permute-start(bf16[152,1024]{1,0:T(8,128)(2,1)} %get-tuple-element.220), channel_id=1, source_target_pairs={{0,24},{8,16},{16,8},{24,0},{1,25},{9,17},{17,9},{25,1},{2,26},{10... | collective-permute-start | bytes 933896 | tf_op jit(solution)/shard_map/ppermute | solution.py:60
  285.5 15.3 %collective-permute-start.44 = (bf16[152,1024]{1,0:T(8,128)(2,1)}, bf16[152,1024]{1,0:T(8,128)(2,1)S(1)}, u32[]{:S(2)}, u32[]{:S(2)}) collective-permute-start(bf16[152,1024]{1,0:T(8,128)(2,1)} %get-tuple-element.218), channel_id=1, source_target_pairs={{0,16},{8,24},{16,0},{24,8},{1,17},{9,25},{17,1},{25,9},{2,18},{10... | collective-permute-start | bytes 933896 | tf_op jit(solution)/shard_map/ppermute | solution.py:60
  306.4 16.2 %collective-permute-start.49 = (bf16[152,1024]{1,0:T(8,128)(2,1)S(1)}, bf16[152,1024]{1,0:T(8,128)(2,1)S(1)}, u32[]{:S(2)}, u32[]{:S(2)}) collective-permute-start(bf16[152,1024]{1,0:T(8,128)(2,1)S(1)} %get-tuple-element.240.refs_1_.refs_12_), channel_id=1, source_target_pairs={{0,16},{8,24},{16,0},{24,8},{1,17},{9,25},{17,1},{25,9},{2,18},{10... | collective-permute-start | bytes 933896 | tf_op jit(solution)/shard_map/ppermute | solution.py:60
  307.8 20.3 %collective-permute-start.47 = (bf16[152,1024]{1,0:T(8,128)(2,1)S(1)}, bf16[152,1024]{1,0:T(8,128)(2,1)S(1)}, u32[]{:S(2)}, u32[]{:S(2)}) collective-permute-start(bf16[152,1024]{1,0:T(8,128)(2,1)S(1)} %get-tuple-element.240.refs_1_.refs_12_), channel_id=1, source_target_pairs={{0,8},{8,0},{16,24},{24,16},{1,9},{9,1},{17,25},{25,17},{2,10},{10... | collective-permute-start | bytes 933896 | tf_op jit(solution)/shard_map/ppermute | solution.py:60
  321.5 17.8 %collective-permute-start.52 = (bf16[152,1024]{1,0:T(8,128)(2,1)}, bf16[152,1024]{1,0:T(8,128)(2,1)S(1)}, u32[]{:S(2)}, u32[]{:S(2)}) collective-permute-start(bf16[152,1024]{1,0:T(8,128)(2,1)} %get-tuple-element.248), channel_id=1, source_target_pairs={{0,24},{8,16},{16,8},{24,0},{1,25},{9,17},{17,9},{25,1},{2,26},{10... | collective-permute-start | bytes 933896 | tf_op jit(solution)/shard_map/ppermute | solution.py:60
  339.4 86.7 %reduce-scatter.11.cloned.1.call-start = ((), (), s32[]{:S(2)}) async-start(), calls=%async_computation.7 | async-start | bytes 4718592 | tf_op jit(solution)/shard_map/reduce_scatter | solution.py:892
  340.1 16.4 %collective-permute-start.25 = (bf16[152,1024]{1,0:T(8,128)(2,1)}, bf16[152,1024]{1,0:T(8,128)(2,1)}, u32[]{:S(2)}, u32[]{:S(2)}) collective-permute-start(bf16[152,1024]{1,0:T(8,128)(2,1)} %get-tuple-element.168), channel_id=1, source_target_pairs={{0,8},{8,0},{16,24},{24,16},{1,9},{9,1},{17,25},{25,17},{2,10},{10... | collective-permute-start | bytes 933896 | tf_op jit(solution)/shard_map/ppermute | solution.py:60
  359.9 20.0 %collective-permute-start.72 = (bf16[256,1024]{1,0:T(8,128)(2,1)S(1)}, bf16[256,1024]{1,0:T(8,128)(2,1)S(1)}, u32[]{:S(2)}, u32[]{:S(2)}) collective-permute-start(bf16[256,1024]{1,0:T(8,128)(2,1)S(1)} %bitcast.136), channel_id=1, source_target_pairs={{0,16},{8,24},{16,0},{24,8},{1,17},{9,25},{17,1},{25,9},{2,18},{10... | collective-permute-start | bytes 1572872 | tf_op jit(solution)/shard_map/ppermute | solution.py:60
  362.4 17.5 %collective-permute-start.73 = (bf16[256,1024]{1,0:T(8,128)(2,1)S(1)}, bf16[256,1024]{1,0:T(8,128)(2,1)S(1)}, u32[]{:S(2)}, u32[]{:S(2)}) collective-permute-start(bf16[256,1024]{1,0:T(8,128)(2,1)S(1)} %bitcast.137), channel_id=1, source_target_pairs={{0,24},{8,16},{16,8},{24,0},{1,25},{9,17},{17,9},{25,1},{2,26},{10... | collective-permute-start | bytes 1572872 | tf_op jit(solution)/shard_map/ppermute | solution.py:60
  368.0 19.6 %collective-permute-start.64 = (bf16[128,1024]{1,0:T(8,128)(2,1)}, bf16[128,1024]{1,0:T(8,128)(2,1)S(1)}, u32[]{:S(2)}, u32[]{:S(2)}) collective-permute-start(bf16[128,1024]{1,0:T(8,128)(2,1)} %bitcast.16.g0), channel_id=1, source_target_pairs={{0,8},{8,0},{16,24},{24,16},{1,9},{9,1},{17,25},{25,17},{2,10},{10... | collective-permute-start | bytes 786440 | tf_op jit(solution)/shard_map/ppermute | solution.py:60
  369.4 16.5 %collective-permute-start.56 = (bf16[145,128]{1,0:T(8,128)(2,1)S(1)}, bf16[145,128]{1,0:T(8,128)(2,1)S(1)}, u32[]{:S(2)}, u32[]{:S(2)}) collective-permute-start(bf16[145,128]{1,0:T(8,128)(2,1)S(1)} %broadcast_select_fusion.20), channel_id=1, source_target_pairs={{0,1},{1,0},{2,3},{3,2},{4,5},{5,4},{6,7},{7,6},{8,9},{9,8},{10,11... | collective-permute-start | bytes 111368 | tf_op jit(solution)/shard_map/ppermute | solution.py:731
  385.9 44.6 %collective-permute-start.57 = (bf16[145,128]{1,0:T(8,128)(2,1)S(1)}, bf16[145,128]{1,0:T(8,128)(2,1)}, u32[]{:S(2)}, u32[]{:S(2)}) collective-permute-start(bf16[145,128]{1,0:T(8,128)(2,1)S(1)} %add_convert_fusion), channel_id=1, source_target_pairs={{0,8},{8,0},{16,24},{24,16},{1,9},{9,1},{17,25},{25,17},{2,10},{10... | collective-permute-start | bytes 111368 | tf_op jit(solution)/shard_map/ppermute | solution.py:60
  386.1 46.9 %collective-permute-start.58 = (bf16[145,128]{1,0:T(8,128)(2,1)S(1)}, bf16[145,128]{1,0:T(8,128)(2,1)}, u32[]{:S(2)}, u32[]{:S(2)}) collective-permute-start(bf16[145,128]{1,0:T(8,128)(2,1)S(1)} %add_convert_fusion), channel_id=1, source_target_pairs={{0,16},{8,24},{16,0},{24,8},{1,17},{9,25},{17,1},{25,9},{2,18},{10... | collective-permute-start | bytes 111368 | tf_op jit(solution)/shard_map/ppermute | solution.py:60
  389.8 36.2 %collective-permute-start.60 = (bf16[128,1024]{1,0:T(8,128)(2,1)}, bf16[128,1024]{1,0:T(8,128)(2,1)S(1)}, u32[]{:S(2)}, u32[]{:S(2)}) collective-permute-start(bf16[128,1024]{1,0:T(8,128)(2,1)} %bitcast.143), channel_id=1, source_target_pairs={{0,8},{8,0},{16,24},{24,16},{1,9},{9,1},{17,25},{25,17},{2,10},{10... | collective-permute-start | bytes 786440 | tf_op jit(solution)/shard_map/ppermute | solution.py:60
  396.1 32.4 %collective-permute-start.61 = (bf16[128,1024]{1,0:T(8,128)(2,1)}, bf16[128,1024]{1,0:T(8,128)(2,1)S(1)}, u32[]{:S(2)}, u32[]{:S(2)}) collective-permute-start(bf16[128,1024]{1,0:T(8,128)(2,1)} %bitcast.144), channel_id=1, source_target_pairs={{0,16},{8,24},{16,0},{24,8},{1,17},{9,25},{17,1},{25,9},{2,18},{10... | collective-permute-start | bytes 786440 | tf_op jit(solution)/shard_map/ppermute | solution.py:60
  398.1 31.8 %collective-permute-start.62 = (bf16[128,1024]{1,0:T(8,128)(2,1)}, bf16[128,1024]{1,0:T(8,128)(2,1)S(1)}, u32[]{:S(2)}, u32[]{:S(2)}) collective-permute-start(bf16[128,1024]{1,0:T(8,128)(2,1)} %bitcast.145), channel_id=1, source_target_pairs={{0,24},{8,16},{16,8},{24,0},{1,25},{9,17},{17,9},{25,1},{2,26},{10... | collective-permute-start | bytes 786440 | tf_op jit(solution)/shard_map/ppermute | solution.py:60
  426.1 26.3 %collective-permute-start.68 = (bf16[256,1024]{1,0:T(8,128)(2,1)}, bf16[256,1024]{1,0:T(8,128)(2,1)S(1)}, u32[]{:S(2)}, u32[]{:S(2)}) collective-permute-start(bf16[256,1024]{1,0:T(8,128)(2,1)} %bitcast.139), channel_id=1, source_target_pairs={{0,8},{8,0},{16,24},{24,16},{1,9},{9,1},{17,25},{25,17},{2,10},{10... | collective-permute-start | bytes 1572872 | tf_op jit(solution)/shard_map/ppermute | solution.py:60
  428.4 23.9 %collective-permute-start.69 = (bf16[256,1024]{1,0:T(8,128)(2,1)}, bf16[256,1024]{1,0:T(8,128)(2,1)S(1)}, u32[]{:S(2)}, u32[]{:S(2)}) collective-permute-start(bf16[256,1024]{1,0:T(8,128)(2,1)} %bitcast.140), channel_id=1, source_target_pairs={{0,16},{8,24},{16,0},{24,8},{1,17},{9,25},{17,1},{25,9},{2,18},{10... | collective-permute-start | bytes 1572872 | tf_op jit(solution)/shard_map/ppermute | solution.py:60
  430.0 22.4 %collective-permute-start.70 = (bf16[256,1024]{1,0:T(8,128)(2,1)}, bf16[256,1024]{1,0:T(8,128)(2,1)S(1)}, u32[]{:S(2)}, u32[]{:S(2)}) collective-permute-start(bf16[256,1024]{1,0:T(8,128)(2,1)} %bitcast.141), channel_id=1, source_target_pairs={{0,24},{8,16},{16,8},{24,0},{1,25},{9,17},{17,9},{25,1},{2,26},{10... | collective-permute-start | bytes 1572872 | tf_op jit(solution)/shard_map/ppermute | solution.py:60
  430.5 20.4 %collective-permute-start.59 = (bf16[145,128]{1,0:T(8,128)(2,1)S(1)}, bf16[145,128]{1,0:T(8,128)(2,1)S(1)}, u32[]{:S(2)}, u32[]{:S(2)}) collective-permute-start(bf16[145,128]{1,0:T(8,128)(2,1)S(1)} %add_convert_fusion), channel_id=1, source_target_pairs={{0,24},{8,16},{16,8},{24,0},{1,25},{9,17},{17,9},{25,1},{2,26},{10... | collective-permute-start | bytes 111368 | tf_op jit(solution)/shard_map/ppermute | solution.py:60
  433.0 23.0 %collective-permute-start.67 = (bf16[2,128,256]{2,1,0:T(8,128)(2,1)}, bf16[2,128,256]{2,1,0:T(8,128)(2,1)S(1)}, u32[]{:S(2)}, u32[]{:S(2)}) collective-permute-start(bf16[2,128,256]{2,1,0:T(8,128)(2,1)} %pad_maximum_fusion.3), channel_id=1, source_target_pairs={{0,1},{1,0},{2,3},{3,2},{4,5},{5,4},{6,7},{7,6},{8,9},{9,8},{10,11... | collective-permute-start | bytes 393224 | tf_op jit(solution)/shard_map/ppermute | solution.py:731
  (167 other events, 1144.4 us)
Sparse Core Ops, SparseCore 0:
  12.7 38.9 all-gather.8
  53.8 45.8 all-gather.10
  102.0 27.5 all-gather.12
  131.6 46.6 all-gather.14
  224.3 47.9 reduce-scatter.4
  275.1 33.7 reduce-scatter.6
  339.5 35.1 reduce-scatter.8
  376.9 49.1 reduce-scatter.10

commit v3 on v2

--- a/solution.py
+++ b/solution.py
@@ -1,3 +1,4 @@
+import functools
 import math
 
 import jax
@@ -382,12 +383,20 @@
     return pl.BlockSpec(memory_space=pltpu.SMEM)
 
 
-def call(body, outs, args, specs=None, scratch=(), flops=0, reads=0, aliases=None, out_specs=None, limit=40):
+def call(body, outs, args, specs=None, scratch=(), flops=0, reads=0, aliases=None, out_specs=None, limit=40, after=()):
     specs = [whole(a.shape) if s is None else s for a, s in zip(args, specs or [None] * len(args))]
+    specs = specs + [pl.BlockSpec(memory_space=pl.ANY)] * len(after)
+    count, extra = len(args), len(after)
     out_shape = [jax.ShapeDtypeStruct(shape, dtype) for shape, dtype in outs]
     moved = sum(math.prod(s) * jnp.dtype(d).itemsize for s, d in outs) + reads
+
+    def run(*refs):
+        body(*refs[:count], *refs[count + extra :])
+
+    name = body.func.__name__ if isinstance(body, functools.partial) else body.__name__
     return pl.pallas_call(
-        body,
+        run,
+        name=name,
         grid=(1,),
         in_specs=specs,
         out_specs=out_specs or [whole(shape) for shape, _ in outs],
@@ -396,7 +405,7 @@
         input_output_aliases=aliases or {},
         cost_estimate=pl.CostEstimate(flops=int(flops), bytes_accessed=int(moved), transcendentals=0),
         compiler_params=pltpu.CompilerParams(vmem_limit_bytes=limit << 20),
-    )(*args)
+    )(*args, *after)
 
 
 def diagonal(gain_row):
@@ -413,11 +422,10 @@
     return jnp.concatenate([block[:, LANES // 2 :], block[:, : LANES // 2]], axis=1)
 
 
-def prepare_attention(me_ref, w_ref, gain_ref, out_ref, packed_ref):
-    side, second = me_ref[0] & 1, me_ref[0] >> 1
-    diag = diagonal(gain_ref[0]).astype(BF16)
-    rows = w_ref.shape[1]
-    low = lane_low(rows)
+def pack_attention(me, w_ref, gain_row, out_ref, packed_ref, top):
+    side, second = me & 1, me >> 1
+    diag = diagonal(gain_row).astype(BF16)
+    low = lane_low(LANES)
 
     def head(t):
         chunk = pl.multiple_of(((t // 4) * 8 + 2 * (t % 4) + side) * LANES, LANES)
@@ -429,20 +437,37 @@
 
     for u in range(6):
         pair = jnp.where(low, head(2 * u), head(2 * u + 1))
-        packed_ref[:, u * LANES : (u + 1) * LANES] = pair.astype(BF16)
+        packed_ref[top : top + LANES, u * LANES : (u + 1) * LANES] = pair.astype(BF16)
     for c in range(4):
-        packed_ref[c * 32 : (c + 1) * 32, 768:1024] = out_ref[:, c * 256 : (c + 1) * 256]
-
-
-def prepare_mlp(me_ref, up_ref, gain_ref, down_ref, packed_ref):
-    me = me_ref[0]
-    diag = diagonal(gain_ref[0]).astype(BF16)
+        packed_ref[top + c * 32 : top + (c + 1) * 32, 768:1024] = out_ref[:, c * 256 : (c + 1) * 256]
+
+
+def pack_up(me, up_ref, gain_row, packed_ref, top):
+    diag = diagonal(gain_row).astype(BF16)
     for j in range(8):
         chunk = pl.multiple_of((j * 4 + me) * LANES, LANES)
-        packed_ref[:LANES, j * LANES : (j + 1) * LANES] = dot(
+        packed_ref[top : top + LANES, j * LANES : (j + 1) * LANES] = dot(
             diag, up_ref[0, :, pl.ds(chunk, LANES)]
         ).astype(BF16)
-    packed_ref[LANES:, :] = down_ref[0, pl.ds(pl.multiple_of(me * LANES, LANES), LANES), :]
+
+
+def pack_down(me, down_ref, packed_ref, top):
+    packed_ref[top : top + LANES, :] = down_ref[0, pl.ds(pl.multiple_of(me * LANES, LANES), LANES), :]
+
+
+def prepare_first(me_ref, w_ref, gain_a, out_ref, up_ref, gain_m, packed_ref):
+    pack_attention(me_ref[0], w_ref, gain_a[0], out_ref, packed_ref, 0)
+    pack_up(me_ref[0], up_ref, gain_m[0], packed_ref, LANES)
+
+
+def prepare_second(me_ref, w_ref, gain_a, out_ref, down_ref, packed_ref):
+    pack_attention(me_ref[0], w_ref, gain_a[0], out_ref, packed_ref, LANES)
+    pack_down(me_ref[0], down_ref, packed_ref, 0)
+
+
+def prepare_third(me_ref, up_ref, gain_m, down_ref, packed_ref):
+    pack_up(me_ref[0], up_ref, gain_m[0], packed_ref, 0)
+    pack_down(me_ref[0], down_ref, packed_ref, LANES)
 
 
 def image_numbers(rows, flag, lens):
@@ -471,34 +496,35 @@
     mixing_ref[...] = jnp.where(flag == 1, high, low).astype(BF16)
 
 
-def write_norm(hidden, xhat_ref, rstd_ref):
-    xhat, rstd = normalize(hidden)
-    xhat_ref[...] = xhat.astype(BF16)
-    rstd_ref[...] = jnp.broadcast_to(rstd, rstd_ref.shape)
-
-
-def embed(z_ref, tokens_ref, mixing_ref, t0, t1, t2, t3, hidden_ref, xhat_ref, rstd_ref, table):
+def write_norm(hidden, xhat_ref):
+    xhat_ref[...] = normalize(hidden)[0].astype(BF16)
+
+
+def embed(z_ref, tokens_ref, mixing_ref, t0, t1, t2, t3, hidden_ref, xhat_ref, table):
     z = z_ref[0]
     for k, piece in enumerate((t0, t1, t2, t3)):
         table[:, pl.ds(pl.multiple_of((z ^ k) * 256, 256), 256)] = piece[...].astype(F32)
     hidden = tokens_ref[...].astype(F32) + dot(mixing_ref[...], table[...].astype(BF16))
     hidden_ref[...] = hidden
-    write_norm(hidden, xhat_ref, rstd_ref)
+    write_norm(hidden, xhat_ref)
 
 
 def added(p0, r1, r2, r3):
     return (p0[...].astype(F32) + r1[...].astype(F32)) + (r2[...].astype(F32) + r3[...].astype(F32))
 
 
-def add_norm(h_ref, p0, r1, r2, r3, middle_ref, xhat_ref, rstd_ref):
+def add_norm(h_ref, p0, r1, r2, r3, middle_ref, xhat_ref):
     middle = h_ref[...] + added(p0, r1, r2, r3)
     middle_ref[...] = middle
-    write_norm(middle, xhat_ref, rstd_ref)
-
-
-def add_norm_backward(g_ref, p0, r1, r2, r3, xhat_ref, rstd_ref, d_ref, low_ref):
-    e = added(p0, r1, r2, r3)
-    d = g_ref[...] + norm_backward(e, xhat_ref[...].astype(F32), rstd_ref[:, :1])
+    write_norm(middle, xhat_ref)
+
+
+def add_output(h_ref, p0, r1, r2, r3, out_ref):
+    out_ref[...] = h_ref[...] + added(p0, r1, r2, r3)
+
+
+def add_norm_backward(g_ref, p0, r1, r2, r3, h_ref, d_ref, low_ref):
+    d = g_ref[...] + norm_backward(added(p0, r1, r2, r3), *normalize(h_ref[...]))
     d_ref[...] = d
     low_ref[...] = d.astype(BF16)
 
@@ -507,7 +533,7 @@
     return packed_ref[:, c * 32 : (c + 1) * 32, 768:1024].reshape(256, 256)
 
 
-def attention_forward(flag_ref, x_ref, w_ref, proj_ref, att_ref, p_ref, *, lens):
+def attention_forward(flag_ref, x_ref, w_ref, proj_ref, p_ref, *, lens):
     rows = x_ref.shape[0]
     flag = flag_ref[0]
     width = x_ref.shape[1]
@@ -531,9 +557,9 @@
             probs = powers * (1.0 / jnp.sum(powers, axis=-1, keepdims=True))
             o = dot(probs.astype(BF16), jnp.where(keep, v, zero))
             total = o if total is None else total + o
-        att_ref[:, u * LANES : (u + 1) * LANES] = total.astype(BF16)
+        proj_ref[:, 768 + u * LANES : 768 + (u + 1) * LANES] = total.astype(BF16)
     for c in range(4):
-        p_ref[:, c * 256 : (c + 1) * 256] = dot(att_ref[...], out_chunk(w_ref, c)).astype(BF16)
+        p_ref[:, c * 256 : (c + 1) * 256] = dot(proj_ref[:, 768:], out_chunk(w_ref, c)).astype(BF16)
 
 
 def attention_backward(flag_ref, d_ref, proj_ref, w_ref, dproj_ref, p_ref, *, lens):
@@ -584,14 +610,18 @@
     return pre * upto, upto + pre * density
 
 
-def mlp_forward(x_ref, up_ref, down_ref, act_ref, slope_ref, p_ref):
+def mlp_up(x_ref, up_ref, both_ref):
     width = x_ref.shape[1]
     for c in range(4):
         cols = slice(c * 256, (c + 1) * 256)
         act, slope = gelu_parts(dot(x_ref[...], up_ref[:, :, cols].reshape(width, 256)))
-        act_ref[:, cols] = act.astype(BF16)
-        slope_ref[:, cols] = slope.astype(BF16)
-    p_ref[...] = dot(act_ref[...], down_ref[...].reshape(width, width)).astype(BF16)
+        both_ref[0, :, cols] = act.astype(BF16)
+        both_ref[1, :, cols] = slope.astype(BF16)
+
+
+def mlp_down(act_ref, down_ref, p_ref):
+    width = p_ref.shape[1]
+    p_ref[...] = dot(act_ref[0], down_ref[...].reshape(width, width)).astype(BF16)
 
 
 def mlp_backward(d_ref, slope_ref, up_ref, down_ref, dpre_ref, p_ref):
@@ -599,7 +629,7 @@
     for c in range(4):
         cols = slice(c * 256, (c + 1) * 256)
         d_act = dot_nt(d_ref[...], down_ref[2 * c : 2 * c + 2].reshape(256, width))
-        dpre_ref[:, cols] = (d_act * slope_ref[:, cols].astype(F32)).astype(BF16)
+        dpre_ref[:, cols] = (d_act * slope_ref[0, :, cols].astype(F32)).astype(BF16)
     p_ref[...] = dot_nt(dpre_ref[...], up_ref[...].reshape(width, width)).astype(BF16)
 
 
@@ -615,48 +645,44 @@
     p_ref[...] = dot(act_ref[...], down_ref[...].reshape(width, width)).astype(BF16)
 
 
+def summed(left, right, rows, cols=slice(None)):
+    total = None
+    for a, b in zip(left, right):
+        term = dot_t(a[:, rows], b[:, cols])
+        total = term if total is None else total + term
+    return total
+
+
 def grads_mlp(*refs):
     x, dpre, act, d, out_ref = refs[:4], refs[4:8], refs[8:12], refs[12:16], refs[16]
+    act = [a.at[0] if len(a.shape) == 3 else a for a in act]
     for half, (left, right) in enumerate(((x, dpre), (act, d))):
         for j in range(8):
-            rows = slice(j * LANES, (j + 1) * LANES)
-            total = None
-            for a, b in zip(left, right):
-                term = dot_t(a[:, rows], b[...])
-                total = term if total is None else total + term
+            total = summed(left, right, slice(j * LANES, (j + 1) * LANES))
             out_ref[j, half * LANES : (half + 1) * LANES, :] = total.astype(BF16)
 
 
 def grads_attention(*refs):
-    x, dproj, att, d, out_ref = refs[:4], refs[4:8], refs[8:12], refs[12:16], refs[16]
+    x, dproj, kept, d, out_ref = refs[:4], refs[4:8], refs[8:12], refs[12:16], refs[16]
     for j in range(8):
-        rows = slice(j * LANES, (j + 1) * LANES)
-        total = None
-        for a, b in zip(x, dproj):
-            term = dot_t(a[:, rows], b[...])
-            total = term if total is None else total + term
-        out_ref[j, :, :768] = total.astype(BF16)
+        out_ref[j, :, :768] = summed(x, dproj, slice(j * LANES, (j + 1) * LANES)).astype(BF16)
     for c in range(4):
-        cols = slice(c * 256, (c + 1) * 256)
-        total = None
-        for a, b in zip(att, d):
-            term = dot_t(a[...], b[:, cols])
-            total = term if total is None else total + term
+        total = summed(kept, d, slice(None), slice(c * 256, (c + 1) * 256))
         out_ref[:, c * 32 : (c + 1) * 32, 768:1024] = total.astype(BF16).reshape(8, 32, 256)
 
 
-def finish_mlp(me_ref, g0, g1, g2, g3, up_ref, gain_ref, *rest):
+def finish_mlp(me_ref, g0, g1, g2, g3_up, g3_down, up_ref, gain_ref, *rest):
     dup_ref, ddown_ref, dgain_ref = rest[-3:]
     me = me_ref[0]
-    diag = diagonal(gain_ref[0])
+    column = jnp.sum(diagonal(gain_ref[0]), axis=1, keepdims=True)
     total = jnp.zeros((LANES, LANES), F32)
-    column = jnp.sum(diag, axis=1, keepdims=True)
-    for k, piece in enumerate((g0, g1, g2, g3)):
-        owner = me ^ k
-        ddown_ref[0, pl.ds(pl.multiple_of(owner * LANES, LANES), LANES), :] = piece[LANES:, :].astype(F32)
+    for k, piece in enumerate((g0[LANES:, :], g1[LANES:, :], g2[LANES:, :], g3_down[...])):
+        rows = pl.ds(pl.multiple_of((me ^ k) * LANES, LANES), LANES)
+        ddown_ref[0, rows, :] = piece.astype(F32)
+    ups = [g0[:LANES, :], g1[:LANES, :], g2[:LANES, :], g3_up[...]]
     for i in range(4):
         got = jnp.where(
-            me == i, g0[:LANES, :], jnp.where(me == i ^ 1, g1[:LANES, :], jnp.where(me == i ^ 2, g2[:LANES, :], g3[:LANES, :]))
+            me == i, ups[0], jnp.where(me == i ^ 1, ups[1], jnp.where(me == i ^ 2, ups[2], ups[3]))
         ).astype(F32)
         for j in range(8):
             cols = slice((j * 4 + i) * LANES, (j * 4 + i + 1) * LANES)
@@ -741,24 +767,19 @@
     out_pieces = jnp.where(core == pair_side, keep, over_fsdp(give, 1))
     gains_a = gain_attn.reshape(layers, 1, LANES)
     gains_m = gain_mlp.reshape(layers, 1, LANES)
-    attn_w, mlp_w = [], []
-    for depth in range(layers):
-        (packed,) = call(
-            prepare_attention,
-            [((LANES, width), BF16)],
-            [me1, w_qkv, gains_a, out_pieces[depth]],
-            [scalars(), layer_of(w_qkv, depth), layer_of(gains_a, depth), None],
-        )
-        attn_w.append(lax.all_gather(packed, "fsdp", axis=0, tiled=False))
-        (packed,) = call(
-            prepare_mlp,
-            [((2 * LANES, width), BF16)],
-            [me1, w_up, gains_m, w_down],
-            [scalars(), layer_of(w_up, depth), layer_of(gains_m, depth), layer_of(w_down, depth)],
-        )
-        mlp_w.append(lax.all_gather(packed, "fsdp", axis=0, tiled=False))
-    up_spec = pl.BlockSpec((8, LANES, width), lambda *_: (0, 0, 0))
-    down_spec = pl.BlockSpec((8, LANES, width), lambda *_: (0, 1, 0))
+
+    def part(top):
+        return pl.BlockSpec((8, LANES, width), lambda *_: (0, top, 0))
+
+    def fetch(body, args, specs, after=()):
+        (packed,) = call(body, [((2 * LANES, width), BF16)], [me1] + args, [scalars()] + specs, after=after)
+        return lax.all_gather(packed, "fsdp", axis=0, tiled=False)
+
+    first_w = fetch(
+        prepare_first,
+        [w_qkv, gains_a, out_pieces[0], w_up, gains_m],
+        [layer_of(w_qkv, 0), layer_of(gains_a, 0), None, layer_of(w_up, 0), layer_of(gains_m, 0)],
+    )
 
     flag = resolution[me]
     flag1 = flag.reshape(1)
@@ -772,165 +793,172 @@
     weight = jnp.where(jnp.arange(rows, dtype=jnp.int32) < live, token_share, 0.0)
     gradient = cotangent.astype(F32) * weight[:, None]
 
+    normed = [(block, F32), (block, BF16)]
     other = over_fsdp(pos_table, 1)
     pair = jnp.concatenate(
         [jnp.where(core == 0, pos_table, other), jnp.where(core == 0, other, pos_table)], axis=1
     )
     pieces = [pair] + [over_fsdp(pair, 2 * k) for k in range(1, 4)]
     (mixing,) = call(
-        lambda *refs: make_mixing(*refs, lens=lens),
+        functools.partial(make_mixing, lens=lens),
         [((rows, len_high), BF16)],
         [flag1, index_lo, index_hi],
         [scalars(), None, None],
     )
-    hidden, xhat, rstd = call(
+    hidden, xhat = call(
         embed,
-        [(block, F32), (block, BF16), ((rows, LANES), F32)],
+        normed,
         [deep1, tokens, mixing] + pieces,
         [scalars()] + [None] * 6,
         scratch=[VMEM((len_high, width), F32)],
         flops=2 * rows * len_high * width,
     )
 
+    second_w = fetch(
+        prepare_second,
+        [w_qkv, gains_a, out_pieces[1], w_down],
+        [layer_of(w_qkv, 1), layer_of(gains_a, 1), None, layer_of(w_down, 0)],
+        [xhat],
+    )
+    third_w = fetch(
+        prepare_third,
+        [w_up, gains_m, w_down],
+        [layer_of(w_up, 1), layer_of(gains_m, 1), layer_of(w_down, 1)],
+        [xhat],
+    )
+    attn_w = [(first_w, part(0)), (second_w, part(1))]
+
+    def tie(*values):
+        return lax.optimization_barrier(values)
+
+    def chain(kernel):
+        done = []
+        for k in blocks:
+            done.append(kernel(k, [d[0] for d in done[-1:]]))
+        return done
+
     def collect(parts):
         return [parts[0]] + [square.swap(parts[k], k) for k in range(1, 4)]
 
     d_top = square.spread(gradient.astype(BF16))
     saved = []
     for depth in range(layers):
-        a_w, m_w = attn_w[depth], mlp_w[depth]
+        a_w, a_part = attn_w[depth]
         xs = square.spread(xhat)
-        got = [
-            call(
-                lambda *refs: attention_forward(*refs, lens=lens),
-                [((rows, 768), BF16), ((rows, 256), BF16), (block, BF16)],
+        got = chain(
+            lambda k, after: call(
+                functools.partial(attention_forward, lens=lens),
+                [(block, BF16)] * 2,
                 [flags[k], xs[k], a_w],
-                [scalars(), None, None],
-                flops=2 * rows * width * 1024,
-                reads=2 * a_w.size,
+                [scalars(), None, a_part],
+                after=after,
             )
-            for k in blocks
-        ]
-        projs, atts = [g[0] for g in got], [g[1] for g in got]
-        middle, xhat_m, rstd_m = call(
-            add_norm,
-            [(block, F32), (block, BF16), ((rows, LANES), F32)],
-            [hidden] + collect([g[2] for g in got]),
-            reads=4 * rows * width,
-        )
-        ms = square.spread(xhat_m)
-        last = depth == layers - 1
-        if last:
-            got = [
-                call(
+        )
+        kept = [g[0] for g in got]
+        es = collect([g[1] for g in got])
+        if depth == 0:
+            es, d_top = tie(es, d_top)
+        before, (middle, xhat) = hidden, call(add_norm, normed, [hidden] + es)
+        ms = square.spread(xhat)
+        if depth < layers - 1:
+            acts = chain(
+                lambda k, after: call(
+                    mlp_up, [((2,) + block, BF16)], [ms[k], first_w], [None, part(1)], after=after
+                )
+            )
+            acts = [a[0] for a in acts]
+            parts = [None] * 4
+            last = acts
+            for k in (1, 2, 3, 0):
+                (parts[k],) = call(
+                    mlp_down, [(block, BF16)], [acts[k], second_w], [None, part(0)], after=last
+                )
+                last = [parts[k]]
+            saved.append((before, xs, kept, middle, ms, acts))
+            hidden, xhat = call(add_norm, normed, [middle] + collect(parts))
+        else:
+            got = chain(
+                lambda k, after: call(
                     mlp_both,
                     [(block, BF16)] * 4,
-                    [ms[k], d_top[k], m_w, m_w],
-                    [None, None, up_spec, down_spec],
-                    flops=8 * rows * width * width,
-                    reads=2 * m_w.size,
+                    [ms[k], d_top[k], third_w, third_w],
+                    [None, None, part(0), part(1)],
+                    after=after,
                 )
-                for k in blocks
-            ]
-            acts, dpres, ps, backs = ([g[t] for g in got] for t in range(4))
-            slopes = None
-        else:
-            got = [
-                call(
-                    mlp_forward,
-                    [(block, BF16)] * 3,
-                    [ms[k], m_w, m_w],
-                    [None, up_spec, down_spec],
-                    flops=4 * rows * width * width,
-                    reads=2 * m_w.size,
-                )
-                for k in blocks
-            ]
-            acts, slopes, ps = ([g[t] for g in got] for t in range(3))
-            dpres = backs = None
-        saved.append((xhat, rstd, xs, projs, atts, xhat_m, rstd_m, ms, acts, slopes))
-        if last:
-            output_parts = ps
-        else:
-            hidden, xhat, rstd = call(
-                add_norm,
-                [(block, F32), (block, BF16), ((rows, LANES), F32)],
-                [middle] + collect(ps),
-                reads=4 * rows * width,
             )
+            acts, dpres, output_parts, backs = ([g[t] for g in got] for t in range(4))
+            saved.append((before, xs, kept, middle, ms, acts))
+
+    def far_halves(x, y):
+        half = x.shape[0] // 2
+        return [square.swap(x[:half], 2), square.swap(y[half:], 1)]
+
+    def home(term):
+        return lax.psum_scatter(term, "fsdp", scatter_dimension=0, tiled=False)
 
     homes_m, homes_a = [None] * layers, [None] * layers
-    held = None
-    output = None
     for depth in reversed(range(layers)):
-        a_w, m_w = attn_w[depth], mlp_w[depth]
-        xhat, rstd, xs, projs, atts, xhat_m, rstd_m, ms, acts, slopes = saved[depth]
-        if depth == layers - 1:
-            ds = d_top
-        else:
-            ds = square.spread(low)
-            got = [
-                call(
+        top = depth == layers - 1
+        a_w, a_part = attn_w[depth]
+        before, xs, kept, middle, ms, acts = saved[depth]
+        ds = d_top if top else square.spread(low)
+        if not top:
+            second_half = pl.BlockSpec((1,) + block, lambda *_: (1, 0, 0))
+            got = chain(
+                lambda k, after: call(
                     mlp_backward,
                     [(block, BF16)] * 2,
-                    [ds[k], slopes[k], m_w, m_w],
-                    [None, None, up_spec, down_spec],
-                    flops=4 * rows * width * width,
-                    reads=2 * m_w.size,
+                    [ds[k], acts[k], first_w, second_w],
+                    [None, second_half, part(1), part(0)],
+                    after=after or late[1][1:],
                 )
-                for k in blocks
-            ]
+            )
             dpres, backs = ([g[t] for g in got] for t in range(2))
         es = collect(backs)
+        first_half = pl.BlockSpec((1,) + block, lambda *_: (0, 0, 0))
         (term,) = call(
             grads_mlp,
             [((8, 2 * LANES, width), BF16)],
             list(ms) + list(dpres) + list(acts) + list(ds),
-            flops=16 * rows * width * width,
-        )
-        es, term = lax.optimization_barrier((es, term))
-        homes_m[depth] = lax.psum_scatter(term, "fsdp", scatter_dimension=0, tiled=False)
-        if depth == layers - 1:
-            outs = collect(output_parts)
-            output = middle + ((outs[0].astype(F32) + outs[1].astype(F32)) + (outs[2].astype(F32) + outs[3].astype(F32)))
-        else:
-            es, homes_m[depth + 1] = lax.optimization_barrier((es, homes_m[depth + 1]))
-        d_middle, low = call(
-            add_norm_backward,
-            [(block, F32), (block, BF16)],
-            [gradient] + es + [xhat_m, rstd_m],
-            reads=8 * rows * width,
-        )
+            [None] * 8 + [None if top else first_half] * 4 + [None] * 4,
+        )
+        es, term = tie(es, term)
+        if not top:
+            es, homes_m[depth + 1] = tie(es, homes_m[depth + 1])
+        homes_m[depth] = home(term)
+        d_middle, low = call(add_norm_backward, normed, [gradient] + es + [middle])
         ds = square.spread(low)
-        got = [
-            call(
-                lambda *refs: attention_backward(*refs, lens=lens),
+        got = chain(
+            lambda k, after: call(
+                functools.partial(attention_backward, lens=lens),
                 [((rows, 768), BF16), (block, BF16)],
-                [flags[k], ds[k], projs[k], a_w],
-                [scalars(), None, None, None],
-                flops=2 * rows * width * 1536,
-                reads=2 * a_w.size,
+                [flags[k], ds[k], kept[k], a_w],
+                [scalars(), None, None, a_part],
+                after=after,
             )
-            for k in blocks
-        ]
+        )
         dprojs = [g[0] for g in got]
         es = collect([g[1] for g in got])
+        if top:
+            outs = collect(output_parts)
+        out_part = pl.BlockSpec((rows, 256), lambda *_: (0, 3))
         (term,) = call(
             grads_attention,
             [((8, LANES, width), BF16)],
-            list(xs) + dprojs + atts + list(ds),
-            flops=8 * rows * width * width,
-        )
-        es, term = lax.optimization_barrier((es, term))
-        homes_a[depth] = lax.psum_scatter(term, "fsdp", scatter_dimension=0, tiled=False)
-        if depth < layers - 1:
-            es, homes_a[depth + 1] = lax.optimization_barrier((es, homes_a[depth + 1]))
-        gradient, low = call(
-            add_norm_backward,
-            [(block, F32), (block, BF16)],
-            [d_middle] + es + [xhat, rstd],
-            reads=8 * rows * width,
-        )
+            list(xs) + dprojs + list(kept) + list(ds),
+            [None] * 8 + [out_part] * 4 + [None] * 4,
+        )
+        es, term = tie(es, term)
+        homes_a[depth] = home(term)
+        if top:
+            late = (middle, outs)
+        else:
+            x, y = square.swap(homes_m[1], 1), square.swap(homes_m[1], 2)
+            es, homes_a[1], x, y = tie(es, homes_a[1], x, y)
+            homes_m[1] = [homes_m[1], x, y] + far_halves(x, y)
+        gradient, low = call(add_norm_backward, normed, [d_middle] + es + [before])
+
+    gradient, low, homes_m[0] = tie(gradient, low, homes_m[0])
 
     rest = (gradient - low.astype(F32)).astype(BF16)
     table_term = (dot_t(mixing, low) + dot_t(mixing, rest)).astype(BF16).reshape(len_high, 4, 256)
@@ -944,13 +972,17 @@
     give = jnp.where(core == 0, mine[:, LANES:], mine[:, :LANES])
     d_table = square.total(keep.astype(F32) + over_fsdp(give, 1).astype(F32))
 
+    homes_a[1] = square.spread(homes_a[1])
+    x, y = square.swap(homes_m[0], 1), square.swap(homes_m[0], 2)
+    homes_m[0] = [homes_m[0], x, y] + far_halves(x, y)
     big = [None] * 6
+    (output,) = call(add_output, [(block, F32)], [late[0]] + late[1])
     for depth in reversed(range(layers)):
-        pieces = square.spread(homes_m[depth])
+        pieces = homes_m[depth]
         prior = big[3:]
         names = [(w_up.shape, F32), (w_down.shape, F32), (gains_m.shape, F32)]
         args = [me1] + pieces + [w_up, gains_m]
-        specs = [scalars()] + [None] * 4 + [layer_of(w_up, depth), layer_of(gains_m, depth)]
+        specs = [scalars()] + [None] * 5 + [layer_of(w_up, depth), layer_of(gains_m, depth)]
         extra = [] if prior[0] is None else prior
         big[3:] = call(
             finish_mlp,
@@ -960,7 +992,10 @@
             aliases={len(args) + t: t for t in range(len(extra))},
             out_specs=[layer_of(jax.ShapeDtypeStruct(s, d), depth) for s, d in names],
         )
-        pieces = square.spread(homes_a[depth])
+        if depth == 0:
+            homes_a[0], big, d_table, output = tie(homes_a[0], big, d_table, output)
+            homes_a[0] = square.spread(homes_a[0])
+        pieces = homes_a[depth]
         packed = [piece[:, 768:1024] for piece in pieces]
         odd_me = (me & 1) == 1
         even = [jnp.where(odd_me, packed[1], packed[0]), jnp.where(odd_me, packed[3], packed[2])]

time: 476 us -> 431 us (0.905)
  waiting for transfers between devices: 151 us -> 113 us
  Pallas kernels: 126 us -> 117 us
  local copies, waits for them, and re-layouts: 69.5 us -> 76.2 us
    reduce_scatter x4, waiting for transfers between devices: 24.4 us -> 0.02 us  [home(): return lax.psum_scatter(term, 'fsdp', scatter_dimension=0, tiled=False)]
    pallas_call x49 -> x53, Pallas kernels: 126 us -> 117 us  [call(): pl.pallas_call(run, name=name, grid=(1,), in_specs=specs, out_specs=out_s...]
    all_gather x4 -> x3, waiting for transfers between devices: 19.7 us -> 12.5 us  [fetch(): return lax.all_gather(packed, 'fsdp', axis=0, tiled=False)]
    unnamed x271 -> x249, local copies, waits for them, and re-layouts: 62.3 us -> 68.5 us
    ppermute x63 -> x65, waiting for transfers between devices: 93.6 us -> 89 us  [swap(): return lax.ppermute(block, 'dp', [(i, i ^ k) for i in range(self.count)])]
    ppermute x63 -> x65, starting transfers between devices: 79.6 us -> 78 us  [swap(): return lax.ppermute(block, 'dp', [(i, i ^ k) for i in range(self.count)])]
  transfers between devices with their start and end apart: 82 -> 83, of which waited for: 28 -> 27; matrix products, arithmetic and copies ran while one was open for 5% -> 4% of each run, Pallas kernels for 26% -> 27%
where the time goes in v3:
time: 431 us; the launch traced here: 426 us
  Pallas kernels  117 us (27%)
  waiting for transfers between devices  113 us (26%)
  starting transfers between devices  89.9 us (21%)
  local copies, waits for them, and re-layouts  76.2 us (18%)
  between operations  17.6 us (4%)
  other arithmetic  10 us (2%)
    pallas_call x53, Pallas kernels, call(): pl.pallas_call(run, name=name, grid=(1,), in_specs=specs, out_specs=out_s...  117 us
    ppermute x65, waiting for transfers between devices, swap(): return lax.ppermute(block, 'dp', [(i, i ^ k) for i in range(self.count)])  89 us
    ppermute x65, starting transfers between devices, swap(): return lax.ppermute(block, 'dp', [(i, i ^ k) for i in range(self.count)])  78 us
    unnamed x249, local copies, waits for them, and re-layouts  68.5 us
    all_gather x3, waiting for transfers between devices, fetch(): return lax.all_gather(packed, 'fsdp', axis=0, tiled=False)  12.5 us
    ppermute x11, waiting for transfers between devices, over_fsdp(): return lax.ppermute(x, 'fsdp', [(j, j ^ k) for j in range(8)])  11.3 us
    ppermute x11, starting transfers between devices, over_fsdp(): return lax.ppermute(x, 'fsdp', [(j, j ^ k) for j in range(8)])  10.8 us
  transfers between devices with their start and end apart: 83, of which 27 were waited for; matrix products, arithmetic and copies ran while one was open for 4% of the time, Pallas kernels for 27%

profile of v3, /device:TPU:0, one launch (start us, length us, event | category | flops | bytes accessed | tf_op | source)
XLA Modules:
  0.0 426.3 jit_solution(11257633149227729739)
XLA Ops:
  15.1 2.8 collective-permute-start.1
  17.9 2.6 collective-permute-start.2
  23.0 4.1 collective-permute-done.2.refs_5_
  51.2 12.5 %all-gather.7.cloned.1.call-done = bf16[2048,1024]{1,0:T(8,128)(2,1)} async-done(((bf16[256,1024]{1,0:T(8,128)(2,1)}), bf16[2048,1024]{1,0:T(8,128)(2,1)}) %all-gather.7.cloned.1.call-update) | async-done | bytes 4194320 | tf_op jit(solution)/shard_map/all_gather | solution.py:776
  65.9 2.4 attention_forward.8
  68.2 2.5 collective-permute-start.13
  70.7 3.3 attention_forward.9
  74.6 3.1 attention_forward.10
  78.5 3.2 attention_forward.11
  83.1 2.4 collective-permute-start.10
  85.5 8.0 %collective-permute-done.8.refs_3_ = bf16[152,1024]{1,0:T(8,128)(2,1)S(1)} collective-permute-done((bf16[152,1024]{1,0:T(8,128)(2,1)S(1)}, bf16[152,1024]{1,0:T(8,128)(2,1)S(1)}, u32[]{:S(2)}, u32[]{:S(2)}) %collective-permute-start.8) | collective-permute-done | bytes 311328 | tf_op jit(solution)/shard_map/ppermute | solution.py:61
  98.9 6.1 %collective-permute-done.16.refs_0_.refs_1_ = bf16[152,1024]{1,0:T(8,128)(2,1)S(1)} collective-permute-done((bf16[152,1024]{1,0:T(8,128)(2,1)S(1)}, bf16[152,1024]{1,0:T(8,128)(2,1)S(1)}, u32[]{:S(2)}, u32[]{:S(2)}) %collective-permute-start.16) | collective-permute-done | bytes 311328 | tf_op jit(solution)/shard_map/ppermute | solution.py:61
  105.7 4.0 collective-permute-done.15.refs_0_.refs_2_
  125.4 5.7 %collective-permute-done.17.refs_2_ = bf16[152,1024]{1,0:T(8,128)(2,1)S(1)} collective-permute-done((bf16[152,1024]{1,0:T(8,128)(2,1)S(1)}, bf16[152,1024]{1,0:T(8,128)(2,1)S(1)}, u32[]{:S(2)}, u32[]{:S(2)}) %collective-permute-start.17) | collective-permute-done | bytes 311328 | tf_op jit(solution)/shard_map/ppermute | solution.py:61
  131.0 7.4 %collective-permute-done.18.refs_3_ = bf16[152,1024]{1,0:T(8,128)(2,1)S(1)} collective-permute-done((bf16[152,1024]{1,0:T(8,128)(2,1)S(1)}, bf16[152,1024]{1,0:T(8,128)(2,1)S(1)}, u32[]{:S(2)}, u32[]{:S(2)}) %collective-permute-start.18) | collective-permute-done | bytes 311328 | tf_op jit(solution)/shard_map/ppermute | solution.py:61
  144.6 4.6 %collective-permute-done.20.refs_1_ = bf16[152,1024]{1,0:T(8,128)(2,1)S(1)} collective-permute-done((bf16[152,1024]{1,0:T(8,128)(2,1)S(1)}, bf16[152,1024]{1,0:T(8,128)(2,1)S(1)}, u32[]{:S(2)}, u32[]{:S(2)}) %collective-permute-start.20) | collective-permute-done | bytes 311328 | tf_op jit(solution)/shard_map/ppermute | solution.py:61
  149.2 2.9 attention_forward.13
  162.5 6.2 %collective-permute-done.23.refs_3_ = bf16[152,1024]{1,0:T(8,128)(2,1)S(1)} collective-permute-done((bf16[152,1024]{1,0:T(8,128)(2,1)S(1)}, bf16[152,1024]{1,0:T(8,128)(2,1)S(1)}, u32[]{:S(2)}, u32[]{:S(2)}) %collective-permute-start.23) | collective-permute-done | bytes 311328 | tf_op jit(solution)/shard_map/ppermute | solution.py:61
  177.4 3.4 mlp_both.4
  181.0 3.7 mlp_both.5
  186.1 3.7 mlp_both.6
  191.6 3.8 mlp_both.7
  196.7 6.0 %grads_mlp.2 = bf16[8,256,1024]{2,1,0:T(8,128)(2,1)S(1)} custom-call(bf16[152,1024]{1,0:T(8,128)(2,1)} %get-tuple-element.169.refs_0_, bf16[152,1024]{1,0:T(8,128)(2,1)} %collective-permute-done.26.refs_0_.refs_1_, bf16[152,1024]{1,0:T(8,128)(2,1)} %collective-permute-done.28.refs_0_.refs_2_, bf16[152,1024]{1,0:T(8,128)(2,1)} %collective-permute-done.30.refs_0_.refs_3_, ...), custom_call_target="tpu_custom_call" | custom-call | bytes 4194304 | tf_op jit(solution)/shard_map/grads_mlp/pallas_call | solution.py:397
  217.2 2.7 attention_backward.8
  220.0 3.5 attention_backward.9
  224.7 3.5 attention_backward.10
  230.0 3.4 attention_backward.11
  234.0 2.4 grads_attention.2
  237.8 6.9 %collective-permute-done.37.refs_4_ = bf16[152,1024]{1,0:T(8,128)(2,1)} collective-permute-done((bf16[152,1024]{1,0:T(8,128)(2,1)}, bf16[152,1024]{1,0:T(8,128)(2,1)}, u32[]{:S(2)}, u32[]{:S(2)}) %collective-permute-start.37) | collective-permute-done | bytes 311328 | tf_op jit(solution)/shard_map/ppermute | solution.py:61
  245.1 3.4 collective-permute-start.40
  257.7 4.3 %collective-permute-done.39.refs_5_.refs_3_ = bf16[152,1024]{1,0:T(8,128)(2,1)S(1)} collective-permute-done((bf16[152,1024]{1,0:T(8,128)(2,1)}, bf16[152,1024]{1,0:T(8,128)(2,1)S(1)}, u32[]{:S(2)}, u32[]{:S(2)}) %collective-permute-start.39) | collective-permute-done | bytes 311328 | tf_op jit(solution)/shard_map/ppermute | solution.py:61
  278.4 4.5 %grads_mlp.3 = bf16[8,256,1024]{2,1,0:T(8,128)(2,1)S(1)} custom-call(bf16[152,1024]{1,0:T(8,128)(2,1)S(1)} %copy-done.62, bf16[152,1024]{1,0:T(8,128)(2,1)S(1)} %copy-done.64, bf16[152,1024]{1,0:T(8,128)(2,1)S(1)} %copy-done.66, bf16[152,1024]{1,0:T(8,128)(2,1)S(1)} %copy-done.68, bf16[152,1024]{1,0:T(8,128)(2,1)S(1)} %get-tuple-element.212.refs_4_, ...), custom_call_target="tpu_custom_call" | custom-call | bytes 4194304 | tf_op jit(solution)/shard_map/grads_mlp/pallas_call | solution.py:397
  296.4 2.8 attention_backward.12
  299.9 3.5 attention_backward.13
  303.6 3.4 attention_backward.14
  308.7 3.5 attention_backward.15
  313.8 3.7 grads_attention.3
  318.8 4.9 %collective-permute-done.52.refs_4_ = bf16[152,1024]{1,0:T(8,128)(2,1)} collective-permute-done((bf16[152,1024]{1,0:T(8,128)(2,1)}, bf16[152,1024]{1,0:T(8,128)(2,1)}, u32[]{:S(2)}, u32[]{:S(2)}) %collective-permute-start.52) | collective-permute-done | bytes 311328 | tf_op jit(solution)/shard_map/ppermute | solution.py:61
  325.2 13.5 %collective-permute-done.53.refs_2_ = bf16[256,1024]{1,0:T(8,128)(2,1)} collective-permute-done((bf16[256,1024]{1,0:T(8,128)(2,1)}, bf16[256,1024]{1,0:T(8,128)(2,1)}, u32[]{:S(2)}, u32[]{:S(2)}) %collective-permute-start.53) | collective-permute-done | bytes 524320 | tf_op jit(solution)/shard_map/ppermute | solution.py:61
  339.9 2.9 collective-permute-start.55
  355.4 2.5 add_norm_backward.7
  361.8 3.8 finish_mlp.2
  377.6 4.4 %collective-permute-done.66 = bf16[145,256]{1,0:T(8,128)(2,1)S(1)} collective-permute-done((bf16[145,256]{1,0:T(8,128)(2,1)S(1)}, bf16[145,256]{1,0:T(8,128)(2,1)S(1)}, u32[]{:S(2)}, u32[]{:S(2)}) %collective-permute-start.66) | collective-permute-done | bytes 74272 | tf_op jit(solution)/shard_map/ppermute | solution.py:757
  387.0 2.9 collective-permute-done.59.refs_2_
  392.9 3.1 finish_attention.2
  398.4 2.6 finish_mlp.3
  404.5 4.6 %collective-permute-done.72.refs_2_ = bf16[128,1024]{1,0:T(8,128)(2,1)S(1)} collective-permute-done((bf16[128,1024]{1,0:T(8,128)(2,1)}, bf16[128,1024]{1,0:T(8,128)(2,1)S(1)}, u32[]{:S(2)}, u32[]{:S(2)}) %collective-permute-start.72) | collective-permute-done | bytes 262176 | tf_op jit(solution)/shard_map/ppermute | solution.py:61
  409.9 3.5 collective-permute-done.73.refs_3_
  (464 shorter events, 204.2 us)
Async XLA Ops:
  7.2 56.4 %all-gather.7.cloned.1.call-start = ((), (), s32[]{:S(2)}) async-start(), calls=%async_computation.8 | async-start | bytes 4718592 | tf_op jit(solution)/shard_map/all_gather | solution.py:776
  13.7 99.9 %all-gather.9.cloned.1.call-start = ((), (), s32[]{:S(2)}) async-start(), calls=%async_computation.9 | async-start | bytes 4718592 | tf_op jit(solution)/shard_map/all_gather | solution.py:776
  37.0 137.3 %all-gather.11.cloned.1.call-start = ((), (), s32[]{:S(2)}) async-start(), calls=%async_computation.10 | async-start | bytes 4718592 | tf_op jit(solution)/shard_map/all_gather | solution.py:776
  39.8 245.7 %reduce-scatter.5.cloned.1.call-start = ((), (), s32[]{:S(2)}) async-start(), calls=%async_computation.4 | async-start | bytes 4718592 | tf_op jit(solution)/shard_map/reduce_scatter | solution.py:897
  42.7 25.5 %collective-permute-start.5 = (bf16[152,1024]{1,0:T(8,128)(2,1)S(1)}, bf16[152,1024]{1,0:T(8,128)(2,1)}, u32[]{:S(2)}, u32[]{:S(2)}) collective-permute-start(bf16[152,1024]{1,0:T(8,128)(2,1)S(1)} %get-tuple-element.146.refs_1_.refs_5_.refs_4_.refs_0_), channel_id=1, source_target_pairs={{0,8},{8,0},{16,24},{24,16},{1,9},{9,1},{17,25},{25,17},{2,10},{10... | collective-permute-start | bytes 933896 | tf_op jit(solution)/shard_map/ppermute | solution.py:61
  44.3 29.8 %collective-permute-start.7 = (bf16[152,1024]{1,0:T(8,128)(2,1)S(1)}, bf16[152,1024]{1,0:T(8,128)(2,1)}, u32[]{:S(2)}, u32[]{:S(2)}) collective-permute-start(bf16[152,1024]{1,0:T(8,128)(2,1)S(1)} %get-tuple-element.146.refs_1_.refs_5_.refs_4_.refs_0_), channel_id=1, source_target_pairs={{0,16},{8,24},{16,0},{24,8},{1,17},{9,25},{17,1},{25,9},{2,18},{10... | collective-permute-start | bytes 933896 | tf_op jit(solution)/shard_map/ppermute | solution.py:61
  45.8 32.0 %collective-permute-start.9 = (bf16[152,1024]{1,0:T(8,128)(2,1)S(1)}, bf16[152,1024]{1,0:T(8,128)(2,1)}, u32[]{:S(2)}, u32[]{:S(2)}) collective-permute-start(bf16[152,1024]{1,0:T(8,128)(2,1)S(1)} %get-tuple-element.146.refs_1_.refs_5_.refs_4_.refs_0_), channel_id=1, source_target_pairs={{0,24},{8,16},{16,8},{24,0},{1,25},{9,17},{17,9},{25,1},{2,26},{10... | collective-permute-start | bytes 933896 | tf_op jit(solution)/shard_map/ppermute | solution.py:61
  48.2 34.9 %collective-permute-start.11 = (bf16[152,1024]{1,0:T(8,128)(2,1)S(1)}, bf16[152,1024]{1,0:T(8,128)(2,1)}, u32[]{:S(2)}, u32[]{:S(2)}) collective-permute-start(bf16[152,1024]{1,0:T(8,128)(2,1)S(1)} %get-tuple-element.170.refs_1_.refs_12_), channel_id=1, source_target_pairs={{0,8},{8,0},{16,24},{24,16},{1,9},{9,1},{17,25},{25,17},{2,10},{10... | collective-permute-start | bytes 933896 | tf_op jit(solution)/shard_map/ppermute | solution.py:61
  49.7 35.8 %collective-permute-start.12 = (bf16[152,1024]{1,0:T(8,128)(2,1)S(1)}, bf16[152,1024]{1,0:T(8,128)(2,1)}, u32[]{:S(2)}, u32[]{:S(2)}) collective-permute-start(bf16[152,1024]{1,0:T(8,128)(2,1)S(1)} %get-tuple-element.170.refs_1_.refs_12_), channel_id=1, source_target_pairs={{0,16},{8,24},{16,0},{24,8},{1,17},{9,25},{17,1},{25,9},{2,18},{10... | collective-permute-start | bytes 933896 | tf_op jit(solution)/shard_map/ppermute | solution.py:61
  68.2 17.2 %collective-permute-start.13 = (bf16[152,1024]{1,0:T(8,128)(2,1)S(1)}, bf16[152,1024]{1,0:T(8,128)(2,1)S(1)}, u32[]{:S(2)}, u32[]{:S(2)}) collective-permute-start(bf16[152,1024]{1,0:T(8,128)(2,1)S(1)} %get-tuple-element.170.refs_1_.refs_12_), channel_id=1, source_target_pairs={{0,24},{8,16},{16,8},{24,0},{1,25},{9,17},{17,9},{25,1},{2,26},{10... | collective-permute-start | bytes 933896 | tf_op jit(solution)/shard_map/ppermute | solution.py:61
  77.8 15.7 %collective-permute-start.8 = (bf16[152,1024]{1,0:T(8,128)(2,1)S(1)}, bf16[152,1024]{1,0:T(8,128)(2,1)S(1)}, u32[]{:S(2)}, u32[]{:S(2)}) collective-permute-start(bf16[152,1024]{1,0:T(8,128)(2,1)S(1)} %get-tuple-element.151), channel_id=1, source_target_pairs={{0,16},{8,24},{16,0},{24,8},{1,17},{9,25},{17,1},{25,9},{2,18},{10... | collective-permute-start | bytes 933896 | tf_op jit(solution)/shard_map/ppermute | solution.py:61
  96.2 13.6 %collective-permute-start.15 = (bf16[152,1024]{1,0:T(8,128)(2,1)S(1)}, bf16[152,1024]{1,0:T(8,128)(2,1)S(1)}, u32[]{:S(2)}, u32[]{:S(2)}) collective-permute-start(bf16[152,1024]{1,0:T(8,128)(2,1)S(1)} %get-tuple-element.159.refs_0_), channel_id=1, source_target_pairs={{0,16},{8,24},{16,0},{24,8},{1,17},{9,25},{17,1},{25,9},{2,18},{10... | collective-permute-start | bytes 933896 | tf_op jit(solution)/shard_map/ppermute | solution.py:61
  96.8 13.7 %collective-permute-start.14 = (bf16[152,1024]{1,0:T(8,128)(2,1)S(1)}, bf16[152,1024]{1,0:T(8,128)(2,1)S(1)}, u32[]{:S(2)}, u32[]{:S(2)}) collective-permute-start(bf16[152,1024]{1,0:T(8,128)(2,1)S(1)} %get-tuple-element.159.refs_0_), channel_id=1, source_target_pairs={{0,24},{8,16},{16,8},{24,0},{1,25},{9,17},{17,9},{25,1},{2,26},{10... | collective-permute-start | bytes 933896 | tf_op jit(solution)/shard_map/ppermute | solution.py:61
  122.5 16.0 %collective-permute-start.18 = (bf16[152,1024]{1,0:T(8,128)(2,1)S(1)}, bf16[152,1024]{1,0:T(8,128)(2,1)S(1)}, u32[]{:S(2)}, u32[]{:S(2)}) collective-permute-start(bf16[152,1024]{1,0:T(8,128)(2,1)S(1)} %mlp_down.5.refs_2_), channel_id=1, source_target_pairs={{0,16},{8,24},{16,0},{24,8},{1,17},{9,25},{17,1},{25,9},{2,18},{10... | collective-permute-start | bytes 933896 | tf_op jit(solution)/shard_map/ppermute | solution.py:61
  123.8 14.6 %collective-permute-start.19 = (bf16[152,1024]{1,0:T(8,128)(2,1)S(1)}, bf16[152,1024]{1,0:T(8,128)(2,1)S(1)}, u32[]{:S(2)}, u32[]{:S(2)}) collective-permute-start(bf16[152,1024]{1,0:T(8,128)(2,1)S(1)} %mlp_down.6.refs_2_), channel_id=1, source_target_pairs={{0,24},{8,16},{16,8},{24,0},{1,25},{9,17},{17,9},{25,1},{2,26},{10... | collective-permute-start | bytes 933896 | tf_op jit(solution)/shard_map/ppermute | solution.py:61
  139.3 13.3 %collective-permute-start.22 = (bf16[152,1024]{1,0:T(8,128)(2,1)S(1)}, bf16[152,1024]{1,0:T(8,128)(2,1)S(1)}, u32[]{:S(2)}, u32[]{:S(2)}) collective-permute-start(bf16[152,1024]{1,0:T(8,128)(2,1)S(1)} %get-tuple-element.161.refs_1_.refs_0_), channel_id=1, source_target_pairs={{0,16},{8,24},{16,0},{24,8},{1,17},{9,25},{17,1},{25,9},{2,18},{10... | collective-permute-start | bytes 933896 | tf_op jit(solution)/shard_map/ppermute | solution.py:61
  140.6 15.9 %collective-permute-start.24 = (bf16[152,1024]{1,0:T(8,128)(2,1)S(1)}, bf16[152,1024]{1,0:T(8,128)(2,1)S(1)}, u32[]{:S(2)}, u32[]{:S(2)}) collective-permute-start(bf16[152,1024]{1,0:T(8,128)(2,1)S(1)} %get-tuple-element.161.refs_1_.refs_0_), channel_id=1, source_target_pairs={{0,24},{8,16},{16,8},{24,0},{1,25},{9,17},{17,9},{25,1},{2,26},{10... | collective-permute-start | bytes 933896 | tf_op jit(solution)/shard_map/ppermute | solution.py:61
  154.8 14.0 %collective-permute-start.23 = (bf16[152,1024]{1,0:T(8,128)(2,1)S(1)}, bf16[152,1024]{1,0:T(8,128)(2,1)S(1)}, u32[]{:S(2)}, u32[]{:S(2)}) collective-permute-start(bf16[152,1024]{1,0:T(8,128)(2,1)S(1)} %get-tuple-element.166), channel_id=1, source_target_pairs={{0,16},{8,24},{16,0},{24,8},{1,17},{9,25},{17,1},{25,9},{2,18},{10... | collective-permute-start | bytes 933896 | tf_op jit(solution)/shard_map/ppermute | solution.py:61
  171.9 14.1 %collective-permute-start.28 = (bf16[152,1024]{1,0:T(8,128)(2,1)}, bf16[152,1024]{1,0:T(8,128)(2,1)}, u32[]{:S(2)}, u32[]{:S(2)}) collective-permute-start(bf16[152,1024]{1,0:T(8,128)(2,1)} %get-tuple-element.169.refs_0_), channel_id=1, source_target_pairs={{0,16},{8,24},{16,0},{24,8},{1,17},{9,25},{17,1},{25,9},{2,18},{10... | collective-permute-start | bytes 933896 | tf_op jit(solution)/shard_map/ppermute | solution.py:61
  173.7 17.9 %collective-permute-start.30 = (bf16[152,1024]{1,0:T(8,128)(2,1)}, bf16[152,1024]{1,0:T(8,128)(2,1)}, u32[]{:S(2)}, u32[]{:S(2)}) collective-permute-start(bf16[152,1024]{1,0:T(8,128)(2,1)} %get-tuple-element.169.refs_0_), channel_id=1, source_target_pairs={{0,24},{8,16},{16,8},{24,0},{1,25},{9,17},{17,9},{25,1},{2,26},{10... | collective-permute-start | bytes 933896 | tf_op jit(solution)/shard_map/ppermute | solution.py:61
  184.8 19.9 %collective-permute-start.27 = (bf16[152,1024]{1,0:T(8,128)(2,1)}, bf16[152,1024]{1,0:T(8,128)(2,1)}, u32[]{:S(2)}, u32[]{:S(2)}) collective-permute-start(bf16[152,1024]{1,0:T(8,128)(2,1)} %get-tuple-element.174), channel_id=1, source_target_pairs={{0,8},{8,0},{16,24},{24,16},{1,9},{9,1},{17,25},{25,17},{2,10},{10... | collective-permute-start | bytes 933896 | tf_op jit(solution)/shard_map/ppermute | solution.py:61
  189.8 14.9 %collective-permute-start.29 = (bf16[152,1024]{1,0:T(8,128)(2,1)}, bf16[152,1024]{1,0:T(8,128)(2,1)}, u32[]{:S(2)}, u32[]{:S(2)}) collective-permute-start(bf16[152,1024]{1,0:T(8,128)(2,1)} %get-tuple-element.177), channel_id=1, source_target_pairs={{0,16},{8,24},{16,0},{24,8},{1,17},{9,25},{17,1},{25,9},{2,18},{10... | collective-permute-start | bytes 933896 | tf_op jit(solution)/shard_map/ppermute | solution.py:61
  204.7 120.5 %reduce-scatter.9.cloned.1.call-start = ((), (), s32[]{:S(2)}) async-start(), calls=%async_computation.6 | async-start | bytes 2359296 | tf_op jit(solution)/shard_map/reduce_scatter | solution.py:897
  211.7 12.9 %collective-permute-start.34 = (bf16[152,1024]{1,0:T(8,128)(2,1)S(1)}, bf16[152,1024]{1,0:T(8,128)(2,1)S(1)}, u32[]{:S(2)}, u32[]{:S(2)}) collective-permute-start(bf16[152,1024]{1,0:T(8,128)(2,1)S(1)} %get-tuple-element.192.refs_1_.refs_12_), channel_id=1, source_target_pairs={{0,16},{8,24},{16,0},{24,8},{1,17},{9,25},{17,1},{25,9},{2,18},{10... | collective-permute-start | bytes 933896 | tf_op jit(solution)/shard_map/ppermute | solution.py:61
  213.5 16.5 %collective-permute-start.36 = (bf16[152,1024]{1,0:T(8,128)(2,1)S(1)}, bf16[152,1024]{1,0:T(8,128)(2,1)S(1)}, u32[]{:S(2)}, u32[]{:S(2)}) collective-permute-start(bf16[152,1024]{1,0:T(8,128)(2,1)S(1)} %get-tuple-element.192.refs_1_.refs_12_), channel_id=1, source_target_pairs={{0,24},{8,16},{16,8},{24,0},{1,25},{9,17},{17,9},{25,1},{2,26},{10... | collective-permute-start | bytes 933896 | tf_op jit(solution)/shard_map/ppermute | solution.py:61
  223.5 14.2 %collective-permute-start.33 = (bf16[152,1024]{1,0:T(8,128)(2,1)}, bf16[152,1024]{1,0:T(8,128)(2,1)}, u32[]{:S(2)}, u32[]{:S(2)}) collective-permute-start(bf16[152,1024]{1,0:T(8,128)(2,1)} %get-tuple-element.195), channel_id=1, source_target_pairs={{0,8},{8,0},{16,24},{24,16},{1,9},{9,1},{17,25},{25,17},{2,10},{10... | collective-permute-start | bytes 933896 | tf_op jit(solution)/shard_map/ppermute | solution.py:61
  244.7 120.9 %reduce-scatter.11.cloned.1.call-start = ((), (), s32[]{:S(2)}) async-start(), calls=%async_computation.7 | async-start | bytes 4718592 | tf_op jit(solution)/shard_map/reduce_scatter | solution.py:897
  245.0 17.0 %collective-permute-start.39 = (bf16[152,1024]{1,0:T(8,128)(2,1)}, bf16[152,1024]{1,0:T(8,128)(2,1)S(1)}, u32[]{:S(2)}, u32[]{:S(2)}) collective-permute-start(bf16[152,1024]{1,0:T(8,128)(2,1)} %copy-done.116), channel_id=1, source_target_pairs={{0,16},{8,24},{16,0},{24,8},{1,17},{9,25},{17,1},{25,9},{2,18},{10... | collective-permute-start | bytes 933896 | tf_op jit(solution)/shard_map/ppermute | solution.py:61
  245.1 16.9 %collective-permute-start.40 = (bf16[152,1024]{1,0:T(8,128)(2,1)}, bf16[152,1024]{1,0:T(8,128)(2,1)S(1)}, u32[]{:S(2)}, u32[]{:S(2)}) collective-permute-start(bf16[152,1024]{1,0:T(8,128)(2,1)} %copy-done.117), channel_id=1, source_target_pairs={{0,24},{8,16},{16,8},{24,0},{1,25},{9,17},{17,9},{25,1},{2,26},{10... | collective-permute-start | bytes 933896 | tf_op jit(solution)/shard_map/ppermute | solution.py:61
  254.2 13.9 %collective-permute-start.41 = (bf16[152,1024]{1,0:T(8,128)(2,1)S(1)}, bf16[152,1024]{1,0:T(8,128)(2,1)S(1)}, u32[]{:S(2)}, u32[]{:S(2)}) collective-permute-start(bf16[152,1024]{1,0:T(8,128)(2,1)S(1)} %get-tuple-element.207.refs_0_.refs_12_), channel_id=1, source_target_pairs={{0,8},{8,0},{16,24},{24,16},{1,9},{9,1},{17,25},{25,17},{2,10},{10... | collective-permute-start | bytes 933896 | tf_op jit(solution)/shard_map/ppermute | solution.py:61
  254.3 16.3 %collective-permute-start.43 = (bf16[152,1024]{1,0:T(8,128)(2,1)S(1)}, bf16[152,1024]{1,0:T(8,128)(2,1)S(1)}, u32[]{:S(2)}, u32[]{:S(2)}) collective-permute-start(bf16[152,1024]{1,0:T(8,128)(2,1)S(1)} %get-tuple-element.207.refs_0_.refs_12_), channel_id=1, source_target_pairs={{0,16},{8,24},{16,0},{24,8},{1,17},{9,25},{17,1},{25,9},{2,18},{10... | collective-permute-start | bytes 933896 | tf_op jit(solution)/shard_map/ppermute | solution.py:61
  255.5 18.5 %collective-permute-start.45 = (bf16[152,1024]{1,0:T(8,128)(2,1)S(1)}, bf16[152,1024]{1,0:T(8,128)(2,1)S(1)}, u32[]{:S(2)}, u32[]{:S(2)}) collective-permute-start(bf16[152,1024]{1,0:T(8,128)(2,1)S(1)} %get-tuple-element.207.refs_0_.refs_12_), channel_id=1, source_target_pairs={{0,24},{8,16},{16,8},{24,0},{1,25},{9,17},{17,9},{25,1},{2,26},{10... | collective-permute-start | bytes 933896 | tf_op jit(solution)/shard_map/ppermute | solution.py:61
  270.4 14.6 %collective-permute-start.42 = (bf16[152,1024]{1,0:T(8,128)(2,1)}, bf16[152,1024]{1,0:T(8,128)(2,1)}, u32[]{:S(2)}, u32[]{:S(2)}) collective-permute-start(bf16[152,1024]{1,0:T(8,128)(2,1)} %get-tuple-element.213), channel_id=1, source_target_pairs={{0,8},{8,0},{16,24},{24,16},{1,9},{9,1},{17,25},{25,17},{2,10},{10... | collective-permute-start | bytes 933896 | tf_op jit(solution)/shard_map/ppermute | solution.py:61
  272.8 12.2 %collective-permute-start.44 = (bf16[152,1024]{1,0:T(8,128)(2,1)}, bf16[152,1024]{1,0:T(8,128)(2,1)}, u32[]{:S(2)}, u32[]{:S(2)}) collective-permute-start(bf16[152,1024]{1,0:T(8,128)(2,1)} %get-tuple-element.215), channel_id=1, source_target_pairs={{0,16},{8,24},{16,0},{24,8},{1,17},{9,25},{17,1},{25,9},{2,18},{10... | collective-permute-start | bytes 933896 | tf_op jit(solution)/shard_map/ppermute | solution.py:61
  285.0 116.0 %reduce-scatter.7.cloned.1.call-start = ((), (), s32[]{:S(2)}) async-start(), calls=%async_computation.5 | async-start | bytes 2359296 | tf_op jit(solution)/shard_map/reduce_scatter | solution.py:897
  290.9 12.8 %collective-permute-start.49 = (bf16[152,1024]{1,0:T(8,128)(2,1)S(1)}, bf16[152,1024]{1,0:T(8,128)(2,1)S(1)}, u32[]{:S(2)}, u32[]{:S(2)}) collective-permute-start(bf16[152,1024]{1,0:T(8,128)(2,1)S(1)} %get-tuple-element.228.refs_1_.refs_12_), channel_id=1, source_target_pairs={{0,16},{8,24},{16,0},{24,8},{1,17},{9,25},{17,1},{25,9},{2,18},{10... | collective-permute-start | bytes 933896 | tf_op jit(solution)/shard_map/ppermute | solution.py:61
  292.5 16.2 %collective-permute-start.51 = (bf16[152,1024]{1,0:T(8,128)(2,1)S(1)}, bf16[152,1024]{1,0:T(8,128)(2,1)S(1)}, u32[]{:S(2)}, u32[]{:S(2)}) collective-permute-start(bf16[152,1024]{1,0:T(8,128)(2,1)S(1)} %get-tuple-element.228.refs_1_.refs_12_), channel_id=1, source_target_pairs={{0,24},{8,16},{16,8},{24,0},{1,25},{9,17},{17,9},{25,1},{2,26},{10... | collective-permute-start | bytes 933896 | tf_op jit(solution)/shard_map/ppermute | solution.py:61
  303.4 15.3 %collective-permute-start.48 = (bf16[152,1024]{1,0:T(8,128)(2,1)}, bf16[152,1024]{1,0:T(8,128)(2,1)}, u32[]{:S(2)}, u32[]{:S(2)}) collective-permute-start(bf16[152,1024]{1,0:T(8,128)(2,1)} %get-tuple-element.231), channel_id=1, source_target_pairs={{0,8},{8,0},{16,24},{24,16},{1,9},{9,1},{17,25},{25,17},{2,10},{10... | collective-permute-start | bytes 933896 | tf_op jit(solution)/shard_map/ppermute | solution.py:61
  307.0 11.8 %collective-permute-start.50 = (bf16[152,1024]{1,0:T(8,128)(2,1)}, bf16[152,1024]{1,0:T(8,128)(2,1)}, u32[]{:S(2)}, u32[]{:S(2)}) collective-permute-start(bf16[152,1024]{1,0:T(8,128)(2,1)} %get-tuple-element.233), channel_id=1, source_target_pairs={{0,16},{8,24},{16,0},{24,8},{1,17},{9,25},{17,1},{25,9},{2,18},{10... | collective-permute-start | bytes 933896 | tf_op jit(solution)/shard_map/ppermute | solution.py:61
  323.7 15.0 %collective-permute-start.53 = (bf16[256,1024]{1,0:T(8,128)(2,1)}, bf16[256,1024]{1,0:T(8,128)(2,1)}, u32[]{:S(2)}, u32[]{:S(2)}) collective-permute-start(bf16[256,1024]{1,0:T(8,128)(2,1)} %bitcast.134), channel_id=1, source_target_pairs={{0,8},{8,0},{16,24},{24,16},{1,9},{9,1},{17,25},{25,17},{2,10},{10... | collective-permute-start | bytes 1572872 | tf_op jit(solution)/shard_map/ppermute | solution.py:61
  324.0 15.9 %collective-permute-start.54 = (bf16[256,1024]{1,0:T(8,128)(2,1)}, bf16[256,1024]{1,0:T(8,128)(2,1)}, u32[]{:S(2)}, u32[]{:S(2)}) collective-permute-start(bf16[256,1024]{1,0:T(8,128)(2,1)} %bitcast.135), channel_id=1, source_target_pairs={{0,16},{8,24},{16,0},{24,8},{1,17},{9,25},{17,1},{25,9},{2,18},{10... | collective-permute-start | bytes 1572872 | tf_op jit(solution)/shard_map/ppermute | solution.py:61
  339.9 18.0 %collective-permute-start.55 = (bf16[128,1024]{1,0:T(8,128)(2,1)}, bf16[128,1024]{1,0:T(8,128)(2,1)}, u32[]{:S(2)}, u32[]{:S(2)}) collective-permute-start(bf16[128,1024]{1,0:T(8,128)(2,1)} %bitcast.140), channel_id=1, source_target_pairs={{0,8},{8,0},{16,24},{24,16},{1,9},{9,1},{17,25},{25,17},{2,10},{10... | collective-permute-start | bytes 786440 | tf_op jit(solution)/shard_map/ppermute | solution.py:61
  342.9 16.6 %collective-permute-start.56 = (bf16[128,1024]{1,0:T(8,128)(2,1)}, bf16[128,1024]{1,0:T(8,128)(2,1)}, u32[]{:S(2)}, u32[]{:S(2)}) collective-permute-start(bf16[128,1024]{1,0:T(8,128)(2,1)} %bitcast.141), channel_id=1, source_target_pairs={{0,16},{8,24},{16,0},{24,8},{1,17},{9,25},{17,1},{25,9},{2,18},{10... | collective-permute-start | bytes 786440 | tf_op jit(solution)/shard_map/ppermute | solution.py:61
  342.9 16.6 %collective-permute-start.57 = (bf16[128,1024]{1,0:T(8,128)(2,1)}, bf16[128,1024]{1,0:T(8,128)(2,1)}, u32[]{:S(2)}, u32[]{:S(2)}) collective-permute-start(bf16[128,1024]{1,0:T(8,128)(2,1)} %bitcast.142), channel_id=1, source_target_pairs={{0,24},{8,16},{16,8},{24,0},{1,25},{9,17},{17,9},{25,1},{2,26},{10... | collective-permute-start | bytes 786440 | tf_op jit(solution)/shard_map/ppermute | solution.py:61
  361.7 12.7 %collective-permute-start.58 = (bf16[2,128,256]{2,1,0:T(8,128)(2,1)}, bf16[2,128,256]{2,1,0:T(8,128)(2,1)}, u32[]{:S(2)}, u32[]{:S(2)}) collective-permute-start(bf16[2,128,256]{2,1,0:T(8,128)(2,1)} %pad_maximum_fusion.2), channel_id=1, source_target_pairs={{0,1},{1,0},{2,3},{3,2},{4,5},{5,4},{6,7},{7,6},{8,9},{9,8},{10,11... | collective-permute-start | bytes 393224 | tf_op jit(solution)/shard_map/ppermute | solution.py:757
  375.5 14.4 %collective-permute-start.59 = (bf16[256,1024]{1,0:T(8,128)(2,1)S(1)}, bf16[256,1024]{1,0:T(8,128)(2,1)S(1)}, u32[]{:S(2)}, u32[]{:S(2)}) collective-permute-start(bf16[256,1024]{1,0:T(8,128)(2,1)S(1)} %bitcast.137), channel_id=1, source_target_pairs={{0,8},{8,0},{16,24},{24,16},{1,9},{9,1},{17,25},{25,17},{2,10},{10... | collective-permute-start | bytes 1572872 | tf_op jit(solution)/shard_map/ppermute | solution.py:61
  376.1 15.8 %collective-permute-start.60 = (bf16[256,1024]{1,0:T(8,128)(2,1)S(1)}, bf16[256,1024]{1,0:T(8,128)(2,1)S(1)}, u32[]{:S(2)}, u32[]{:S(2)}) collective-permute-start(bf16[256,1024]{1,0:T(8,128)(2,1)S(1)} %bitcast.138), channel_id=1, source_target_pairs={{0,16},{8,24},{16,0},{24,8},{1,17},{9,25},{17,1},{25,9},{2,18},{10... | collective-permute-start | bytes 1572872 | tf_op jit(solution)/shard_map/ppermute | solution.py:61
  383.4 12.5 %collective-permute-start.71 = (bf16[145,128]{1,0:T(8,128)(2,1)S(1)}, bf16[145,128]{1,0:T(8,128)(2,1)S(1)}, u32[]{:S(2)}, u32[]{:S(2)}) collective-permute-start(bf16[145,128]{1,0:T(8,128)(2,1)S(1)} %add_convert_fusion), channel_id=1, source_target_pairs={{0,24},{8,16},{16,8},{24,0},{1,25},{9,17},{17,9},{25,1},{2,26},{10... | collective-permute-start | bytes 111368 | tf_op jit(solution)/shard_map/ppermute | solution.py:61
  (157 other events, 1105.8 us)
Sparse Core Ops, SparseCore 0:
  13.8 49.8 all-gather.6
  65.8 47.2 all-gather.8
  114.8 45.8 all-gather.10
  204.8 48.5 reduce-scatter.4
  256.1 33.9 reduce-scatter.8
  292.2 48.6 reduce-scatter.10
  343.2 34.8 reduce-scatter.6

commit v4 on v3

--- a/solution.py
+++ b/solution.py
@@ -422,8 +422,10 @@
     return jnp.concatenate([block[:, LANES // 2 :], block[:, : LANES // 2]], axis=1)
 
 
-def pack_attention(me, w_ref, gain_row, out_ref, packed_ref, top):
+def pack_attention(who_ref, w_ref, gain_row, keep, got, packed_ref, top):
+    me, core = who_ref[0], who_ref[1]
     side, second = me & 1, me >> 1
+    out = jnp.where(core == side, keep, got)
     diag = diagonal(gain_row).astype(BF16)
     low = lane_low(LANES)
 
@@ -439,7 +441,7 @@
         pair = jnp.where(low, head(2 * u), head(2 * u + 1))
         packed_ref[top : top + LANES, u * LANES : (u + 1) * LANES] = pair.astype(BF16)
     for c in range(4):
-        packed_ref[top + c * 32 : top + (c + 1) * 32, 768:1024] = out_ref[:, c * 256 : (c + 1) * 256]
+        packed_ref[top + c * 32 : top + (c + 1) * 32, 768:1024] = out[:, c * 256 : (c + 1) * 256]
 
 
 def pack_up(me, up_ref, gain_row, packed_ref, top):
@@ -455,19 +457,19 @@
     packed_ref[top : top + LANES, :] = down_ref[0, pl.ds(pl.multiple_of(me * LANES, LANES), LANES), :]
 
 
-def prepare_first(me_ref, w_ref, gain_a, out_ref, up_ref, gain_m, packed_ref):
-    pack_attention(me_ref[0], w_ref, gain_a[0], out_ref, packed_ref, 0)
-    pack_up(me_ref[0], up_ref, gain_m[0], packed_ref, LANES)
-
-
-def prepare_second(me_ref, w_ref, gain_a, out_ref, down_ref, packed_ref):
-    pack_attention(me_ref[0], w_ref, gain_a[0], out_ref, packed_ref, LANES)
-    pack_down(me_ref[0], down_ref, packed_ref, 0)
-
-
-def prepare_third(me_ref, up_ref, gain_m, down_ref, packed_ref):
-    pack_up(me_ref[0], up_ref, gain_m[0], packed_ref, 0)
-    pack_down(me_ref[0], down_ref, packed_ref, LANES)
+def prepare_first(who_ref, w_ref, gain_a, keep_ref, got_ref, up_ref, gain_m, packed_ref):
+    pack_attention(who_ref, w_ref, gain_a[0:1, :], keep_ref[0], got_ref[0], packed_ref, 0)
+    pack_up(who_ref[0], up_ref, gain_m[0:1, :], packed_ref, LANES)
+
+
+def prepare_second(who_ref, w_ref, gain_a, keep_ref, got_ref, down_ref, packed_ref):
+    pack_attention(who_ref, w_ref, gain_a[1:2, :], keep_ref[1], got_ref[1], packed_ref, LANES)
+    pack_down(who_ref[0], down_ref, packed_ref, 0)
+
+
+def prepare_third(who_ref, up_ref, gain_m, down_ref, packed_ref):
+    pack_up(who_ref[0], up_ref, gain_m[1:2, :], packed_ref, 0)
+    pack_down(who_ref[0], down_ref, packed_ref, LANES)
 
 
 def image_numbers(rows, flag, lens):
@@ -500,11 +502,18 @@
     xhat_ref[...] = normalize(hidden)[0].astype(BF16)
 
 
-def embed(z_ref, tokens_ref, mixing_ref, t0, t1, t2, t3, hidden_ref, xhat_ref, table):
-    z = z_ref[0]
+def join_table(z_ref, p0, p1, p2, p3, out_ref, table):
+    for k, piece in enumerate((p0, p1, p2, p3)):
+        table[:, pl.ds(pl.multiple_of((z_ref[0] ^ k) * 256, 256), 256)] = piece[...].astype(F32)
+    out_ref[...] = table[...].astype(BF16)
+
+
+def embed(who_ref, tokens_ref, mixing_ref, t0, t1, t2, t3, hidden_ref, xhat_ref, table):
+    size = t0.shape[0]
     for k, piece in enumerate((t0, t1, t2, t3)):
-        table[:, pl.ds(pl.multiple_of((z ^ k) * 256, 256), 256)] = piece[...].astype(F32)
-    hidden = tokens_ref[...].astype(F32) + dot(mixing_ref[...], table[...].astype(BF16))
+        table[pl.ds(pl.multiple_of((who_ref[0] ^ k) * size, 8), size), :] = piece[...].astype(F32)
+    rows = table[: mixing_ref.shape[1], :].astype(BF16)
+    hidden = tokens_ref[...].astype(F32) + dot(mixing_ref[...], rows)
     hidden_ref[...] = hidden
     write_norm(hidden, xhat_ref)
 
@@ -671,15 +680,39 @@
         out_ref[:, c * 32 : (c + 1) * 32, 768:1024] = total.astype(BF16).reshape(8, 32, 256)
 
 
-def finish_mlp(me_ref, g0, g1, g2, g3_up, g3_down, up_ref, gain_ref, *rest):
-    dup_ref, ddown_ref, dgain_ref = rest[-3:]
+def rows_of(j):
+    return pl.ds(pl.multiple_of(j * LANES, LANES), LANES)
+
+
+def last_norm(z_ref, g_ref, p0, r1, r2, r3, h_ref, mixing_ref, d_ref, t0, t1, t2, t3, term_ref):
+    d = g_ref[...] + norm_backward(added(p0, r1, r2, r3), *normalize(h_ref[...]))
+    d_ref[...] = d
+    high = d.astype(BF16)
+    low = (d - high.astype(F32)).astype(BF16)
+    term_ref[...] = dot_t(mixing_ref[...], high) + dot_t(mixing_ref[...], low)
+    for k, out_ref in enumerate((t0, t1, t2, t3)):
+        cols = pl.ds(pl.multiple_of((z_ref[0] ^ k) * 256, 256), 256)
+        out_ref[...] = term_ref[:, cols].astype(BF16)
+
+
+def table_halves(core_ref, t0, r1, r2, r3, keep_ref, give_ref):
+    total = added(t0, r1, r2, r3).astype(BF16)
+    first, second = total[:, :LANES], total[:, LANES:]
+    keep_ref[...] = jnp.where(core_ref[0] == 0, first, second)
+    give_ref[...] = jnp.where(core_ref[0] == 0, second, first)
+
+
+def finish_mlp(me_ref, *refs, merged):
+    g, up_ref, gain_ref, dup_ref, ddown_ref, dgain_ref = refs[:5], refs[5], refs[6], *refs[-3:]
     me = me_ref[0]
+    low = 192 if merged else LANES
     column = jnp.sum(diagonal(gain_ref[0]), axis=1, keepdims=True)
     total = jnp.zeros((LANES, LANES), F32)
-    for k, piece in enumerate((g0[LANES:, :], g1[LANES:, :], g2[LANES:, :], g3_down[...])):
+    downs = [piece[low : low + LANES, :] for piece in g[:3]] + [g[4][:LANES, :]]
+    for k, piece in enumerate(downs):
         rows = pl.ds(pl.multiple_of((me ^ k) * LANES, LANES), LANES)
         ddown_ref[0, rows, :] = piece.astype(F32)
-    ups = [g0[:LANES, :], g1[:LANES, :], g2[:LANES, :], g3_up[...]]
+    ups = [piece[:LANES, :] for piece in g[:4]]
     for i in range(4):
         got = jnp.where(
             me == i, ups[0], jnp.where(me == i ^ 1, ups[1], jnp.where(me == i ^ 2, ups[2], ups[3]))
@@ -692,19 +725,37 @@
     dgain_ref[0] = jnp.sum(total.T, axis=0, keepdims=True)
 
 
-def finish_attention(me_ref, g0, g1, g2, g3, w_ref, gain_ref, out_ref, *rest):
-    dqkv_ref, dout_ref, dgain_ref = rest[-3:]
-    me = me_ref[0]
+def attention_rows(refs):
+    if len(refs) == 4:
+        return [ref[...] for ref in refs]
+    rows = [jnp.concatenate([ref[128:192, :], ref[320:384, :]], axis=0) for ref in refs[:3]]
+    return rows + [jnp.concatenate([ref[128:192, :] for ref in refs[3:]], axis=0)]
+
+
+def by_owner(me, pieces, i):
+    g0, g1, g2, g3 = pieces
+    return jnp.where(me == i, g0, jnp.where(me == i ^ 1, g1, jnp.where(me == i ^ 2, g2, g3)))
+
+
+def split_out(who_ref, *refs):
+    keep_ref, give_ref = refs[-2:]
+    packed = [piece[:, 768:] for piece in attention_rows(refs[:-2])]
+    me, core = who_ref[0], who_ref[1]
+    for second in range(2):
+        even, odd = by_owner(me, packed, 2 * second), by_owner(me, packed, 2 * second + 1)
+        keep_ref[second] = jnp.where(core == 0, even, odd)
+        give_ref[second] = jnp.where(core == 0, odd, even)
+
+
+def finish_attention(who_ref, *refs, count):
+    g, (w_ref, gain_ref, keep_ref, got_ref) = refs[:count], refs[count : count + 4]
+    dqkv_ref, dout_ref, dgain_ref = refs[-3:]
+    me, core = who_ref[0], who_ref[1]
     column = jnp.sum(diagonal(gain_ref[0]), axis=1, keepdims=True)
     total = jnp.zeros((LANES, LANES), F32)
     low = lane_low(LANES)
-    owned = []
-    for i in range(4):
-        owned.append(
-            jnp.where(
-                me == i, g0[:, :768], jnp.where(me == i ^ 1, g1[:, :768], jnp.where(me == i ^ 2, g2[:, :768], g3[:, :768]))
-            ).astype(F32)
-        )
+    rows = [piece[:, :768] for piece in attention_rows(g)]
+    owned = [by_owner(me, rows, i).astype(F32) for i in range(4)]
     for t in range(12):
         u = t // 2
         for side in range(2):
@@ -719,11 +770,13 @@
             dqkv_ref[0, :, cols] = part * column
             total = total + part * w_ref[0, :, cols].astype(F32)
     dgain_ref[0] = jnp.sum(total.T, axis=0, keepdims=True)
-    for h in range(4):
-        for c in range(4):
-            dout_ref[0, h * 32 : (h + 1) * 32, c * 256 : (c + 1) * 256] = out_ref[
-                h, c * 32 : (c + 1) * 32, :
-            ].astype(F32)
+    for second in range(2):
+        keep, got = keep_ref[second], got_ref[second]
+        halves = (jnp.where(core == 0, keep, got), jnp.where(core == 0, got, keep))
+        for h, part in enumerate(halves):
+            for c in range(4):
+                top = (2 * second + h) * 32
+                dout_ref[0, top : top + 32, c * 256 : (c + 1) * 256] = part[c * 32 : (c + 1) * 32, :].astype(F32)
 
 
 def local_fast(
@@ -759,12 +812,13 @@
     def layer_of(array, depth):
         return pl.BlockSpec((1,) + array.shape[1:], lambda *_: (depth,) + (0,) * (array.ndim - 1))
 
-    pair_side, head_side = me & 1, me >> 1
-    view = w_out.reshape(layers, 2, 2, 32, width)
-    mine = jnp.where(head_side == 1, view[:, 1], view[:, 0])
-    keep = jnp.where(core == 1, mine[:, 1], mine[:, 0])
-    give = jnp.where(core == 1, mine[:, 0], mine[:, 1])
-    out_pieces = jnp.where(core == pair_side, keep, over_fsdp(give, 1))
+    who = jnp.stack([me, core]).astype(jnp.int32)
+    head_side = me >> 1
+
+    def out_rows(half):
+        return lax.dynamic_slice(w_out, (0, (head_side * 2 + half) * 32, 0), (layers, 32, width))
+
+    keep, got = out_rows(core), over_fsdp(out_rows(1 - core), 1)
     gains_a = gain_attn.reshape(layers, 1, LANES)
     gains_m = gain_mlp.reshape(layers, 1, LANES)
 
@@ -772,13 +826,15 @@
         return pl.BlockSpec((8, LANES, width), lambda *_: (0, top, 0))
 
     def fetch(body, args, specs, after=()):
-        (packed,) = call(body, [((2 * LANES, width), BF16)], [me1] + args, [scalars()] + specs, after=after)
+        (packed,) = call(
+            body, [((2 * LANES, width), BF16)], [who] + args, [scalars()] + specs, after=after, limit=60
+        )
         return lax.all_gather(packed, "fsdp", axis=0, tiled=False)
 
     first_w = fetch(
         prepare_first,
-        [w_qkv, gains_a, out_pieces[0], w_up, gains_m],
-        [layer_of(w_qkv, 0), layer_of(gains_a, 0), None, layer_of(w_up, 0), layer_of(gains_m, 0)],
+        [w_qkv, gain_attn, keep, got, w_up, gain_mlp],
+        [layer_of(w_qkv, 0), None, None, None, layer_of(w_up, 0), None],
     )
 
     flag = resolution[me]
@@ -794,11 +850,20 @@
     gradient = cotangent.astype(F32) * weight[:, None]
 
     normed = [(block, F32), (block, BF16)]
-    other = over_fsdp(pos_table, 1)
-    pair = jnp.concatenate(
-        [jnp.where(core == 0, pos_table, other), jnp.where(core == 0, other, pos_table)], axis=1
-    )
+    size = -(-len_high // 32) * 8
+    mine = lax.dynamic_slice(
+        jnp.pad(pos_table, ((0, 4 * size - len_high), (0, 0))), (me * size, 0), (size, LANES)
+    )
+    other = over_fsdp(mine, 1)
+    pair = jnp.concatenate([jnp.where(core == 0, mine, other), jnp.where(core == 0, other, mine)], axis=1)
     pieces = [pair] + [over_fsdp(pair, 2 * k) for k in range(1, 4)]
+    (mine,) = call(
+        join_table,
+        [((size, width), BF16)],
+        [deep1] + pieces,
+        [scalars()] + [None] * 4,
+        scratch=[VMEM((size, width), F32)],
+    )
     (mixing,) = call(
         functools.partial(make_mixing, lens=lens),
         [((rows, len_high), BF16)],
@@ -808,28 +873,31 @@
     hidden, xhat = call(
         embed,
         normed,
-        [deep1, tokens, mixing] + pieces,
+        [who, tokens, mixing] + square.spread(mine),
         [scalars()] + [None] * 6,
-        scratch=[VMEM((len_high, width), F32)],
-        flops=2 * rows * len_high * width,
-    )
-
+        scratch=[VMEM((4 * size, width), F32)],
+    )
     second_w = fetch(
         prepare_second,
-        [w_qkv, gains_a, out_pieces[1], w_down],
-        [layer_of(w_qkv, 1), layer_of(gains_a, 1), None, layer_of(w_down, 0)],
+        [w_qkv, gain_attn, keep, got, w_down],
+        [layer_of(w_qkv, 1), None, None, None, layer_of(w_down, 0)],
         [xhat],
     )
     third_w = fetch(
         prepare_third,
-        [w_up, gains_m, w_down],
-        [layer_of(w_up, 1), layer_of(gains_m, 1), layer_of(w_down, 1)],
+        [w_up, gain_mlp, w_down],
+        [layer_of(w_up, 1), None, layer_of(w_down, 1)],
         [xhat],
     )
     attn_w = [(first_w, part(0)), (second_w, part(1))]
 
     def tie(*values):
         return lax.optimization_barrier(values)
+
+    def tie_last(es, term):
+        near, term = tie(es[:3], term)
+        far, near, term = tie(es[3], near, term)
+        return near + [far], term
 
     def chain(kernel):
         done = []
@@ -893,6 +961,8 @@
         half = x.shape[0] // 2
         return [square.swap(x[:half], 2), square.swap(y[half:], 1)]
 
+    core1 = core.reshape(1).astype(jnp.int32)
+
     def home(term):
         return lax.psum_scatter(term, "fsdp", scatter_dimension=0, tiled=False)
 
@@ -910,7 +980,7 @@
                     [(block, BF16)] * 2,
                     [ds[k], acts[k], first_w, second_w],
                     [None, second_half, part(1), part(0)],
-                    after=after or late[1][1:],
+                    after=after or late[1][1:] + [homes_m[1]],
                 )
             )
             dpres, backs = ([g[t] for g in got] for t in range(2))
@@ -922,11 +992,12 @@
             list(ms) + list(dpres) + list(acts) + list(ds),
             [None] * 8 + [None if top else first_half] * 4 + [None] * 4,
         )
-        es, term = tie(es, term)
+        es, term = tie_last(es, term)
+        homes_m[depth] = home(term)
+        d_middle, low = call(add_norm_backward, normed, [gradient] + es + [middle], limit=60)
         if not top:
-            es, homes_m[depth + 1] = tie(es, homes_m[depth + 1])
-        homes_m[depth] = home(term)
-        d_middle, low = call(add_norm_backward, normed, [gradient] + es + [middle])
+            m, a = homes_m[1], homes_a[1]
+            merged = jnp.concatenate([m[:LANES], a[:64], m[LANES:], a[64:]], axis=0)
         ds = square.spread(low)
         got = chain(
             lambda k, after: call(
@@ -934,7 +1005,7 @@
                 [((rows, 768), BF16), (block, BF16)],
                 [flags[k], ds[k], kept[k], a_w],
                 [scalars(), None, None, a_part],
-                after=after,
+                after=after or ([] if top else [merged]),
             )
         )
         dprojs = [g[0] for g in got]
@@ -942,88 +1013,72 @@
         if top:
             outs = collect(output_parts)
         out_part = pl.BlockSpec((rows, 256), lambda *_: (0, 3))
-        (term,) = call(
-            grads_attention,
-            [((8, LANES, width), BF16)],
-            list(xs) + dprojs + list(kept) + list(ds),
-            [None] * 8 + [out_part] * 4 + [None] * 4,
-        )
-        es, term = tie(es, term)
-        homes_a[depth] = home(term)
+        operands = list(xs) + dprojs + list(kept) + list(ds)
+        specs = [None] * 8 + [out_part] * 4 + [None] * 4
         if top:
+            (term,) = call(grads_attention, [((8, LANES, width), BF16)], operands, specs)
+            es, term = tie_last(es, term)
+            homes_a[depth] = home(term)
             late = (middle, outs)
+            gradient, low = call(add_norm_backward, normed, [d_middle] + es + [before], limit=60)
         else:
-            x, y = square.swap(homes_m[1], 1), square.swap(homes_m[1], 2)
-            es, homes_a[1], x, y = tie(es, homes_a[1], x, y)
-            homes_m[1] = [homes_m[1], x, y] + far_halves(x, y)
-        gradient, low = call(add_norm_backward, normed, [d_middle] + es + [before])
-
-    gradient, low, homes_m[0] = tie(gradient, low, homes_m[0])
-
-    rest = (gradient - low.astype(F32)).astype(BF16)
-    table_term = (dot_t(mixing, low) + dot_t(mixing, rest)).astype(BF16).reshape(len_high, 4, 256)
-    table_term = table_term.transpose(1, 0, 2)
-    mine = lax.dynamic_index_in_dim(table_term, deep, 0, keepdims=False).astype(F32)
-    for k in range(1, 4):
-        sent = lax.dynamic_index_in_dim(table_term, deep ^ k, 0, keepdims=False)
-        mine = mine + over_fsdp(sent, 2 * k).astype(F32)
-    mine = mine.astype(BF16)
-    keep = jnp.where(core == 0, mine[:, :LANES], mine[:, LANES:])
-    give = jnp.where(core == 0, mine[:, LANES:], mine[:, :LANES])
+            near = [square.swap(merged, 1), square.swap(merged, 2)]
+            (term,) = call(grads_attention, [((8, LANES, width), BF16)], operands, specs, after=near)
+            es, term = tie_last(es, term)
+            homes_a[0] = home(term)
+            gradient, *tables = call(
+                last_norm,
+                [(block, F32)] + [((len_high, 256), BF16)] * 4,
+                [deep1, d_middle] + es + [before, mixing],
+                [scalars()] + [None] * 7,
+                scratch=[VMEM((len_high, width), F32)],
+            )
+
+    merged = [merged, *near] + far_halves(*near)
+
+    tables = [tables[0]] + [over_fsdp(tables[k], 2 * k) for k in range(1, 4)]
+    keep, give = call(table_halves, [((len_high, LANES), BF16)] * 2, [core1] + tables, [scalars()] + [None] * 4)
     d_table = square.total(keep.astype(F32) + over_fsdp(give, 1).astype(F32))
 
-    homes_a[1] = square.spread(homes_a[1])
+    (output,) = call(add_output, [(block, F32)], [late[0]] + late[1], after=tables[:1])
+    homes_m[0], _ = tie(homes_m[0], tables[0])
     x, y = square.swap(homes_m[0], 1), square.swap(homes_m[0], 2)
     homes_m[0] = [homes_m[0], x, y] + far_halves(x, y)
     big = [None] * 6
-    (output,) = call(add_output, [(block, F32)], [late[0]] + late[1])
-    for depth in reversed(range(layers)):
-        pieces = homes_m[depth]
-        prior = big[3:]
-        names = [(w_up.shape, F32), (w_down.shape, F32), (gains_m.shape, F32)]
-        args = [me1] + pieces + [w_up, gains_m]
-        specs = [scalars()] + [None] * 5 + [layer_of(w_up, depth), layer_of(gains_m, depth)]
+
+    def finish(body, depth, args, shapes, prior):
         extra = [] if prior[0] is None else prior
-        big[3:] = call(
-            finish_mlp,
-            names,
-            args + extra,
-            specs + [pl.BlockSpec(memory_space=pl.ANY)] * len(extra),
-            aliases={len(args) + t: t for t in range(len(extra))},
-            out_specs=[layer_of(jax.ShapeDtypeStruct(s, d), depth) for s, d in names],
-        )
-        if depth == 0:
-            homes_a[0], big, d_table, output = tie(homes_a[0], big, d_table, output)
-            homes_a[0] = square.spread(homes_a[0])
-        pieces = homes_a[depth]
-        packed = [piece[:, 768:1024] for piece in pieces]
-        odd_me = (me & 1) == 1
-        even = [jnp.where(odd_me, packed[1], packed[0]), jnp.where(odd_me, packed[3], packed[2])]
-        odd = [jnp.where(odd_me, packed[0], packed[1]), jnp.where(odd_me, packed[2], packed[3])]
-        keep = [jnp.where(core == 0, a, b) for a, b in zip(even, odd)]
-        give = jnp.stack([jnp.where(core == 0, b, a) for a, b in zip(even, odd)])
-        got = over_fsdp(give, 1)
-        high_me = head_side == 1
-        keep = [jnp.where(high_me, keep[1], keep[0]), jnp.where(high_me, keep[0], keep[1])]
-        got = [jnp.where(high_me, got[1], got[0]), jnp.where(high_me, got[0], got[1])]
-        halves = []
-        for h in range(2):
-            halves.append(jnp.where(core == 0, keep[h], got[h]))
-            halves.append(jnp.where(core == 0, got[h], keep[h]))
-        outs = jnp.stack(halves)
-        prior = big[:3]
-        names = [(w_qkv.shape, F32), (w_out.shape, F32), (gains_a.shape, F32)]
-        args = [me1] + pieces + [w_qkv, gains_a, outs]
-        specs = [scalars()] + [None] * 4 + [layer_of(w_qkv, depth), layer_of(gains_a, depth), None]
-        extra = [] if prior[0] is None else prior
-        big[:3] = call(
-            finish_attention,
-            names,
-            args + extra,
-            specs + [pl.BlockSpec(memory_space=pl.ANY)] * len(extra),
-            aliases={len(args) + t: t for t in range(len(extra))},
-            out_specs=[layer_of(jax.ShapeDtypeStruct(s, d), depth) for s, d in names],
-        )
+        specs = [layer_of(a, depth) if a is w_up or a is w_qkv or a is gains_a or a is gains_m else None for a in args]
+        return call(
+            body,
+            [(shape, F32) for shape in shapes],
+            [who] + args + extra,
+            [scalars()] + specs + [pl.BlockSpec(memory_space=pl.ANY)] * len(extra),
+            aliases={1 + len(args) + t: t for t in range(len(extra))},
+            out_specs=[layer_of(jax.ShapeDtypeStruct(shape, F32), depth) for shape in shapes],
+        )
+
+    def finish_m(depth, pieces):
+        shapes = [w_up.shape, w_down.shape, gains_m.shape]
+        body = functools.partial(finish_mlp, merged=depth > 0)
+        big[3:] = finish(body, depth, pieces + [w_up, gains_m], shapes, big[3:])
+
+    def finish_a(depth, pieces):
+        keep, give = call(
+            split_out, [((2, LANES, 256), BF16)] * 2, [who] + pieces, [scalars()] + [None] * len(pieces)
+        )
+        shapes = [w_qkv.shape, w_out.shape, gains_a.shape]
+        body = functools.partial(finish_attention, count=len(pieces))
+        args = pieces + [w_qkv, gains_a, keep, over_fsdp(give, 1)]
+        big[:3] = finish(body, depth, args, shapes, big[:3])
+
+    homes_a[0], homes_m[0], merged, d_table, output = tie(homes_a[0], homes_m[0], merged, d_table, output)
+    pieces = square.spread(homes_a[0])
+    finish_m(1, merged)
+    finish_a(1, merged)
+    finish_m(0, homes_m[0])
+    pieces, big = tie(pieces, big)
+    finish_a(0, pieces)
     return (
         output,
         gradient,

time: 431 us -> 416 us (0.965)
  local copies, waits for them, and re-layouts: 76.2 us -> 49.9 us
  Pallas kernels: 117 us -> 132 us
  waiting for transfers between devices: 113 us -> 122 us
  other arithmetic: 10 us -> 3 us
    unnamed x249 -> x232, local copies, waits for them, and re-layouts: 68.5 us -> 45.1 us
    pallas_call x53 -> x57, Pallas kernels: 117 us -> 132 us  [call(): pl.pallas_call(run, name=name, grid=(1,), in_specs=specs, out_specs=out_s...]
    ppermute x11, waiting for transfers between devices: 11.3 us -> 18 us  [over_fsdp(): return lax.ppermute(x, 'fsdp', [(j, j ^ k) for j in range(8)])]
    ppermute x65, starting transfers between devices: 78 us -> 71.5 us  [swap(): return lax.ppermute(block, 'dp', [(i, i ^ k) for i in range(self.count)])]
    another operation x12 -> x1, other arithmetic: 6.63 us -> 0.66 us  [local_fast(): who = jnp.stack([me, core]).astype(jnp.int32)]
  transfers between devices with their start and end apart: 83 -> 83, of which waited for: 27 -> 29; matrix products, arithmetic and copies ran while one was open for 4% -> 2% of each run, Pallas kernels for 27% -> 31%
where the time goes in v4:
time: 416 us; the launch traced here: 412 us
  Pallas kernels  132 us (32%)
  waiting for transfers between devices  122 us (29%)
  starting transfers between devices  87.5 us (21%)
  local copies, waits for them, and re-layouts  49.9 us (12%)
  between operations  17.7 us (4%)
    pallas_call x57, Pallas kernels, call(): pl.pallas_call(run, name=name, grid=(1,), in_specs=specs, out_specs=out_s...  132 us
    ppermute x65, waiting for transfers between devices, swap(): return lax.ppermute(block, 'dp', [(i, i ^ k) for i in range(self.count)])  90.9 us
    ppermute x65, starting transfers between devices, swap(): return lax.ppermute(block, 'dp', [(i, i ^ k) for i in range(self.count)])  71.5 us
    unnamed x232, local copies, waits for them, and re-layouts  45.1 us
    ppermute x11, waiting for transfers between devices, over_fsdp(): return lax.ppermute(x, 'fsdp', [(j, j ^ k) for j in range(8)])  18 us
    ppermute x11, starting transfers between devices, over_fsdp(): return lax.ppermute(x, 'fsdp', [(j, j ^ k) for j in range(8)])  14.8 us
    all_gather x3, waiting for transfers between devices, fetch(): return lax.all_gather(packed, 'fsdp', axis=0, tiled=False)  12.8 us
  transfers between devices with their start and end apart: 83, of which 29 were waited for; matrix products, arithmetic and copies ran while one was open for 2% of the time, Pallas kernels for 31%

profile of v4, /device:TPU:0, one launch (start us, length us, event | category | flops | bytes accessed | tf_op | source)
XLA Modules:
  0.0 411.8 jit_solution(7911348180843696299)
XLA Ops:
  11.0 2.8 prepare_first.1
  15.2 3.0 collective-permute-start.1
  22.9 3.5 collective-permute-done.3.refs_4_
  36.6 3.0 prepare_second.1
  39.7 2.7 prepare_third.1
  51.0 12.8 %all-gather.7.cloned.1.call-done = bf16[2048,1024]{1,0:T(8,128)(2,1)} async-done(((bf16[256,1024]{1,0:T(8,128)(2,1)}), bf16[2048,1024]{1,0:T(8,128)(2,1)}) %all-gather.7.cloned.1.call-update) | async-done | bytes 4194320 | tf_op jit(solution)/shard_map/all_gather | solution.py:832
  82.7 3.5 collective-permute-done.9.refs_2_
  86.3 6.0 %collective-permute-done.13.refs_4_ = bf16[152,1024]{1,0:T(8,128)(2,1)S(1)} collective-permute-done((bf16[152,1024]{1,0:T(8,128)(2,1)S(1)}, bf16[152,1024]{1,0:T(8,128)(2,1)S(1)}, u32[]{:S(2)}, u32[]{:S(2)}) %collective-permute-start.13) | collective-permute-done | bytes 311328 | tf_op jit(solution)/shard_map/ppermute | solution.py:61
  97.7 6.0 %collective-permute-done.19.refs_0_.refs_1_ = bf16[152,1024]{1,0:T(8,128)(2,1)S(1)} collective-permute-done((bf16[152,1024]{1,0:T(8,128)(2,1)S(1)}, bf16[152,1024]{1,0:T(8,128)(2,1)S(1)}, u32[]{:S(2)}, u32[]{:S(2)}) %collective-permute-start.19) | collective-permute-done | bytes 311328 | tf_op jit(solution)/shard_map/ppermute | solution.py:61
  104.5 5.6 %collective-permute-done.18.refs_0_.refs_2_ = bf16[152,1024]{1,0:T(8,128)(2,1)S(1)} collective-permute-done((bf16[152,1024]{1,0:T(8,128)(2,1)S(1)}, bf16[152,1024]{1,0:T(8,128)(2,1)S(1)}, u32[]{:S(2)}, u32[]{:S(2)}) %collective-permute-start.18) | collective-permute-done | bytes 311328 | tf_op jit(solution)/shard_map/ppermute | solution.py:61
  121.8 5.7 %collective-permute-done.20.refs_2_ = bf16[152,1024]{1,0:T(8,128)(2,1)S(1)} collective-permute-done((bf16[152,1024]{1,0:T(8,128)(2,1)S(1)}, bf16[152,1024]{1,0:T(8,128)(2,1)S(1)}, u32[]{:S(2)}, u32[]{:S(2)}) %collective-permute-start.20) | collective-permute-done | bytes 311328 | tf_op jit(solution)/shard_map/ppermute | solution.py:61
  127.5 7.3 %collective-permute-done.21.refs_3_ = bf16[152,1024]{1,0:T(8,128)(2,1)S(1)} collective-permute-done((bf16[152,1024]{1,0:T(8,128)(2,1)S(1)}, bf16[152,1024]{1,0:T(8,128)(2,1)S(1)}, u32[]{:S(2)}, u32[]{:S(2)}) %collective-permute-start.21) | collective-permute-done | bytes 311328 | tf_op jit(solution)/shard_map/ppermute | solution.py:61
  141.0 4.5 %collective-permute-done.23.refs_1_ = bf16[152,1024]{1,0:T(8,128)(2,1)S(1)} collective-permute-done((bf16[152,1024]{1,0:T(8,128)(2,1)S(1)}, bf16[152,1024]{1,0:T(8,128)(2,1)S(1)}, u32[]{:S(2)}, u32[]{:S(2)}) %collective-permute-start.23) | collective-permute-done | bytes 311328 | tf_op jit(solution)/shard_map/ppermute | solution.py:61
  145.5 2.8 attention_forward.13
  158.1 7.3 %collective-permute-done.26.refs_3_ = bf16[152,1024]{1,0:T(8,128)(2,1)S(1)} collective-permute-done((bf16[152,1024]{1,0:T(8,128)(2,1)S(1)}, bf16[152,1024]{1,0:T(8,128)(2,1)S(1)}, u32[]{:S(2)}, u32[]{:S(2)}) %collective-permute-start.26) | collective-permute-done | bytes 311328 | tf_op jit(solution)/shard_map/ppermute | solution.py:61
  174.0 3.4 mlp_both.4
  178.1 3.7 mlp_both.5
  183.0 3.6 mlp_both.6
  188.5 3.7 mlp_both.7
  193.4 5.8 %grads_mlp.2 = bf16[8,256,1024]{2,1,0:T(8,128)(2,1)S(1)} custom-call(bf16[152,1024]{1,0:T(8,128)(2,1)} %get-tuple-element.194.refs_0_, bf16[152,1024]{1,0:T(8,128)(2,1)} %collective-permute-done.31.refs_0_.refs_1_, bf16[152,1024]{1,0:T(8,128)(2,1)} %collective-permute-done.30.refs_0_.refs_2_, bf16[152,1024]{1,0:T(8,128)(2,1)} %collective-permute-done.29.refs_0_.refs_3_, ...), custom_call_target="tpu_custom_call" | custom-call | bytes 4194304 | tf_op jit(solution)/shard_map/grads_mlp/pallas_call | solution.py:397
  201.3 3.1 add_norm_backward.3
  211.1 2.8 attention_backward.8
  213.9 3.5 attention_backward.9
  218.6 3.5 attention_backward.10
  223.9 3.5 attention_backward.11
  231.7 7.3 %collective-permute-done.38.refs_4_ = bf16[152,1024]{1,0:T(8,128)(2,1)} collective-permute-done((bf16[152,1024]{1,0:T(8,128)(2,1)}, bf16[152,1024]{1,0:T(8,128)(2,1)}, u32[]{:S(2)}, u32[]{:S(2)}) %collective-permute-start.38) | collective-permute-done | bytes 311328 | tf_op jit(solution)/shard_map/ppermute | solution.py:61
  239.5 3.4 collective-permute-start.46
  242.9 3.1 add_norm_backward.4
  246.6 3.3 collective-permute-done.44.refs_4_.refs_2_
  250.6 5.6 %collective-permute-done.45.refs_5_.refs_3_ = bf16[152,1024]{1,0:T(8,128)(2,1)} collective-permute-done((bf16[152,1024]{1,0:T(8,128)(2,1)}, bf16[152,1024]{1,0:T(8,128)(2,1)}, u32[]{:S(2)}, u32[]{:S(2)}) %collective-permute-start.45) | collective-permute-done | bytes 311328 | tf_op jit(solution)/shard_map/ppermute | solution.py:61
  265.2 3.3 mlp_backward.5
  268.6 3.2 mlp_backward.6
  272.8 3.3 mlp_backward.7
  278.7 5.7 %grads_mlp.3 = bf16[8,256,1024]{2,1,0:T(8,128)(2,1)S(1)} custom-call(bf16[152,1024]{1,0:T(8,128)(2,1)S(1)} %copy-done.57, bf16[152,1024]{1,0:T(8,128)(2,1)S(1)} %copy-done.59, bf16[152,1024]{1,0:T(8,128)(2,1)S(1)} %copy-done.61, bf16[152,1024]{1,0:T(8,128)(2,1)S(1)} %copy-done.63, bf16[152,1024]{1,0:T(8,128)(2,1)S(1)} %get-tuple-element.245.refs_4_, ...), custom_call_target="tpu_custom_call" | custom-call | bytes 4194304 | tf_op jit(solution)/shard_map/grads_mlp/pallas_call | solution.py:397
  290.7 3.1 add_norm_backward.5
  300.5 2.9 attention_backward.12
  304.1 11.2 %collective-permute-done.52.refs_1_.refs_13_ = bf16[152,1024]{1,0:T(8,128)(2,1)S(1)} collective-permute-done((bf16[152,1024]{1,0:T(8,128)(2,1)}, bf16[152,1024]{1,0:T(8,128)(2,1)S(1)}, u32[]{:S(2)}, u32[]{:S(2)}) %collective-permute-start.52) | collective-permute-done | bytes 311328 | tf_op jit(solution)/shard_map/ppermute | solution.py:61
  315.2 3.5 attention_backward.13
  319.9 3.5 attention_backward.14
  324.9 3.5 attention_backward.15
  333.0 3.4 collective-permute-done.53.refs_5_
  338.6 2.6 last_norm.1
  342.7 7.7 %collective-permute-start.65 = (bf16[145,256]{1,0:T(8,128)(2,1)S(1)}, bf16[145,256]{1,0:T(8,128)(2,1)S(1)}, u32[]{:S(2)}, u32[]{:S(2)}) collective-permute-start(bf16[145,256]{1,0:T(8,128)(2,1)S(1)} %get-tuple-element.286), channel_id=1, source_target_pairs={{0,4},{1,5},{2,6},{3,7},{4,0},{5,1},{6,2},{7,3},{8,12},{9,13},{10,... | collective-permute-start | bytes 222728 | tf_op jit(solution)/shard_map/ppermute | solution.py:810
  350.3 8.3 %collective-permute-done.65.refs_3_ = bf16[145,256]{1,0:T(8,128)(2,1)S(1)} collective-permute-done((bf16[145,256]{1,0:T(8,128)(2,1)S(1)}, bf16[145,256]{1,0:T(8,128)(2,1)S(1)}, u32[]{:S(2)}, u32[]{:S(2)}) %collective-permute-start.65) | collective-permute-done | bytes 74272 | tf_op jit(solution)/shard_map/ppermute | solution.py:810
  368.2 6.7 %collective-permute-done.70 = bf16[145,128]{1,0:T(8,128)(2,1)S(1)} collective-permute-done((bf16[145,128]{1,0:T(8,128)(2,1)S(1)}, bf16[145,128]{1,0:T(8,128)(2,1)S(1)}, u32[]{:S(2)}, u32[]{:S(2)}) %collective-permute-start.70) | collective-permute-done | bytes 37152 | tf_op jit(solution)/shard_map/ppermute | solution.py:61
  379.8 2.7 collective-permute-done.60.refs_4_
  390.6 3.1 finish_mlp.2
  393.7 3.8 finish_mlp.3
  (434 shorter events, 177.0 us)
Async XLA Ops:
  7.2 56.6 %all-gather.7.cloned.1.call-start = ((), (), s32[]{:S(2)}) async-start(), calls=%async_computation.8 | async-start | bytes 4718592 | tf_op jit(solution)/shard_map/all_gather | solution.py:832
  13.9 98.4 %all-gather.9.cloned.1.call-start = ((), (), s32[]{:S(2)}) async-start(), calls=%async_computation.9 | async-start | bytes 4718592 | tf_op jit(solution)/shard_map/all_gather | solution.py:832
  39.6 131.2 %all-gather.11.cloned.1.call-start = ((), (), s32[]{:S(2)}) async-start(), calls=%async_computation.10 | async-start | bytes 4718592 | tf_op jit(solution)/shard_map/all_gather | solution.py:832
  42.4 213.9 %reduce-scatter.5.cloned.1.call-start = ((), (), s32[]{:S(2)}) async-start(), calls=%async_computation.4 | async-start | bytes 4718592 | tf_op jit(solution)/shard_map/reduce_scatter | solution.py:967
  45.4 23.0 %collective-permute-start.8 = (bf16[152,1024]{1,0:T(8,128)(2,1)S(1)}, bf16[152,1024]{1,0:T(8,128)(2,1)S(1)}, u32[]{:S(2)}, u32[]{:S(2)}) collective-permute-start(bf16[152,1024]{1,0:T(8,128)(2,1)S(1)} %copy-done.24), channel_id=1, source_target_pairs={{0,8},{8,0},{16,24},{24,16},{1,9},{9,1},{17,25},{25,17},{2,10},{10... | collective-permute-start | bytes 933896 | tf_op jit(solution)/shard_map/ppermute | solution.py:61
  45.9 27.1 %collective-permute-start.10 = (bf16[152,1024]{1,0:T(8,128)(2,1)S(1)}, bf16[152,1024]{1,0:T(8,128)(2,1)S(1)}, u32[]{:S(2)}, u32[]{:S(2)}) collective-permute-start(bf16[152,1024]{1,0:T(8,128)(2,1)S(1)} %copy-done.24), channel_id=1, source_target_pairs={{0,16},{8,24},{16,0},{24,8},{1,17},{9,25},{17,1},{25,9},{2,18},{10... | collective-permute-start | bytes 933896 | tf_op jit(solution)/shard_map/ppermute | solution.py:61
  46.5 29.4 %collective-permute-start.12 = (bf16[152,1024]{1,0:T(8,128)(2,1)S(1)}, bf16[152,1024]{1,0:T(8,128)(2,1)S(1)}, u32[]{:S(2)}, u32[]{:S(2)}) collective-permute-start(bf16[152,1024]{1,0:T(8,128)(2,1)S(1)} %copy-done.24), channel_id=1, source_target_pairs={{0,24},{8,16},{16,8},{24,0},{1,25},{9,17},{17,9},{25,1},{2,26},{10... | collective-permute-start | bytes 933896 | tf_op jit(solution)/shard_map/ppermute | solution.py:61
  49.9 29.7 %collective-permute-start.14 = (bf16[152,1024]{1,0:T(8,128)(2,1)S(1)}, bf16[152,1024]{1,0:T(8,128)(2,1)S(1)}, u32[]{:S(2)}, u32[]{:S(2)}) collective-permute-start(bf16[152,1024]{1,0:T(8,128)(2,1)S(1)} %get-tuple-element.198.refs_1_.refs_12_), channel_id=1, source_target_pairs={{0,8},{8,0},{16,24},{24,16},{1,9},{9,1},{17,25},{25,17},{2,10},{10... | collective-permute-start | bytes 933896 | tf_op jit(solution)/shard_map/ppermute | solution.py:61
  50.4 31.6 %collective-permute-start.15 = (bf16[152,1024]{1,0:T(8,128)(2,1)S(1)}, bf16[152,1024]{1,0:T(8,128)(2,1)S(1)}, u32[]{:S(2)}, u32[]{:S(2)}) collective-permute-start(bf16[152,1024]{1,0:T(8,128)(2,1)S(1)} %get-tuple-element.198.refs_1_.refs_12_), channel_id=1, source_target_pairs={{0,16},{8,24},{16,0},{24,8},{1,17},{9,25},{17,1},{25,9},{2,18},{10... | collective-permute-start | bytes 933896 | tf_op jit(solution)/shard_map/ppermute | solution.py:61
  68.4 13.6 %collective-permute-start.16 = (bf16[152,1024]{1,0:T(8,128)(2,1)S(1)}, bf16[152,1024]{1,0:T(8,128)(2,1)S(1)}, u32[]{:S(2)}, u32[]{:S(2)}) collective-permute-start(bf16[152,1024]{1,0:T(8,128)(2,1)S(1)} %get-tuple-element.198.refs_1_.refs_12_), channel_id=1, source_target_pairs={{0,24},{8,16},{16,8},{24,0},{1,25},{9,17},{17,9},{25,1},{2,26},{10... | collective-permute-start | bytes 933896 | tf_op jit(solution)/shard_map/ppermute | solution.py:61
  95.0 15.1 %collective-permute-start.18 = (bf16[152,1024]{1,0:T(8,128)(2,1)S(1)}, bf16[152,1024]{1,0:T(8,128)(2,1)S(1)}, u32[]{:S(2)}, u32[]{:S(2)}) collective-permute-start(bf16[152,1024]{1,0:T(8,128)(2,1)S(1)} %get-tuple-element.184.refs_0_), channel_id=1, source_target_pairs={{0,16},{8,24},{16,0},{24,8},{1,17},{9,25},{17,1},{25,9},{2,18},{10... | collective-permute-start | bytes 933896 | tf_op jit(solution)/shard_map/ppermute | solution.py:61
  96.3 14.5 %collective-permute-start.17 = (bf16[152,1024]{1,0:T(8,128)(2,1)S(1)}, bf16[152,1024]{1,0:T(8,128)(2,1)S(1)}, u32[]{:S(2)}, u32[]{:S(2)}) collective-permute-start(bf16[152,1024]{1,0:T(8,128)(2,1)S(1)} %get-tuple-element.184.refs_0_), channel_id=1, source_target_pairs={{0,24},{8,16},{16,8},{24,0},{1,25},{9,17},{17,9},{25,1},{2,26},{10... | collective-permute-start | bytes 933896 | tf_op jit(solution)/shard_map/ppermute | solution.py:61
  118.8 16.0 %collective-permute-start.21 = (bf16[152,1024]{1,0:T(8,128)(2,1)S(1)}, bf16[152,1024]{1,0:T(8,128)(2,1)S(1)}, u32[]{:S(2)}, u32[]{:S(2)}) collective-permute-start(bf16[152,1024]{1,0:T(8,128)(2,1)S(1)} %mlp_down.5.refs_2_), channel_id=1, source_target_pairs={{0,16},{8,24},{16,0},{24,8},{1,17},{9,25},{17,1},{25,9},{2,18},{10... | collective-permute-start | bytes 933896 | tf_op jit(solution)/shard_map/ppermute | solution.py:61
  120.4 14.4 %collective-permute-start.22 = (bf16[152,1024]{1,0:T(8,128)(2,1)S(1)}, bf16[152,1024]{1,0:T(8,128)(2,1)S(1)}, u32[]{:S(2)}, u32[]{:S(2)}) collective-permute-start(bf16[152,1024]{1,0:T(8,128)(2,1)S(1)} %mlp_down.6.refs_2_), channel_id=1, source_target_pairs={{0,24},{8,16},{16,8},{24,0},{1,25},{9,17},{17,9},{25,1},{2,26},{10... | collective-permute-start | bytes 933896 | tf_op jit(solution)/shard_map/ppermute | solution.py:61
  135.9 13.2 %collective-permute-start.25 = (bf16[152,1024]{1,0:T(8,128)(2,1)S(1)}, bf16[152,1024]{1,0:T(8,128)(2,1)S(1)}, u32[]{:S(2)}, u32[]{:S(2)}) collective-permute-start(bf16[152,1024]{1,0:T(8,128)(2,1)S(1)} %get-tuple-element.186.refs_1_.refs_0_), channel_id=1, source_target_pairs={{0,16},{8,24},{16,0},{24,8},{1,17},{9,25},{17,1},{25,9},{2,18},{10... | collective-permute-start | bytes 933896 | tf_op jit(solution)/shard_map/ppermute | solution.py:61
  137.2 15.9 %collective-permute-start.27 = (bf16[152,1024]{1,0:T(8,128)(2,1)S(1)}, bf16[152,1024]{1,0:T(8,128)(2,1)S(1)}, u32[]{:S(2)}, u32[]{:S(2)}) collective-permute-start(bf16[152,1024]{1,0:T(8,128)(2,1)S(1)} %get-tuple-element.186.refs_1_.refs_0_), channel_id=1, source_target_pairs={{0,24},{8,16},{16,8},{24,0},{1,25},{9,17},{17,9},{25,1},{2,26},{10... | collective-permute-start | bytes 933896 | tf_op jit(solution)/shard_map/ppermute | solution.py:61
  151.4 14.0 %collective-permute-start.26 = (bf16[152,1024]{1,0:T(8,128)(2,1)S(1)}, bf16[152,1024]{1,0:T(8,128)(2,1)S(1)}, u32[]{:S(2)}, u32[]{:S(2)}) collective-permute-start(bf16[152,1024]{1,0:T(8,128)(2,1)S(1)} %get-tuple-element.191), channel_id=1, source_target_pairs={{0,16},{8,24},{16,0},{24,8},{1,17},{9,25},{17,1},{25,9},{2,18},{10... | collective-permute-start | bytes 933896 | tf_op jit(solution)/shard_map/ppermute | solution.py:61
  168.5 14.5 %collective-permute-start.30 = (bf16[152,1024]{1,0:T(8,128)(2,1)}, bf16[152,1024]{1,0:T(8,128)(2,1)}, u32[]{:S(2)}, u32[]{:S(2)}) collective-permute-start(bf16[152,1024]{1,0:T(8,128)(2,1)} %get-tuple-element.194.refs_0_), channel_id=1, source_target_pairs={{0,16},{8,24},{16,0},{24,8},{1,17},{9,25},{17,1},{25,9},{2,18},{10... | collective-permute-start | bytes 933896 | tf_op jit(solution)/shard_map/ppermute | solution.py:61
  170.4 18.2 %collective-permute-start.29 = (bf16[152,1024]{1,0:T(8,128)(2,1)}, bf16[152,1024]{1,0:T(8,128)(2,1)}, u32[]{:S(2)}, u32[]{:S(2)}) collective-permute-start(bf16[152,1024]{1,0:T(8,128)(2,1)} %get-tuple-element.194.refs_0_), channel_id=1, source_target_pairs={{0,24},{8,16},{16,8},{24,0},{1,25},{9,17},{17,9},{25,1},{2,26},{10... | collective-permute-start | bytes 933896 | tf_op jit(solution)/shard_map/ppermute | solution.py:61
  181.8 19.4 %collective-permute-start.33 = (bf16[152,1024]{1,0:T(8,128)(2,1)}, bf16[152,1024]{1,0:T(8,128)(2,1)}, u32[]{:S(2)}, u32[]{:S(2)}) collective-permute-start(bf16[152,1024]{1,0:T(8,128)(2,1)} %get-tuple-element.204), channel_id=1, source_target_pairs={{0,8},{8,0},{16,24},{24,16},{1,9},{9,1},{17,25},{25,17},{2,10},{10... | collective-permute-start | bytes 933896 | tf_op jit(solution)/shard_map/ppermute | solution.py:61
  186.7 14.5 %collective-permute-start.34 = (bf16[152,1024]{1,0:T(8,128)(2,1)}, bf16[152,1024]{1,0:T(8,128)(2,1)}, u32[]{:S(2)}, u32[]{:S(2)}) collective-permute-start(bf16[152,1024]{1,0:T(8,128)(2,1)} %get-tuple-element.205), channel_id=1, source_target_pairs={{0,16},{8,24},{16,0},{24,8},{1,17},{9,25},{17,1},{25,9},{2,18},{10... | collective-permute-start | bytes 933896 | tf_op jit(solution)/shard_map/ppermute | solution.py:61
  201.2 85.7 %reduce-scatter.7.cloned.1.call-start = ((), (), s32[]{:S(2)}) async-start(), calls=%async_computation.5 | async-start | bytes 2359296 | tf_op jit(solution)/shard_map/reduce_scatter | solution.py:967
  207.5 16.4 %collective-permute-start.35 = (bf16[152,1024]{1,0:T(8,128)(2,1)}, bf16[152,1024]{1,0:T(8,128)(2,1)S(1)}, u32[]{:S(2)}, u32[]{:S(2)}) collective-permute-start(bf16[152,1024]{1,0:T(8,128)(2,1)} %get-tuple-element.221.refs_1_.refs_12_), channel_id=1, source_target_pairs={{0,24},{8,16},{16,8},{24,0},{1,25},{9,17},{17,9},{25,1},{2,26},{10... | collective-permute-start | bytes 933896 | tf_op jit(solution)/shard_map/ppermute | solution.py:61
  217.4 14.3 %collective-permute-start.39 = (bf16[152,1024]{1,0:T(8,128)(2,1)}, bf16[152,1024]{1,0:T(8,128)(2,1)}, u32[]{:S(2)}, u32[]{:S(2)}) collective-permute-start(bf16[152,1024]{1,0:T(8,128)(2,1)} %get-tuple-element.228), channel_id=1, source_target_pairs={{0,8},{8,0},{16,24},{24,16},{1,9},{9,1},{17,25},{25,17},{2,10},{10... | collective-permute-start | bytes 933896 | tf_op jit(solution)/shard_map/ppermute | solution.py:61
  239.1 102.1 %reduce-scatter.11.cloned.1.call-start = ((), (), s32[]{:S(2)}) async-start(), calls=%async_computation.7 | async-start | bytes 4718592 | tf_op jit(solution)/shard_map/reduce_scatter | solution.py:967
  239.4 16.9 %collective-permute-start.45 = (bf16[152,1024]{1,0:T(8,128)(2,1)}, bf16[152,1024]{1,0:T(8,128)(2,1)}, u32[]{:S(2)}, u32[]{:S(2)}) collective-permute-start(bf16[152,1024]{1,0:T(8,128)(2,1)} %copy-done.105), channel_id=1, source_target_pairs={{0,16},{8,24},{16,0},{24,8},{1,17},{9,25},{17,1},{25,9},{2,18},{10... | collective-permute-start | bytes 933896 | tf_op jit(solution)/shard_map/ppermute | solution.py:61
  239.5 16.8 %collective-permute-start.46 = (bf16[152,1024]{1,0:T(8,128)(2,1)}, bf16[152,1024]{1,0:T(8,128)(2,1)}, u32[]{:S(2)}, u32[]{:S(2)}) collective-permute-start(bf16[152,1024]{1,0:T(8,128)(2,1)} %copy-done.106), channel_id=1, source_target_pairs={{0,24},{8,16},{16,8},{24,0},{1,25},{9,17},{17,9},{25,1},{2,26},{10... | collective-permute-start | bytes 933896 | tf_op jit(solution)/shard_map/ppermute | solution.py:61
  246.0 19.2 %collective-permute-start.43 = (bf16[152,1024]{1,0:T(8,128)(2,1)}, bf16[152,1024]{1,0:T(8,128)(2,1)}, u32[]{:S(2)}, u32[]{:S(2)}) collective-permute-start(bf16[152,1024]{1,0:T(8,128)(2,1)} %get-tuple-element.240.refs_0_.refs_12_), channel_id=1, source_target_pairs={{0,8},{8,0},{16,24},{24,16},{1,9},{9,1},{17,25},{25,17},{2,10},{10... | collective-permute-start | bytes 933896 | tf_op jit(solution)/shard_map/ppermute | solution.py:61
  246.1 22.5 %collective-permute-start.42 = (bf16[152,1024]{1,0:T(8,128)(2,1)}, bf16[152,1024]{1,0:T(8,128)(2,1)}, u32[]{:S(2)}, u32[]{:S(2)}) collective-permute-start(bf16[152,1024]{1,0:T(8,128)(2,1)} %get-tuple-element.240.refs_0_.refs_12_), channel_id=1, source_target_pairs={{0,16},{8,24},{16,0},{24,8},{1,17},{9,25},{17,1},{25,9},{2,18},{10... | collective-permute-start | bytes 933896 | tf_op jit(solution)/shard_map/ppermute | solution.py:61
  250.6 22.2 %collective-permute-start.41 = (bf16[152,1024]{1,0:T(8,128)(2,1)}, bf16[152,1024]{1,0:T(8,128)(2,1)}, u32[]{:S(2)}, u32[]{:S(2)}) collective-permute-start(bf16[152,1024]{1,0:T(8,128)(2,1)} %get-tuple-element.240.refs_0_.refs_12_), channel_id=1, source_target_pairs={{0,24},{8,16},{16,8},{24,0},{1,25},{9,17},{17,9},{25,1},{2,26},{10... | collective-permute-start | bytes 933896 | tf_op jit(solution)/shard_map/ppermute | solution.py:61
  268.6 17.8 %collective-permute-start.48 = (bf16[152,1024]{1,0:T(8,128)(2,1)}, bf16[152,1024]{1,0:T(8,128)(2,1)}, u32[]{:S(2)}, u32[]{:S(2)}) collective-permute-start(bf16[152,1024]{1,0:T(8,128)(2,1)} %get-tuple-element.250), channel_id=1, source_target_pairs={{0,8},{8,0},{16,24},{24,16},{1,9},{9,1},{17,25},{25,17},{2,10},{10... | collective-permute-start | bytes 933896 | tf_op jit(solution)/shard_map/ppermute | solution.py:61
  271.8 14.6 %collective-permute-start.49 = (bf16[152,1024]{1,0:T(8,128)(2,1)}, bf16[152,1024]{1,0:T(8,128)(2,1)}, u32[]{:S(2)}, u32[]{:S(2)}) collective-permute-start(bf16[152,1024]{1,0:T(8,128)(2,1)} %get-tuple-element.251), channel_id=1, source_target_pairs={{0,16},{8,24},{16,0},{24,8},{1,17},{9,25},{17,1},{25,9},{2,18},{10... | collective-permute-start | bytes 933896 | tf_op jit(solution)/shard_map/ppermute | solution.py:61
  286.4 93.4 %reduce-scatter.9.cloned.1.call-start = ((), (), s32[]{:S(2)}) async-start(), calls=%async_computation.6 | async-start | bytes 2359296 | tf_op jit(solution)/shard_map/reduce_scatter | solution.py:967
  288.0 41.2 %collective-permute-start.56 = (bf16[384,1024]{1,0:T(8,128)(2,1)S(1)}, bf16[384,1024]{1,0:T(8,128)(2,1)S(1)}, u32[]{:S(2)}, u32[]{:S(2)}) collective-permute-start(bf16[384,1024]{1,0:T(8,128)(2,1)S(1)} %pad_maximum_fusion.refs_4_.refs_1_), channel_id=1, source_target_pairs={{0,8},{8,0},{16,24},{24,16},{1,9},{9,1},{17,25},{25,17},{2,10},{10... | collective-permute-start | bytes 2359304 | tf_op jit(solution)/shard_map/ppermute | solution.py:61
  289.3 40.0 %collective-permute-start.57 = (bf16[384,1024]{1,0:T(8,128)(2,1)S(1)}, bf16[384,1024]{1,0:T(8,128)(2,1)S(1)}, u32[]{:S(2)}, u32[]{:S(2)}) collective-permute-start(bf16[384,1024]{1,0:T(8,128)(2,1)S(1)} %pad_maximum_fusion.refs_4_.refs_1_), channel_id=1, source_target_pairs={{0,16},{8,24},{16,0},{24,8},{1,17},{9,25},{17,1},{25,9},{2,18},{10... | collective-permute-start | bytes 2359304 | tf_op jit(solution)/shard_map/ppermute | solution.py:61
  293.8 21.4 %collective-permute-start.52 = (bf16[152,1024]{1,0:T(8,128)(2,1)}, bf16[152,1024]{1,0:T(8,128)(2,1)S(1)}, u32[]{:S(2)}, u32[]{:S(2)}) collective-permute-start(bf16[152,1024]{1,0:T(8,128)(2,1)} %get-tuple-element.261.refs_1_.refs_12_), channel_id=1, source_target_pairs={{0,8},{8,0},{16,24},{24,16},{1,9},{9,1},{17,25},{25,17},{2,10},{10... | collective-permute-start | bytes 933896 | tf_op jit(solution)/shard_map/ppermute | solution.py:61
  294.4 25.4 %collective-permute-start.51 = (bf16[152,1024]{1,0:T(8,128)(2,1)}, bf16[152,1024]{1,0:T(8,128)(2,1)S(1)}, u32[]{:S(2)}, u32[]{:S(2)}) collective-permute-start(bf16[152,1024]{1,0:T(8,128)(2,1)} %get-tuple-element.261.refs_1_.refs_12_), channel_id=1, source_target_pairs={{0,16},{8,24},{16,0},{24,8},{1,17},{9,25},{17,1},{25,9},{2,18},{10... | collective-permute-start | bytes 933896 | tf_op jit(solution)/shard_map/ppermute | solution.py:61
  295.2 29.6 %collective-permute-start.50 = (bf16[152,1024]{1,0:T(8,128)(2,1)}, bf16[152,1024]{1,0:T(8,128)(2,1)S(1)}, u32[]{:S(2)}, u32[]{:S(2)}) collective-permute-start(bf16[152,1024]{1,0:T(8,128)(2,1)} %get-tuple-element.261.refs_1_.refs_12_), channel_id=1, source_target_pairs={{0,24},{8,16},{16,8},{24,0},{1,25},{9,17},{17,9},{25,1},{2,26},{10... | collective-permute-start | bytes 933896 | tf_op jit(solution)/shard_map/ppermute | solution.py:61
  318.7 14.3 %collective-permute-start.54 = (bf16[152,1024]{1,0:T(8,128)(2,1)}, bf16[152,1024]{1,0:T(8,128)(2,1)}, u32[]{:S(2)}, u32[]{:S(2)}) collective-permute-start(bf16[152,1024]{1,0:T(8,128)(2,1)} %get-tuple-element.269), channel_id=1, source_target_pairs={{0,8},{8,0},{16,24},{24,16},{1,9},{9,1},{17,25},{25,17},{2,10},{10... | collective-permute-start | bytes 933896 | tf_op jit(solution)/shard_map/ppermute | solution.py:61
  341.2 23.4 %collective-permute-start.58 = (bf16[256,1024]{1,0:T(8,128)(2,1)}, bf16[256,1024]{1,0:T(8,128)(2,1)S(1)}, u32[]{:S(2)}, u32[]{:S(2)}) collective-permute-start(bf16[256,1024]{1,0:T(8,128)(2,1)} %bitcast.68), channel_id=1, source_target_pairs={{0,8},{8,0},{16,24},{24,16},{1,9},{9,1},{17,25},{25,17},{2,10},{10... | collective-permute-start | bytes 1572872 | tf_op jit(solution)/shard_map/ppermute | solution.py:61
  341.9 22.7 %collective-permute-start.59 = (bf16[256,1024]{1,0:T(8,128)(2,1)}, bf16[256,1024]{1,0:T(8,128)(2,1)S(1)}, u32[]{:S(2)}, u32[]{:S(2)}) collective-permute-start(bf16[256,1024]{1,0:T(8,128)(2,1)} %bitcast.69), channel_id=1, source_target_pairs={{0,16},{8,24},{16,0},{24,8},{1,17},{9,25},{17,1},{25,9},{2,18},{10... | collective-permute-start | bytes 1572872 | tf_op jit(solution)/shard_map/ppermute | solution.py:61
  342.7 15.9 %collective-permute-start.65 = (bf16[145,256]{1,0:T(8,128)(2,1)S(1)}, bf16[145,256]{1,0:T(8,128)(2,1)S(1)}, u32[]{:S(2)}, u32[]{:S(2)}) collective-permute-start(bf16[145,256]{1,0:T(8,128)(2,1)S(1)} %get-tuple-element.286), channel_id=1, source_target_pairs={{0,4},{1,5},{2,6},{3,7},{4,0},{5,1},{6,2},{7,3},{8,12},{9,13},{10,... | collective-permute-start | bytes 222728 | tf_op jit(solution)/shard_map/ppermute | solution.py:810
  360.8 18.2 %collective-permute-start.62 = (bf16[192,1024]{1,0:T(8,128)(2,1)S(1)}, bf16[192,1024]{1,0:T(8,128)(2,1)S(1)}, u32[]{:S(2)}, u32[]{:S(2)}) collective-permute-start(bf16[192,1024]{1,0:T(8,128)(2,1)S(1)} %slice.54), channel_id=1, source_target_pairs={{0,16},{8,24},{16,0},{24,8},{1,17},{9,25},{17,1},{25,9},{2,18},{10... | collective-permute-start | bytes 1179656 | tf_op jit(solution)/shard_map/ppermute | solution.py:61
  360.9 18.1 %collective-permute-start.63 = (bf16[192,1024]{1,0:T(8,128)(2,1)S(1)}, bf16[192,1024]{1,0:T(8,128)(2,1)S(1)}, u32[]{:S(2)}, u32[]{:S(2)}) collective-permute-start(bf16[192,1024]{1,0:T(8,128)(2,1)S(1)} %slice.55), channel_id=1, source_target_pairs={{0,8},{8,0},{16,24},{24,16},{1,9},{9,1},{17,25},{25,17},{2,10},{10... | collective-permute-start | bytes 1179656 | tf_op jit(solution)/shard_map/ppermute | solution.py:61
  364.6 13.8 %collective-permute-start.68 = (bf16[145,128]{1,0:T(8,128)(2,1)S(1)}, bf16[145,128]{1,0:T(8,128)(2,1)S(1)}, u32[]{:S(2)}, u32[]{:S(2)}) collective-permute-start(bf16[145,128]{1,0:T(8,128)(2,1)S(1)} %add_convert_fusion), channel_id=1, source_target_pairs={{0,8},{8,0},{16,24},{24,16},{1,9},{9,1},{17,25},{25,17},{2,10},{10... | collective-permute-start | bytes 111368 | tf_op jit(solution)/shard_map/ppermute | solution.py:61
  382.9 17.2 %collective-permute-start.71 = (bf16[128,1024]{1,0:T(8,128)(2,1)}, bf16[128,1024]{1,0:T(8,128)(2,1)S(1)}, u32[]{:S(2)}, u32[]{:S(2)}) collective-permute-start(bf16[128,1024]{1,0:T(8,128)(2,1)} %bitcast.63), channel_id=1, source_target_pairs={{0,8},{8,0},{16,24},{24,16},{1,9},{9,1},{17,25},{25,17},{2,10},{10... | collective-permute-start | bytes 786440 | tf_op jit(solution)/shard_map/ppermute | solution.py:61
  383.7 16.3 %collective-permute-start.72 = (bf16[128,1024]{1,0:T(8,128)(2,1)}, bf16[128,1024]{1,0:T(8,128)(2,1)S(1)}, u32[]{:S(2)}, u32[]{:S(2)}) collective-permute-start(bf16[128,1024]{1,0:T(8,128)(2,1)} %bitcast.64), channel_id=1, source_target_pairs={{0,16},{8,24},{16,0},{24,8},{1,17},{9,25},{17,1},{25,9},{2,18},{10... | collective-permute-start | bytes 786440 | tf_op jit(solution)/shard_map/ppermute | solution.py:61
  384.9 15.1 %collective-permute-start.73 = (bf16[128,1024]{1,0:T(8,128)(2,1)}, bf16[128,1024]{1,0:T(8,128)(2,1)S(1)}, u32[]{:S(2)}, u32[]{:S(2)}) collective-permute-start(bf16[128,1024]{1,0:T(8,128)(2,1)} %bitcast.65), channel_id=1, source_target_pairs={{0,24},{8,16},{16,8},{24,0},{1,25},{9,17},{17,9},{25,1},{2,26},{10... | collective-permute-start | bytes 786440 | tf_op jit(solution)/shard_map/ppermute | solution.py:61
  (150 other events, 1085.4 us)
Sparse Core Ops, SparseCore 0:
  14.0 49.7 all-gather.6
  65.9 45.8 all-gather.8
  114.0 45.7 all-gather.10
  201.3 48.5 reduce-scatter.4
  252.7 33.7 reduce-scatter.6
  289.2 48.9 reduce-scatter.10
  341.0 38.1 reduce-scatter.8

commit v5 on v4

--- a/solution.py
+++ b/solution.py
@@ -528,6 +528,12 @@
     write_norm(middle, xhat_ref)
 
 
+def output_parts(a0, a1, a2, a3, down_ref, *outs):
+    down = down_ref[...].reshape(-1, down_ref.shape[2])
+    for act_ref, out_ref in zip((a0, a1, a2, a3), outs):
+        out_ref[...] = dot(act_ref[...], down).astype(BF16)
+
+
 def add_output(h_ref, p0, r1, r2, r3, out_ref):
     out_ref[...] = h_ref[...] + added(p0, r1, r2, r3)
 
@@ -628,9 +634,11 @@
         both_ref[1, :, cols] = slope.astype(BF16)
 
 
-def mlp_down(act_ref, down_ref, p_ref):
-    width = p_ref.shape[1]
-    p_ref[...] = dot(act_ref[0], down_ref[...].reshape(width, width)).astype(BF16)
+def mlp_down(*refs):
+    count = len(refs) // 2
+    down = refs[count][...].reshape(-1, refs[count].shape[2])
+    for act_ref, out_ref in zip(refs[:count], refs[count + 1 :]):
+        out_ref[...] = dot(act_ref[0], down).astype(BF16)
 
 
 def mlp_backward(d_ref, slope_ref, up_ref, down_ref, dpre_ref, p_ref):
@@ -642,7 +650,7 @@
     p_ref[...] = dot_nt(dpre_ref[...], up_ref[...].reshape(width, width)).astype(BF16)
 
 
-def mlp_both(x_ref, d_ref, up_ref, down_ref, act_ref, dpre_ref, p_ref, back_ref):
+def mlp_both(x_ref, d_ref, up_ref, down_ref, act_ref, dpre_ref, back_ref):
     width = x_ref.shape[1]
     for c in range(4):
         cols = slice(c * 256, (c + 1) * 256)
@@ -651,7 +659,6 @@
         d_act = dot_nt(d_ref[...], down_ref[2 * c : 2 * c + 2].reshape(256, width))
         dpre_ref[:, cols] = (d_act * slope).astype(BF16)
     back_ref[...] = dot_nt(dpre_ref[...], up_ref[...].reshape(width, width)).astype(BF16)
-    p_ref[...] = dot(act_ref[...], down_ref[...].reshape(width, width)).astype(BF16)
 
 
 def summed(left, right, rows, cols=slice(None)):
@@ -662,21 +669,44 @@
     return total
 
 
+def stack_rows(blocks, out_ref):
+    rows = blocks[0].shape[0]
+    tall = -(-rows // 32) * 32
+    for k, block in enumerate(blocks):
+        out_ref[k * tall + rows // 16 * 16 : (k + 1) * tall, :] = jnp.zeros(
+            (tall - rows // 16 * 16, out_ref.shape[1]), BF16
+        )
+        out_ref[k * tall : k * tall + rows, :] = block
+
+
 def grads_mlp(*refs):
-    x, dpre, act, d, out_ref = refs[:4], refs[4:8], refs[8:12], refs[12:16], refs[16]
-    act = [a.at[0] if len(a.shape) == 3 else a for a in act]
-    for half, (left, right) in enumerate(((x, dpre), (act, d))):
-        for j in range(8):
-            total = summed(left, right, slice(j * LANES, (j + 1) * LANES))
-            out_ref[j, half * LANES : (half + 1) * LANES, :] = total.astype(BF16)
+    x, dpre, act, d, out_ref, left, right = refs[:4], refs[4:8], refs[8:12], refs[12:16], *refs[16:]
+    acts = [a[0] if len(a.shape) == 3 else a[...] for a in act]
+    pairs = (([a[...] for a in x], dpre), (acts, d))
+    for half, (first, second) in enumerate(pairs):
+        stack_rows(first, left)
+        stack_rows([b[...] for b in second], right)
+        for t in range(4):
+            total = dot_t(left[:, t * 256 : (t + 1) * 256], right[...]).astype(BF16)
+            out_ref[2 * t : 2 * t + 2, half * LANES : (half + 1) * LANES, :] = total.reshape(2, LANES, -1)
+
+
+def stack_attention(refs, left, right, narrow):
+    x, dproj, kept, d = refs[:4], refs[4:8], refs[8:12], refs[12:16]
+    stack_rows([a[...] for a in x], left)
+    stack_rows([a[...] for a in dproj], right.at[:, :768])
+    stack_rows([a[...] for a in kept], narrow)
 
 
 def grads_attention(*refs):
-    x, dproj, kept, d, out_ref = refs[:4], refs[4:8], refs[8:12], refs[12:16], refs[16]
-    for j in range(8):
-        out_ref[j, :, :768] = summed(x, dproj, slice(j * LANES, (j + 1) * LANES)).astype(BF16)
+    out_ref, left, right, narrow = refs[16:]
+    stack_attention(refs, left, right, narrow)
+    for t in range(4):
+        total = dot_t(left[:, t * 256 : (t + 1) * 256], right[:, :768]).astype(BF16)
+        out_ref[2 * t : 2 * t + 2, :LANES, :768] = total.reshape(2, LANES, -1)
+    stack_rows([a[...] for a in refs[12:16]], right)
     for c in range(4):
-        total = summed(kept, d, slice(None), slice(c * 256, (c + 1) * 256))
+        total = dot_t(narrow[...], right[:, c * 256 : (c + 1) * 256])
         out_ref[:, c * 32 : (c + 1) * 32, 768:1024] = total.astype(BF16).reshape(8, 32, 256)
 
 
@@ -684,22 +714,52 @@
     return pl.ds(pl.multiple_of(j * LANES, LANES), LANES)
 
 
-def last_norm(z_ref, g_ref, p0, r1, r2, r3, h_ref, mixing_ref, d_ref, t0, t1, t2, t3, term_ref):
+def grads_attention_sides(core_ref, *refs):
+    theirs, mine, (left, right, narrow) = refs[16:20], refs[20], refs[21:]
+    core = core_ref[0]
+    stack_attention(refs, left, right, narrow)
+    for z in range(4):
+        theirs[z][:, :768] = dot_t(left[:, rows_of(z * 2 + 1 - core)], right[:, :768]).astype(BF16)
+    for z in range(4):
+        mine[z, :, :768] = dot_t(left[:, rows_of(z * 2 + core)], right[:, :768]).astype(BF16)
+    stack_rows([a[...] for a in refs[12:16]], right)
+    for c in range(4):
+        total = dot_t(narrow[...], right[:, c * 256 : (c + 1) * 256]).astype(BF16).reshape(8, 32, 256)
+        rows = slice(c * 32, (c + 1) * 32)
+        for z in range(4):
+            first, second = total[2 * z], total[2 * z + 1]
+            theirs[z][rows, 768:1024] = jnp.where(core == 0, second, first)
+            mine[z, rows, 768:1024] = jnp.where(core == 0, first, second)
+
+
+def add_pair(mine_ref, *refs):
+    for z in range(4):
+        refs[4][z] = (mine_ref[z].astype(F32) + refs[z][...].astype(F32)).astype(BF16)
+
+
+def last_norm(g_ref, p0, r1, r2, r3, h_ref, mixing_ref, term_ref, d_ref, out_ref, packed, sem):
     d = g_ref[...] + norm_backward(added(p0, r1, r2, r3), *normalize(h_ref[...]))
     d_ref[...] = d
     high = d.astype(BF16)
     low = (d - high.astype(F32)).astype(BF16)
-    term_ref[...] = dot_t(mixing_ref[...], high) + dot_t(mixing_ref[...], low)
-    for k, out_ref in enumerate((t0, t1, t2, t3)):
-        cols = pl.ds(pl.multiple_of((z_ref[0] ^ k) * 256, 256), 256)
-        out_ref[...] = term_ref[:, cols].astype(BF16)
-
-
-def table_halves(core_ref, t0, r1, r2, r3, keep_ref, give_ref):
-    total = added(t0, r1, r2, r3).astype(BF16)
-    first, second = total[:, :LANES], total[:, LANES:]
-    keep_ref[...] = jnp.where(core_ref[0] == 0, first, second)
-    give_ref[...] = jnp.where(core_ref[0] == 0, second, first)
+    table = dot_t(mixing_ref[...], high) + dot_t(mixing_ref[...], low)
+    packed[...] = jnp.zeros(packed.shape, BF16)
+    for j in range(8):
+        for c in range(-(-table.shape[0] // 32)):
+            size = min(32, table.shape[0] - 32 * c)
+            part = table[32 * c : 32 * c + size, j * LANES : (j + 1) * LANES]
+            packed[j, :size, c * LANES : (c + 1) * LANES] = part.astype(BF16)
+    copy = pltpu.make_async_copy(packed, out_ref.at[:, LANES : LANES + 32, :], sem.at[0])
+    copy.start()
+    copy.wait()
+
+
+def unpack_table(refs, out_ref):
+    g = [ref[LANES : LANES + 32, :].astype(F32) for ref in refs]
+    total = (g[0] + g[1]) + (g[2] + g[3])
+    for c in range(-(-out_ref.shape[0] // 32)):
+        size = min(32, out_ref.shape[0] - 32 * c)
+        out_ref[32 * c : 32 * c + size, :] = total[:size, c * LANES : (c + 1) * LANES]
 
 
 def finish_mlp(me_ref, *refs, merged):
@@ -727,7 +787,7 @@
 
 def attention_rows(refs):
     if len(refs) == 4:
-        return [ref[...] for ref in refs]
+        return [ref[:LANES, :] for ref in refs]
     rows = [jnp.concatenate([ref[128:192, :], ref[320:384, :]], axis=0) for ref in refs[:3]]
     return rows + [jnp.concatenate([ref[128:192, :] for ref in refs[3:]], axis=0)]
 
@@ -749,6 +809,9 @@
 
 def finish_attention(who_ref, *refs, count):
     g, (w_ref, gain_ref, keep_ref, got_ref) = refs[:count], refs[count : count + 4]
+    if count == 4:
+        unpack_table(g, refs[-1])
+        refs = refs[:-1]
     dqkv_ref, dout_ref, dgain_ref = refs[-3:]
     me, core = who_ref[0], who_ref[1]
     column = jnp.sum(diagonal(gain_ref[0]), axis=1, keepdims=True)
@@ -935,26 +998,28 @@
                 )
             )
             acts = [a[0] for a in acts]
-            parts = [None] * 4
-            last = acts
-            for k in (1, 2, 3, 0):
-                (parts[k],) = call(
-                    mlp_down, [(block, BF16)], [acts[k], second_w], [None, part(0)], after=last
-                )
-                last = [parts[k]]
+            first_half = pl.BlockSpec((1,) + block, lambda *_: (0, 0, 0))
+            parts = call(
+                mlp_down, [(block, BF16)] * 3, acts[1:] + [second_w], [first_half] * 3 + [part(0)], after=acts[:1]
+            )
+            (own,) = call(
+                mlp_down, [(block, BF16)], [acts[0], second_w], [first_half, part(0)], after=parts[:1]
+            )
+            parts = [own] + list(parts)
             saved.append((before, xs, kept, middle, ms, acts))
             hidden, xhat = call(add_norm, normed, [middle] + collect(parts))
         else:
             got = chain(
                 lambda k, after: call(
                     mlp_both,
-                    [(block, BF16)] * 4,
+                    [(block, BF16)] * 3,
                     [ms[k], d_top[k], third_w, third_w],
                     [None, None, part(0), part(1)],
                     after=after,
                 )
             )
-            acts, dpres, output_parts, backs = ([g[t] for g in got] for t in range(4))
+            acts, dpres, backs = ([g[t] for g in got] for t in range(3))
+            top_acts = acts
             saved.append((before, xs, kept, middle, ms, acts))
 
     def far_halves(x, y):
@@ -962,6 +1027,7 @@
         return [square.swap(x[:half], 2), square.swap(y[half:], 1)]
 
     core1 = core.reshape(1).astype(jnp.int32)
+    tall = 4 * (-(-rows // 32) * 32)
 
     def home(term):
         return lax.psum_scatter(term, "fsdp", scatter_dimension=0, tiled=False)
@@ -980,7 +1046,7 @@
                     [(block, BF16)] * 2,
                     [ds[k], acts[k], first_w, second_w],
                     [None, second_half, part(1), part(0)],
-                    after=after or late[1][1:] + [homes_m[1]],
+                    after=after or [homes_m[1]],
                 )
             )
             dpres, backs = ([g[t] for g in got] for t in range(2))
@@ -991,6 +1057,7 @@
             [((8, 2 * LANES, width), BF16)],
             list(ms) + list(dpres) + list(acts) + list(ds),
             [None] * 8 + [None if top else first_half] * 4 + [None] * 4,
+            scratch=[VMEM((tall, width), BF16)] * 2,
         )
         es, term = tie_last(es, term)
         homes_m[depth] = home(term)
@@ -1010,38 +1077,50 @@
         )
         dprojs = [g[0] for g in got]
         es = collect([g[1] for g in got])
-        if top:
-            outs = collect(output_parts)
         out_part = pl.BlockSpec((rows, 256), lambda *_: (0, 3))
+        stacks = [VMEM((tall, width), BF16)] * 2 + [VMEM((tall, 256), BF16)]
         operands = list(xs) + dprojs + list(kept) + list(ds)
         specs = [None] * 8 + [out_part] * 4 + [None] * 4
         if top:
-            (term,) = call(grads_attention, [((8, LANES, width), BF16)], operands, specs)
-            es, term = tie_last(es, term)
-            homes_a[depth] = home(term)
-            late = (middle, outs)
+            *theirs, mine = call(
+                grads_attention_sides,
+                [((LANES, width), BF16)] * 4 + [((4, LANES, width), BF16)],
+                [core1] + operands,
+                [scalars()] + specs,
+                scratch=stacks,
+            )
+            got = [over_fsdp(part, 1) for part in theirs]
+            es, mine = tie_last(es, mine)
+            (term,) = call(add_pair, [(mine.shape, BF16)], [mine] + got, after=[es[3]])
+            es, term = tie(es, term)
+            homes_a[depth] = lax.psum_scatter(
+                term, "fsdp", scatter_dimension=0, tiled=False, axis_index_groups=[[0, 2, 4, 6], [1, 3, 5, 7]]
+            )
+            last_middle = middle
             gradient, low = call(add_norm_backward, normed, [d_middle] + es + [before], limit=60)
         else:
             near = [square.swap(merged, 1), square.swap(merged, 2)]
-            (term,) = call(grads_attention, [((8, LANES, width), BF16)], operands, specs, after=near)
+            (term,) = call(grads_attention, [((8, LANES + 32, width), BF16)], operands, specs, after=near, scratch=stacks)
             es, term = tie_last(es, term)
+            anywhere = pl.BlockSpec(memory_space=pl.ANY)
+            gradient, term = call(
+                last_norm,
+                [(block, F32), (term.shape, BF16)],
+                [d_middle] + es + [before, mixing, term],
+                [None] * 7 + [anywhere],
+                out_specs=[whole(block), anywhere],
+                aliases={7: 1},
+                scratch=[VMEM((8, 32, width), BF16), pltpu.SemaphoreType.DMA((1,))],
+            )
             homes_a[0] = home(term)
-            gradient, *tables = call(
-                last_norm,
-                [(block, F32)] + [((len_high, 256), BF16)] * 4,
-                [deep1, d_middle] + es + [before, mixing],
-                [scalars()] + [None] * 7,
-                scratch=[VMEM((len_high, width), F32)],
-            )
 
     merged = [merged, *near] + far_halves(*near)
 
-    tables = [tables[0]] + [over_fsdp(tables[k], 2 * k) for k in range(1, 4)]
-    keep, give = call(table_halves, [((len_high, LANES), BF16)] * 2, [core1] + tables, [scalars()] + [None] * 4)
-    d_table = square.total(keep.astype(F32) + over_fsdp(give, 1).astype(F32))
-
-    (output,) = call(add_output, [(block, F32)], [late[0]] + late[1], after=tables[:1])
-    homes_m[0], _ = tie(homes_m[0], tables[0])
+    outs = call(
+        output_parts, [(block, BF16)] * 4, top_acts + [third_w], [None] * 4 + [part(1)], after=[gradient]
+    )
+    (output,) = call(add_output, [(block, F32)], [last_middle] + collect(outs))
+    homes_m[0], gradient = tie(homes_m[0], gradient)
     x, y = square.swap(homes_m[0], 1), square.swap(homes_m[0], 2)
     homes_m[0] = [homes_m[0], x, y] + far_halves(x, y)
     big = [None] * 6
@@ -1055,7 +1134,10 @@
             [who] + args + extra,
             [scalars()] + specs + [pl.BlockSpec(memory_space=pl.ANY)] * len(extra),
             aliases={1 + len(args) + t: t for t in range(len(extra))},
-            out_specs=[layer_of(jax.ShapeDtypeStruct(shape, F32), depth) for shape in shapes],
+            out_specs=[
+                layer_of(jax.ShapeDtypeStruct(shape, F32), depth) if len(shape) == 3 else whole(shape)
+                for shape in shapes
+            ],
         )
 
     def finish_m(depth, pieces):
@@ -1070,15 +1152,18 @@
         shapes = [w_qkv.shape, w_out.shape, gains_a.shape]
         body = functools.partial(finish_attention, count=len(pieces))
         args = pieces + [w_qkv, gains_a, keep, over_fsdp(give, 1)]
+        if len(pieces) == 4:
+            shapes = shapes + [(len_high, LANES)]
         big[:3] = finish(body, depth, args, shapes, big[:3])
 
-    homes_a[0], homes_m[0], merged, d_table, output = tie(homes_a[0], homes_m[0], merged, d_table, output)
-    pieces = square.spread(homes_a[0])
     finish_m(1, merged)
     finish_a(1, merged)
+    homes_a[0], homes_m[0], big, output = tie(homes_a[0], homes_m[0], big, output)
+    pieces = square.spread(homes_a[0])
     finish_m(0, homes_m[0])
     pieces, big = tie(pieces, big)
     finish_a(0, pieces)
+    d_table = big.pop(3)
     return (
         output,
         gradient,

time: 416 us -> 400 us (0.962)
  Pallas kernels: 132 us -> 124 us
  starting transfers between devices: 87.5 us -> 82.4 us
    ppermute x11, waiting for transfers between devices: 18 us -> 8.11 us  [over_fsdp(): return lax.ppermute(x, 'fsdp', [(j, j ^ k) for j in range(8)])]
    pallas_call x57 -> x56, Pallas kernels: 132 us -> 124 us  [call(): pl.pallas_call(run, name=name, grid=(1,), in_specs=specs, out_specs=out_s...]
    ppermute x11, starting transfers between devices: 14.8 us -> 7.26 us  [over_fsdp(): return lax.ppermute(x, 'fsdp', [(j, j ^ k) for j in range(8)])]
    reduce_scatter x4 -> x3, waiting for transfers between devices: 0.02 us -> 5.2 us  [home(): return lax.psum_scatter(term, 'fsdp', scatter_dimension=0, tiled=False)]
    ppermute x65 -> x62, starting transfers between devices: 71.5 us -> 74.2 us  [swap(): return lax.ppermute(block, 'dp', [(i, i ^ k) for i in range(self.count)])]
    ppermute x65 -> x62, waiting for transfers between devices: 90.9 us -> 93 us  [swap(): return lax.ppermute(block, 'dp', [(i, i ^ k) for i in range(self.count)])]
    unnamed x232 -> x234, local copies, waits for them, and re-layouts: 45.1 us -> 43.1 us
  transfers between devices with their start and end apart: 83 -> 80, of which waited for: 29 -> 31; matrix products, arithmetic and copies ran while one was open for 2% -> 1% of each run, Pallas kernels for 31% -> 30%
where the time goes in v5:
time: 400 us; the launch traced here: 395 us
  Pallas kernels  124 us (31%)
  waiting for transfers between devices  121 us (30%)
  starting transfers between devices  82.4 us (21%)
  local copies, waits for them, and re-layouts  47.9 us (12%)
  between operations  17.9 us (4%)
    pallas_call x56, Pallas kernels, call(): pl.pallas_call(run, name=name, grid=(1,), in_specs=specs, out_specs=out_s...  124 us
    ppermute x62, waiting for transfers between devices, swap(): return lax.ppermute(block, 'dp', [(i, i ^ k) for i in range(self.count)])  93 us
    ppermute x62, starting transfers between devices, swap(): return lax.ppermute(block, 'dp', [(i, i ^ k) for i in range(self.count)])  74.2 us
    unnamed x234, local copies, waits for them, and re-layouts  43.1 us
    all_gather x3, waiting for transfers between devices, fetch(): return lax.all_gather(packed, 'fsdp', axis=0, tiled=False)  14.5 us
    ppermute x11, waiting for transfers between devices, over_fsdp(): return lax.ppermute(x, 'fsdp', [(j, j ^ k) for j in range(8)])  8.11 us
  transfers between devices with their start and end apart: 80, of which 31 were waited for; matrix products, arithmetic and copies ran while one was open for 1% of the time, Pallas kernels for 30%

profile of v5, /device:TPU:0, one launch (start us, length us, event | category | flops | bytes accessed | tf_op | source)
XLA Modules:
  0.0 395.1 jit_solution(5675911619862490140)
XLA Ops:
  11.0 2.8 prepare_first.1
  15.2 5.0 %collective-permute-start.3 = (bf16[40,256]{1,0:T(8,128)(2,1)S(1)}, bf16[40,256]{1,0:T(8,128)(2,1)S(1)}, u32[]{:S(2)}, u32[]{:S(2)}) collective-permute-start(bf16[40,256]{1,0:T(8,128)(2,1)S(1)} %pad_maximum_fusion.1.refs_1_), channel_id=1, source_target_pairs={{0,6},{1,7},{2,4},{3,5},{4,2},{5,3},{6,0},{7,1},{8,14},{9,15},{10,... | collective-permute-start | bytes 61448 | tf_op jit(solution)/shard_map/ppermute | solution.py:873
  22.0 2.9 collective-permute-done.2.refs_3_
  25.0 2.5 collective-permute-start.6
  34.2 3.0 prepare_second.1
  37.3 2.7 prepare_third.1
  49.3 14.5 %all-gather.7.cloned.1.call-done = bf16[2048,1024]{1,0:T(8,128)(2,1)} async-done(((bf16[256,1024]{1,0:T(8,128)(2,1)}), bf16[2048,1024]{1,0:T(8,128)(2,1)}) %all-gather.7.cloned.1.call-update) | async-done | bytes 4194320 | tf_op jit(solution)/shard_map/all_gather | solution.py:895
  82.4 2.8 collective-permute-done.9.refs_2_
  85.2 6.9 %collective-permute-done.13.refs_4_ = bf16[152,1024]{1,0:T(8,128)(2,1)S(1)} collective-permute-done((bf16[152,1024]{1,0:T(8,128)(2,1)S(1)}, bf16[152,1024]{1,0:T(8,128)(2,1)S(1)}, u32[]{:S(2)}, u32[]{:S(2)}) %collective-permute-start.13) | collective-permute-done | bytes 311328 | tf_op jit(solution)/shard_map/ppermute | solution.py:61
  97.5 6.1 %collective-permute-done.17.refs_0_.refs_1_ = bf16[152,1024]{1,0:T(8,128)(2,1)S(1)} collective-permute-done((bf16[152,1024]{1,0:T(8,128)(2,1)S(1)}, bf16[152,1024]{1,0:T(8,128)(2,1)S(1)}, u32[]{:S(2)}, u32[]{:S(2)}) %collective-permute-start.17) | collective-permute-done | bytes 311328 | tf_op jit(solution)/shard_map/ppermute | solution.py:61
  104.3 5.6 %collective-permute-done.18.refs_0_.refs_2_ = bf16[152,1024]{1,0:T(8,128)(2,1)S(1)} collective-permute-done((bf16[152,1024]{1,0:T(8,128)(2,1)S(1)}, bf16[152,1024]{1,0:T(8,128)(2,1)S(1)}, u32[]{:S(2)}, u32[]{:S(2)}) %collective-permute-start.18) | collective-permute-done | bytes 311328 | tf_op jit(solution)/shard_map/ppermute | solution.py:61
  119.6 11.8 %collective-permute-done.21.refs_3_ = bf16[152,1024]{1,0:T(8,128)(2,1)S(1)} collective-permute-done((bf16[152,1024]{1,0:T(8,128)(2,1)S(1)}, bf16[152,1024]{1,0:T(8,128)(2,1)S(1)}, u32[]{:S(2)}, u32[]{:S(2)}) %collective-permute-start.21) | collective-permute-done | bytes 311328 | tf_op jit(solution)/shard_map/ppermute | solution.py:61
  138.8 4.6 %collective-permute-done.23.refs_1_.refs_2_ = bf16[152,1024]{1,0:T(8,128)(2,1)S(1)} collective-permute-done((bf16[152,1024]{1,0:T(8,128)(2,1)S(1)}, bf16[152,1024]{1,0:T(8,128)(2,1)S(1)}, u32[]{:S(2)}, u32[]{:S(2)}) %collective-permute-start.23) | collective-permute-done | bytes 311328 | tf_op jit(solution)/shard_map/ppermute | solution.py:61
  143.4 2.6 attention_forward.13
  150.2 2.5 collective-permute-start.26
  156.8 7.4 %collective-permute-done.26.refs_3_ = bf16[152,1024]{1,0:T(8,128)(2,1)S(1)} collective-permute-done((bf16[152,1024]{1,0:T(8,128)(2,1)S(1)}, bf16[152,1024]{1,0:T(8,128)(2,1)S(1)}, u32[]{:S(2)}, u32[]{:S(2)}) %collective-permute-start.26) | collective-permute-done | bytes 311328 | tf_op jit(solution)/shard_map/ppermute | solution.py:61
  172.8 2.9 mlp_both.4
  176.5 3.6 mlp_both.5
  180.3 3.5 mlp_both.6
  185.3 3.5 mlp_both.7
  190.7 4.9 %grads_mlp.2 = bf16[8,256,1024]{2,1,0:T(8,128)(2,1)S(1)} custom-call(bf16[152,1024]{1,0:T(8,128)(2,1)} %get-tuple-element.207.refs_0_, bf16[152,1024]{1,0:T(8,128)(2,1)} %collective-permute-done.31.refs_0_.refs_1_, bf16[152,1024]{1,0:T(8,128)(2,1)} %collective-permute-done.30.refs_0_.refs_2_, bf16[152,1024]{1,0:T(8,128)(2,1)} %collective-permute-done.29.refs_0_.refs_3_, ...), custom_call_target="tpu_custom_call" | custom-call | bytes 4194304 | tf_op jit(solution)/shard_map/grads_mlp/pallas_call | solution.py:397
  198.4 3.1 add_norm_backward.3
  208.2 2.7 attention_backward.8
  212.0 2.7 attention_backward.9
  215.0 2.6 attention_backward.10
  219.3 2.7 attention_backward.11
  226.5 3.8 collective-permute-done.40.refs_3_
  234.1 3.2 add_norm_backward.4
  240.8 5.2 %reduce-scatter.5.cloned.1.call-done = bf16[1,256,1024]{2,1,0:T(8,128)(2,1)} async-done(((bf16[8,256,1024]{2,1,0:T(8,128)(2,1)}), bf16[1,256,1024]{2,1,0:T(8,128)(2,1)}) %reduce-scatter.5.cloned.1.call-update) | async-done | bytes 524304 | tf_op jit(solution)/shard_map/reduce_scatter | solution.py:1033
  254.6 3.2 mlp_backward.5
  259.2 3.2 mlp_backward.6
  264.0 3.3 mlp_backward.7
  267.9 4.6 %grads_mlp.3 = bf16[8,256,1024]{2,1,0:T(8,128)(2,1)S(1)} custom-call(bf16[152,1024]{1,0:T(8,128)(2,1)S(1)} %copy-done.63, bf16[152,1024]{1,0:T(8,128)(2,1)S(1)} %copy-done.65, bf16[152,1024]{1,0:T(8,128)(2,1)S(1)} %copy-done.67, bf16[152,1024]{1,0:T(8,128)(2,1)S(1)} %copy-done.69, bf16[152,1024]{1,0:T(8,128)(2,1)S(1)} %get-tuple-element.265.refs_4_, ...), custom_call_target="tpu_custom_call" | custom-call | bytes 4194304 | tf_op jit(solution)/shard_map/grads_mlp/pallas_call | solution.py:397
  279.9 3.1 add_norm_backward.5
  289.7 2.8 attention_backward.12
  292.5 14.0 %collective-permute-done.53.refs_1_.refs_13_ = bf16[152,1024]{1,0:T(8,128)(2,1)S(1)} collective-permute-done((bf16[152,1024]{1,0:T(8,128)(2,1)}, bf16[152,1024]{1,0:T(8,128)(2,1)S(1)}, u32[]{:S(2)}, u32[]{:S(2)}) %collective-permute-start.53) | collective-permute-done | bytes 311328 | tf_op jit(solution)/shard_map/ppermute | solution.py:61
  306.5 2.7 attention_backward.13
  309.9 2.6 attention_backward.14
  313.2 2.7 attention_backward.15
  318.4 3.4 grads_attention.1.refs_7_
  324.0 2.6 last_norm.1
  338.4 3.4 collective-permute-done.60.refs_3_
  346.3 5.2 %collective-permute-done.64.refs_5_ = bf16[192,1024]{1,0:T(8,128)(2,1)S(1)} collective-permute-done((bf16[192,1024]{1,0:T(8,128)(2,1)S(1)}, bf16[192,1024]{1,0:T(8,128)(2,1)S(1)}, u32[]{:S(2)}, u32[]{:S(2)}) %collective-permute-start.64) | collective-permute-done | bytes 393248 | tf_op jit(solution)/shard_map/ppermute | solution.py:61
  354.7 3.4 collective-permute-done.66.refs_2_
  358.2 3.1 finish_mlp.2
  373.7 3.1 finish_mlp.3
  378.8 4.4 %collective-permute-done.70.refs_3_ = bf16[160,1024]{1,0:T(8,128)(2,1)S(1)} collective-permute-done((bf16[160,1024]{1,0:T(8,128)(2,1)}, bf16[160,1024]{1,0:T(8,128)(2,1)S(1)}, u32[]{:S(2)}, u32[]{:S(2)}) %collective-permute-start.70) | collective-permute-done | bytes 327712 | tf_op jit(solution)/shard_map/ppermute | solution.py:61
  385.2 2.5 finish_attention.3
  (427 shorter events, 175.7 us)
Async XLA Ops:
  7.2 56.6 %all-gather.7.cloned.1.call-start = ((), (), s32[]{:S(2)}) async-start(), calls=%async_computation.8 | async-start | bytes 4718592 | tf_op jit(solution)/shard_map/all_gather | solution.py:895
  13.8 98.3 %all-gather.9.cloned.1.call-start = ((), (), s32[]{:S(2)}) async-start(), calls=%async_computation.9 | async-start | bytes 4718592 | tf_op jit(solution)/shard_map/all_gather | solution.py:895
  37.2 132.4 %all-gather.11.cloned.1.call-start = ((), (), s32[]{:S(2)}) async-start(), calls=%async_computation.10 | async-start | bytes 4718592 | tf_op jit(solution)/shard_map/all_gather | solution.py:895
  40.0 205.9 %reduce-scatter.5.cloned.1.call-start = ((), (), s32[]{:S(2)}) async-start(), calls=%async_computation.4 | async-start | bytes 4718592 | tf_op jit(solution)/shard_map/reduce_scatter | solution.py:1033
  42.8 32.1 %collective-permute-start.12 = (bf16[152,1024]{1,0:T(8,128)(2,1)S(1)}, bf16[152,1024]{1,0:T(8,128)(2,1)S(1)}, u32[]{:S(2)}, u32[]{:S(2)}) collective-permute-start(bf16[152,1024]{1,0:T(8,128)(2,1)S(1)} %copy-done.22), channel_id=1, source_target_pairs={{0,24},{8,16},{16,8},{24,0},{1,25},{9,17},{17,9},{25,1},{2,26},{10... | collective-permute-start | bytes 933896 | tf_op jit(solution)/shard_map/ppermute | solution.py:61
  44.3 27.8 %collective-permute-start.10 = (bf16[152,1024]{1,0:T(8,128)(2,1)S(1)}, bf16[152,1024]{1,0:T(8,128)(2,1)S(1)}, u32[]{:S(2)}, u32[]{:S(2)}) collective-permute-start(bf16[152,1024]{1,0:T(8,128)(2,1)S(1)} %copy-done.22), channel_id=1, source_target_pairs={{0,16},{8,24},{16,0},{24,8},{1,17},{9,25},{17,1},{25,9},{2,18},{10... | collective-permute-start | bytes 933896 | tf_op jit(solution)/shard_map/ppermute | solution.py:61
  44.8 23.4 %collective-permute-start.8 = (bf16[152,1024]{1,0:T(8,128)(2,1)S(1)}, bf16[152,1024]{1,0:T(8,128)(2,1)S(1)}, u32[]{:S(2)}, u32[]{:S(2)}) collective-permute-start(bf16[152,1024]{1,0:T(8,128)(2,1)S(1)} %copy-done.22), channel_id=1, source_target_pairs={{0,8},{8,0},{16,24},{24,16},{1,9},{9,1},{17,25},{25,17},{2,10},{10... | collective-permute-start | bytes 933896 | tf_op jit(solution)/shard_map/ppermute | solution.py:61
  47.3 32.8 %collective-permute-start.16 = (bf16[152,1024]{1,0:T(8,128)(2,1)S(1)}, bf16[152,1024]{1,0:T(8,128)(2,1)S(1)}, u32[]{:S(2)}, u32[]{:S(2)}) collective-permute-start(bf16[152,1024]{1,0:T(8,128)(2,1)S(1)} %get-tuple-element.211.refs_1_.refs_12_), channel_id=1, source_target_pairs={{0,24},{8,16},{16,8},{24,0},{1,25},{9,17},{17,9},{25,1},{2,26},{10... | collective-permute-start | bytes 933896 | tf_op jit(solution)/shard_map/ppermute | solution.py:61
  48.7 32.9 %collective-permute-start.15 = (bf16[152,1024]{1,0:T(8,128)(2,1)S(1)}, bf16[152,1024]{1,0:T(8,128)(2,1)S(1)}, u32[]{:S(2)}, u32[]{:S(2)}) collective-permute-start(bf16[152,1024]{1,0:T(8,128)(2,1)S(1)} %get-tuple-element.211.refs_1_.refs_12_), channel_id=1, source_target_pairs={{0,16},{8,24},{16,0},{24,8},{1,17},{9,25},{17,1},{25,9},{2,18},{10... | collective-permute-start | bytes 933896 | tf_op jit(solution)/shard_map/ppermute | solution.py:61
  68.3 13.3 %collective-permute-start.14 = (bf16[152,1024]{1,0:T(8,128)(2,1)S(1)}, bf16[152,1024]{1,0:T(8,128)(2,1)S(1)}, u32[]{:S(2)}, u32[]{:S(2)}) collective-permute-start(bf16[152,1024]{1,0:T(8,128)(2,1)S(1)} %get-tuple-element.211.refs_1_.refs_12_), channel_id=1, source_target_pairs={{0,8},{8,0},{16,24},{24,16},{1,9},{9,1},{17,25},{25,17},{2,10},{10... | collective-permute-start | bytes 933896 | tf_op jit(solution)/shard_map/ppermute | solution.py:61
  94.8 15.2 %collective-permute-start.18 = (bf16[152,1024]{1,0:T(8,128)(2,1)S(1)}, bf16[152,1024]{1,0:T(8,128)(2,1)S(1)}, u32[]{:S(2)}, u32[]{:S(2)}) collective-permute-start(bf16[152,1024]{1,0:T(8,128)(2,1)S(1)} %get-tuple-element.194.refs_0_), channel_id=1, source_target_pairs={{0,16},{8,24},{16,0},{24,8},{1,17},{9,25},{17,1},{25,9},{2,18},{10... | collective-permute-start | bytes 933896 | tf_op jit(solution)/shard_map/ppermute | solution.py:61
  95.3 15.4 %collective-permute-start.19 = (bf16[152,1024]{1,0:T(8,128)(2,1)S(1)}, bf16[152,1024]{1,0:T(8,128)(2,1)S(1)}, u32[]{:S(2)}, u32[]{:S(2)}) collective-permute-start(bf16[152,1024]{1,0:T(8,128)(2,1)S(1)} %get-tuple-element.194.refs_0_), channel_id=1, source_target_pairs={{0,24},{8,16},{16,8},{24,0},{1,25},{9,17},{17,9},{25,1},{2,26},{10... | collective-permute-start | bytes 933896 | tf_op jit(solution)/shard_map/ppermute | solution.py:61
  115.5 15.9 %collective-permute-start.21 = (bf16[152,1024]{1,0:T(8,128)(2,1)S(1)}, bf16[152,1024]{1,0:T(8,128)(2,1)S(1)}, u32[]{:S(2)}, u32[]{:S(2)}) collective-permute-start(bf16[152,1024]{1,0:T(8,128)(2,1)S(1)} %get-tuple-element.196), channel_id=1, source_target_pairs={{0,16},{8,24},{16,0},{24,8},{1,17},{9,25},{17,1},{25,9},{2,18},{10... | collective-permute-start | bytes 933896 | tf_op jit(solution)/shard_map/ppermute | solution.py:61
  116.8 14.6 %collective-permute-start.22 = (bf16[152,1024]{1,0:T(8,128)(2,1)S(1)}, bf16[152,1024]{1,0:T(8,128)(2,1)S(1)}, u32[]{:S(2)}, u32[]{:S(2)}) collective-permute-start(bf16[152,1024]{1,0:T(8,128)(2,1)S(1)} %get-tuple-element.197), channel_id=1, source_target_pairs={{0,24},{8,16},{16,8},{24,0},{1,25},{9,17},{17,9},{25,1},{2,26},{10... | collective-permute-start | bytes 933896 | tf_op jit(solution)/shard_map/ppermute | solution.py:61
  118.2 14.4 %collective-permute-start.20 = (bf16[152,1024]{1,0:T(8,128)(2,1)S(1)}, bf16[152,1024]{1,0:T(8,128)(2,1)S(1)}, u32[]{:S(2)}, u32[]{:S(2)}) collective-permute-start(bf16[152,1024]{1,0:T(8,128)(2,1)S(1)} %get-tuple-element.195.refs_2_), channel_id=1, source_target_pairs={{0,8},{8,0},{16,24},{24,16},{1,9},{9,1},{17,25},{25,17},{2,10},{10... | collective-permute-start | bytes 933896 | tf_op jit(solution)/shard_map/ppermute | solution.py:61
  134.6 13.4 %collective-permute-start.25 = (bf16[152,1024]{1,0:T(8,128)(2,1)S(1)}, bf16[152,1024]{1,0:T(8,128)(2,1)S(1)}, u32[]{:S(2)}, u32[]{:S(2)}) collective-permute-start(bf16[152,1024]{1,0:T(8,128)(2,1)S(1)} %get-tuple-element.199.refs_1_), channel_id=1, source_target_pairs={{0,16},{8,24},{16,0},{24,8},{1,17},{9,25},{17,1},{25,9},{2,18},{10... | collective-permute-start | bytes 933896 | tf_op jit(solution)/shard_map/ppermute | solution.py:61
  136.1 16.6 %collective-permute-start.27 = (bf16[152,1024]{1,0:T(8,128)(2,1)S(1)}, bf16[152,1024]{1,0:T(8,128)(2,1)S(1)}, u32[]{:S(2)}, u32[]{:S(2)}) collective-permute-start(bf16[152,1024]{1,0:T(8,128)(2,1)S(1)} %get-tuple-element.199.refs_1_), channel_id=1, source_target_pairs={{0,24},{8,16},{16,8},{24,0},{1,25},{9,17},{17,9},{25,1},{2,26},{10... | collective-permute-start | bytes 933896 | tf_op jit(solution)/shard_map/ppermute | solution.py:61
  150.2 14.0 %collective-permute-start.26 = (bf16[152,1024]{1,0:T(8,128)(2,1)S(1)}, bf16[152,1024]{1,0:T(8,128)(2,1)S(1)}, u32[]{:S(2)}, u32[]{:S(2)}) collective-permute-start(bf16[152,1024]{1,0:T(8,128)(2,1)S(1)} %get-tuple-element.204), channel_id=1, source_target_pairs={{0,16},{8,24},{16,0},{24,8},{1,17},{9,25},{17,1},{25,9},{2,18},{10... | collective-permute-start | bytes 933896 | tf_op jit(solution)/shard_map/ppermute | solution.py:61
  166.2 14.1 %collective-permute-start.30 = (bf16[152,1024]{1,0:T(8,128)(2,1)}, bf16[152,1024]{1,0:T(8,128)(2,1)}, u32[]{:S(2)}, u32[]{:S(2)}) collective-permute-start(bf16[152,1024]{1,0:T(8,128)(2,1)} %get-tuple-element.207.refs_0_), channel_id=1, source_target_pairs={{0,16},{8,24},{16,0},{24,8},{1,17},{9,25},{17,1},{25,9},{2,18},{10... | collective-permute-start | bytes 933896 | tf_op jit(solution)/shard_map/ppermute | solution.py:61
  167.8 17.5 %collective-permute-start.29 = (bf16[152,1024]{1,0:T(8,128)(2,1)}, bf16[152,1024]{1,0:T(8,128)(2,1)}, u32[]{:S(2)}, u32[]{:S(2)}) collective-permute-start(bf16[152,1024]{1,0:T(8,128)(2,1)} %get-tuple-element.207.refs_0_), channel_id=1, source_target_pairs={{0,24},{8,16},{16,8},{24,0},{1,25},{9,17},{17,9},{25,1},{2,26},{10... | collective-permute-start | bytes 933896 | tf_op jit(solution)/shard_map/ppermute | solution.py:61
  180.1 18.2 %collective-permute-start.33 = (bf16[152,1024]{1,0:T(8,128)(2,1)}, bf16[152,1024]{1,0:T(8,128)(2,1)}, u32[]{:S(2)}, u32[]{:S(2)}) collective-permute-start(bf16[152,1024]{1,0:T(8,128)(2,1)} %get-tuple-element.217), channel_id=1, source_target_pairs={{0,8},{8,0},{16,24},{24,16},{1,9},{9,1},{17,25},{25,17},{2,10},{10... | collective-permute-start | bytes 933896 | tf_op jit(solution)/shard_map/ppermute | solution.py:61
  183.9 14.5 %collective-permute-start.34 = (bf16[152,1024]{1,0:T(8,128)(2,1)}, bf16[152,1024]{1,0:T(8,128)(2,1)}, u32[]{:S(2)}, u32[]{:S(2)}) collective-permute-start(bf16[152,1024]{1,0:T(8,128)(2,1)} %get-tuple-element.218), channel_id=1, source_target_pairs={{0,16},{8,24},{16,0},{24,8},{1,17},{9,25},{17,1},{25,9},{2,18},{10... | collective-permute-start | bytes 933896 | tf_op jit(solution)/shard_map/ppermute | solution.py:61
  198.3 78.4 %reduce-scatter.7.cloned.1.call-start = ((), (), s32[]{:S(2)}) async-start(), calls=%async_computation.5 | async-start | bytes 1310720 | tf_op jit(solution)/shard_map/reduce_scatter | solution.py:1096
  201.8 13.2 %collective-permute-start.36 = (bf16[152,1024]{1,0:T(8,128)(2,1)}, bf16[152,1024]{1,0:T(8,128)(2,1)S(1)}, u32[]{:S(2)}, u32[]{:S(2)}) collective-permute-start(bf16[152,1024]{1,0:T(8,128)(2,1)} %get-tuple-element.234.refs_1_.refs_13_), channel_id=1, source_target_pairs={{0,16},{8,24},{16,0},{24,8},{1,17},{9,25},{17,1},{25,9},{2,18},{10... | collective-permute-start | bytes 933896 | tf_op jit(solution)/shard_map/ppermute | solution.py:61
  203.2 16.0 %collective-permute-start.35 = (bf16[152,1024]{1,0:T(8,128)(2,1)}, bf16[152,1024]{1,0:T(8,128)(2,1)S(1)}, u32[]{:S(2)}, u32[]{:S(2)}) collective-permute-start(bf16[152,1024]{1,0:T(8,128)(2,1)} %get-tuple-element.234.refs_1_.refs_13_), channel_id=1, source_target_pairs={{0,24},{8,16},{16,8},{24,0},{1,25},{9,17},{17,9},{25,1},{2,26},{10... | collective-permute-start | bytes 933896 | tf_op jit(solution)/shard_map/ppermute | solution.py:61
  233.8 92.8 %reduce-scatter.11.cloned.1.call-start = ((), (), s32[]{:S(2)}) async-start(), calls=%async_computation.7 | async-start | bytes 4718592 | tf_op jit(solution)/shard_map/reduce_scatter | solution.py:1033
  237.3 17.3 %collective-permute-start.47 = (bf16[152,1024]{1,0:T(8,128)(2,1)}, bf16[152,1024]{1,0:T(8,128)(2,1)}, u32[]{:S(2)}, u32[]{:S(2)}) collective-permute-start(bf16[152,1024]{1,0:T(8,128)(2,1)} %get-tuple-element.263.refs_0_.refs_12_), channel_id=1, source_target_pairs={{0,8},{8,0},{16,24},{24,16},{1,9},{9,1},{17,25},{25,17},{2,10},{10... | collective-permute-start | bytes 933896 | tf_op jit(solution)/shard_map/ppermute | solution.py:61
  238.4 20.9 %collective-permute-start.46 = (bf16[152,1024]{1,0:T(8,128)(2,1)}, bf16[152,1024]{1,0:T(8,128)(2,1)}, u32[]{:S(2)}, u32[]{:S(2)}) collective-permute-start(bf16[152,1024]{1,0:T(8,128)(2,1)} %get-tuple-element.263.refs_0_.refs_12_), channel_id=1, source_target_pairs={{0,16},{8,24},{16,0},{24,8},{1,17},{9,25},{17,1},{25,9},{2,18},{10... | collective-permute-start | bytes 933896 | tf_op jit(solution)/shard_map/ppermute | solution.py:61
  239.7 24.3 %collective-permute-start.45 = (bf16[152,1024]{1,0:T(8,128)(2,1)}, bf16[152,1024]{1,0:T(8,128)(2,1)}, u32[]{:S(2)}, u32[]{:S(2)}) collective-permute-start(bf16[152,1024]{1,0:T(8,128)(2,1)} %get-tuple-element.263.refs_0_.refs_12_), channel_id=1, source_target_pairs={{0,24},{8,16},{16,8},{24,0},{1,25},{9,17},{17,9},{25,1},{2,26},{10... | collective-permute-start | bytes 933896 | tf_op jit(solution)/shard_map/ppermute | solution.py:61
  257.8 16.7 %collective-permute-start.49 = (bf16[152,1024]{1,0:T(8,128)(2,1)}, bf16[152,1024]{1,0:T(8,128)(2,1)}, u32[]{:S(2)}, u32[]{:S(2)}) collective-permute-start(bf16[152,1024]{1,0:T(8,128)(2,1)} %get-tuple-element.270), channel_id=1, source_target_pairs={{0,8},{8,0},{16,24},{24,16},{1,9},{9,1},{17,25},{25,17},{2,10},{10... | collective-permute-start | bytes 933896 | tf_op jit(solution)/shard_map/ppermute | solution.py:61
  262.5 13.9 %collective-permute-start.50 = (bf16[152,1024]{1,0:T(8,128)(2,1)}, bf16[152,1024]{1,0:T(8,128)(2,1)}, u32[]{:S(2)}, u32[]{:S(2)}) collective-permute-start(bf16[152,1024]{1,0:T(8,128)(2,1)} %get-tuple-element.271), channel_id=1, source_target_pairs={{0,16},{8,24},{16,0},{24,8},{1,17},{9,25},{17,1},{25,9},{2,18},{10... | collective-permute-start | bytes 933896 | tf_op jit(solution)/shard_map/ppermute | solution.py:61
  276.4 90.6 %reduce-scatter.9.cloned.1.call-start = ((), (), s32[]{:S(2)}) async-start(), calls=%async_computation.6 | async-start | bytes 2949120 | tf_op jit(solution)/shard_map/reduce_scatter | solution.py:1033
  277.8 40.5 %collective-permute-start.58 = (bf16[384,1024]{1,0:T(8,128)(2,1)S(1)}, bf16[384,1024]{1,0:T(8,128)(2,1)S(1)}, u32[]{:S(2)}, u32[]{:S(2)}) collective-permute-start(bf16[384,1024]{1,0:T(8,128)(2,1)S(1)} %pad_maximum_fusion.refs_4_.refs_1_), channel_id=1, source_target_pairs={{0,16},{8,24},{16,0},{24,8},{1,17},{9,25},{17,1},{25,9},{2,18},{10... | collective-permute-start | bytes 2359304 | tf_op jit(solution)/shard_map/ppermute | solution.py:61
  279.4 39.0 %collective-permute-start.57 = (bf16[384,1024]{1,0:T(8,128)(2,1)S(1)}, bf16[384,1024]{1,0:T(8,128)(2,1)S(1)}, u32[]{:S(2)}, u32[]{:S(2)}) collective-permute-start(bf16[384,1024]{1,0:T(8,128)(2,1)S(1)} %pad_maximum_fusion.refs_4_.refs_1_), channel_id=1, source_target_pairs={{0,8},{8,0},{16,24},{24,16},{1,9},{9,1},{17,25},{25,17},{2,10},{10... | collective-permute-start | bytes 2359304 | tf_op jit(solution)/shard_map/ppermute | solution.py:61
  283.0 23.5 %collective-permute-start.53 = (bf16[152,1024]{1,0:T(8,128)(2,1)}, bf16[152,1024]{1,0:T(8,128)(2,1)S(1)}, u32[]{:S(2)}, u32[]{:S(2)}) collective-permute-start(bf16[152,1024]{1,0:T(8,128)(2,1)} %get-tuple-element.282.refs_1_.refs_12_), channel_id=1, source_target_pairs={{0,8},{8,0},{16,24},{24,16},{1,9},{9,1},{17,25},{25,17},{2,10},{10... | collective-permute-start | bytes 933896 | tf_op jit(solution)/shard_map/ppermute | solution.py:61
  284.5 25.3 %collective-permute-start.52 = (bf16[152,1024]{1,0:T(8,128)(2,1)}, bf16[152,1024]{1,0:T(8,128)(2,1)S(1)}, u32[]{:S(2)}, u32[]{:S(2)}) collective-permute-start(bf16[152,1024]{1,0:T(8,128)(2,1)} %get-tuple-element.282.refs_1_.refs_12_), channel_id=1, source_target_pairs={{0,16},{8,24},{16,0},{24,8},{1,17},{9,25},{17,1},{25,9},{2,18},{10... | collective-permute-start | bytes 933896 | tf_op jit(solution)/shard_map/ppermute | solution.py:61
  285.1 28.1 %collective-permute-start.51 = (bf16[152,1024]{1,0:T(8,128)(2,1)}, bf16[152,1024]{1,0:T(8,128)(2,1)S(1)}, u32[]{:S(2)}, u32[]{:S(2)}) collective-permute-start(bf16[152,1024]{1,0:T(8,128)(2,1)} %get-tuple-element.282.refs_1_.refs_12_), channel_id=1, source_target_pairs={{0,24},{8,16},{16,8},{24,0},{1,25},{9,17},{17,9},{25,1},{2,26},{10... | collective-permute-start | bytes 933896 | tf_op jit(solution)/shard_map/ppermute | solution.py:61
  326.7 15.1 %collective-permute-start.60 = (bf16[256,1024]{1,0:T(8,128)(2,1)}, bf16[256,1024]{1,0:T(8,128)(2,1)S(1)}, u32[]{:S(2)}, u32[]{:S(2)}) collective-permute-start(bf16[256,1024]{1,0:T(8,128)(2,1)} %bitcast.67), channel_id=1, source_target_pairs={{0,16},{8,24},{16,0},{24,8},{1,17},{9,25},{17,1},{25,9},{2,18},{10... | collective-permute-start | bytes 1572872 | tf_op jit(solution)/shard_map/ppermute | solution.py:61
  328.0 15.1 %collective-permute-start.59 = (bf16[256,1024]{1,0:T(8,128)(2,1)}, bf16[256,1024]{1,0:T(8,128)(2,1)S(1)}, u32[]{:S(2)}, u32[]{:S(2)}) collective-permute-start(bf16[256,1024]{1,0:T(8,128)(2,1)} %bitcast.68), channel_id=1, source_target_pairs={{0,8},{8,0},{16,24},{24,16},{1,9},{9,1},{17,25},{25,17},{2,10},{10... | collective-permute-start | bytes 1572872 | tf_op jit(solution)/shard_map/ppermute | solution.py:61
  329.5 22.0 %collective-permute-start.64 = (bf16[192,1024]{1,0:T(8,128)(2,1)S(1)}, bf16[192,1024]{1,0:T(8,128)(2,1)S(1)}, u32[]{:S(2)}, u32[]{:S(2)}) collective-permute-start(bf16[192,1024]{1,0:T(8,128)(2,1)S(1)} %slice.55), channel_id=1, source_target_pairs={{0,8},{8,0},{16,24},{24,16},{1,9},{9,1},{17,25},{25,17},{2,10},{10... | collective-permute-start | bytes 1179656 | tf_op jit(solution)/shard_map/ppermute | solution.py:61
  330.1 22.8 %collective-permute-start.63 = (bf16[192,1024]{1,0:T(8,128)(2,1)S(1)}, bf16[192,1024]{1,0:T(8,128)(2,1)S(1)}, u32[]{:S(2)}, u32[]{:S(2)}) collective-permute-start(bf16[192,1024]{1,0:T(8,128)(2,1)S(1)} %slice.54), channel_id=1, source_target_pairs={{0,16},{8,24},{16,0},{24,8},{1,17},{9,25},{17,1},{25,9},{2,18},{10... | collective-permute-start | bytes 1179656 | tf_op jit(solution)/shard_map/ppermute | solution.py:61
  336.8 21.3 %collective-permute-start.66 = (bf16[152,1024]{1,0:T(8,128)(2,1)S(1)}, bf16[152,1024]{1,0:T(8,128)(2,1)S(1)}, u32[]{:S(2)}, u32[]{:S(2)}) collective-permute-start(bf16[152,1024]{1,0:T(8,128)(2,1)S(1)} %get-tuple-element.315), channel_id=1, source_target_pairs={{0,8},{8,0},{16,24},{24,16},{1,9},{9,1},{17,25},{25,17},{2,10},{10... | collective-permute-start | bytes 933896 | tf_op jit(solution)/shard_map/ppermute | solution.py:61
  341.8 19.5 %collective-permute-start.67 = (bf16[152,1024]{1,0:T(8,128)(2,1)S(1)}, bf16[152,1024]{1,0:T(8,128)(2,1)S(1)}, u32[]{:S(2)}, u32[]{:S(2)}) collective-permute-start(bf16[152,1024]{1,0:T(8,128)(2,1)S(1)} %get-tuple-element.316), channel_id=1, source_target_pairs={{0,16},{8,24},{16,0},{24,8},{1,17},{9,25},{17,1},{25,9},{2,18},{10... | collective-permute-start | bytes 933896 | tf_op jit(solution)/shard_map/ppermute | solution.py:61
  343.0 20.4 %collective-permute-start.68 = (bf16[152,1024]{1,0:T(8,128)(2,1)S(1)}, bf16[152,1024]{1,0:T(8,128)(2,1)S(1)}, u32[]{:S(2)}, u32[]{:S(2)}) collective-permute-start(bf16[152,1024]{1,0:T(8,128)(2,1)S(1)} %get-tuple-element.317), channel_id=1, source_target_pairs={{0,24},{8,16},{16,8},{24,0},{1,25},{9,17},{17,9},{25,1},{2,26},{10... | collective-permute-start | bytes 933896 | tf_op jit(solution)/shard_map/ppermute | solution.py:61
  351.4 15.5 %collective-permute-start.62 = (bf16[128,1024]{1,0:T(8,128)(2,1)}, bf16[128,1024]{1,0:T(8,128)(2,1)S(1)}, u32[]{:S(2)}, u32[]{:S(2)}) collective-permute-start(bf16[128,1024]{1,0:T(8,128)(2,1)} %slice.53), channel_id=1, source_target_pairs={{0,8},{8,0},{16,24},{24,16},{1,9},{9,1},{17,25},{25,17},{2,10},{10... | collective-permute-start | bytes 786440 | tf_op jit(solution)/shard_map/ppermute | solution.py:61
  352.9 14.0 %collective-permute-start.61 = (bf16[128,1024]{1,0:T(8,128)(2,1)}, bf16[128,1024]{1,0:T(8,128)(2,1)S(1)}, u32[]{:S(2)}, u32[]{:S(2)}) collective-permute-start(bf16[128,1024]{1,0:T(8,128)(2,1)} %slice.52), channel_id=1, source_target_pairs={{0,16},{8,24},{16,0},{24,8},{1,17},{9,25},{17,1},{25,9},{2,18},{10... | collective-permute-start | bytes 786440 | tf_op jit(solution)/shard_map/ppermute | solution.py:61
  369.4 13.7 %collective-permute-start.70 = (bf16[160,1024]{1,0:T(8,128)(2,1)}, bf16[160,1024]{1,0:T(8,128)(2,1)S(1)}, u32[]{:S(2)}, u32[]{:S(2)}) collective-permute-start(bf16[160,1024]{1,0:T(8,128)(2,1)} %bitcast.63), channel_id=1, source_target_pairs={{0,16},{8,24},{16,0},{24,8},{1,17},{9,25},{17,1},{25,9},{2,18},{10... | collective-permute-start | bytes 983048 | tf_op jit(solution)/shard_map/ppermute | solution.py:61
  370.0 13.2 %collective-permute-start.69 = (bf16[160,1024]{1,0:T(8,128)(2,1)}, bf16[160,1024]{1,0:T(8,128)(2,1)S(1)}, u32[]{:S(2)}, u32[]{:S(2)}) collective-permute-start(bf16[160,1024]{1,0:T(8,128)(2,1)} %bitcast.64), channel_id=1, source_target_pairs={{0,8},{8,0},{16,24},{24,16},{1,9},{9,1},{17,25},{25,17},{2,10},{10... | collective-permute-start | bytes 983048 | tf_op jit(solution)/shard_map/ppermute | solution.py:61
  (148 other events, 1152.2 us)
Sparse Core Ops, SparseCore 0:
  14.0 49.7 all-gather.6
  65.9 45.7 all-gather.8
  113.9 45.8 all-gather.10
  198.5 47.4 reduce-scatter.4
  248.6 25.2 reduce-scatter.6
  276.8 49.0 reduce-scatter.10
  328.3 37.4 reduce-scatter.8

commit v6 on v5

--- a/solution.py
+++ b/solution.py
@@ -990,6 +990,8 @@
         if depth == 0:
             es, d_top = tie(es, d_top)
         before, (middle, xhat) = hidden, call(add_norm, normed, [hidden] + es)
+        if depth > 0:
+            xhat, third_w = tie(xhat, third_w)
         ms = square.spread(xhat)
         if depth < layers - 1:
             acts = chain(

time: 400 us -> 397 us (level)
  Pallas kernels: 124 us -> 118 us
    pallas_call x56, Pallas kernels: 124 us -> 118 us  [call(): pl.pallas_call(run, name=name, grid=(1,), in_specs=specs, out_specs=out_s...]
    unnamed x234 -> x240, local copies, waits for them, and re-layouts: 43.1 us -> 45.6 us
  transfers between devices with their start and end apart: 80 -> 80, of which waited for: 31 -> 34; matrix products, arithmetic and copies ran while one was open for 1% -> 1% of each run, Pallas kernels for 30% -> 29%
where the time goes in v6:
time: 397 us; the launch traced here: 392 us
  waiting for transfers between devices  122 us (31%)
  Pallas kernels  118 us (30%)
  starting transfers between devices  82.5 us (21%)
  local copies, waits for them, and re-layouts  49.7 us (13%)
  between operations  17.9 us (5%)
    pallas_call x56, Pallas kernels, call(): pl.pallas_call(run, name=name, grid=(1,), in_specs=specs, out_specs=out_s...  118 us
    ppermute x62, waiting for transfers between devices, swap(): return lax.ppermute(block, 'dp', [(i, i ^ k) for i in range(self.count)])  94.3 us
    ppermute x62, starting transfers between devices, swap(): return lax.ppermute(block, 'dp', [(i, i ^ k) for i in range(self.count)])  74.1 us
    unnamed x240, local copies, waits for them, and re-layouts  45.6 us
    all_gather x3, waiting for transfers between devices, fetch(): return lax.all_gather(packed, 'fsdp', axis=0, tiled=False)  14.4 us
  transfers between devices with their start and end apart: 80, of which 34 were waited for; matrix products, arithmetic and copies ran while one was open for 1% of the time, Pallas kernels for 29%

profile of v6, /device:TPU:0, one launch (start us, length us, event | category | flops | bytes accessed | tf_op | source)
XLA Modules:
  0.0 392.4 jit_solution(2051021291760498358)
XLA Ops:
  11.0 2.8 prepare_first.1
  15.2 5.0 %collective-permute-start.3 = (bf16[40,256]{1,0:T(8,128)(2,1)S(1)}, bf16[40,256]{1,0:T(8,128)(2,1)S(1)}, u32[]{:S(2)}, u32[]{:S(2)}) collective-permute-start(bf16[40,256]{1,0:T(8,128)(2,1)S(1)} %pad_maximum_fusion.1.refs_1_), channel_id=1, source_target_pairs={{0,6},{1,7},{2,4},{3,5},{4,2},{5,3},{6,0},{7,1},{8,14},{9,15},{10,... | collective-permute-start | bytes 61448 | tf_op jit(solution)/shard_map/ppermute | solution.py:873
  22.0 2.9 collective-permute-done.2.refs_3_
  24.9 2.5 collective-permute-start.6
  34.2 3.0 prepare_second.1
  37.3 2.7 prepare_third.1
  49.4 14.4 %all-gather.7.cloned.1.call-done = bf16[2048,1024]{1,0:T(8,128)(2,1)} async-done(((bf16[256,1024]{1,0:T(8,128)(2,1)}), bf16[2048,1024]{1,0:T(8,128)(2,1)}) %all-gather.7.cloned.1.call-update) | async-done | bytes 4194320 | tf_op jit(solution)/shard_map/all_gather | solution.py:895
  82.6 2.7 collective-permute-done.9.refs_2_
  85.3 6.9 %collective-permute-done.13.refs_4_ = bf16[152,1024]{1,0:T(8,128)(2,1)S(1)} collective-permute-done((bf16[152,1024]{1,0:T(8,128)(2,1)S(1)}, bf16[152,1024]{1,0:T(8,128)(2,1)S(1)}, u32[]{:S(2)}, u32[]{:S(2)}) %collective-permute-start.13) | collective-permute-done | bytes 311328 | tf_op jit(solution)/shard_map/ppermute | solution.py:61
  97.6 6.1 %collective-permute-done.17.refs_0_.refs_1_ = bf16[152,1024]{1,0:T(8,128)(2,1)S(1)} collective-permute-done((bf16[152,1024]{1,0:T(8,128)(2,1)S(1)}, bf16[152,1024]{1,0:T(8,128)(2,1)S(1)}, u32[]{:S(2)}, u32[]{:S(2)}) %collective-permute-start.17) | collective-permute-done | bytes 311328 | tf_op jit(solution)/shard_map/ppermute | solution.py:61
  104.4 5.6 %collective-permute-done.18.refs_0_.refs_2_ = bf16[152,1024]{1,0:T(8,128)(2,1)S(1)} collective-permute-done((bf16[152,1024]{1,0:T(8,128)(2,1)S(1)}, bf16[152,1024]{1,0:T(8,128)(2,1)S(1)}, u32[]{:S(2)}, u32[]{:S(2)}) %collective-permute-start.18) | collective-permute-done | bytes 311328 | tf_op jit(solution)/shard_map/ppermute | solution.py:61
  119.7 11.8 %collective-permute-done.21.refs_3_ = bf16[152,1024]{1,0:T(8,128)(2,1)S(1)} collective-permute-done((bf16[152,1024]{1,0:T(8,128)(2,1)S(1)}, bf16[152,1024]{1,0:T(8,128)(2,1)S(1)}, u32[]{:S(2)}, u32[]{:S(2)}) %collective-permute-start.21) | collective-permute-done | bytes 311328 | tf_op jit(solution)/shard_map/ppermute | solution.py:61
  138.9 4.6 %collective-permute-done.23.refs_1_.refs_2_ = bf16[152,1024]{1,0:T(8,128)(2,1)S(1)} collective-permute-done((bf16[152,1024]{1,0:T(8,128)(2,1)S(1)}, bf16[152,1024]{1,0:T(8,128)(2,1)S(1)}, u32[]{:S(2)}, u32[]{:S(2)}) %collective-permute-start.23) | collective-permute-done | bytes 311328 | tf_op jit(solution)/shard_map/ppermute | solution.py:61
  143.5 2.7 attention_forward.13
  156.4 7.8 %collective-permute-done.26.refs_3_ = bf16[152,1024]{1,0:T(8,128)(2,1)S(1)} collective-permute-done((bf16[152,1024]{1,0:T(8,128)(2,1)S(1)}, bf16[152,1024]{1,0:T(8,128)(2,1)S(1)}, u32[]{:S(2)}, u32[]{:S(2)}) %collective-permute-start.26) | collective-permute-done | bytes 311328 | tf_op jit(solution)/shard_map/ppermute | solution.py:61
  176.3 2.5 mlp_both.5
  179.1 2.5 mlp_both.6
  183.1 2.5 mlp_both.7
  187.3 3.5 grads_mlp.2
  195.1 3.1 add_norm_backward.3
  204.9 2.7 attention_backward.8
  208.7 2.8 attention_backward.9
  212.6 2.7 attention_backward.10
  216.8 2.7 attention_backward.11
  223.4 2.8 collective-permute-done.40.refs_3_
  230.0 3.2 add_norm_backward.4
  233.2 2.5 collective-permute-start.47
  237.1 6.1 %reduce-scatter.5.cloned.1.call-done = bf16[1,256,1024]{2,1,0:T(8,128)(2,1)} async-done(((bf16[8,256,1024]{2,1,0:T(8,128)(2,1)}), bf16[1,256,1024]{2,1,0:T(8,128)(2,1)}) %reduce-scatter.5.cloned.1.call-update) | async-done | bytes 524304 | tf_op jit(solution)/shard_map/reduce_scatter | solution.py:1035
  251.8 3.2 mlp_backward.5
  256.5 3.2 mlp_backward.6
  261.3 3.3 mlp_backward.7
  265.2 4.6 %grads_mlp.3 = bf16[8,256,1024]{2,1,0:T(8,128)(2,1)S(1)} custom-call(bf16[152,1024]{1,0:T(8,128)(2,1)S(1)} %copy-done.63, bf16[152,1024]{1,0:T(8,128)(2,1)S(1)} %copy-done.65, bf16[152,1024]{1,0:T(8,128)(2,1)S(1)} %copy-done.67, bf16[152,1024]{1,0:T(8,128)(2,1)S(1)} %copy-done.69, bf16[152,1024]{1,0:T(8,128)(2,1)S(1)} %get-tuple-element.269.refs_4_, ...), custom_call_target="tpu_custom_call" | custom-call | bytes 4194304 | tf_op jit(solution)/shard_map/grads_mlp/pallas_call | solution.py:397
  277.2 3.1 add_norm_backward.5
  287.0 2.8 attention_backward.12
  289.9 13.9 %collective-permute-done.53.refs_1_.refs_13_ = bf16[152,1024]{1,0:T(8,128)(2,1)S(1)} collective-permute-done((bf16[152,1024]{1,0:T(8,128)(2,1)}, bf16[152,1024]{1,0:T(8,128)(2,1)S(1)}, u32[]{:S(2)}, u32[]{:S(2)}) %collective-permute-start.53) | collective-permute-done | bytes 311328 | tf_op jit(solution)/shard_map/ppermute | solution.py:61
  303.8 2.8 attention_backward.13
  307.2 2.7 attention_backward.14
  310.6 2.7 attention_backward.15
  315.8 3.4 grads_attention.1.refs_7_
  321.3 2.5 last_norm.1
  335.7 3.4 collective-permute-done.60.refs_3_
  342.8 6.0 %collective-permute-done.64.refs_5_ = bf16[192,1024]{1,0:T(8,128)(2,1)S(1)} collective-permute-done((bf16[192,1024]{1,0:T(8,128)(2,1)S(1)}, bf16[192,1024]{1,0:T(8,128)(2,1)S(1)}, u32[]{:S(2)}, u32[]{:S(2)}) %collective-permute-start.64) | collective-permute-done | bytes 393248 | tf_op jit(solution)/shard_map/ppermute | solution.py:61
  351.7 3.8 collective-permute-done.66.refs_2_
  355.6 3.1 finish_mlp.2
  361.8 2.5 finish_attention.2
  371.0 3.5 finish_mlp.3
  376.1 4.4 %collective-permute-done.70.refs_3_ = bf16[160,1024]{1,0:T(8,128)(2,1)S(1)} collective-permute-done((bf16[160,1024]{1,0:T(8,128)(2,1)}, bf16[160,1024]{1,0:T(8,128)(2,1)S(1)}, u32[]{:S(2)}, u32[]{:S(2)}) %collective-permute-start.70) | collective-permute-done | bytes 327712 | tf_op jit(solution)/shard_map/ppermute | solution.py:61
  382.6 2.5 finish_attention.3
  (433 shorter events, 176.0 us)
Async XLA Ops:
  7.2 56.6 %all-gather.7.cloned.1.call-start = ((), (), s32[]{:S(2)}) async-start(), calls=%async_computation.8 | async-start | bytes 4718592 | tf_op jit(solution)/shard_map/all_gather | solution.py:895
  13.8 98.4 %all-gather.9.cloned.1.call-start = ((), (), s32[]{:S(2)}) async-start(), calls=%async_computation.9 | async-start | bytes 4718592 | tf_op jit(solution)/shard_map/all_gather | solution.py:895
  37.2 128.9 %all-gather.11.cloned.1.call-start = ((), (), s32[]{:S(2)}) async-start(), calls=%async_computation.10 | async-start | bytes 4718592 | tf_op jit(solution)/shard_map/all_gather | solution.py:895
  40.0 203.2 %reduce-scatter.5.cloned.1.call-start = ((), (), s32[]{:S(2)}) async-start(), calls=%async_computation.4 | async-start | bytes 4718592 | tf_op jit(solution)/shard_map/reduce_scatter | solution.py:1035
  42.9 32.2 %collective-permute-start.12 = (bf16[152,1024]{1,0:T(8,128)(2,1)S(1)}, bf16[152,1024]{1,0:T(8,128)(2,1)S(1)}, u32[]{:S(2)}, u32[]{:S(2)}) collective-permute-start(bf16[152,1024]{1,0:T(8,128)(2,1)S(1)} %copy-done.22), channel_id=1, source_target_pairs={{0,24},{8,16},{16,8},{24,0},{1,25},{9,17},{17,9},{25,1},{2,26},{10... | collective-permute-start | bytes 933896 | tf_op jit(solution)/shard_map/ppermute | solution.py:61
  44.4 27.8 %collective-permute-start.10 = (bf16[152,1024]{1,0:T(8,128)(2,1)S(1)}, bf16[152,1024]{1,0:T(8,128)(2,1)S(1)}, u32[]{:S(2)}, u32[]{:S(2)}) collective-permute-start(bf16[152,1024]{1,0:T(8,128)(2,1)S(1)} %copy-done.22), channel_id=1, source_target_pairs={{0,16},{8,24},{16,0},{24,8},{1,17},{9,25},{17,1},{25,9},{2,18},{10... | collective-permute-start | bytes 933896 | tf_op jit(solution)/shard_map/ppermute | solution.py:61
  44.9 23.4 %collective-permute-start.8 = (bf16[152,1024]{1,0:T(8,128)(2,1)S(1)}, bf16[152,1024]{1,0:T(8,128)(2,1)S(1)}, u32[]{:S(2)}, u32[]{:S(2)}) collective-permute-start(bf16[152,1024]{1,0:T(8,128)(2,1)S(1)} %copy-done.22), channel_id=1, source_target_pairs={{0,8},{8,0},{16,24},{24,16},{1,9},{9,1},{17,25},{25,17},{2,10},{10... | collective-permute-start | bytes 933896 | tf_op jit(solution)/shard_map/ppermute | solution.py:61
  47.4 33.0 %collective-permute-start.16 = (bf16[152,1024]{1,0:T(8,128)(2,1)S(1)}, bf16[152,1024]{1,0:T(8,128)(2,1)S(1)}, u32[]{:S(2)}, u32[]{:S(2)}) collective-permute-start(bf16[152,1024]{1,0:T(8,128)(2,1)S(1)} %get-tuple-element.215.refs_1_.refs_12_), channel_id=1, source_target_pairs={{0,24},{8,16},{16,8},{24,0},{1,25},{9,17},{17,9},{25,1},{2,26},{10... | collective-permute-start | bytes 933896 | tf_op jit(solution)/shard_map/ppermute | solution.py:61
  48.8 33.0 %collective-permute-start.15 = (bf16[152,1024]{1,0:T(8,128)(2,1)S(1)}, bf16[152,1024]{1,0:T(8,128)(2,1)S(1)}, u32[]{:S(2)}, u32[]{:S(2)}) collective-permute-start(bf16[152,1024]{1,0:T(8,128)(2,1)S(1)} %get-tuple-element.215.refs_1_.refs_12_), channel_id=1, source_target_pairs={{0,16},{8,24},{16,0},{24,8},{1,17},{9,25},{17,1},{25,9},{2,18},{10... | collective-permute-start | bytes 933896 | tf_op jit(solution)/shard_map/ppermute | solution.py:61
  68.4 13.5 %collective-permute-start.14 = (bf16[152,1024]{1,0:T(8,128)(2,1)S(1)}, bf16[152,1024]{1,0:T(8,128)(2,1)S(1)}, u32[]{:S(2)}, u32[]{:S(2)}) collective-permute-start(bf16[152,1024]{1,0:T(8,128)(2,1)S(1)} %get-tuple-element.215.refs_1_.refs_12_), channel_id=1, source_target_pairs={{0,8},{8,0},{16,24},{24,16},{1,9},{9,1},{17,25},{25,17},{2,10},{10... | collective-permute-start | bytes 933896 | tf_op jit(solution)/shard_map/ppermute | solution.py:61
  72.2 13.1 %collective-permute-start.9 = (bf16[152,1024]{1,0:T(8,128)(2,1)S(1)}, bf16[152,1024]{1,0:T(8,128)(2,1)S(1)}, u32[]{:S(2)}, u32[]{:S(2)}) collective-permute-start(bf16[152,1024]{1,0:T(8,128)(2,1)S(1)} %get-tuple-element.186), channel_id=1, source_target_pairs={{0,8},{8,0},{16,24},{24,16},{1,9},{9,1},{17,25},{25,17},{2,10},{10... | collective-permute-start | bytes 933896 | tf_op jit(solution)/shard_map/ppermute | solution.py:61
  94.8 15.2 %collective-permute-start.18 = (bf16[152,1024]{1,0:T(8,128)(2,1)S(1)}, bf16[152,1024]{1,0:T(8,128)(2,1)S(1)}, u32[]{:S(2)}, u32[]{:S(2)}) collective-permute-start(bf16[152,1024]{1,0:T(8,128)(2,1)S(1)} %get-tuple-element.196.refs_0_), channel_id=1, source_target_pairs={{0,16},{8,24},{16,0},{24,8},{1,17},{9,25},{17,1},{25,9},{2,18},{10... | collective-permute-start | bytes 933896 | tf_op jit(solution)/shard_map/ppermute | solution.py:61
  95.4 15.4 %collective-permute-start.19 = (bf16[152,1024]{1,0:T(8,128)(2,1)S(1)}, bf16[152,1024]{1,0:T(8,128)(2,1)S(1)}, u32[]{:S(2)}, u32[]{:S(2)}) collective-permute-start(bf16[152,1024]{1,0:T(8,128)(2,1)S(1)} %get-tuple-element.196.refs_0_), channel_id=1, source_target_pairs={{0,24},{8,16},{16,8},{24,0},{1,25},{9,17},{17,9},{25,1},{2,26},{10... | collective-permute-start | bytes 933896 | tf_op jit(solution)/shard_map/ppermute | solution.py:61
  115.6 15.9 %collective-permute-start.21 = (bf16[152,1024]{1,0:T(8,128)(2,1)S(1)}, bf16[152,1024]{1,0:T(8,128)(2,1)S(1)}, u32[]{:S(2)}, u32[]{:S(2)}) collective-permute-start(bf16[152,1024]{1,0:T(8,128)(2,1)S(1)} %get-tuple-element.198), channel_id=1, source_target_pairs={{0,16},{8,24},{16,0},{24,8},{1,17},{9,25},{17,1},{25,9},{2,18},{10... | collective-permute-start | bytes 933896 | tf_op jit(solution)/shard_map/ppermute | solution.py:61
  116.8 14.7 %collective-permute-start.22 = (bf16[152,1024]{1,0:T(8,128)(2,1)S(1)}, bf16[152,1024]{1,0:T(8,128)(2,1)S(1)}, u32[]{:S(2)}, u32[]{:S(2)}) collective-permute-start(bf16[152,1024]{1,0:T(8,128)(2,1)S(1)} %get-tuple-element.199), channel_id=1, source_target_pairs={{0,24},{8,16},{16,8},{24,0},{1,25},{9,17},{17,9},{25,1},{2,26},{10... | collective-permute-start | bytes 933896 | tf_op jit(solution)/shard_map/ppermute | solution.py:61
  118.3 14.4 %collective-permute-start.20 = (bf16[152,1024]{1,0:T(8,128)(2,1)S(1)}, bf16[152,1024]{1,0:T(8,128)(2,1)S(1)}, u32[]{:S(2)}, u32[]{:S(2)}) collective-permute-start(bf16[152,1024]{1,0:T(8,128)(2,1)S(1)} %get-tuple-element.197.refs_2_), channel_id=1, source_target_pairs={{0,8},{8,0},{16,24},{24,16},{1,9},{9,1},{17,25},{25,17},{2,10},{10... | collective-permute-start | bytes 933896 | tf_op jit(solution)/shard_map/ppermute | solution.py:61
  134.7 13.4 %collective-permute-start.25 = (bf16[152,1024]{1,0:T(8,128)(2,1)S(1)}, bf16[152,1024]{1,0:T(8,128)(2,1)S(1)}, u32[]{:S(2)}, u32[]{:S(2)}) collective-permute-start(bf16[152,1024]{1,0:T(8,128)(2,1)S(1)} %get-tuple-element.201.refs_1_), channel_id=1, source_target_pairs={{0,16},{8,24},{16,0},{24,8},{1,17},{9,25},{17,1},{25,9},{2,18},{10... | collective-permute-start | bytes 933896 | tf_op jit(solution)/shard_map/ppermute | solution.py:61
  136.1 16.6 %collective-permute-start.27 = (bf16[152,1024]{1,0:T(8,128)(2,1)S(1)}, bf16[152,1024]{1,0:T(8,128)(2,1)S(1)}, u32[]{:S(2)}, u32[]{:S(2)}) collective-permute-start(bf16[152,1024]{1,0:T(8,128)(2,1)S(1)} %get-tuple-element.201.refs_1_), channel_id=1, source_target_pairs={{0,24},{8,16},{16,8},{24,0},{1,25},{9,17},{17,9},{25,1},{2,26},{10... | collective-permute-start | bytes 933896 | tf_op jit(solution)/shard_map/ppermute | solution.py:61
  150.3 13.9 %collective-permute-start.26 = (bf16[152,1024]{1,0:T(8,128)(2,1)S(1)}, bf16[152,1024]{1,0:T(8,128)(2,1)S(1)}, u32[]{:S(2)}, u32[]{:S(2)}) collective-permute-start(bf16[152,1024]{1,0:T(8,128)(2,1)S(1)} %get-tuple-element.206), channel_id=1, source_target_pairs={{0,16},{8,24},{16,0},{24,8},{1,17},{9,25},{17,1},{25,9},{2,18},{10... | collective-permute-start | bytes 933896 | tf_op jit(solution)/shard_map/ppermute | solution.py:61
  167.9 15.2 %collective-permute-start.29 = (bf16[152,1024]{1,0:T(8,128)(2,1)}, bf16[152,1024]{1,0:T(8,128)(2,1)S(1)}, u32[]{:S(2)}, u32[]{:S(2)}) collective-permute-start(bf16[152,1024]{1,0:T(8,128)(2,1)} %copy-done.92), channel_id=1, source_target_pairs={{0,24},{8,16},{16,8},{24,0},{1,25},{9,17},{17,9},{25,1},{2,26},{10... | collective-permute-start | bytes 933896 | tf_op jit(solution)/shard_map/ppermute | solution.py:61
  178.8 14.7 %collective-permute-start.33 = (bf16[152,1024]{1,0:T(8,128)(2,1)}, bf16[152,1024]{1,0:T(8,128)(2,1)}, u32[]{:S(2)}, u32[]{:S(2)}) collective-permute-start(bf16[152,1024]{1,0:T(8,128)(2,1)} %get-tuple-element.221), channel_id=1, source_target_pairs={{0,8},{8,0},{16,24},{24,16},{1,9},{9,1},{17,25},{25,17},{2,10},{10... | collective-permute-start | bytes 933896 | tf_op jit(solution)/shard_map/ppermute | solution.py:61
  181.6 13.2 %collective-permute-start.34 = (bf16[152,1024]{1,0:T(8,128)(2,1)}, bf16[152,1024]{1,0:T(8,128)(2,1)}, u32[]{:S(2)}, u32[]{:S(2)}) collective-permute-start(bf16[152,1024]{1,0:T(8,128)(2,1)} %get-tuple-element.222), channel_id=1, source_target_pairs={{0,16},{8,24},{16,0},{24,8},{1,17},{9,25},{17,1},{25,9},{2,18},{10... | collective-permute-start | bytes 933896 | tf_op jit(solution)/shard_map/ppermute | solution.py:61
  194.9 79.1 %reduce-scatter.7.cloned.1.call-start = ((), (), s32[]{:S(2)}) async-start(), calls=%async_computation.5 | async-start | bytes 1310720 | tf_op jit(solution)/shard_map/reduce_scatter | solution.py:1098
  199.2 13.3 %collective-permute-start.36 = (bf16[152,1024]{1,0:T(8,128)(2,1)}, bf16[152,1024]{1,0:T(8,128)(2,1)S(1)}, u32[]{:S(2)}, u32[]{:S(2)}) collective-permute-start(bf16[152,1024]{1,0:T(8,128)(2,1)} %get-tuple-element.238.refs_1_.refs_13_), channel_id=1, source_target_pairs={{0,16},{8,24},{16,0},{24,8},{1,17},{9,25},{17,1},{25,9},{2,18},{10... | collective-permute-start | bytes 933896 | tf_op jit(solution)/shard_map/ppermute | solution.py:61
  200.6 16.2 %collective-permute-start.35 = (bf16[152,1024]{1,0:T(8,128)(2,1)}, bf16[152,1024]{1,0:T(8,128)(2,1)S(1)}, u32[]{:S(2)}, u32[]{:S(2)}) collective-permute-start(bf16[152,1024]{1,0:T(8,128)(2,1)} %get-tuple-element.238.refs_1_.refs_13_), channel_id=1, source_target_pairs={{0,24},{8,16},{16,8},{24,0},{1,25},{9,17},{17,9},{25,1},{2,26},{10... | collective-permute-start | bytes 933896 | tf_op jit(solution)/shard_map/ppermute | solution.py:61
  229.7 94.2 %reduce-scatter.11.cloned.1.call-start = ((), (), s32[]{:S(2)}) async-start(), calls=%async_computation.7 | async-start | bytes 4718592 | tf_op jit(solution)/shard_map/reduce_scatter | solution.py:1035
  233.2 18.7 %collective-permute-start.47 = (bf16[152,1024]{1,0:T(8,128)(2,1)}, bf16[152,1024]{1,0:T(8,128)(2,1)}, u32[]{:S(2)}, u32[]{:S(2)}) collective-permute-start(bf16[152,1024]{1,0:T(8,128)(2,1)} %get-tuple-element.267.refs_0_.refs_12_), channel_id=1, source_target_pairs={{0,8},{8,0},{16,24},{24,16},{1,9},{9,1},{17,25},{25,17},{2,10},{10... | collective-permute-start | bytes 933896 | tf_op jit(solution)/shard_map/ppermute | solution.py:61
  235.6 20.9 %collective-permute-start.46 = (bf16[152,1024]{1,0:T(8,128)(2,1)}, bf16[152,1024]{1,0:T(8,128)(2,1)}, u32[]{:S(2)}, u32[]{:S(2)}) collective-permute-start(bf16[152,1024]{1,0:T(8,128)(2,1)} %get-tuple-element.267.refs_0_.refs_12_), channel_id=1, source_target_pairs={{0,16},{8,24},{16,0},{24,8},{1,17},{9,25},{17,1},{25,9},{2,18},{10... | collective-permute-start | bytes 933896 | tf_op jit(solution)/shard_map/ppermute | solution.py:61
  237.0 24.3 %collective-permute-start.45 = (bf16[152,1024]{1,0:T(8,128)(2,1)}, bf16[152,1024]{1,0:T(8,128)(2,1)}, u32[]{:S(2)}, u32[]{:S(2)}) collective-permute-start(bf16[152,1024]{1,0:T(8,128)(2,1)} %get-tuple-element.267.refs_0_.refs_12_), channel_id=1, source_target_pairs={{0,24},{8,16},{16,8},{24,0},{1,25},{9,17},{17,9},{25,1},{2,26},{10... | collective-permute-start | bytes 933896 | tf_op jit(solution)/shard_map/ppermute | solution.py:61
  255.1 16.8 %collective-permute-start.49 = (bf16[152,1024]{1,0:T(8,128)(2,1)}, bf16[152,1024]{1,0:T(8,128)(2,1)}, u32[]{:S(2)}, u32[]{:S(2)}) collective-permute-start(bf16[152,1024]{1,0:T(8,128)(2,1)} %get-tuple-element.274), channel_id=1, source_target_pairs={{0,8},{8,0},{16,24},{24,16},{1,9},{9,1},{17,25},{25,17},{2,10},{10... | collective-permute-start | bytes 933896 | tf_op jit(solution)/shard_map/ppermute | solution.py:61
  259.8 13.9 %collective-permute-start.50 = (bf16[152,1024]{1,0:T(8,128)(2,1)}, bf16[152,1024]{1,0:T(8,128)(2,1)}, u32[]{:S(2)}, u32[]{:S(2)}) collective-permute-start(bf16[152,1024]{1,0:T(8,128)(2,1)} %get-tuple-element.275), channel_id=1, source_target_pairs={{0,16},{8,24},{16,0},{24,8},{1,17},{9,25},{17,1},{25,9},{2,18},{10... | collective-permute-start | bytes 933896 | tf_op jit(solution)/shard_map/ppermute | solution.py:61
  273.7 90.6 %reduce-scatter.9.cloned.1.call-start = ((), (), s32[]{:S(2)}) async-start(), calls=%async_computation.6 | async-start | bytes 2949120 | tf_op jit(solution)/shard_map/reduce_scatter | solution.py:1035
  275.1 40.6 %collective-permute-start.58 = (bf16[384,1024]{1,0:T(8,128)(2,1)S(1)}, bf16[384,1024]{1,0:T(8,128)(2,1)S(1)}, u32[]{:S(2)}, u32[]{:S(2)}) collective-permute-start(bf16[384,1024]{1,0:T(8,128)(2,1)S(1)} %pad_maximum_fusion.refs_4_.refs_1_), channel_id=1, source_target_pairs={{0,16},{8,24},{16,0},{24,8},{1,17},{9,25},{17,1},{25,9},{2,18},{10... | collective-permute-start | bytes 2359304 | tf_op jit(solution)/shard_map/ppermute | solution.py:61
  276.6 39.1 %collective-permute-start.57 = (bf16[384,1024]{1,0:T(8,128)(2,1)S(1)}, bf16[384,1024]{1,0:T(8,128)(2,1)S(1)}, u32[]{:S(2)}, u32[]{:S(2)}) collective-permute-start(bf16[384,1024]{1,0:T(8,128)(2,1)S(1)} %pad_maximum_fusion.refs_4_.refs_1_), channel_id=1, source_target_pairs={{0,8},{8,0},{16,24},{24,16},{1,9},{9,1},{17,25},{25,17},{2,10},{10... | collective-permute-start | bytes 2359304 | tf_op jit(solution)/shard_map/ppermute | solution.py:61
  280.3 23.5 %collective-permute-start.53 = (bf16[152,1024]{1,0:T(8,128)(2,1)}, bf16[152,1024]{1,0:T(8,128)(2,1)S(1)}, u32[]{:S(2)}, u32[]{:S(2)}) collective-permute-start(bf16[152,1024]{1,0:T(8,128)(2,1)} %get-tuple-element.286.refs_1_.refs_12_), channel_id=1, source_target_pairs={{0,8},{8,0},{16,24},{24,16},{1,9},{9,1},{17,25},{25,17},{2,10},{10... | collective-permute-start | bytes 933896 | tf_op jit(solution)/shard_map/ppermute | solution.py:61
  281.8 25.4 %collective-permute-start.52 = (bf16[152,1024]{1,0:T(8,128)(2,1)}, bf16[152,1024]{1,0:T(8,128)(2,1)S(1)}, u32[]{:S(2)}, u32[]{:S(2)}) collective-permute-start(bf16[152,1024]{1,0:T(8,128)(2,1)} %get-tuple-element.286.refs_1_.refs_12_), channel_id=1, source_target_pairs={{0,16},{8,24},{16,0},{24,8},{1,17},{9,25},{17,1},{25,9},{2,18},{10... | collective-permute-start | bytes 933896 | tf_op jit(solution)/shard_map/ppermute | solution.py:61
  282.3 28.2 %collective-permute-start.51 = (bf16[152,1024]{1,0:T(8,128)(2,1)}, bf16[152,1024]{1,0:T(8,128)(2,1)S(1)}, u32[]{:S(2)}, u32[]{:S(2)}) collective-permute-start(bf16[152,1024]{1,0:T(8,128)(2,1)} %get-tuple-element.286.refs_1_.refs_12_), channel_id=1, source_target_pairs={{0,24},{8,16},{16,8},{24,0},{1,25},{9,17},{17,9},{25,1},{2,26},{10... | collective-permute-start | bytes 933896 | tf_op jit(solution)/shard_map/ppermute | solution.py:61
  323.9 15.1 %collective-permute-start.60 = (bf16[256,1024]{1,0:T(8,128)(2,1)}, bf16[256,1024]{1,0:T(8,128)(2,1)S(1)}, u32[]{:S(2)}, u32[]{:S(2)}) collective-permute-start(bf16[256,1024]{1,0:T(8,128)(2,1)} %bitcast.67), channel_id=1, source_target_pairs={{0,16},{8,24},{16,0},{24,8},{1,17},{9,25},{17,1},{25,9},{2,18},{10... | collective-permute-start | bytes 1572872 | tf_op jit(solution)/shard_map/ppermute | solution.py:61
  325.3 15.1 %collective-permute-start.59 = (bf16[256,1024]{1,0:T(8,128)(2,1)}, bf16[256,1024]{1,0:T(8,128)(2,1)S(1)}, u32[]{:S(2)}, u32[]{:S(2)}) collective-permute-start(bf16[256,1024]{1,0:T(8,128)(2,1)} %bitcast.68), channel_id=1, source_target_pairs={{0,8},{8,0},{16,24},{24,16},{1,9},{9,1},{17,25},{25,17},{2,10},{10... | collective-permute-start | bytes 1572872 | tf_op jit(solution)/shard_map/ppermute | solution.py:61
  326.8 22.0 %collective-permute-start.64 = (bf16[192,1024]{1,0:T(8,128)(2,1)S(1)}, bf16[192,1024]{1,0:T(8,128)(2,1)S(1)}, u32[]{:S(2)}, u32[]{:S(2)}) collective-permute-start(bf16[192,1024]{1,0:T(8,128)(2,1)S(1)} %slice.55), channel_id=1, source_target_pairs={{0,8},{8,0},{16,24},{24,16},{1,9},{9,1},{17,25},{25,17},{2,10},{10... | collective-permute-start | bytes 1179656 | tf_op jit(solution)/shard_map/ppermute | solution.py:61
  327.5 22.8 %collective-permute-start.63 = (bf16[192,1024]{1,0:T(8,128)(2,1)S(1)}, bf16[192,1024]{1,0:T(8,128)(2,1)S(1)}, u32[]{:S(2)}, u32[]{:S(2)}) collective-permute-start(bf16[192,1024]{1,0:T(8,128)(2,1)S(1)} %slice.54), channel_id=1, source_target_pairs={{0,16},{8,24},{16,0},{24,8},{1,17},{9,25},{17,1},{25,9},{2,18},{10... | collective-permute-start | bytes 1179656 | tf_op jit(solution)/shard_map/ppermute | solution.py:61
  334.1 21.4 %collective-permute-start.66 = (bf16[152,1024]{1,0:T(8,128)(2,1)S(1)}, bf16[152,1024]{1,0:T(8,128)(2,1)S(1)}, u32[]{:S(2)}, u32[]{:S(2)}) collective-permute-start(bf16[152,1024]{1,0:T(8,128)(2,1)S(1)} %get-tuple-element.319), channel_id=1, source_target_pairs={{0,8},{8,0},{16,24},{24,16},{1,9},{9,1},{17,25},{25,17},{2,10},{10... | collective-permute-start | bytes 933896 | tf_op jit(solution)/shard_map/ppermute | solution.py:61
  339.1 19.6 %collective-permute-start.67 = (bf16[152,1024]{1,0:T(8,128)(2,1)S(1)}, bf16[152,1024]{1,0:T(8,128)(2,1)S(1)}, u32[]{:S(2)}, u32[]{:S(2)}) collective-permute-start(bf16[152,1024]{1,0:T(8,128)(2,1)S(1)} %get-tuple-element.320), channel_id=1, source_target_pairs={{0,16},{8,24},{16,0},{24,8},{1,17},{9,25},{17,1},{25,9},{2,18},{10... | collective-permute-start | bytes 933896 | tf_op jit(solution)/shard_map/ppermute | solution.py:61
  340.4 20.4 %collective-permute-start.68 = (bf16[152,1024]{1,0:T(8,128)(2,1)S(1)}, bf16[152,1024]{1,0:T(8,128)(2,1)S(1)}, u32[]{:S(2)}, u32[]{:S(2)}) collective-permute-start(bf16[152,1024]{1,0:T(8,128)(2,1)S(1)} %get-tuple-element.321), channel_id=1, source_target_pairs={{0,24},{8,16},{16,8},{24,0},{1,25},{9,17},{17,9},{25,1},{2,26},{10... | collective-permute-start | bytes 933896 | tf_op jit(solution)/shard_map/ppermute | solution.py:61
  348.8 15.4 %collective-permute-start.62 = (bf16[128,1024]{1,0:T(8,128)(2,1)}, bf16[128,1024]{1,0:T(8,128)(2,1)S(1)}, u32[]{:S(2)}, u32[]{:S(2)}) collective-permute-start(bf16[128,1024]{1,0:T(8,128)(2,1)} %slice.53), channel_id=1, source_target_pairs={{0,8},{8,0},{16,24},{24,16},{1,9},{9,1},{17,25},{25,17},{2,10},{10... | collective-permute-start | bytes 786440 | tf_op jit(solution)/shard_map/ppermute | solution.py:61
  350.3 14.0 %collective-permute-start.61 = (bf16[128,1024]{1,0:T(8,128)(2,1)S(1)}, bf16[128,1024]{1,0:T(8,128)(2,1)}, u32[]{:S(2)}, u32[]{:S(2)}) collective-permute-start(bf16[128,1024]{1,0:T(8,128)(2,1)S(1)} %slice.52), channel_id=1, source_target_pairs={{0,16},{8,24},{16,0},{24,8},{1,17},{9,25},{17,1},{25,9},{2,18},{10... | collective-permute-start | bytes 786440 | tf_op jit(solution)/shard_map/ppermute | solution.py:61
  366.7 13.8 %collective-permute-start.70 = (bf16[160,1024]{1,0:T(8,128)(2,1)}, bf16[160,1024]{1,0:T(8,128)(2,1)S(1)}, u32[]{:S(2)}, u32[]{:S(2)}) collective-permute-start(bf16[160,1024]{1,0:T(8,128)(2,1)} %bitcast.63), channel_id=1, source_target_pairs={{0,16},{8,24},{16,0},{24,8},{1,17},{9,25},{17,1},{25,9},{2,18},{10... | collective-permute-start | bytes 983048 | tf_op jit(solution)/shard_map/ppermute | solution.py:61
  367.3 13.3 %collective-permute-start.69 = (bf16[160,1024]{1,0:T(8,128)(2,1)}, bf16[160,1024]{1,0:T(8,128)(2,1)S(1)}, u32[]{:S(2)}, u32[]{:S(2)}) collective-permute-start(bf16[160,1024]{1,0:T(8,128)(2,1)} %bitcast.64), channel_id=1, source_target_pairs={{0,8},{8,0},{16,24},{24,16},{1,9},{9,1},{17,25},{25,17},{2,10},{10... | collective-permute-start | bytes 983048 | tf_op jit(solution)/shard_map/ppermute | solution.py:61
  (151 other events, 1117.8 us)
Sparse Core Ops, SparseCore 0:
  14.0 49.7 all-gather.6
  65.9 45.8 all-gather.8
  114.0 45.8 all-gather.10
  195.0 48.1 reduce-scatter.4
  245.9 25.2 reduce-scatter.6
  274.1 49.0 reduce-scatter.10
  325.6 37.4 reduce-scatter.8

commit v7 on v6

--- a/solution.py
+++ b/solution.py
@@ -1061,8 +1061,14 @@
             [None] * 8 + [None if top else first_half] * 4 + [None] * 4,
             scratch=[VMEM((tall, width), BF16)] * 2,
         )
-        es, term = tie_last(es, term)
-        homes_m[depth] = home(term)
+        if top:
+            near, term = tie(es[:3], term)
+            homes_m[depth] = home(term)
+            far, near, _ = tie(es[3], near, term)
+            es = near + [far]
+        else:
+            es, term = tie_last(es, term)
+            homes_m[depth] = home(term)
         d_middle, low = call(add_norm_backward, normed, [gradient] + es + [middle], limit=60)
         if not top:
             m, a = homes_m[1], homes_a[1]

time: 397 us -> 396 us (level)
    reduce_scatter x3, waiting for transfers between devices: 6.16 us -> 0.26 us  [home(): return lax.psum_scatter(term, 'fsdp', scatter_dimension=0, tiled=False)]
    ppermute x62, waiting for transfers between devices: 94.3 us -> 100 us  [swap(): return lax.ppermute(block, 'dp', [(i, i ^ k) for i in range(self.count)])]
    unnamed x240 -> x242, local copies, waits for them, and re-layouts: 45.6 us -> 46.4 us
  transfers between devices with their start and end apart: 80 -> 80, of which waited for: 34 -> 33; matrix products, arithmetic and copies ran while one was open for 1% -> 1% of each run, Pallas kernels for 29% -> 28%
where the time goes in v7:
time: 396 us; the launch traced here: 392 us
  waiting for transfers between devices  122 us (31%)
  Pallas kernels  117 us (30%)
  starting transfers between devices  82.1 us (21%)
  local copies, waits for them, and re-layouts  50.6 us (13%)
  between operations  17.9 us (5%)
    pallas_call x56, Pallas kernels, call(): pl.pallas_call(run, name=name, grid=(1,), in_specs=specs, out_specs=out_s...  117 us
    ppermute x62, waiting for transfers between devices, swap(): return lax.ppermute(block, 'dp', [(i, i ^ k) for i in range(self.count)])  100 us
    ppermute x62, starting transfers between devices, swap(): return lax.ppermute(block, 'dp', [(i, i ^ k) for i in range(self.count)])  73.3 us
    unnamed x242, local copies, waits for them, and re-layouts  46.4 us
    all_gather x3, waiting for transfers between devices, fetch(): return lax.all_gather(packed, 'fsdp', axis=0, tiled=False)  14.5 us
  transfers between devices with their start and end apart: 80, of which 33 were waited for; matrix products, arithmetic and copies ran while one was open for 1% of the time, Pallas kernels for 28%

profile of v7, /device:TPU:0, one launch (start us, length us, event | category | flops | bytes accessed | tf_op | source)
XLA Modules:
  0.0 391.7 jit_solution(7224435204078466043)
XLA Ops:
  11.0 2.8 prepare_first.1
  15.2 5.0 %collective-permute-start.3 = (bf16[40,256]{1,0:T(8,128)(2,1)S(1)}, bf16[40,256]{1,0:T(8,128)(2,1)S(1)}, u32[]{:S(2)}, u32[]{:S(2)}) collective-permute-start(bf16[40,256]{1,0:T(8,128)(2,1)S(1)} %pad_maximum_fusion.1.refs_1_), channel_id=1, source_target_pairs={{0,6},{1,7},{2,4},{3,5},{4,2},{5,3},{6,0},{7,1},{8,14},{9,15},{10,... | collective-permute-start | bytes 61448 | tf_op jit(solution)/shard_map/ppermute | solution.py:873
  22.0 2.9 collective-permute-done.2.refs_3_
  24.9 2.5 collective-permute-start.6
  34.2 3.0 prepare_second.1
  37.3 2.7 prepare_third.1
  49.3 14.5 %all-gather.7.cloned.1.call-done = bf16[2048,1024]{1,0:T(8,128)(2,1)} async-done(((bf16[256,1024]{1,0:T(8,128)(2,1)}), bf16[2048,1024]{1,0:T(8,128)(2,1)}) %all-gather.7.cloned.1.call-update) | async-done | bytes 4194320 | tf_op jit(solution)/shard_map/all_gather | solution.py:895
  82.5 2.7 collective-permute-done.9.refs_2_
  85.2 6.9 %collective-permute-done.13.refs_4_ = bf16[152,1024]{1,0:T(8,128)(2,1)S(1)} collective-permute-done((bf16[152,1024]{1,0:T(8,128)(2,1)S(1)}, bf16[152,1024]{1,0:T(8,128)(2,1)S(1)}, u32[]{:S(2)}, u32[]{:S(2)}) %collective-permute-start.13) | collective-permute-done | bytes 311328 | tf_op jit(solution)/shard_map/ppermute | solution.py:61
  97.5 6.1 %collective-permute-done.17.refs_0_.refs_1_ = bf16[152,1024]{1,0:T(8,128)(2,1)S(1)} collective-permute-done((bf16[152,1024]{1,0:T(8,128)(2,1)S(1)}, bf16[152,1024]{1,0:T(8,128)(2,1)S(1)}, u32[]{:S(2)}, u32[]{:S(2)}) %collective-permute-start.17) | collective-permute-done | bytes 311328 | tf_op jit(solution)/shard_map/ppermute | solution.py:61
  104.3 5.6 %collective-permute-done.18.refs_0_.refs_2_ = bf16[152,1024]{1,0:T(8,128)(2,1)S(1)} collective-permute-done((bf16[152,1024]{1,0:T(8,128)(2,1)S(1)}, bf16[152,1024]{1,0:T(8,128)(2,1)S(1)}, u32[]{:S(2)}, u32[]{:S(2)}) %collective-permute-start.18) | collective-permute-done | bytes 311328 | tf_op jit(solution)/shard_map/ppermute | solution.py:61
  119.6 11.8 %collective-permute-done.21.refs_3_ = bf16[152,1024]{1,0:T(8,128)(2,1)S(1)} collective-permute-done((bf16[152,1024]{1,0:T(8,128)(2,1)S(1)}, bf16[152,1024]{1,0:T(8,128)(2,1)S(1)}, u32[]{:S(2)}, u32[]{:S(2)}) %collective-permute-start.21) | collective-permute-done | bytes 311328 | tf_op jit(solution)/shard_map/ppermute | solution.py:61
  138.8 4.6 %collective-permute-done.23.refs_1_.refs_2_ = bf16[152,1024]{1,0:T(8,128)(2,1)S(1)} collective-permute-done((bf16[152,1024]{1,0:T(8,128)(2,1)S(1)}, bf16[152,1024]{1,0:T(8,128)(2,1)S(1)}, u32[]{:S(2)}, u32[]{:S(2)}) %collective-permute-start.23) | collective-permute-done | bytes 311328 | tf_op jit(solution)/shard_map/ppermute | solution.py:61
  143.4 2.6 attention_forward.13
  156.3 7.9 %collective-permute-done.26.refs_3_ = bf16[152,1024]{1,0:T(8,128)(2,1)S(1)} collective-permute-done((bf16[152,1024]{1,0:T(8,128)(2,1)S(1)}, bf16[152,1024]{1,0:T(8,128)(2,1)S(1)}, u32[]{:S(2)}, u32[]{:S(2)}) %collective-permute-start.26) | collective-permute-done | bytes 311328 | tf_op jit(solution)/shard_map/ppermute | solution.py:61
  176.3 2.5 mlp_both.5
  179.1 2.5 mlp_both.6
  185.6 3.5 grads_mlp.2
  193.8 6.4 %collective-permute-done.32.refs_4_ = bf16[152,1024]{1,0:T(8,128)(2,1)} collective-permute-done((bf16[152,1024]{1,0:T(8,128)(2,1)}, bf16[152,1024]{1,0:T(8,128)(2,1)}, u32[]{:S(2)}, u32[]{:S(2)}) %collective-permute-start.32) | collective-permute-done | bytes 311328 | tf_op jit(solution)/shard_map/ppermute | solution.py:61
  200.3 3.1 add_norm_backward.3
  210.2 2.7 attention_backward.8
  214.0 2.7 attention_backward.9
  218.8 2.8 attention_backward.10
  222.7 2.7 attention_backward.11
  229.1 4.1 %collective-permute-done.38.refs_5_.refs_4_ = bf16[152,1024]{1,0:T(8,128)(2,1)S(1)} collective-permute-done((bf16[152,1024]{1,0:T(8,128)(2,1)S(1)}, bf16[152,1024]{1,0:T(8,128)(2,1)S(1)}, u32[]{:S(2)}, u32[]{:S(2)}) %collective-permute-start.38) | collective-permute-done | bytes 311328 | tf_op jit(solution)/shard_map/ppermute | solution.py:61
  235.6 3.2 add_norm_backward.4
  250.9 3.2 mlp_backward.5
  254.3 3.2 mlp_backward.6
  258.6 3.3 mlp_backward.7
  264.3 4.6 %grads_mlp.3 = bf16[8,256,1024]{2,1,0:T(8,128)(2,1)S(1)} custom-call(bf16[152,1024]{1,0:T(8,128)(2,1)S(1)} %copy-done.63, bf16[152,1024]{1,0:T(8,128)(2,1)S(1)} %copy-done.65, bf16[152,1024]{1,0:T(8,128)(2,1)S(1)} %copy-done.67, bf16[152,1024]{1,0:T(8,128)(2,1)S(1)} %copy-done.69, bf16[152,1024]{1,0:T(8,128)(2,1)S(1)} %get-tuple-element.267.refs_4_, ...), custom_call_target="tpu_custom_call" | custom-call | bytes 4194304 | tf_op jit(solution)/shard_map/grads_mlp/pallas_call | solution.py:397
  275.8 3.1 add_norm_backward.5
  285.6 2.8 attention_backward.12
  288.3 13.4 %collective-permute-done.53.refs_1_.refs_13_ = bf16[152,1024]{1,0:T(8,128)(2,1)S(1)} collective-permute-done((bf16[152,1024]{1,0:T(8,128)(2,1)}, bf16[152,1024]{1,0:T(8,128)(2,1)S(1)}, u32[]{:S(2)}, u32[]{:S(2)}) %collective-permute-start.53) | collective-permute-done | bytes 311328 | tf_op jit(solution)/shard_map/ppermute | solution.py:61
  301.8 2.7 attention_backward.13
  305.8 2.8 attention_backward.14
  309.7 2.7 attention_backward.15
  313.8 3.4 grads_attention.1.refs_7_
  317.2 3.0 collective-permute-done.54.refs_4_
  320.3 2.5 last_norm.1
  334.8 3.4 collective-permute-done.60.refs_3_
  341.9 6.2 %collective-permute-done.64.refs_5_ = bf16[192,1024]{1,0:T(8,128)(2,1)S(1)} collective-permute-done((bf16[192,1024]{1,0:T(8,128)(2,1)S(1)}, bf16[192,1024]{1,0:T(8,128)(2,1)S(1)}, u32[]{:S(2)}, u32[]{:S(2)}) %collective-permute-start.64) | collective-permute-done | bytes 393248 | tf_op jit(solution)/shard_map/ppermute | solution.py:61
  351.0 3.7 collective-permute-done.66.refs_2_
  354.8 3.1 finish_mlp.2
  358.0 2.7 collective-permute-done.68.refs_4_
  361.7 2.5 finish_attention.2
  370.9 3.5 finish_mlp.3
  376.1 3.8 collective-permute-done.70.refs_3_
  381.9 2.5 finish_attention.3
  (435 shorter events, 173.8 us)
Async XLA Ops:
  7.2 56.6 %all-gather.7.cloned.1.call-start = ((), (), s32[]{:S(2)}) async-start(), calls=%async_computation.8 | async-start | bytes 4718592 | tf_op jit(solution)/shard_map/all_gather | solution.py:895
  13.8 98.3 %all-gather.9.cloned.1.call-start = ((), (), s32[]{:S(2)}) async-start(), calls=%async_computation.9 | async-start | bytes 4718592 | tf_op jit(solution)/shard_map/all_gather | solution.py:895
  37.2 128.9 %all-gather.11.cloned.1.call-start = ((), (), s32[]{:S(2)}) async-start(), calls=%async_computation.10 | async-start | bytes 4718592 | tf_op jit(solution)/shard_map/all_gather | solution.py:895
  40.0 202.2 %reduce-scatter.5.cloned.1.call-start = ((), (), s32[]{:S(2)}) async-start(), calls=%async_computation.4 | async-start | bytes 4718592 | tf_op jit(solution)/shard_map/reduce_scatter | solution.py:1035
  42.8 32.2 %collective-permute-start.12 = (bf16[152,1024]{1,0:T(8,128)(2,1)S(1)}, bf16[152,1024]{1,0:T(8,128)(2,1)S(1)}, u32[]{:S(2)}, u32[]{:S(2)}) collective-permute-start(bf16[152,1024]{1,0:T(8,128)(2,1)S(1)} %copy-done.22), channel_id=1, source_target_pairs={{0,24},{8,16},{16,8},{24,0},{1,25},{9,17},{17,9},{25,1},{2,26},{10... | collective-permute-start | bytes 933896 | tf_op jit(solution)/shard_map/ppermute | solution.py:61
  44.3 27.8 %collective-permute-start.10 = (bf16[152,1024]{1,0:T(8,128)(2,1)S(1)}, bf16[152,1024]{1,0:T(8,128)(2,1)S(1)}, u32[]{:S(2)}, u32[]{:S(2)}) collective-permute-start(bf16[152,1024]{1,0:T(8,128)(2,1)S(1)} %copy-done.22), channel_id=1, source_target_pairs={{0,16},{8,24},{16,0},{24,8},{1,17},{9,25},{17,1},{25,9},{2,18},{10... | collective-permute-start | bytes 933896 | tf_op jit(solution)/shard_map/ppermute | solution.py:61
  44.8 23.4 %collective-permute-start.8 = (bf16[152,1024]{1,0:T(8,128)(2,1)S(1)}, bf16[152,1024]{1,0:T(8,128)(2,1)S(1)}, u32[]{:S(2)}, u32[]{:S(2)}) collective-permute-start(bf16[152,1024]{1,0:T(8,128)(2,1)S(1)} %copy-done.22), channel_id=1, source_target_pairs={{0,8},{8,0},{16,24},{24,16},{1,9},{9,1},{17,25},{25,17},{2,10},{10... | collective-permute-start | bytes 933896 | tf_op jit(solution)/shard_map/ppermute | solution.py:61
  47.3 33.0 %collective-permute-start.16 = (bf16[152,1024]{1,0:T(8,128)(2,1)S(1)}, bf16[152,1024]{1,0:T(8,128)(2,1)S(1)}, u32[]{:S(2)}, u32[]{:S(2)}) collective-permute-start(bf16[152,1024]{1,0:T(8,128)(2,1)S(1)} %get-tuple-element.214.refs_1_.refs_12_), channel_id=1, source_target_pairs={{0,24},{8,16},{16,8},{24,0},{1,25},{9,17},{17,9},{25,1},{2,26},{10... | collective-permute-start | bytes 933896 | tf_op jit(solution)/shard_map/ppermute | solution.py:61
  48.7 33.0 %collective-permute-start.15 = (bf16[152,1024]{1,0:T(8,128)(2,1)S(1)}, bf16[152,1024]{1,0:T(8,128)(2,1)S(1)}, u32[]{:S(2)}, u32[]{:S(2)}) collective-permute-start(bf16[152,1024]{1,0:T(8,128)(2,1)S(1)} %get-tuple-element.214.refs_1_.refs_12_), channel_id=1, source_target_pairs={{0,16},{8,24},{16,0},{24,8},{1,17},{9,25},{17,1},{25,9},{2,18},{10... | collective-permute-start | bytes 933896 | tf_op jit(solution)/shard_map/ppermute | solution.py:61
  68.3 13.5 %collective-permute-start.14 = (bf16[152,1024]{1,0:T(8,128)(2,1)S(1)}, bf16[152,1024]{1,0:T(8,128)(2,1)S(1)}, u32[]{:S(2)}, u32[]{:S(2)}) collective-permute-start(bf16[152,1024]{1,0:T(8,128)(2,1)S(1)} %get-tuple-element.214.refs_1_.refs_12_), channel_id=1, source_target_pairs={{0,8},{8,0},{16,24},{24,16},{1,9},{9,1},{17,25},{25,17},{2,10},{10... | collective-permute-start | bytes 933896 | tf_op jit(solution)/shard_map/ppermute | solution.py:61
  72.1 13.1 %collective-permute-start.9 = (bf16[152,1024]{1,0:T(8,128)(2,1)S(1)}, bf16[152,1024]{1,0:T(8,128)(2,1)S(1)}, u32[]{:S(2)}, u32[]{:S(2)}) collective-permute-start(bf16[152,1024]{1,0:T(8,128)(2,1)S(1)} %get-tuple-element.185), channel_id=1, source_target_pairs={{0,8},{8,0},{16,24},{24,16},{1,9},{9,1},{17,25},{25,17},{2,10},{10... | collective-permute-start | bytes 933896 | tf_op jit(solution)/shard_map/ppermute | solution.py:61
  94.8 15.2 %collective-permute-start.18 = (bf16[152,1024]{1,0:T(8,128)(2,1)S(1)}, bf16[152,1024]{1,0:T(8,128)(2,1)S(1)}, u32[]{:S(2)}, u32[]{:S(2)}) collective-permute-start(bf16[152,1024]{1,0:T(8,128)(2,1)S(1)} %get-tuple-element.195.refs_0_), channel_id=1, source_target_pairs={{0,16},{8,24},{16,0},{24,8},{1,17},{9,25},{17,1},{25,9},{2,18},{10... | collective-permute-start | bytes 933896 | tf_op jit(solution)/shard_map/ppermute | solution.py:61
  95.3 15.4 %collective-permute-start.19 = (bf16[152,1024]{1,0:T(8,128)(2,1)S(1)}, bf16[152,1024]{1,0:T(8,128)(2,1)S(1)}, u32[]{:S(2)}, u32[]{:S(2)}) collective-permute-start(bf16[152,1024]{1,0:T(8,128)(2,1)S(1)} %get-tuple-element.195.refs_0_), channel_id=1, source_target_pairs={{0,24},{8,16},{16,8},{24,0},{1,25},{9,17},{17,9},{25,1},{2,26},{10... | collective-permute-start | bytes 933896 | tf_op jit(solution)/shard_map/ppermute | solution.py:61
  115.5 15.9 %collective-permute-start.21 = (bf16[152,1024]{1,0:T(8,128)(2,1)S(1)}, bf16[152,1024]{1,0:T(8,128)(2,1)S(1)}, u32[]{:S(2)}, u32[]{:S(2)}) collective-permute-start(bf16[152,1024]{1,0:T(8,128)(2,1)S(1)} %get-tuple-element.197), channel_id=1, source_target_pairs={{0,16},{8,24},{16,0},{24,8},{1,17},{9,25},{17,1},{25,9},{2,18},{10... | collective-permute-start | bytes 933896 | tf_op jit(solution)/shard_map/ppermute | solution.py:61
  116.7 14.7 %collective-permute-start.22 = (bf16[152,1024]{1,0:T(8,128)(2,1)S(1)}, bf16[152,1024]{1,0:T(8,128)(2,1)S(1)}, u32[]{:S(2)}, u32[]{:S(2)}) collective-permute-start(bf16[152,1024]{1,0:T(8,128)(2,1)S(1)} %get-tuple-element.198), channel_id=1, source_target_pairs={{0,24},{8,16},{16,8},{24,0},{1,25},{9,17},{17,9},{25,1},{2,26},{10... | collective-permute-start | bytes 933896 | tf_op jit(solution)/shard_map/ppermute | solution.py:61
  118.2 14.5 %collective-permute-start.20 = (bf16[152,1024]{1,0:T(8,128)(2,1)S(1)}, bf16[152,1024]{1,0:T(8,128)(2,1)S(1)}, u32[]{:S(2)}, u32[]{:S(2)}) collective-permute-start(bf16[152,1024]{1,0:T(8,128)(2,1)S(1)} %get-tuple-element.196.refs_2_), channel_id=1, source_target_pairs={{0,8},{8,0},{16,24},{24,16},{1,9},{9,1},{17,25},{25,17},{2,10},{10... | collective-permute-start | bytes 933896 | tf_op jit(solution)/shard_map/ppermute | solution.py:61
  134.6 13.4 %collective-permute-start.25 = (bf16[152,1024]{1,0:T(8,128)(2,1)S(1)}, bf16[152,1024]{1,0:T(8,128)(2,1)S(1)}, u32[]{:S(2)}, u32[]{:S(2)}) collective-permute-start(bf16[152,1024]{1,0:T(8,128)(2,1)S(1)} %get-tuple-element.200.refs_1_), channel_id=1, source_target_pairs={{0,16},{8,24},{16,0},{24,8},{1,17},{9,25},{17,1},{25,9},{2,18},{10... | collective-permute-start | bytes 933896 | tf_op jit(solution)/shard_map/ppermute | solution.py:61
  136.0 16.6 %collective-permute-start.27 = (bf16[152,1024]{1,0:T(8,128)(2,1)S(1)}, bf16[152,1024]{1,0:T(8,128)(2,1)S(1)}, u32[]{:S(2)}, u32[]{:S(2)}) collective-permute-start(bf16[152,1024]{1,0:T(8,128)(2,1)S(1)} %get-tuple-element.200.refs_1_), channel_id=1, source_target_pairs={{0,24},{8,16},{16,8},{24,0},{1,25},{9,17},{17,9},{25,1},{2,26},{10... | collective-permute-start | bytes 933896 | tf_op jit(solution)/shard_map/ppermute | solution.py:61
  150.3 13.9 %collective-permute-start.26 = (bf16[152,1024]{1,0:T(8,128)(2,1)S(1)}, bf16[152,1024]{1,0:T(8,128)(2,1)S(1)}, u32[]{:S(2)}, u32[]{:S(2)}) collective-permute-start(bf16[152,1024]{1,0:T(8,128)(2,1)S(1)} %get-tuple-element.205), channel_id=1, source_target_pairs={{0,16},{8,24},{16,0},{24,8},{1,17},{9,25},{17,1},{25,9},{2,18},{10... | collective-permute-start | bytes 933896 | tf_op jit(solution)/shard_map/ppermute | solution.py:61
  166.1 13.0 %collective-permute-start.30 = (bf16[152,1024]{1,0:T(8,128)(2,1)}, bf16[152,1024]{1,0:T(8,128)(2,1)S(1)}, u32[]{:S(2)}, u32[]{:S(2)}) collective-permute-start(bf16[152,1024]{1,0:T(8,128)(2,1)} %copy-done.92), channel_id=1, source_target_pairs={{0,16},{8,24},{16,0},{24,8},{1,17},{9,25},{17,1},{25,9},{2,18},{10... | collective-permute-start | bytes 933896 | tf_op jit(solution)/shard_map/ppermute | solution.py:61
  167.8 15.2 %collective-permute-start.29 = (bf16[152,1024]{1,0:T(8,128)(2,1)}, bf16[152,1024]{1,0:T(8,128)(2,1)S(1)}, u32[]{:S(2)}, u32[]{:S(2)}) collective-permute-start(bf16[152,1024]{1,0:T(8,128)(2,1)} %copy-done.92), channel_id=1, source_target_pairs={{0,24},{8,16},{16,8},{24,0},{1,25},{9,17},{17,9},{25,1},{2,26},{10... | collective-permute-start | bytes 933896 | tf_op jit(solution)/shard_map/ppermute | solution.py:61
  178.8 13.0 %collective-permute-start.33 = (bf16[152,1024]{1,0:T(8,128)(2,1)}, bf16[152,1024]{1,0:T(8,128)(2,1)}, u32[]{:S(2)}, u32[]{:S(2)}) collective-permute-start(bf16[152,1024]{1,0:T(8,128)(2,1)} %get-tuple-element.220), channel_id=1, source_target_pairs={{0,8},{8,0},{16,24},{24,16},{1,9},{9,1},{17,25},{25,17},{2,10},{10... | collective-permute-start | bytes 933896 | tf_op jit(solution)/shard_map/ppermute | solution.py:61
  191.8 80.6 %reduce-scatter.7.cloned.1.call-start = ((), (), s32[]{:S(2)}) async-start(), calls=%async_computation.5 | async-start | bytes 1310720 | tf_op jit(solution)/shard_map/reduce_scatter | solution.py:1104
  205.5 13.3 %collective-permute-start.36 = (bf16[152,1024]{1,0:T(8,128)(2,1)}, bf16[152,1024]{1,0:T(8,128)(2,1)S(1)}, u32[]{:S(2)}, u32[]{:S(2)}) collective-permute-start(bf16[152,1024]{1,0:T(8,128)(2,1)} %get-tuple-element.237.refs_1_.refs_13_), channel_id=1, source_target_pairs={{0,16},{8,24},{16,0},{24,8},{1,17},{9,25},{17,1},{25,9},{2,18},{10... | collective-permute-start | bytes 933896 | tf_op jit(solution)/shard_map/ppermute | solution.py:61
  206.5 16.2 %collective-permute-start.35 = (bf16[152,1024]{1,0:T(8,128)(2,1)}, bf16[152,1024]{1,0:T(8,128)(2,1)S(1)}, u32[]{:S(2)}, u32[]{:S(2)}) collective-permute-start(bf16[152,1024]{1,0:T(8,128)(2,1)} %get-tuple-element.237.refs_1_.refs_13_), channel_id=1, source_target_pairs={{0,24},{8,16},{16,8},{24,0},{1,25},{9,17},{17,9},{25,1},{2,26},{10... | collective-permute-start | bytes 933896 | tf_op jit(solution)/shard_map/ppermute | solution.py:61
  235.3 87.8 %reduce-scatter.11.cloned.1.call-start = ((), (), s32[]{:S(2)}) async-start(), calls=%async_computation.7 | async-start | bytes 4718592 | tf_op jit(solution)/shard_map/reduce_scatter | solution.py:1035
  238.7 15.6 %collective-permute-start.46 = (bf16[152,1024]{1,0:T(8,128)(2,1)}, bf16[152,1024]{1,0:T(8,128)(2,1)}, u32[]{:S(2)}, u32[]{:S(2)}) collective-permute-start(bf16[152,1024]{1,0:T(8,128)(2,1)} %get-tuple-element.266.refs_0_.refs_12_), channel_id=1, source_target_pairs={{0,16},{8,24},{16,0},{24,8},{1,17},{9,25},{17,1},{25,9},{2,18},{10... | collective-permute-start | bytes 933896 | tf_op jit(solution)/shard_map/ppermute | solution.py:61
  239.8 18.8 %collective-permute-start.45 = (bf16[152,1024]{1,0:T(8,128)(2,1)}, bf16[152,1024]{1,0:T(8,128)(2,1)}, u32[]{:S(2)}, u32[]{:S(2)}) collective-permute-start(bf16[152,1024]{1,0:T(8,128)(2,1)} %get-tuple-element.266.refs_0_.refs_12_), channel_id=1, source_target_pairs={{0,24},{8,16},{16,8},{24,0},{1,25},{9,17},{17,9},{25,1},{2,26},{10... | collective-permute-start | bytes 933896 | tf_op jit(solution)/shard_map/ppermute | solution.py:61
  254.2 16.8 %collective-permute-start.49 = (bf16[152,1024]{1,0:T(8,128)(2,1)}, bf16[152,1024]{1,0:T(8,128)(2,1)}, u32[]{:S(2)}, u32[]{:S(2)}) collective-permute-start(bf16[152,1024]{1,0:T(8,128)(2,1)} %get-tuple-element.272), channel_id=1, source_target_pairs={{0,8},{8,0},{16,24},{24,16},{1,9},{9,1},{17,25},{25,17},{2,10},{10... | collective-permute-start | bytes 933896 | tf_op jit(solution)/shard_map/ppermute | solution.py:61
  257.6 14.5 %collective-permute-start.50 = (bf16[152,1024]{1,0:T(8,128)(2,1)}, bf16[152,1024]{1,0:T(8,128)(2,1)}, u32[]{:S(2)}, u32[]{:S(2)}) collective-permute-start(bf16[152,1024]{1,0:T(8,128)(2,1)} %get-tuple-element.273), channel_id=1, source_target_pairs={{0,16},{8,24},{16,0},{24,8},{1,17},{9,25},{17,1},{25,9},{2,18},{10... | collective-permute-start | bytes 933896 | tf_op jit(solution)/shard_map/ppermute | solution.py:61
  272.1 92.1 %reduce-scatter.9.cloned.1.call-start = ((), (), s32[]{:S(2)}) async-start(), calls=%async_computation.6 | async-start | bytes 2949120 | tf_op jit(solution)/shard_map/reduce_scatter | solution.py:1035
  273.5 40.2 %collective-permute-start.58 = (bf16[384,1024]{1,0:T(8,128)(2,1)S(1)}, bf16[384,1024]{1,0:T(8,128)(2,1)S(1)}, u32[]{:S(2)}, u32[]{:S(2)}) collective-permute-start(bf16[384,1024]{1,0:T(8,128)(2,1)S(1)} %pad_maximum_fusion.refs_4_.refs_1_), channel_id=1, source_target_pairs={{0,16},{8,24},{16,0},{24,8},{1,17},{9,25},{17,1},{25,9},{2,18},{10... | collective-permute-start | bytes 2359304 | tf_op jit(solution)/shard_map/ppermute | solution.py:61
  274.6 39.1 %collective-permute-start.57 = (bf16[384,1024]{1,0:T(8,128)(2,1)S(1)}, bf16[384,1024]{1,0:T(8,128)(2,1)S(1)}, u32[]{:S(2)}, u32[]{:S(2)}) collective-permute-start(bf16[384,1024]{1,0:T(8,128)(2,1)S(1)} %pad_maximum_fusion.refs_4_.refs_1_), channel_id=1, source_target_pairs={{0,8},{8,0},{16,24},{24,16},{1,9},{9,1},{17,25},{25,17},{2,10},{10... | collective-permute-start | bytes 2359304 | tf_op jit(solution)/shard_map/ppermute | solution.py:61
  278.9 22.8 %collective-permute-start.53 = (bf16[152,1024]{1,0:T(8,128)(2,1)}, bf16[152,1024]{1,0:T(8,128)(2,1)S(1)}, u32[]{:S(2)}, u32[]{:S(2)}) collective-permute-start(bf16[152,1024]{1,0:T(8,128)(2,1)} %get-tuple-element.284.refs_1_.refs_12_), channel_id=1, source_target_pairs={{0,8},{8,0},{16,24},{24,16},{1,9},{9,1},{17,25},{25,17},{2,10},{10... | collective-permute-start | bytes 933896 | tf_op jit(solution)/shard_map/ppermute | solution.py:61
  279.7 26.0 %collective-permute-start.52 = (bf16[152,1024]{1,0:T(8,128)(2,1)}, bf16[152,1024]{1,0:T(8,128)(2,1)S(1)}, u32[]{:S(2)}, u32[]{:S(2)}) collective-permute-start(bf16[152,1024]{1,0:T(8,128)(2,1)} %get-tuple-element.284.refs_1_.refs_12_), channel_id=1, source_target_pairs={{0,16},{8,24},{16,0},{24,8},{1,17},{9,25},{17,1},{25,9},{2,18},{10... | collective-permute-start | bytes 933896 | tf_op jit(solution)/shard_map/ppermute | solution.py:61
  280.7 28.9 %collective-permute-start.51 = (bf16[152,1024]{1,0:T(8,128)(2,1)}, bf16[152,1024]{1,0:T(8,128)(2,1)S(1)}, u32[]{:S(2)}, u32[]{:S(2)}) collective-permute-start(bf16[152,1024]{1,0:T(8,128)(2,1)} %get-tuple-element.284.refs_1_.refs_12_), channel_id=1, source_target_pairs={{0,24},{8,16},{16,8},{24,0},{1,25},{9,17},{17,9},{25,1},{2,26},{10... | collective-permute-start | bytes 933896 | tf_op jit(solution)/shard_map/ppermute | solution.py:61
  304.5 12.7 %collective-permute-start.55 = (bf16[152,1024]{1,0:T(8,128)(2,1)S(1)}, bf16[152,1024]{1,0:T(8,128)(2,1)S(1)}, u32[]{:S(2)}, u32[]{:S(2)}) collective-permute-start(bf16[152,1024]{1,0:T(8,128)(2,1)S(1)} %get-tuple-element.292), channel_id=1, source_target_pairs={{0,8},{8,0},{16,24},{24,16},{1,9},{9,1},{17,25},{25,17},{2,10},{10... | collective-permute-start | bytes 933896 | tf_op jit(solution)/shard_map/ppermute | solution.py:61
  323.1 15.1 %collective-permute-start.60 = (bf16[256,1024]{1,0:T(8,128)(2,1)}, bf16[256,1024]{1,0:T(8,128)(2,1)S(1)}, u32[]{:S(2)}, u32[]{:S(2)}) collective-permute-start(bf16[256,1024]{1,0:T(8,128)(2,1)} %bitcast.67), channel_id=1, source_target_pairs={{0,16},{8,24},{16,0},{24,8},{1,17},{9,25},{17,1},{25,9},{2,18},{10... | collective-permute-start | bytes 1572872 | tf_op jit(solution)/shard_map/ppermute | solution.py:61
  324.6 15.1 %collective-permute-start.59 = (bf16[256,1024]{1,0:T(8,128)(2,1)}, bf16[256,1024]{1,0:T(8,128)(2,1)S(1)}, u32[]{:S(2)}, u32[]{:S(2)}) collective-permute-start(bf16[256,1024]{1,0:T(8,128)(2,1)} %bitcast.68), channel_id=1, source_target_pairs={{0,8},{8,0},{16,24},{24,16},{1,9},{9,1},{17,25},{25,17},{2,10},{10... | collective-permute-start | bytes 1572872 | tf_op jit(solution)/shard_map/ppermute | solution.py:61
  326.1 22.0 %collective-permute-start.64 = (bf16[192,1024]{1,0:T(8,128)(2,1)S(1)}, bf16[192,1024]{1,0:T(8,128)(2,1)S(1)}, u32[]{:S(2)}, u32[]{:S(2)}) collective-permute-start(bf16[192,1024]{1,0:T(8,128)(2,1)S(1)} %slice.55), channel_id=1, source_target_pairs={{0,8},{8,0},{16,24},{24,16},{1,9},{9,1},{17,25},{25,17},{2,10},{10... | collective-permute-start | bytes 1179656 | tf_op jit(solution)/shard_map/ppermute | solution.py:61
  326.8 22.8 %collective-permute-start.63 = (bf16[192,1024]{1,0:T(8,128)(2,1)S(1)}, bf16[192,1024]{1,0:T(8,128)(2,1)S(1)}, u32[]{:S(2)}, u32[]{:S(2)}) collective-permute-start(bf16[192,1024]{1,0:T(8,128)(2,1)S(1)} %slice.54), channel_id=1, source_target_pairs={{0,16},{8,24},{16,0},{24,8},{1,17},{9,25},{17,1},{25,9},{2,18},{10... | collective-permute-start | bytes 1179656 | tf_op jit(solution)/shard_map/ppermute | solution.py:61
  333.2 21.6 %collective-permute-start.66 = (bf16[152,1024]{1,0:T(8,128)(2,1)S(1)}, bf16[152,1024]{1,0:T(8,128)(2,1)S(1)}, u32[]{:S(2)}, u32[]{:S(2)}) collective-permute-start(bf16[152,1024]{1,0:T(8,128)(2,1)S(1)} %get-tuple-element.317), channel_id=1, source_target_pairs={{0,8},{8,0},{16,24},{24,16},{1,9},{9,1},{17,25},{25,17},{2,10},{10... | collective-permute-start | bytes 933896 | tf_op jit(solution)/shard_map/ppermute | solution.py:61
  338.2 19.8 %collective-permute-start.67 = (bf16[152,1024]{1,0:T(8,128)(2,1)S(1)}, bf16[152,1024]{1,0:T(8,128)(2,1)S(1)}, u32[]{:S(2)}, u32[]{:S(2)}) collective-permute-start(bf16[152,1024]{1,0:T(8,128)(2,1)S(1)} %get-tuple-element.318), channel_id=1, source_target_pairs={{0,16},{8,24},{16,0},{24,8},{1,17},{9,25},{17,1},{25,9},{2,18},{10... | collective-permute-start | bytes 933896 | tf_op jit(solution)/shard_map/ppermute | solution.py:61
  339.7 21.0 %collective-permute-start.68 = (bf16[152,1024]{1,0:T(8,128)(2,1)S(1)}, bf16[152,1024]{1,0:T(8,128)(2,1)S(1)}, u32[]{:S(2)}, u32[]{:S(2)}) collective-permute-start(bf16[152,1024]{1,0:T(8,128)(2,1)S(1)} %get-tuple-element.319), channel_id=1, source_target_pairs={{0,24},{8,16},{16,8},{24,0},{1,25},{9,17},{17,9},{25,1},{2,26},{10... | collective-permute-start | bytes 933896 | tf_op jit(solution)/shard_map/ppermute | solution.py:61
  348.1 16.1 %collective-permute-start.62 = (bf16[128,1024]{1,0:T(8,128)(2,1)}, bf16[128,1024]{1,0:T(8,128)(2,1)S(1)}, u32[]{:S(2)}, u32[]{:S(2)}) collective-permute-start(bf16[128,1024]{1,0:T(8,128)(2,1)} %slice.53), channel_id=1, source_target_pairs={{0,8},{8,0},{16,24},{24,16},{1,9},{9,1},{17,25},{25,17},{2,10},{10... | collective-permute-start | bytes 786440 | tf_op jit(solution)/shard_map/ppermute | solution.py:61
  349.6 14.6 %collective-permute-start.61 = (bf16[128,1024]{1,0:T(8,128)(2,1)S(1)}, bf16[128,1024]{1,0:T(8,128)(2,1)}, u32[]{:S(2)}, u32[]{:S(2)}) collective-permute-start(bf16[128,1024]{1,0:T(8,128)(2,1)S(1)} %slice.52), channel_id=1, source_target_pairs={{0,16},{8,24},{16,0},{24,8},{1,17},{9,25},{17,1},{25,9},{2,18},{10... | collective-permute-start | bytes 786440 | tf_op jit(solution)/shard_map/ppermute | solution.py:61
  366.7 13.1 %collective-permute-start.70 = (bf16[160,1024]{1,0:T(8,128)(2,1)}, bf16[160,1024]{1,0:T(8,128)(2,1)S(1)}, u32[]{:S(2)}, u32[]{:S(2)}) collective-permute-start(bf16[160,1024]{1,0:T(8,128)(2,1)} %bitcast.63), channel_id=1, source_target_pairs={{0,16},{8,24},{16,0},{24,8},{1,17},{9,25},{17,1},{25,9},{2,18},{10... | collective-permute-start | bytes 983048 | tf_op jit(solution)/shard_map/ppermute | solution.py:61
  367.2 12.6 %collective-permute-start.69 = (bf16[160,1024]{1,0:T(8,128)(2,1)}, bf16[160,1024]{1,0:T(8,128)(2,1)S(1)}, u32[]{:S(2)}, u32[]{:S(2)}) collective-permute-start(bf16[160,1024]{1,0:T(8,128)(2,1)} %bitcast.64), channel_id=1, source_target_pairs={{0,8},{8,0},{16,24},{24,16},{1,9},{9,1},{17,25},{25,17},{2,10},{10... | collective-permute-start | bytes 983048 | tf_op jit(solution)/shard_map/ppermute | solution.py:61
  (152 other events, 1125.7 us)
Sparse Core Ops, SparseCore 0:
  14.0 49.7 all-gather.6
  65.9 45.8 all-gather.8
  114.0 46.1 all-gather.10
  191.9 48.5 reduce-scatter.4
  243.2 25.2 reduce-scatter.6
  272.2 50.8 reduce-scatter.10
  325.5 35.5 reduce-scatter.8

commit v8 on v7

--- a/solution.py
+++ b/solution.py
@@ -1118,6 +1118,7 @@
                 [None] * 7 + [anywhere],
                 out_specs=[whole(block), anywhere],
                 aliases={7: 1},
+                limit=60,
                 scratch=[VMEM((8, 32, width), BF16), pltpu.SemaphoreType.DMA((1,))],
             )
             homes_a[0] = home(term)

time: 396 us -> 396 us (level)
    unnamed x242 -> x250, local copies, waits for them, and re-layouts: 46.4 us -> 48.9 us
  transfers between devices with their start and end apart: 80 -> 80, of which waited for: 33 -> 33; matrix products, arithmetic and copies ran while one was open for 1% -> 1% of each run, Pallas kernels for 28% -> 29%
where the time goes in v8:
time: 396 us; the launch traced here: 392 us
  waiting for transfers between devices  120 us (30%)
  Pallas kernels  118 us (30%)
  starting transfers between devices  80.8 us (20%)
  local copies, waits for them, and re-layouts  53 us (13%)
  between operations  18 us (5%)
    pallas_call x56, Pallas kernels, call(): pl.pallas_call(run, name=name, grid=(1,), in_specs=specs, out_specs=out_s...  118 us
    ppermute x62, waiting for transfers between devices, swap(): return lax.ppermute(block, 'dp', [(i, i ^ k) for i in range(self.count)])  98.4 us
    ppermute x62, starting transfers between devices, swap(): return lax.ppermute(block, 'dp', [(i, i ^ k) for i in range(self.count)])  72 us
    unnamed x250, local copies, waits for them, and re-layouts  48.9 us
    all_gather x3, waiting for transfers between devices, fetch(): return lax.all_gather(packed, 'fsdp', axis=0, tiled=False)  14.4 us
  transfers between devices with their start and end apart: 80, of which 33 were waited for; matrix products, arithmetic and copies ran while one was open for 1% of the time, Pallas kernels for 29%

profile of v8, /device:TPU:0, one launch (start us, length us, event | category | flops | bytes accessed | tf_op | source)
XLA Modules:
  0.0 391.6 jit_solution(11250337985343945427)
XLA Ops:
  11.0 2.8 prepare_first.1
  15.2 5.0 %collective-permute-start.3 = (bf16[40,256]{1,0:T(8,128)(2,1)S(1)}, bf16[40,256]{1,0:T(8,128)(2,1)S(1)}, u32[]{:S(2)}, u32[]{:S(2)}) collective-permute-start(bf16[40,256]{1,0:T(8,128)(2,1)S(1)} %pad_maximum_fusion.1.refs_1_), channel_id=1, source_target_pairs={{0,6},{1,7},{2,4},{3,5},{4,2},{5,3},{6,0},{7,1},{8,14},{9,15},{10,... | collective-permute-start | bytes 61448 | tf_op jit(solution)/shard_map/ppermute | solution.py:873
  22.0 2.9 collective-permute-done.2.refs_3_
  24.9 2.5 collective-permute-start.6
  34.2 3.0 prepare_second.1
  37.3 2.7 prepare_third.1
  49.4 14.4 %all-gather.7.cloned.1.call-done = bf16[2048,1024]{1,0:T(8,128)(2,1)} async-done(((bf16[256,1024]{1,0:T(8,128)(2,1)}), bf16[2048,1024]{1,0:T(8,128)(2,1)}) %all-gather.7.cloned.1.call-update) | async-done | bytes 4194320 | tf_op jit(solution)/shard_map/all_gather | solution.py:895
  82.5 2.8 collective-permute-done.9.refs_2_
  85.3 6.9 %collective-permute-done.13.refs_4_ = bf16[152,1024]{1,0:T(8,128)(2,1)S(1)} collective-permute-done((bf16[152,1024]{1,0:T(8,128)(2,1)S(1)}, bf16[152,1024]{1,0:T(8,128)(2,1)S(1)}, u32[]{:S(2)}, u32[]{:S(2)}) %collective-permute-start.13) | collective-permute-done | bytes 311328 | tf_op jit(solution)/shard_map/ppermute | solution.py:61
  97.6 6.1 %collective-permute-done.17.refs_0_.refs_1_ = bf16[152,1024]{1,0:T(8,128)(2,1)S(1)} collective-permute-done((bf16[152,1024]{1,0:T(8,128)(2,1)S(1)}, bf16[152,1024]{1,0:T(8,128)(2,1)S(1)}, u32[]{:S(2)}, u32[]{:S(2)}) %collective-permute-start.17) | collective-permute-done | bytes 311328 | tf_op jit(solution)/shard_map/ppermute | solution.py:61
  104.4 5.6 %collective-permute-done.18.refs_0_.refs_2_ = bf16[152,1024]{1,0:T(8,128)(2,1)S(1)} collective-permute-done((bf16[152,1024]{1,0:T(8,128)(2,1)S(1)}, bf16[152,1024]{1,0:T(8,128)(2,1)S(1)}, u32[]{:S(2)}, u32[]{:S(2)}) %collective-permute-start.18) | collective-permute-done | bytes 311328 | tf_op jit(solution)/shard_map/ppermute | solution.py:61
  119.7 11.8 %collective-permute-done.21.refs_3_ = bf16[152,1024]{1,0:T(8,128)(2,1)S(1)} collective-permute-done((bf16[152,1024]{1,0:T(8,128)(2,1)S(1)}, bf16[152,1024]{1,0:T(8,128)(2,1)S(1)}, u32[]{:S(2)}, u32[]{:S(2)}) %collective-permute-start.21) | collective-permute-done | bytes 311328 | tf_op jit(solution)/shard_map/ppermute | solution.py:61
  138.9 4.6 %collective-permute-done.23.refs_1_.refs_2_ = bf16[152,1024]{1,0:T(8,128)(2,1)S(1)} collective-permute-done((bf16[152,1024]{1,0:T(8,128)(2,1)S(1)}, bf16[152,1024]{1,0:T(8,128)(2,1)S(1)}, u32[]{:S(2)}, u32[]{:S(2)}) %collective-permute-start.23) | collective-permute-done | bytes 311328 | tf_op jit(solution)/shard_map/ppermute | solution.py:61
  143.4 2.6 attention_forward.13
  156.5 7.8 %collective-permute-done.26.refs_3_ = bf16[152,1024]{1,0:T(8,128)(2,1)S(1)} collective-permute-done((bf16[152,1024]{1,0:T(8,128)(2,1)S(1)}, bf16[152,1024]{1,0:T(8,128)(2,1)S(1)}, u32[]{:S(2)}, u32[]{:S(2)}) %collective-permute-start.26) | collective-permute-done | bytes 311328 | tf_op jit(solution)/shard_map/ppermute | solution.py:61
  176.3 2.5 mlp_both.5
  179.2 2.5 mlp_both.6
  185.6 3.5 grads_mlp.2
  193.9 6.4 %collective-permute-done.32.refs_4_ = bf16[152,1024]{1,0:T(8,128)(2,1)} collective-permute-done((bf16[152,1024]{1,0:T(8,128)(2,1)}, bf16[152,1024]{1,0:T(8,128)(2,1)}, u32[]{:S(2)}, u32[]{:S(2)}) %collective-permute-start.32) | collective-permute-done | bytes 311328 | tf_op jit(solution)/shard_map/ppermute | solution.py:61
  200.3 3.1 add_norm_backward.3
  210.2 2.7 attention_backward.8
  214.1 2.7 attention_backward.9
  218.8 2.7 attention_backward.10
  222.8 2.7 attention_backward.11
  229.1 4.2 %collective-permute-done.38.refs_5_.refs_4_ = bf16[152,1024]{1,0:T(8,128)(2,1)S(1)} collective-permute-done((bf16[152,1024]{1,0:T(8,128)(2,1)S(1)}, bf16[152,1024]{1,0:T(8,128)(2,1)S(1)}, u32[]{:S(2)}, u32[]{:S(2)}) %collective-permute-start.38) | collective-permute-done | bytes 311328 | tf_op jit(solution)/shard_map/ppermute | solution.py:61
  235.6 3.1 add_norm_backward.4
  239.8 2.5 collective-permute-start.45
  250.9 3.2 mlp_backward.5
  254.3 3.2 mlp_backward.6
  258.6 3.3 mlp_backward.7
  264.2 4.6 %grads_mlp.3 = bf16[8,256,1024]{2,1,0:T(8,128)(2,1)S(1)} custom-call(bf16[152,1024]{1,0:T(8,128)(2,1)S(1)} %copy-done.63, bf16[152,1024]{1,0:T(8,128)(2,1)S(1)} %copy-done.65, bf16[152,1024]{1,0:T(8,128)(2,1)S(1)} %copy-done.67, bf16[152,1024]{1,0:T(8,128)(2,1)S(1)} %copy-done.69, bf16[152,1024]{1,0:T(8,128)(2,1)S(1)} %get-tuple-element.267.refs_4_, ...), custom_call_target="tpu_custom_call" | custom-call | bytes 4194304 | tf_op jit(solution)/shard_map/grads_mlp/pallas_call | solution.py:397
  275.8 3.3 add_norm_backward.5
  285.8 2.8 attention_backward.12
  288.7 13.1 %collective-permute-done.53.refs_1_.refs_13_ = bf16[152,1024]{1,0:T(8,128)(2,1)S(1)} collective-permute-done((bf16[152,1024]{1,0:T(8,128)(2,1)}, bf16[152,1024]{1,0:T(8,128)(2,1)S(1)}, u32[]{:S(2)}, u32[]{:S(2)}) %collective-permute-start.53) | collective-permute-done | bytes 311328 | tf_op jit(solution)/shard_map/ppermute | solution.py:61
  301.8 2.7 attention_backward.13
  305.7 2.7 attention_backward.14
  309.6 2.7 attention_backward.15
  317.2 3.0 collective-permute-done.54.refs_4_
  320.9 4.2 %last_norm.1 = (f32[152,1024]{1,0:T(8,128)}, bf16[8,160,1024]{2,1,0:T(8,128)(2,1)}) custom-call(f32[152,1024]{1,0:T(8,128)} %get-tuple-element.283.refs_0_, bf16[152,1024]{1,0:T(8,128)(2,1)} %copy-done.103, bf16[152,1024]{1,0:T(8,128)(2,1)} %copy-done.112, bf16[152,1024]{1,0:T(8,128)(2,1)} %copy-done.113, ...), custom_call_target="tpu_custom_call", output_to_operand_aliasing={{1}: (7, {})} | custom-call | bytes 3244032 | tf_op jit(solution)/shard_map/last_norm/pallas_call | solution.py:397
  329.5 2.4 copy-done.11
  336.5 3.8 collective-permute-done.60.refs_3_
  343.5 6.2 %collective-permute-done.64.refs_5_ = bf16[192,1024]{1,0:T(8,128)(2,1)S(1)} collective-permute-done((bf16[192,1024]{1,0:T(8,128)(2,1)S(1)}, bf16[192,1024]{1,0:T(8,128)(2,1)S(1)}, u32[]{:S(2)}, u32[]{:S(2)}) %collective-permute-start.64) | collective-permute-done | bytes 393248 | tf_op jit(solution)/shard_map/ppermute | solution.py:61
  354.8 3.1 finish_mlp.2
  359.2 2.5 finish_attention.2
  362.0 2.5 collective-permute-start.71
  368.7 3.5 finish_mlp.3
  373.9 5.9 %collective-permute-done.70.refs_3_ = bf16[160,1024]{1,0:T(8,128)(2,1)S(1)} collective-permute-done((bf16[160,1024]{1,0:T(8,128)(2,1)}, bf16[160,1024]{1,0:T(8,128)(2,1)S(1)}, u32[]{:S(2)}, u32[]{:S(2)}) %collective-permute-start.70) | collective-permute-done | bytes 327712 | tf_op jit(solution)/shard_map/ppermute | solution.py:61
  381.8 2.5 finish_attention.3
  (443 shorter events, 172.2 us)
Async XLA Ops:
  7.2 56.6 %all-gather.7.cloned.1.call-start = ((), (), s32[]{:S(2)}) async-start(), calls=%async_computation.8 | async-start | bytes 4718592 | tf_op jit(solution)/shard_map/all_gather | solution.py:895
  13.8 98.4 %all-gather.9.cloned.1.call-start = ((), (), s32[]{:S(2)}) async-start(), calls=%async_computation.9 | async-start | bytes 4718592 | tf_op jit(solution)/shard_map/all_gather | solution.py:895
  37.2 128.9 %all-gather.11.cloned.1.call-start = ((), (), s32[]{:S(2)}) async-start(), calls=%async_computation.10 | async-start | bytes 4718592 | tf_op jit(solution)/shard_map/all_gather | solution.py:895
  40.0 202.3 %reduce-scatter.5.cloned.1.call-start = ((), (), s32[]{:S(2)}) async-start(), calls=%async_computation.4 | async-start | bytes 4718592 | tf_op jit(solution)/shard_map/reduce_scatter | solution.py:1035
  42.9 32.1 %collective-permute-start.12 = (bf16[152,1024]{1,0:T(8,128)(2,1)S(1)}, bf16[152,1024]{1,0:T(8,128)(2,1)S(1)}, u32[]{:S(2)}, u32[]{:S(2)}) collective-permute-start(bf16[152,1024]{1,0:T(8,128)(2,1)S(1)} %copy-done.23), channel_id=1, source_target_pairs={{0,24},{8,16},{16,8},{24,0},{1,25},{9,17},{17,9},{25,1},{2,26},{10... | collective-permute-start | bytes 933896 | tf_op jit(solution)/shard_map/ppermute | solution.py:61
  44.4 27.8 %collective-permute-start.10 = (bf16[152,1024]{1,0:T(8,128)(2,1)S(1)}, bf16[152,1024]{1,0:T(8,128)(2,1)S(1)}, u32[]{:S(2)}, u32[]{:S(2)}) collective-permute-start(bf16[152,1024]{1,0:T(8,128)(2,1)S(1)} %copy-done.23), channel_id=1, source_target_pairs={{0,16},{8,24},{16,0},{24,8},{1,17},{9,25},{17,1},{25,9},{2,18},{10... | collective-permute-start | bytes 933896 | tf_op jit(solution)/shard_map/ppermute | solution.py:61
  44.9 23.4 %collective-permute-start.8 = (bf16[152,1024]{1,0:T(8,128)(2,1)S(1)}, bf16[152,1024]{1,0:T(8,128)(2,1)S(1)}, u32[]{:S(2)}, u32[]{:S(2)}) collective-permute-start(bf16[152,1024]{1,0:T(8,128)(2,1)S(1)} %copy-done.23), channel_id=1, source_target_pairs={{0,8},{8,0},{16,24},{24,16},{1,9},{9,1},{17,25},{25,17},{2,10},{10... | collective-permute-start | bytes 933896 | tf_op jit(solution)/shard_map/ppermute | solution.py:61
  47.4 32.9 %collective-permute-start.16 = (bf16[152,1024]{1,0:T(8,128)(2,1)S(1)}, bf16[152,1024]{1,0:T(8,128)(2,1)S(1)}, u32[]{:S(2)}, u32[]{:S(2)}) collective-permute-start(bf16[152,1024]{1,0:T(8,128)(2,1)S(1)} %get-tuple-element.214.refs_1_.refs_12_), channel_id=1, source_target_pairs={{0,24},{8,16},{16,8},{24,0},{1,25},{9,17},{17,9},{25,1},{2,26},{10... | collective-permute-start | bytes 933896 | tf_op jit(solution)/shard_map/ppermute | solution.py:61
  48.8 32.9 %collective-permute-start.15 = (bf16[152,1024]{1,0:T(8,128)(2,1)S(1)}, bf16[152,1024]{1,0:T(8,128)(2,1)S(1)}, u32[]{:S(2)}, u32[]{:S(2)}) collective-permute-start(bf16[152,1024]{1,0:T(8,128)(2,1)S(1)} %get-tuple-element.214.refs_1_.refs_12_), channel_id=1, source_target_pairs={{0,16},{8,24},{16,0},{24,8},{1,17},{9,25},{17,1},{25,9},{2,18},{10... | collective-permute-start | bytes 933896 | tf_op jit(solution)/shard_map/ppermute | solution.py:61
  68.4 13.4 %collective-permute-start.14 = (bf16[152,1024]{1,0:T(8,128)(2,1)S(1)}, bf16[152,1024]{1,0:T(8,128)(2,1)S(1)}, u32[]{:S(2)}, u32[]{:S(2)}) collective-permute-start(bf16[152,1024]{1,0:T(8,128)(2,1)S(1)} %get-tuple-element.214.refs_1_.refs_12_), channel_id=1, source_target_pairs={{0,8},{8,0},{16,24},{24,16},{1,9},{9,1},{17,25},{25,17},{2,10},{10... | collective-permute-start | bytes 933896 | tf_op jit(solution)/shard_map/ppermute | solution.py:61
  72.1 13.1 %collective-permute-start.9 = (bf16[152,1024]{1,0:T(8,128)(2,1)S(1)}, bf16[152,1024]{1,0:T(8,128)(2,1)S(1)}, u32[]{:S(2)}, u32[]{:S(2)}) collective-permute-start(bf16[152,1024]{1,0:T(8,128)(2,1)S(1)} %get-tuple-element.185), channel_id=1, source_target_pairs={{0,8},{8,0},{16,24},{24,16},{1,9},{9,1},{17,25},{25,17},{2,10},{10... | collective-permute-start | bytes 933896 | tf_op jit(solution)/shard_map/ppermute | solution.py:61
  94.8 15.2 %collective-permute-start.18 = (bf16[152,1024]{1,0:T(8,128)(2,1)S(1)}, bf16[152,1024]{1,0:T(8,128)(2,1)S(1)}, u32[]{:S(2)}, u32[]{:S(2)}) collective-permute-start(bf16[152,1024]{1,0:T(8,128)(2,1)S(1)} %get-tuple-element.195.refs_0_), channel_id=1, source_target_pairs={{0,16},{8,24},{16,0},{24,8},{1,17},{9,25},{17,1},{25,9},{2,18},{10... | collective-permute-start | bytes 933896 | tf_op jit(solution)/shard_map/ppermute | solution.py:61
  95.4 15.4 %collective-permute-start.19 = (bf16[152,1024]{1,0:T(8,128)(2,1)S(1)}, bf16[152,1024]{1,0:T(8,128)(2,1)S(1)}, u32[]{:S(2)}, u32[]{:S(2)}) collective-permute-start(bf16[152,1024]{1,0:T(8,128)(2,1)S(1)} %get-tuple-element.195.refs_0_), channel_id=1, source_target_pairs={{0,24},{8,16},{16,8},{24,0},{1,25},{9,17},{17,9},{25,1},{2,26},{10... | collective-permute-start | bytes 933896 | tf_op jit(solution)/shard_map/ppermute | solution.py:61
  115.6 15.9 %collective-permute-start.21 = (bf16[152,1024]{1,0:T(8,128)(2,1)S(1)}, bf16[152,1024]{1,0:T(8,128)(2,1)S(1)}, u32[]{:S(2)}, u32[]{:S(2)}) collective-permute-start(bf16[152,1024]{1,0:T(8,128)(2,1)S(1)} %get-tuple-element.197), channel_id=1, source_target_pairs={{0,16},{8,24},{16,0},{24,8},{1,17},{9,25},{17,1},{25,9},{2,18},{10... | collective-permute-start | bytes 933896 | tf_op jit(solution)/shard_map/ppermute | solution.py:61
  116.8 14.6 %collective-permute-start.22 = (bf16[152,1024]{1,0:T(8,128)(2,1)S(1)}, bf16[152,1024]{1,0:T(8,128)(2,1)S(1)}, u32[]{:S(2)}, u32[]{:S(2)}) collective-permute-start(bf16[152,1024]{1,0:T(8,128)(2,1)S(1)} %get-tuple-element.198), channel_id=1, source_target_pairs={{0,24},{8,16},{16,8},{24,0},{1,25},{9,17},{17,9},{25,1},{2,26},{10... | collective-permute-start | bytes 933896 | tf_op jit(solution)/shard_map/ppermute | solution.py:61
  118.3 14.4 %collective-permute-start.20 = (bf16[152,1024]{1,0:T(8,128)(2,1)S(1)}, bf16[152,1024]{1,0:T(8,128)(2,1)S(1)}, u32[]{:S(2)}, u32[]{:S(2)}) collective-permute-start(bf16[152,1024]{1,0:T(8,128)(2,1)S(1)} %get-tuple-element.196.refs_2_), channel_id=1, source_target_pairs={{0,8},{8,0},{16,24},{24,16},{1,9},{9,1},{17,25},{25,17},{2,10},{10... | collective-permute-start | bytes 933896 | tf_op jit(solution)/shard_map/ppermute | solution.py:61
  134.7 13.3 %collective-permute-start.25 = (bf16[152,1024]{1,0:T(8,128)(2,1)S(1)}, bf16[152,1024]{1,0:T(8,128)(2,1)S(1)}, u32[]{:S(2)}, u32[]{:S(2)}) collective-permute-start(bf16[152,1024]{1,0:T(8,128)(2,1)S(1)} %get-tuple-element.200.refs_1_), channel_id=1, source_target_pairs={{0,16},{8,24},{16,0},{24,8},{1,17},{9,25},{17,1},{25,9},{2,18},{10... | collective-permute-start | bytes 933896 | tf_op jit(solution)/shard_map/ppermute | solution.py:61
  136.1 16.6 %collective-permute-start.27 = (bf16[152,1024]{1,0:T(8,128)(2,1)S(1)}, bf16[152,1024]{1,0:T(8,128)(2,1)S(1)}, u32[]{:S(2)}, u32[]{:S(2)}) collective-permute-start(bf16[152,1024]{1,0:T(8,128)(2,1)S(1)} %get-tuple-element.200.refs_1_), channel_id=1, source_target_pairs={{0,24},{8,16},{16,8},{24,0},{1,25},{9,17},{17,9},{25,1},{2,26},{10... | collective-permute-start | bytes 933896 | tf_op jit(solution)/shard_map/ppermute | solution.py:61
  150.3 14.0 %collective-permute-start.26 = (bf16[152,1024]{1,0:T(8,128)(2,1)S(1)}, bf16[152,1024]{1,0:T(8,128)(2,1)S(1)}, u32[]{:S(2)}, u32[]{:S(2)}) collective-permute-start(bf16[152,1024]{1,0:T(8,128)(2,1)S(1)} %get-tuple-element.205), channel_id=1, source_target_pairs={{0,16},{8,24},{16,0},{24,8},{1,17},{9,25},{17,1},{25,9},{2,18},{10... | collective-permute-start | bytes 933896 | tf_op jit(solution)/shard_map/ppermute | solution.py:61
  166.2 13.0 %collective-permute-start.30 = (bf16[152,1024]{1,0:T(8,128)(2,1)}, bf16[152,1024]{1,0:T(8,128)(2,1)S(1)}, u32[]{:S(2)}, u32[]{:S(2)}) collective-permute-start(bf16[152,1024]{1,0:T(8,128)(2,1)} %copy-done.92), channel_id=1, source_target_pairs={{0,16},{8,24},{16,0},{24,8},{1,17},{9,25},{17,1},{25,9},{2,18},{10... | collective-permute-start | bytes 933896 | tf_op jit(solution)/shard_map/ppermute | solution.py:61
  167.9 15.2 %collective-permute-start.29 = (bf16[152,1024]{1,0:T(8,128)(2,1)}, bf16[152,1024]{1,0:T(8,128)(2,1)S(1)}, u32[]{:S(2)}, u32[]{:S(2)}) collective-permute-start(bf16[152,1024]{1,0:T(8,128)(2,1)} %copy-done.92), channel_id=1, source_target_pairs={{0,24},{8,16},{16,8},{24,0},{1,25},{9,17},{17,9},{25,1},{2,26},{10... | collective-permute-start | bytes 933896 | tf_op jit(solution)/shard_map/ppermute | solution.py:61
  178.8 13.0 %collective-permute-start.33 = (bf16[152,1024]{1,0:T(8,128)(2,1)}, bf16[152,1024]{1,0:T(8,128)(2,1)}, u32[]{:S(2)}, u32[]{:S(2)}) collective-permute-start(bf16[152,1024]{1,0:T(8,128)(2,1)} %get-tuple-element.220), channel_id=1, source_target_pairs={{0,8},{8,0},{16,24},{24,16},{1,9},{9,1},{17,25},{25,17},{2,10},{10... | collective-permute-start | bytes 933896 | tf_op jit(solution)/shard_map/ppermute | solution.py:61
  191.9 80.7 %reduce-scatter.7.cloned.1.call-start = ((), (), s32[]{:S(2)}) async-start(), calls=%async_computation.5 | async-start | bytes 1310720 | tf_op jit(solution)/shard_map/reduce_scatter | solution.py:1104
  205.5 13.3 %collective-permute-start.36 = (bf16[152,1024]{1,0:T(8,128)(2,1)}, bf16[152,1024]{1,0:T(8,128)(2,1)S(1)}, u32[]{:S(2)}, u32[]{:S(2)}) collective-permute-start(bf16[152,1024]{1,0:T(8,128)(2,1)} %get-tuple-element.237.refs_1_.refs_13_), channel_id=1, source_target_pairs={{0,16},{8,24},{16,0},{24,8},{1,17},{9,25},{17,1},{25,9},{2,18},{10... | collective-permute-start | bytes 933896 | tf_op jit(solution)/shard_map/ppermute | solution.py:61
  206.6 16.2 %collective-permute-start.35 = (bf16[152,1024]{1,0:T(8,128)(2,1)}, bf16[152,1024]{1,0:T(8,128)(2,1)S(1)}, u32[]{:S(2)}, u32[]{:S(2)}) collective-permute-start(bf16[152,1024]{1,0:T(8,128)(2,1)} %get-tuple-element.237.refs_1_.refs_13_), channel_id=1, source_target_pairs={{0,24},{8,16},{16,8},{24,0},{1,25},{9,17},{17,9},{25,1},{2,26},{10... | collective-permute-start | bytes 933896 | tf_op jit(solution)/shard_map/ppermute | solution.py:61
  235.4 89.8 %reduce-scatter.11.cloned.1.call-start = ((), (), s32[]{:S(2)}) async-start(), calls=%async_computation.7 | async-start | bytes 4718592 | tf_op jit(solution)/shard_map/reduce_scatter | solution.py:1035
  238.8 12.1 %collective-permute-start.47 = (bf16[152,1024]{1,0:T(8,128)(2,1)}, bf16[152,1024]{1,0:T(8,128)(2,1)}, u32[]{:S(2)}, u32[]{:S(2)}) collective-permute-start(bf16[152,1024]{1,0:T(8,128)(2,1)} %get-tuple-element.266.refs_0_.refs_12_), channel_id=1, source_target_pairs={{0,8},{8,0},{16,24},{24,16},{1,9},{9,1},{17,25},{25,17},{2,10},{10... | collective-permute-start | bytes 933896 | tf_op jit(solution)/shard_map/ppermute | solution.py:61
  238.8 15.5 %collective-permute-start.46 = (bf16[152,1024]{1,0:T(8,128)(2,1)}, bf16[152,1024]{1,0:T(8,128)(2,1)}, u32[]{:S(2)}, u32[]{:S(2)}) collective-permute-start(bf16[152,1024]{1,0:T(8,128)(2,1)} %get-tuple-element.266.refs_0_.refs_12_), channel_id=1, source_target_pairs={{0,16},{8,24},{16,0},{24,8},{1,17},{9,25},{17,1},{25,9},{2,18},{10... | collective-permute-start | bytes 933896 | tf_op jit(solution)/shard_map/ppermute | solution.py:61
  239.8 18.8 %collective-permute-start.45 = (bf16[152,1024]{1,0:T(8,128)(2,1)}, bf16[152,1024]{1,0:T(8,128)(2,1)}, u32[]{:S(2)}, u32[]{:S(2)}) collective-permute-start(bf16[152,1024]{1,0:T(8,128)(2,1)} %get-tuple-element.266.refs_0_.refs_12_), channel_id=1, source_target_pairs={{0,24},{8,16},{16,8},{24,0},{1,25},{9,17},{17,9},{25,1},{2,26},{10... | collective-permute-start | bytes 933896 | tf_op jit(solution)/shard_map/ppermute | solution.py:61
  254.1 16.7 %collective-permute-start.49 = (bf16[152,1024]{1,0:T(8,128)(2,1)}, bf16[152,1024]{1,0:T(8,128)(2,1)}, u32[]{:S(2)}, u32[]{:S(2)}) collective-permute-start(bf16[152,1024]{1,0:T(8,128)(2,1)} %get-tuple-element.272), channel_id=1, source_target_pairs={{0,8},{8,0},{16,24},{24,16},{1,9},{9,1},{17,25},{25,17},{2,10},{10... | collective-permute-start | bytes 933896 | tf_op jit(solution)/shard_map/ppermute | solution.py:61
  257.6 14.7 %collective-permute-start.50 = (bf16[152,1024]{1,0:T(8,128)(2,1)}, bf16[152,1024]{1,0:T(8,128)(2,1)}, u32[]{:S(2)}, u32[]{:S(2)}) collective-permute-start(bf16[152,1024]{1,0:T(8,128)(2,1)} %get-tuple-element.273), channel_id=1, source_target_pairs={{0,16},{8,24},{16,0},{24,8},{1,17},{9,25},{17,1},{25,9},{2,18},{10... | collective-permute-start | bytes 933896 | tf_op jit(solution)/shard_map/ppermute | solution.py:61
  272.3 89.7 %reduce-scatter.9.cloned.1.call-start = ((), (), s32[]{:S(2)}) async-start(), calls=%async_computation.6 | async-start | bytes 2949120 | tf_op jit(solution)/shard_map/reduce_scatter | solution.py:1035
  273.7 39.9 %collective-permute-start.58 = (bf16[384,1024]{1,0:T(8,128)(2,1)S(1)}, bf16[384,1024]{1,0:T(8,128)(2,1)S(1)}, u32[]{:S(2)}, u32[]{:S(2)}) collective-permute-start(bf16[384,1024]{1,0:T(8,128)(2,1)S(1)} %pad_maximum_fusion.refs_4_.refs_1_), channel_id=1, source_target_pairs={{0,16},{8,24},{16,0},{24,8},{1,17},{9,25},{17,1},{25,9},{2,18},{10... | collective-permute-start | bytes 2359304 | tf_op jit(solution)/shard_map/ppermute | solution.py:61
  274.7 39.0 %collective-permute-start.57 = (bf16[384,1024]{1,0:T(8,128)(2,1)S(1)}, bf16[384,1024]{1,0:T(8,128)(2,1)S(1)}, u32[]{:S(2)}, u32[]{:S(2)}) collective-permute-start(bf16[384,1024]{1,0:T(8,128)(2,1)S(1)} %pad_maximum_fusion.refs_4_.refs_1_), channel_id=1, source_target_pairs={{0,8},{8,0},{16,24},{24,16},{1,9},{9,1},{17,25},{25,17},{2,10},{10... | collective-permute-start | bytes 2359304 | tf_op jit(solution)/shard_map/ppermute | solution.py:61
  279.1 22.7 %collective-permute-start.53 = (bf16[152,1024]{1,0:T(8,128)(2,1)}, bf16[152,1024]{1,0:T(8,128)(2,1)S(1)}, u32[]{:S(2)}, u32[]{:S(2)}) collective-permute-start(bf16[152,1024]{1,0:T(8,128)(2,1)} %get-tuple-element.284.refs_1_.refs_12_), channel_id=1, source_target_pairs={{0,8},{8,0},{16,24},{24,16},{1,9},{9,1},{17,25},{25,17},{2,10},{10... | collective-permute-start | bytes 933896 | tf_op jit(solution)/shard_map/ppermute | solution.py:61
  279.8 25.9 %collective-permute-start.52 = (bf16[152,1024]{1,0:T(8,128)(2,1)}, bf16[152,1024]{1,0:T(8,128)(2,1)S(1)}, u32[]{:S(2)}, u32[]{:S(2)}) collective-permute-start(bf16[152,1024]{1,0:T(8,128)(2,1)} %get-tuple-element.284.refs_1_.refs_12_), channel_id=1, source_target_pairs={{0,16},{8,24},{16,0},{24,8},{1,17},{9,25},{17,1},{25,9},{2,18},{10... | collective-permute-start | bytes 933896 | tf_op jit(solution)/shard_map/ppermute | solution.py:61
  281.0 28.7 %collective-permute-start.51 = (bf16[152,1024]{1,0:T(8,128)(2,1)}, bf16[152,1024]{1,0:T(8,128)(2,1)S(1)}, u32[]{:S(2)}, u32[]{:S(2)}) collective-permute-start(bf16[152,1024]{1,0:T(8,128)(2,1)} %get-tuple-element.284.refs_1_.refs_12_), channel_id=1, source_target_pairs={{0,24},{8,16},{16,8},{24,0},{1,25},{9,17},{17,9},{25,1},{2,26},{10... | collective-permute-start | bytes 933896 | tf_op jit(solution)/shard_map/ppermute | solution.py:61
  304.5 12.7 %collective-permute-start.55 = (bf16[152,1024]{1,0:T(8,128)(2,1)S(1)}, bf16[152,1024]{1,0:T(8,128)(2,1)S(1)}, u32[]{:S(2)}, u32[]{:S(2)}) collective-permute-start(bf16[152,1024]{1,0:T(8,128)(2,1)S(1)} %get-tuple-element.292), channel_id=1, source_target_pairs={{0,8},{8,0},{16,24},{24,16},{1,9},{9,1},{17,25},{25,17},{2,10},{10... | collective-permute-start | bytes 933896 | tf_op jit(solution)/shard_map/ppermute | solution.py:61
  325.2 15.2 %collective-permute-start.60 = (bf16[256,1024]{1,0:T(8,128)(2,1)}, bf16[256,1024]{1,0:T(8,128)(2,1)S(1)}, u32[]{:S(2)}, u32[]{:S(2)}) collective-permute-start(bf16[256,1024]{1,0:T(8,128)(2,1)} %bitcast.67), channel_id=1, source_target_pairs={{0,16},{8,24},{16,0},{24,8},{1,17},{9,25},{17,1},{25,9},{2,18},{10... | collective-permute-start | bytes 1572872 | tf_op jit(solution)/shard_map/ppermute | solution.py:61
  326.2 15.1 %collective-permute-start.59 = (bf16[256,1024]{1,0:T(8,128)(2,1)}, bf16[256,1024]{1,0:T(8,128)(2,1)S(1)}, u32[]{:S(2)}, u32[]{:S(2)}) collective-permute-start(bf16[256,1024]{1,0:T(8,128)(2,1)} %bitcast.68), channel_id=1, source_target_pairs={{0,8},{8,0},{16,24},{24,16},{1,9},{9,1},{17,25},{25,17},{2,10},{10... | collective-permute-start | bytes 1572872 | tf_op jit(solution)/shard_map/ppermute | solution.py:61
  327.1 22.5 %collective-permute-start.64 = (bf16[192,1024]{1,0:T(8,128)(2,1)S(1)}, bf16[192,1024]{1,0:T(8,128)(2,1)S(1)}, u32[]{:S(2)}, u32[]{:S(2)}) collective-permute-start(bf16[192,1024]{1,0:T(8,128)(2,1)S(1)} %slice.55), channel_id=1, source_target_pairs={{0,8},{8,0},{16,24},{24,16},{1,9},{9,1},{17,25},{25,17},{2,10},{10... | collective-permute-start | bytes 1179656 | tf_op jit(solution)/shard_map/ppermute | solution.py:61
  328.3 22.3 %collective-permute-start.63 = (bf16[192,1024]{1,0:T(8,128)(2,1)S(1)}, bf16[192,1024]{1,0:T(8,128)(2,1)S(1)}, u32[]{:S(2)}, u32[]{:S(2)}) collective-permute-start(bf16[192,1024]{1,0:T(8,128)(2,1)S(1)} %slice.54), channel_id=1, source_target_pairs={{0,16},{8,24},{16,0},{24,8},{1,17},{9,25},{17,1},{25,9},{2,18},{10... | collective-permute-start | bytes 1179656 | tf_op jit(solution)/shard_map/ppermute | solution.py:61
  335.6 19.2 %collective-permute-start.66 = (bf16[152,1024]{1,0:T(8,128)(2,1)S(1)}, bf16[152,1024]{1,0:T(8,128)(2,1)S(1)}, u32[]{:S(2)}, u32[]{:S(2)}) collective-permute-start(bf16[152,1024]{1,0:T(8,128)(2,1)S(1)} %get-tuple-element.317), channel_id=1, source_target_pairs={{0,8},{8,0},{16,24},{24,16},{1,9},{9,1},{17,25},{25,17},{2,10},{10... | collective-permute-start | bytes 933896 | tf_op jit(solution)/shard_map/ppermute | solution.py:61
  340.4 17.5 %collective-permute-start.67 = (bf16[152,1024]{1,0:T(8,128)(2,1)S(1)}, bf16[152,1024]{1,0:T(8,128)(2,1)S(1)}, u32[]{:S(2)}, u32[]{:S(2)}) collective-permute-start(bf16[152,1024]{1,0:T(8,128)(2,1)S(1)} %get-tuple-element.318), channel_id=1, source_target_pairs={{0,16},{8,24},{16,0},{24,8},{1,17},{9,25},{17,1},{25,9},{2,18},{10... | collective-permute-start | bytes 933896 | tf_op jit(solution)/shard_map/ppermute | solution.py:61
  341.3 16.9 %collective-permute-start.68 = (bf16[152,1024]{1,0:T(8,128)(2,1)S(1)}, bf16[152,1024]{1,0:T(8,128)(2,1)S(1)}, u32[]{:S(2)}, u32[]{:S(2)}) collective-permute-start(bf16[152,1024]{1,0:T(8,128)(2,1)S(1)} %get-tuple-element.319), channel_id=1, source_target_pairs={{0,24},{8,16},{16,8},{24,0},{1,25},{9,17},{17,9},{25,1},{2,26},{10... | collective-permute-start | bytes 933896 | tf_op jit(solution)/shard_map/ppermute | solution.py:61
  349.7 12.3 %collective-permute-start.62 = (bf16[128,1024]{1,0:T(8,128)(2,1)}, bf16[128,1024]{1,0:T(8,128)(2,1)S(1)}, u32[]{:S(2)}, u32[]{:S(2)}) collective-permute-start(bf16[128,1024]{1,0:T(8,128)(2,1)} %slice.53), channel_id=1, source_target_pairs={{0,8},{8,0},{16,24},{24,16},{1,9},{9,1},{17,25},{25,17},{2,10},{10... | collective-permute-start | bytes 786440 | tf_op jit(solution)/shard_map/ppermute | solution.py:61
  364.5 15.2 %collective-permute-start.70 = (bf16[160,1024]{1,0:T(8,128)(2,1)}, bf16[160,1024]{1,0:T(8,128)(2,1)S(1)}, u32[]{:S(2)}, u32[]{:S(2)}) collective-permute-start(bf16[160,1024]{1,0:T(8,128)(2,1)} %bitcast.63), channel_id=1, source_target_pairs={{0,16},{8,24},{16,0},{24,8},{1,17},{9,25},{17,1},{25,9},{2,18},{10... | collective-permute-start | bytes 983048 | tf_op jit(solution)/shard_map/ppermute | solution.py:61
  365.2 14.6 %collective-permute-start.69 = (bf16[160,1024]{1,0:T(8,128)(2,1)}, bf16[160,1024]{1,0:T(8,128)(2,1)S(1)}, u32[]{:S(2)}, u32[]{:S(2)}) collective-permute-start(bf16[160,1024]{1,0:T(8,128)(2,1)} %bitcast.64), channel_id=1, source_target_pairs={{0,8},{8,0},{16,24},{24,16},{1,9},{9,1},{17,25},{25,17},{2,10},{10... | collective-permute-start | bytes 983048 | tf_op jit(solution)/shard_map/ppermute | solution.py:61
  (156 other events, 1134.0 us)
Sparse Core Ops, SparseCore 0:
  14.0 49.7 all-gather.6
  65.9 45.8 all-gather.8
  114.0 45.8 all-gather.10
  192.0 48.0 reduce-scatter.4
  242.8 25.2 reduce-scatter.6
  272.4 48.0 reduce-scatter.10
  325.3 36.7 reduce-scatter.8
